TPU v7x, 32 devices: a whole 2x2x4 slice. The times are simulated.
32 devices in a mesh: grp: 2 (over x), gz: 16 (over z, y, core).
Axes of the slice: x: 2, y: 2, z: 4, core: 2. Of those that a mesh axis runs over, the one named last changes fastest.
Arguments:
- vectors: bfloat16 [4, 384, 3, 16, 768], P('grp', None, None, 'gz'), parts along dimension 0, may hold values from -6 to 6
- links: float32 [4, 2, 3, 3, 16, 768], P('grp', None, None, None, 'gz'), parts along dimension 0, may hold values from -6 to 6
Outputs:
- elementals: float32 [384, 8, 384], P('gz', 'grp'), parts along dimension 1
There are 2 independent parts, one for each index of `grp`. A program takes and returns all parts, laid end to end along the dimension named above; each array names one. Nothing has to cross between parts.
All inputs are finite; a program needn't handle non-finite values.
Results may differ from a plain program's by a relative error of at most 0.008.
Values may be sent and summed in bfloat16 or wider, within the bound.
No kernel may reach another device: no remote copies, remote signals or barrier semaphores. Data moves between devices by JAX's collectives and lax.ppermute only.
A program may use at most 64 MiB of HBM per device.

v0:
```python
import math

import jax
import jax.numpy as jnp
from jax import lax
from jax.sharding import PartitionSpec as P

X = 64


def passed_along(block, axis, distance):
    devices = range(lax.axis_size(axis))
    route = [((i - distance) % len(devices), i) for i in devices]
    return lax.ppermute(block, axis, route)


def forward_hop(links_part, field):

    def contract(first, second):
        return jnp.einsum("ab...,vb...->va...", first, second)

    real_part = contract(links_part[0], field[0]) - contract(links_part[1], field[1])
    imag_part = contract(links_part[0], field[1]) + contract(links_part[1], field[0])
    return jnp.stack([real_part, imag_part], axis=0)


def roll_sites(array, amount, width):
    shape = array.shape
    reshaped = array.reshape(shape[:-1] + (shape[-1] // width, width))
    return jnp.roll(reshaped, amount, axis=-1).reshape(shape)


def elemental_block(left, right):
    rows = left.shape[1]
    cols = right.shape[1]
    left_flat = left.reshape(2, rows, -1)
    right_flat = right.reshape(2, cols, -1)

    def inner(first, second):
        return lax.dot_general(
            first, second, (((1,), (1,)), ((), ())), preferred_element_type=jnp.float32
        )

    real_part = inner(left_flat[0], right_flat[0]) + inner(left_flat[1], right_flat[1])
    imag_part = inner(left_flat[0], right_flat[1]) - inner(left_flat[1], right_flat[0])
    return jnp.stack([real_part, imag_part], axis=1)


def shards(vectors, links):
    slabs = lax.axis_size("gz")
    planes = vectors.shape[3]
    plane_sites = vectors.shape[4]
    scale = 1.0 / math.sqrt(12.0 * plane_sites * planes * slabs)
    links_x = links[:, 0]
    links_z = links[:, 1]
    face = passed_along(vectors, "gz", -1)
    after = jnp.concatenate([vectors[:, :, :, 1:planes], face], axis=3)
    here_float = vectors.astype(jnp.float32)
    disp_x = forward_hop(links_x, roll_sites(here_float, -1, X)).astype(jnp.bfloat16)
    disp_z = forward_hop(links_z, after.astype(jnp.float32)).astype(jnp.bfloat16)
    partial_value = jnp.concatenate(
        [elemental_block(vectors, disp_x), elemental_block(vectors, disp_z)], axis=1
    )
    signs = jnp.array([1.0, -1.0, 1.0, -1.0], jnp.float32).reshape(1, 4, 1)
    whole_term = partial_value - signs * jnp.transpose(partial_value, (2, 1, 0))
    summed = lax.psum_scatter(whole_term, "gz", scatter_dimension=0, tiled=True)
    return summed * scale


def solution(mesh):
    return jax.shard_map(
        shards,
        mesh=mesh,
        in_specs=(P("grp", None, None, "gz", None), P("grp", None, None, None, "gz", None)),
        out_specs=P("gz", "grp", None),
        check_vma=False,
    )
```

profile of v0, /device:TPU:0, one launch (start us, length us, event | category | flops | bytes accessed | tf_op | source)
XLA Modules:
  0.0 223.6 jit_solution(12509654232229319468)
XLA Ops:
  6.5 0.0 all-reduce.3.cloned.1.call-start
  6.5 5.4 %collective-permute-start = (bf16[2,384,3,1,768]{4,1,3,2,0:T(8,128)(2,1)}, bf16[2,384,3,1,768]{4,1,3,2,0:T(8,128)(2,1)}, u32[]{:S(2)}, u32[]{:S(2)}) collective-permute-start(bf16[2,384,3,1,768]{4,1,3,2,0:T(8,128)(2,1)} %param.3), channel_id=1, source_target_pairs={{1,0},{2,1},{3,2},{4,3},{5,4},{6,5},{7,6},{8,7},{9,8},{10,9},{11,1... | collective-permute-start | bytes 10616840 | tf_op jit(solution)/shard_map/ppermute | solution.py:14
  12.0 4.6 %copy.43 = bf16[2,384,3,1,768]{1,4,2,0,3:T(8,128)(2,1)S(1)} copy(bf16[2,384,3,1,768]{4,1,3,2,0:T(8,128)(2,1)} %param.3) | data formatting | bytes 7077888 | tf_op args[0]
  16.6 2.0 slice.90
  18.6 0.1 slice.91
  18.7 1.8 pad_maximum_fusion
  20.5 1.5 copy.46
  22.0 0.0 copy-done.19
  22.1 0.1 fusion.36
  22.1 0.6 copy.64
  22.8 4.4 %copy.44 = bf16[1,384,3,1,12,64]{1,2,5,4,3,0:T(4,128)(2,1)} copy(bf16[1,384,3,1,12,64]{1,5,4,2,0,3:T(8,128)(2,1)} %get-tuple-element.6) | data formatting | bytes 3538944 | tf_op jit(solution)/shard_map/slice | solution.py:22
  27.2 1.3 copy.65
  28.4 1.8 fusion.23
  30.2 0.0 copy-done
  30.2 0.1 copy-done.17
  30.3 3.2 %fusion.2 = bf16[384,3,768]{0,1,2:T(4,128)(2,1)} fusion(f32[768,384,3]{1,2,0:T(4,128)S(1)} %fusion.23, bf16[384,3,768]{0,1,2:T(4,128)(2,1)S(1)} %bitcast.144, bf16[1,1,3,3,1,768]{3,2,5,4,1,0:T(4,128)(2,1)S(1)} %copy-done.17), kind=kOutput, calls=%fused_computation.9 | convolution fusion | flops 7077888 | bytes 7091712 | tf_op jit(solution)/shard_map/ab...,vb...->va.../dot_general | solution.py:20
  33.5 5.3 %copy.51 = bf16[384,3,768]{2,0,1:T(8,128)(2,1)} copy(bf16[384,3,768]{0,1,2:T(4,128)(2,1)} %fusion.2) | data formatting | bytes 3538944 | tf_op jit(solution)/shard_map/reshape.79
  38.8 3.5 %fusion.25 = f32[768,384,3]{1,2,0:T(4,128)S(1)} fusion(bf16[384,3,768]{0,1,2:T(4,128)(2,1)} %bitcast.143, bf16[1,1,3,3,1,768]{3,2,5,4,1,0:T(4,128)(2,1)S(1)} %copy.64), kind=kOutput, calls=%fused_computation.32 | convolution fusion | flops 5308416 | bytes 5322240 | tf_op jit(solution)/shard_map/ab...,vb...->va.../dot_general | solution.py:20
  42.3 0.0 copy-done.18
  42.3 3.3 %fusion.1 = bf16[384,3,768]{0,1,2:T(4,128)(2,1)} fusion(f32[768,384,3]{1,2,0:T(4,128)S(1)} %fusion.25, bf16[384,3,768]{0,1,2:T(4,128)(2,1)S(1)} %bitcast.142, bf16[1,1,3,3,1,768]{3,2,5,4,1,0:T(4,128)(2,1)S(1)} %copy-done.18), kind=kOutput, calls=%fused_computation.8 | convolution fusion | flops 7077888 | bytes 7091712 | tf_op jit(solution)/shard_map/ab...,vb...->va.../dot_general | solution.py:20
  45.6 5.4 %copy.49 = bf16[384,3,768]{2,0,1:T(8,128)(2,1)} copy(bf16[384,3,768]{0,1,2:T(4,128)(2,1)} %fusion.1) | data formatting | bytes 3538944 | tf_op jit(solution)/shard_map/reshape.77
  51.0 0.6 copy.69
  51.6 1.3 copy.67
  52.9 0.0 copy-done.11
  52.9 2.7 %convolution_bitcast_fusion.6 = f32[384,384]{1,0:T(8,128)S(1)} fusion(bf16[384,3,768]{2,0,1:T(8,128)(2,1)S(1)} %copy-done.11, bf16[2,384,3,1,768]{4,1,2,3,0:T(8,128)(2,1)} %bitcast.145), kind=kOutput, calls=%fused_computation.40 | convolution fusion | flops 679477248 | bytes 4128768 | tf_op jit(solution)/shard_map/dot_general | solution.py:40
  55.6 0.0 copy-done.3
  55.6 0.3 copy-done.13
  56.0 1.1 convolution_bitcast_fusion.4
  57.1 1.9 fusion.28
  59.0 1.9 fusion.30
  60.9 0.0 collective-permute-done
  60.9 4.0 %fusion.35 = (bf16[1,384,3,1,768]{4,1,3,2,0:T(8,128)(2,1)}, bf16[1,384,3,1,768]{4,1,3,2,0:T(8,128)(2,1)}) fusion(bf16[2,384,3,1,768]{4,1,3,2,0:T(8,128)(2,1)} %collective-permute-done), kind=kLoop, calls=%fused_computation.51 | loop fusion | bytes 7077888 | tf_op jit(solution)/shard_map/slice | solution.py:22
  65.0 4.0 %copy.66 = bf16[1,384,3,1,768]{1,2,4,3,0:T(4,128)(2,1)S(1)} copy(bf16[1,384,3,1,768]{4,1,3,2,0:T(8,128)(2,1)} %get-tuple-element.7) | data formatting | bytes 3538944
  68.9 5.2 %copy.68 = bf16[1,384,3,1,768]{1,2,4,3,0:T(4,128)(2,1)} copy(bf16[1,384,3,1,768]{4,1,3,2,0:T(8,128)(2,1)} %get-tuple-element.8) | data formatting | bytes 3538944
  74.1 1.8 fusion.9
  75.9 0.0 copy-done.1
  75.9 0.0 copy-start.15
  75.9 3.9 %fusion.7 = f32[768,384,3]{1,2,0:T(4,128)} fusion(bf16[1,384,3,1,768]{1,2,4,3,0:T(4,128)(2,1)S(1)} %copy-done.1, bf16[1,1,3,3,1,768]{3,2,5,4,1,0:T(4,128)(2,1)S(1)} %copy.69), kind=kOutput, calls=%fused_computation.16 | convolution fusion | flops 5308416 | bytes 5322240 | tf_op jit(solution)/shard_map/ab...,vb...->va.../dot_general | solution.py:20
  79.9 0.0 copy-done.15
  79.9 3.2 %fusion.4 = bf16[384,3,768]{0,1,2:T(4,128)(2,1)} fusion(f32[768,384,3]{1,2,0:T(4,128)S(1)} %fusion.9, bf16[1,384,3,1,768]{1,2,4,3,0:T(4,128)(2,1)S(1)} %copy-done.1, bf16[1,1,3,3,1,768]{3,2,5,4,1,0:T(4,128)(2,1)S(1)} %copy-done.15), kind=kOutput, calls=%fused_computation.11 | convolution fusion | flops 7077888 | bytes 7091712 | tf_op jit(solution)/shard_map/ab...,vb...->va.../dot_general | solution.py:20
  83.1 5.3 %copy.59 = bf16[384,3,768]{2,0,1:T(8,128)(2,1)} copy(bf16[384,3,768]{0,1,2:T(4,128)(2,1)} %fusion.4) | data formatting | bytes 3538944 | tf_op jit(solution)/shard_map/reshape.99
  88.4 4.1 %convolution_bitcast_fusion.2 = f32[384,384]{1,0:T(8,128)} fusion(bf16[384,3,768]{2,0,1:T(8,128)(2,1)} %copy.59, bf16[2,384,3,1,768]{4,1,2,3,0:T(8,128)(2,1)} %bitcast.146), kind=kOutput, calls=%fused_computation.36 | convolution fusion | flops 679477248 | bytes 4128768 | tf_op jit(solution)/shard_map/dot_general | solution.py:40
  92.4 0.0 copy-done.2
  92.4 0.0 copy-done.16
  92.5 3.3 %fusion.3 = bf16[384,3,768]{0,1,2:T(4,128)(2,1)} fusion(f32[768,384,3]{1,2,0:T(4,128)S(1)} %copy-done.2, bf16[1,384,3,1,768]{1,2,4,3,0:T(4,128)(2,1)S(1)} %copy.66, bf16[1,1,3,3,1,768]{3,2,5,4,1,0:T(4,128)(2,1)S(1)} %copy-done.16), kind=kOutput, calls=%fused_computation.10 | convolution fusion | flops 7077888 | bytes 7091712 | tf_op jit(solution)/shard_map/ab...,vb...->va.../dot_general | solution.py:20
  95.8 5.4 %copy.58 = bf16[384,3,768]{2,0,1:T(8,128)(2,1)} copy(bf16[384,3,768]{0,1,2:T(4,128)(2,1)} %fusion.3) | data formatting | bytes 3538944 | tf_op jit(solution)/shard_map/reshape.97
  101.2 2.7 %convolution_bitcast_fusion = f32[384,384]{1,0:T(8,128)S(1)} fusion(bf16[384,3,768]{2,0,1:T(8,128)(2,1)} %copy.58, bf16[2,384,3,1,768]{4,1,2,3,0:T(8,128)(2,1)S(1)} %bitcast.150), kind=kOutput, calls=%fused_computation.34 | convolution fusion | flops 679477248 | bytes 4128768 | tf_op jit(solution)/shard_map/dot_general | solution.py:40
  104.0 1.1 fusion.32
  105.1 0.4 copy-done.12
  105.5 1.1 fusion.34
  106.6 0.8 copy-done.10
  107.4 0.0 copy-done.5
  107.4 1.6 pad_maximum_fusion.1
  109.0 2.1 copy.62
  111.2 0.0 copy-done.6
  111.2 0.0 copy-done.8
  111.2 0.0 copy-done.20
  111.2 3.0 %bitcast_subtract_fusion = f32[384,4,384]{0,2,1:T(8,128)} fusion(f32[384,4,384]{2,0,1:T(8,128)S(1)} %copy.62, f32[4]{0:T(128)S(1)} %copy-done.20, f32[384,1,384]{0,2,1:T(8,128)} %copy-done.10, f32[384,1,384]{0,2,1:T(8,128)} %copy-done.9, f32[384,1,384]{0,2,1:T(8,128)S(1)} %copy-done.8, f32[384,1,384]{0,2,1:T(8,128)S(1)} %copy-done.6), kind=kLoop, calls=%fused_computation.13 | loop fusion | flops 2949120 | bytes 7077904 | tf_op jit(solution)/shard_map/sub | solution.py:65
  114.2 4.3 %copy.63 = f32[384,4,384]{2,1,0:T(4,128)} copy(f32[384,4,384]{0,2,1:T(8,128)} %bitcast_subtract_fusion) | data formatting | bytes 4718592 | tf_op jit(solution)/shard_map/sub | solution.py:65
  118.4 0.0 all-reduce.3.cloned.1.call-update
  118.5 0.6 copy-done.21
  119.1 0.6 dynamic-slice
  120.3 94.8 %all-reduce.3.cloned.1.call-done = f32[384,4,384]{2,1,0:T(4,128)} async-done(((f32[384,4,384]{2,1,0:T(4,128)}), f32[384,4,384]{2,1,0:T(4,128)}) %all-reduce.3.cloned.1.call-update) | async-done | bytes 2359312
  215.1 1.6 dynamic-slice_multiply_fusion
  (27 shorter events, 0.0 us)
Async XLA Ops:
  6.5 208.6 %all-reduce.3.cloned.1.call-start = ((), (), s32[]{:S(2)}) async-start(), calls=%async_computation | async-start | bytes 4718592
  6.5 54.4 %collective-permute-start = (bf16[2,384,3,1,768]{4,1,3,2,0:T(8,128)(2,1)}, bf16[2,384,3,1,768]{4,1,3,2,0:T(8,128)(2,1)}, u32[]{:S(2)}, u32[]{:S(2)}) collective-permute-start(bf16[2,384,3,1,768]{4,1,3,2,0:T(8,128)(2,1)} %param.3), channel_id=1, source_target_pairs={{1,0},{2,1},{3,2},{4,3},{5,4},{6,5},{7,6},{8,7},{9,8},{10,9},{11,1... | collective-permute-start | bytes 10616840 | tf_op jit(solution)/shard_map/ppermute | solution.py:14
  20.5 1.5 copy-start.19
  28.4 1.8 copy-start
  28.4 1.8 copy-start.17
  38.8 3.5 %copy-start.18 = (bf16[1,1,3,3,1,768]{3,2,5,4,1,0:T(4,128)(2,1)S(1)}, bf16[1,1,3,3,1,768]{3,2,5,4,1,0:T(4,128)(2,1)}, u32[]{:S(2)}) copy-start(bf16[1,1,3,3,1,768]{3,2,5,4,1,0:T(4,128)(2,1)} %copy.65) | copy-start | bytes 41476
  45.6 7.3 %copy-start.11 = (bf16[384,3,768]{2,0,1:T(8,128)(2,1)S(1)}, bf16[384,3,768]{2,0,1:T(8,128)(2,1)}, u32[]{:S(2)}) copy-start(bf16[384,3,768]{2,0,1:T(8,128)(2,1)} %copy.51) | copy-start | bytes 5308420
  52.9 2.7 %copy-start.3 = (bf16[2,384,3,1,768]{4,1,3,2,0:T(8,128)(2,1)S(1)}, bf16[2,384,3,1,768]{4,1,3,2,0:T(8,128)(2,1)}, u32[]{:S(2)}) copy-start(bf16[2,384,3,1,768]{4,1,3,2,0:T(8,128)(2,1)} %param.3) | copy-start | bytes 10616836
  52.9 3.1 %copy-start.13 = (bf16[384,3,768]{2,0,1:T(8,128)(2,1)S(1)}, bf16[384,3,768]{2,0,1:T(8,128)(2,1)}, u32[]{:S(2)}) copy-start(bf16[384,3,768]{2,0,1:T(8,128)(2,1)} %copy.49) | copy-start | bytes 5308420
  74.1 1.8 copy-start.1
  75.9 4.0 %copy-start.15 = (bf16[1,1,3,3,1,768]{3,2,5,4,1,0:T(4,128)(2,1)S(1)}, bf16[1,1,3,3,1,768]{3,2,5,4,1,0:T(4,128)(2,1)}, u32[]{:S(2)}) copy-start(bf16[1,1,3,3,1,768]{3,2,5,4,1,0:T(4,128)(2,1)} %copy.67) | copy-start | bytes 41476
  88.4 4.1 %copy-start.2 = (f32[768,384,3]{1,2,0:T(4,128)S(1)}, f32[768,384,3]{1,2,0:T(4,128)}, u32[]{:S(2)}) copy-start(f32[768,384,3]{1,2,0:T(4,128)} %fusion.7) | copy-start | bytes 10616836
  88.4 4.1 %copy-start.16 = (bf16[1,1,3,3,1,768]{3,2,5,4,1,0:T(4,128)(2,1)S(1)}, bf16[1,1,3,3,1,768]{3,2,5,4,1,0:T(4,128)(2,1)}, u32[]{:S(2)}) copy-start(bf16[1,1,3,3,1,768]{3,2,5,4,1,0:T(4,128)(2,1)} %copy.67) | copy-start | bytes 41476
  95.8 5.4 %copy-start.4 = (bf16[2,384,3,1,768]{4,1,3,2,0:T(8,128)(2,1)S(1)}, bf16[2,384,3,1,768]{4,1,3,2,0:T(8,128)(2,1)}, u32[]{:S(2)}) copy-start(bf16[2,384,3,1,768]{4,1,3,2,0:T(8,128)(2,1)} %param.3) | copy-start | bytes 10616836
  101.2 2.7 %copy-start.14 = (bf16[384,3,768]{2,0,1:T(8,128)(2,1)S(1)}, bf16[384,3,768]{2,0,1:T(8,128)(2,1)}, u32[]{:S(2)}) copy-start(bf16[384,3,768]{2,0,1:T(8,128)(2,1)} %copy.58) | copy-start | bytes 5308420
  101.2 2.7 %copy-start.22 = (f32[384,384]{1,0:T(8,128)S(1)}, f32[384,384]{1,0:T(8,128)}, u32[]{:S(2)}) copy-start(f32[384,384]{1,0:T(8,128)} %convolution_bitcast_fusion.2) | copy-start | bytes 1769476
  104.0 1.5 copy-start.12
  105.5 1.1 copy-start.9
  105.5 2.0 copy-start.5
  105.5 2.0 copy-start.7
  106.6 0.8 copy-start.10
  109.0 2.1 copy-start.6
  109.0 2.2 copy-start.8
  109.0 2.2 copy-start.20
  118.4 0.7 copy-start.21
Sparse Core Ops, SparseCore 0:
  118.6 96.5 all-reduce.2
where the time goes:
time: 225 us; the launch traced here: 224 us
  waiting for transfers between devices  94.8 us (42%)
  local copies, waits for them, and re-layouts  60.3 us (27%)
  matrix products  40.7 us (18%)
  between operations  14.3 us (6%)
  other arithmetic  8.02 us (4%)
  starting transfers between devices  5.45 us (2%)
    unnamed x2, waiting for transfers between devices  94.8 us
    dot_general x8, matrix products, contract(): return jnp.einsum('ab...,vb...->va...', first, second)  24 us
    another operation x4, local copies, waits for them, and re-layouts  21.4 us
    unnamed x54, local copies, waits for them, and re-layouts  20.3 us
    dot_general x8, matrix products, inner(): lax.dot_general(first, second, (((1,), (1,)), ((), ())), preferred_elemen...  16.7 us
    slice x2, local copies, waits for them, and re-layouts, forward_hop(): field[0]  8.44 us
    ppermute x1, starting transfers between devices, passed_along(): return lax.ppermute(block, axis, route)  5.44 us
  transfers between devices with their start and end apart: 2, of which 1 were waited for; matrix products, arithmetic and copies ran while one was open for 22% of the time, Pallas kernels for 0%

commit v1 on v0

v1 whole, which is shorter than its diff:
```python
import functools
import math

import jax
import jax.numpy as jnp
from jax import lax
from jax.experimental import pallas as pl
from jax.experimental.pallas import tpu as pltpu
from jax.sharding import PartitionSpec as P

X = 64
LANES = 128
ROWS = 16


def passed_along(block, axis, distance):
    devices = range(lax.axis_size(axis))
    route = [((i - distance) % len(devices), i) for i in devices]
    return lax.ppermute(block, axis, route)


def displace(field_ref, u_ref, d_ref, roll):
    count, sites = field_ref.shape[1:]
    for t in range(sites // LANES):
        lanes = slice(t * LANES, (t + 1) * LANES)

        def link(part, a, b):
            row = (part * 3 + a) * 3 + b
            return jnp.broadcast_to(u_ref[row : row + 1, lanes], (ROWS, LANES))

        u = [[[link(p, a, b) for b in range(3)] for a in range(3)] for p in range(2)]
        if roll:
            lane = lax.broadcasted_iota(jnp.int32, (ROWS, LANES), 1)
            last = (lane & (X - 1)) == X - 1

        def body(m, carry):
            rows = pl.ds(pl.multiple_of(m * ROWS, ROWS), ROWS)
            v = []
            for k in range(6):
                value = field_ref[k, rows, lanes].astype(jnp.float32)
                if roll:
                    ahead = pltpu.roll(value, LANES - 1, 1)
                    around = pltpu.roll(value, X - 1, 1)
                    value = jnp.where(last, around, ahead)
                v.append(value)
            re, im = v[:3], v[3:]
            for a in range(3):
                ur, ui = u[0][a], u[1][a]
                dr = ur[0] * re[0] - ui[0] * im[0]
                di = ur[0] * im[0] + ui[0] * re[0]
                for b in (1, 2):
                    dr = dr + (ur[b] * re[b] - ui[b] * im[b])
                    di = di + (ur[b] * im[b] + ui[b] * re[b])
                d_ref[a, rows, lanes] = dr.astype(jnp.bfloat16)
                rows_i = pl.ds(pl.multiple_of(count + m * ROWS, ROWS), ROWS)
                d_ref[a, rows_i, lanes] = di.astype(jnp.bfloat16)
            return carry

        lax.fori_loop(0, count // ROWS, body, 0, unroll=2)


def kernel(roll, own, left_ref, *refs):
    if roll:
        u_ref, out_ref, d_ref = refs
        field_ref = left_ref
    else:
        field_ref, u_ref, out_ref, d_ref = refs
    count = left_ref.shape[1]
    displace(field_ref, u_ref, d_ref, roll)

    def inner(part):
        total = None
        for a in range(3):
            term = lax.dot_general(
                left_ref[part * 3 + a], d_ref[a], (((1,), (1,)), ((), ())),
                preferred_element_type=jnp.float32,
            )
            total = term if total is None else total + term
        return total

    from_re, from_im = inner(0), inner(1)
    sum_re = from_re[:, :count] + from_im[:, count:]
    sum_im = from_re[:, count:] - from_im[:, :count]
    re = sum_re - sum_re.T
    im = sum_im + sum_im.T
    if own % 8 == 0:
        for g in range(count // own):
            rows = slice(g * own, (g + 1) * own)
            both = jnp.concatenate([re[rows], im[rows]], axis=0)
            out_ref[g] = both.astype(jnp.bfloat16)
    else:
        out_ref[0] = re.astype(jnp.bfloat16)
        out_ref[1] = im.astype(jnp.bfloat16)


def direction(left, field, u, slabs):
    count, sites = left.shape[1:]
    own = count // slabs
    roll = field is None
    blocks = (slabs, 2 * own, count) if own % 8 == 0 else (2, count, count)
    operands = (left, u) if roll else (left, field, u)
    out = pl.pallas_call(
        functools.partial(kernel, roll, own),
        out_shape=jax.ShapeDtypeStruct(blocks, jnp.bfloat16),
        in_specs=[pl.BlockSpec(memory_space=pltpu.VMEM)] * len(operands),
        out_specs=pl.BlockSpec(memory_space=pltpu.VMEM),
        scratch_shapes=[pltpu.VMEM((3, 2 * count, sites), jnp.bfloat16)],
        compiler_params=pltpu.CompilerParams(vmem_limit_bytes=40 * 2**20),
        cost_estimate=pl.CostEstimate(
            flops=8 * count * count * 3 * sites,
            bytes_accessed=4 * 6 * count * sites,
            transcendentals=0,
        ),
    )(*operands)
    if own % 8 != 0:
        out = out.reshape(2, slabs, own, count).transpose(1, 0, 2, 3).reshape(slabs, 2 * own, count)
    return out


def shards(vectors, links):
    slabs = lax.axis_size("gz")
    count, planes, sites = vectors.shape[1], vectors.shape[3], vectors.shape[4]
    assert planes == 1
    own = count // slabs
    scale = 1.0 / math.sqrt(12.0 * sites * planes * slabs)
    field = jnp.transpose(vectors, (0, 2, 3, 1, 4)).reshape(6, count, sites)
    face = passed_along(field, "gz", -1)
    links_x = links[:, 0].reshape(18, sites)
    links_z = links[:, 1].reshape(18, sites)
    term_x = direction(field, None, links_x, slabs)
    got_x = lax.all_to_all(term_x, "gz", 0, 0)
    term_z = direction(field, face, links_z, slabs)
    got_z = lax.all_to_all(term_z, "gz", 0, 0)

    def total(got):
        return jnp.sum(got.astype(jnp.float32), axis=0).reshape(2, own, count)

    both = jnp.concatenate([total(got_x), total(got_z)], axis=0)
    return jnp.transpose(both, (1, 0, 2)) * scale


def solution(mesh):
    return jax.shard_map(
        shards,
        mesh=mesh,
        in_specs=(P("grp", None, None, "gz", None), P("grp", None, None, None, "gz", None)),
        out_specs=P("gz", "grp", None),
        check_vma=False,
    )
```

time: 225 us -> 83.9 us (0.37)
  waiting for transfers between devices: 94.8 us -> 39.9 us
  local copies, waits for them, and re-layouts: 60.3 us -> 5.92 us
  matrix products: 40.7 us -> 0 us
  Pallas kernels: 0 us -> 22.4 us
  between operations: 14.3 us -> 0.06 us
  starting transfers between devices: 5.45 us -> 15 us
  other arithmetic: 8.02 us -> 0.19 us
    unnamed x2 -> x0, waiting for transfers between devices: 94.8 us -> none
    dot_general x16 -> x0, matrix products: 40.7 us -> none  [the longest x8 24 us: contract(): return jnp.einsum('ab...,vb...->va...', first, second)]
    ppermute x1, waiting for transfers between devices: 0.01 us -> 24.4 us  [passed_along(): return lax.ppermute(block, axis, route)]
    pallas_call x0 -> x2, Pallas kernels: none -> 22.4 us  [direction(): pl.pallas_call(functools.partial(kernel, roll, own), out_shape=jax.ShapeD...]
    another operation x4 -> x2, local copies, waits for them, and re-layouts: 21.4 us -> 0.06 us  [the longest x1 0.03 us: shards(): links_x = links[:, 0].reshape(18, sites)]
    unnamed x54 -> x4, local copies, waits for them, and re-layouts: 20.3 us -> 4 us
    all_to_all x0 -> x2, waiting for transfers between devices: none -> 15.5 us  [the longest x1 15.5 us: shards(): got_z = lax.all_to_all(term_z, 'gz', 0, 0)]
    slice x6 -> x1, local copies, waits for them, and re-layouts: 12.1 us -> 1.16 us  [shards(): links_x = links[:, 0].reshape(18, sites)]
  transfers between devices with their start and end apart: 2 -> 3, of which waited for: 1 -> 2; matrix products, arithmetic and copies ran while one was open for 22% -> 2% of each run, Pallas kernels for 0% -> 27%
where the time goes in v1:
time: 83.9 us; the launch traced here: 83.5 us
  waiting for transfers between devices  39.9 us (48%)
  Pallas kernels  22.4 us (27%)
  starting transfers between devices  15 us (18%)
  local copies, waits for them, and re-layouts  5.92 us (7%)
    ppermute x1, waiting for transfers between devices, passed_along(): return lax.ppermute(block, axis, route)  24.4 us
    pallas_call x2, Pallas kernels, direction(): pl.pallas_call(functools.partial(kernel, roll, own), out_shape=jax.ShapeD...  22.4 us
    all_to_all x1, waiting for transfers between devices, shards(): got_z = lax.all_to_all(term_z, 'gz', 0, 0)  15.5 us
    all_to_all x1, starting transfers between devices, shards(): got_z = lax.all_to_all(term_z, 'gz', 0, 0)  5.99 us
    ppermute x1, starting transfers between devices, passed_along(): return lax.ppermute(block, axis, route)  5.44 us
    unnamed x4, local copies, waits for them, and re-layouts  4 us
    all_to_all x1, starting transfers between devices, shards(): got_x = lax.all_to_all(term_x, 'gz', 0, 0)  3.58 us
  transfers between devices with their start and end apart: 3, of which 2 were waited for; matrix products, arithmetic and copies ran while one was open for 2% of the time, Pallas kernels for 27%

profile of v1, /device:TPU:0, one launch (start us, length us, event | category | flops | bytes accessed | tf_op | source)
XLA Modules:
  0.0 83.5 jit_solution(14877987218327159795)
XLA Ops:
  0.0 5.4 %collective-permute-start = (bf16[6,384,768]{2,1,0:T(8,128)(2,1)}, bf16[6,384,768]{2,1,0:T(8,128)(2,1)}, u32[]{:S(2)}, u32[]{:S(2)}) collective-permute-start(bf16[6,384,768]{2,1,0:T(8,128)(2,1)} %bitcast.7), channel_id=1, source_target_pairs={{1,0},{2,1},{3,2},{4,3},{5,4},{6,5},{7,6},{8,7},{9,8},{10,9},{11,1... | collective-permute-start | bytes 10616840 | tf_op jit(solution)/shard_map/ppermute | solution.py:19
  5.4 1.2 %slice_reduce_fusion.1 = (f32[2,3,3,768]{3,2,1,0:T(4,128)S(1)}, f32[2,3,3,768]{3,2,1,0:T(4,128)S(1)}) fusion(f32[2,2,3,3,1,768]{5,4,3,2,1,0:T(1,128)} %param.3), kind=kLoop, calls=%fused_computation.5 | loop fusion | bytes 221184 | tf_op jit(solution)/shard_map/slice | solution.py:128
  6.6 0.0 copy-start
  6.7 2.0 %copy-done = bf16[2,384,3,1,768]{4,1,3,2,0:T(8,128)(2,1)S(1)} copy-done((bf16[2,384,3,1,768]{4,1,3,2,0:T(8,128)(2,1)S(1)}, bf16[2,384,3,1,768]{4,1,3,2,0:T(8,128)(2,1)}, u32[]{:S(2)}) %copy-start) | copy-done | bytes 3538968
  8.7 12.9 %shard_map.28 = bf16[16,48,384]{2,1,0:T(8,128)(2,1)} custom-call(bf16[6,384,768]{2,1,0:T(8,128)(2,1)S(1)} %bitcast.8, f32[18,768]{1,0:T(8,128)S(1)} %reshape_squeeze.6.refs_0_), custom_call_target="tpu_custom_call" | custom-call | flops 2717908992 | bytes 7077888 | tf_op jit(solution)/shard_map/pallas_call | solution.py:102
  21.5 3.6 %all-to-all-start = ((bf16[16,48,384]{2,1,0:T(8,128)(2,1)}), bf16[16,48,384]{2,1,0:T(8,128)(2,1)S(1)}, u32[]{:S(2)}, u32[]{:S(2)}) async-start(bf16[16,48,384]{2,1,0:T(8,128)(2,1)} %shard_map.28), calls=%async_computation | async-start | bytes 1179648 | tf_op jit(solution)/shard_map/all_to_all | solution.py:131
  25.2 24.4 %collective-permute-done.refs_0_ = bf16[6,384,768]{2,1,0:T(8,128)(2,1)} collective-permute-done((bf16[6,384,768]{2,1,0:T(8,128)(2,1)}, bf16[6,384,768]{2,1,0:T(8,128)(2,1)}, u32[]{:S(2)}, u32[]{:S(2)}) %collective-permute-start) | collective-permute-done | bytes 3538976 | tf_op jit(solution)/shard_map/ppermute | solution.py:19
  49.5 0.0 copy-start.1
  49.5 2.0 %copy-done.1 = bf16[2,384,3,1,768]{4,1,3,2,0:T(8,128)(2,1)S(1)} copy-done((bf16[2,384,3,1,768]{4,1,3,2,0:T(8,128)(2,1)S(1)}, bf16[2,384,3,1,768]{4,1,3,2,0:T(8,128)(2,1)}, u32[]{:S(2)}) %copy-start.1) | copy-done | bytes 3538968
  51.5 9.6 %shard_map.29 = bf16[16,48,384]{2,1,0:T(8,128)(2,1)} custom-call(bf16[6,384,768]{2,1,0:T(8,128)(2,1)S(1)} %bitcast.9, bf16[6,384,768]{2,1,0:T(8,128)(2,1)} %collective-permute-done.refs_0_, f32[18,768]{1,0:T(8,128)S(1)} %reshape_squeeze.7.refs_1_), custom_call_target="tpu_custom_call" | custom-call | flops 2717908992 | bytes 7077888 | tf_op jit(solution)/shard_map/pallas_call | solution.py:102
  61.1 0.0 all-to-all-done
  61.1 6.0 %all-to-all-start.1 = ((bf16[16,48,384]{2,1,0:T(8,128)(2,1)}), bf16[16,48,384]{2,1,0:T(8,128)(2,1)S(1)}, u32[]{:S(2)}, u32[]{:S(2)}) async-start(bf16[16,48,384]{2,1,0:T(8,128)(2,1)} %shard_map.29), calls=%async_computation.1 | async-start | bytes 1179648 | tf_op jit(solution)/shard_map/all_to_all | solution.py:133
  67.1 0.1 convert_reduce_fusion.1
  67.2 15.5 %all-to-all-done.1 = bf16[16,48,384]{2,1,0:T(8,128)(2,1)S(1)} async-done(((bf16[16,48,384]{2,1,0:T(8,128)(2,1)}), bf16[16,48,384]{2,1,0:T(8,128)(2,1)S(1)}, u32[]{:S(2)}, u32[]{:S(2)}) %all-to-all-start.1) | async-done | bytes 589856 | tf_op jit(solution)/shard_map/all_to_all | solution.py:133
  82.7 0.1 convert_reduce_fusion
  82.8 0.7 copy.3
  (3 shorter events, 0.1 us)
Async XLA Ops:
  0.0 49.5 %collective-permute-start = (bf16[6,384,768]{2,1,0:T(8,128)(2,1)}, bf16[6,384,768]{2,1,0:T(8,128)(2,1)}, u32[]{:S(2)}, u32[]{:S(2)}) collective-permute-start(bf16[6,384,768]{2,1,0:T(8,128)(2,1)} %bitcast.7), channel_id=1, source_target_pairs={{1,0},{2,1},{3,2},{4,3},{5,4},{6,5},{7,6},{8,7},{9,8},{10,9},{11,1... | collective-permute-start | bytes 10616840 | tf_op jit(solution)/shard_map/ppermute | solution.py:19
  6.6 2.0 %copy-start = (bf16[2,384,3,1,768]{4,1,3,2,0:T(8,128)(2,1)S(1)}, bf16[2,384,3,1,768]{4,1,3,2,0:T(8,128)(2,1)}, u32[]{:S(2)}) copy-start(bf16[2,384,3,1,768]{4,1,3,2,0:T(8,128)(2,1)} %param.2) | copy-start | bytes 10616836
  21.5 39.6 %all-to-all-start = ((bf16[16,48,384]{2,1,0:T(8,128)(2,1)}), bf16[16,48,384]{2,1,0:T(8,128)(2,1)S(1)}, u32[]{:S(2)}, u32[]{:S(2)}) async-start(bf16[16,48,384]{2,1,0:T(8,128)(2,1)} %shard_map.28), calls=%async_computation | async-start | bytes 1179648 | tf_op jit(solution)/shard_map/all_to_all | solution.py:131
  49.5 2.0 %copy-start.1 = (bf16[2,384,3,1,768]{4,1,3,2,0:T(8,128)(2,1)S(1)}, bf16[2,384,3,1,768]{4,1,3,2,0:T(8,128)(2,1)}, u32[]{:S(2)}) copy-start(bf16[2,384,3,1,768]{4,1,3,2,0:T(8,128)(2,1)} %param.2) | copy-start | bytes 10616836
  61.1 21.5 %all-to-all-start.1 = ((bf16[16,48,384]{2,1,0:T(8,128)(2,1)}), bf16[16,48,384]{2,1,0:T(8,128)(2,1)S(1)}, u32[]{:S(2)}, u32[]{:S(2)}) async-start(bf16[16,48,384]{2,1,0:T(8,128)(2,1)} %shard_map.29), calls=%async_computation.1 | async-start | bytes 1179648 | tf_op jit(solution)/shard_map/all_to_all | solution.py:133

commit v2 on v1

v2 whole, which is shorter than its diff:
```python
import functools
import math

import jax
import jax.numpy as jnp
from jax import lax
from jax.experimental import pallas as pl
from jax.experimental.pallas import tpu as pltpu
from jax.sharding import PartitionSpec as P

X = 64
LANES = 128
ROWS = 16
CHUNKS = 3


def passed_along(block, axis, distance):
    devices = range(lax.axis_size(axis))
    route = [((i - distance) % len(devices), i) for i in devices]
    return lax.ppermute(block, axis, route)


def swapped(block, axis):
    return lax.ppermute(block, axis, [(i, i ^ 1) for i in range(lax.axis_size(axis))])


def displace(field_ref, u_ref, d_ref, roll):
    sites = field_ref.shape[2]
    count = d_ref.shape[0] // 2
    half = ROWS // 2
    for t in range(sites // LANES):
        lanes = slice(t * LANES, (t + 1) * LANES)

        def link(part, a, b):
            row = (part * 3 + a) * 3 + b
            return jnp.broadcast_to(u_ref[row : row + 1, lanes], (half, LANES))

        u = [[[link(p, a, b) for b in range(3)] for a in range(3)] for p in range(2)]
        if roll:
            lane = lax.broadcasted_iota(jnp.int32, (ROWS, LANES), 1)
            last = (lane & (X - 1)) == X - 1

        def body(m, carry):
            rows = pl.ds(pl.multiple_of(m * ROWS, ROWS), ROWS)
            v = []
            for k in range(6):
                value = field_ref[k, rows, lanes].astype(jnp.float32)
                if roll:
                    ahead = pltpu.roll(value, LANES - 1, 1)
                    around = pltpu.roll(value, X - 1, 1)
                    value = jnp.where(last, around, ahead)
                v.append((value[:half], value[half:]))
            for a in range(3):
                ur, ui = u[0][a], u[1][a]
                outs_r, outs_i = [], []
                for h in range(2):
                    re = [v[b][h] for b in range(3)]
                    im = [v[3 + b][h] for b in range(3)]
                    dr = ur[0] * re[0] - ui[0] * im[0]
                    di = ur[0] * im[0] + ui[0] * re[0]
                    for b in (1, 2):
                        dr = dr + (ur[b] * re[b] - ui[b] * im[b])
                        di = di + (ur[b] * im[b] + ui[b] * re[b])
                    outs_r.append(dr)
                    outs_i.append(di)
                columns = slice(a * sites + t * LANES, a * sites + (t + 1) * LANES)
                to_r = pl.ds(pl.multiple_of(m * ROWS, ROWS), ROWS)
                to_i = pl.ds(pl.multiple_of(count + m * ROWS, ROWS), ROWS)
                d_ref[to_r, columns] = jnp.concatenate(outs_r, axis=0).astype(jnp.bfloat16)
                d_ref[to_i, columns] = jnp.concatenate(outs_i, axis=0).astype(jnp.bfloat16)
            return carry

        lax.fori_loop(0, count // ROWS, body, 0, unroll=2)


def kernel(roll, first, last, start, odd_ref, *refs):
    refs = list(refs)
    left_hbm = refs.pop(0)
    face_ref = None if roll else refs.pop(0)
    u_ref = refs.pop(0)
    acc_hbm = None if first else refs.pop(0)
    outs = [refs.pop(0) for _ in range(2 if last else 1)]
    left, d_ref, acc, sems = refs[:4]
    count, sites = left_hbm.shape[1:]
    n = d_ref.shape[0] // 2
    j = slice(start, start + n)

    if roll:
        face_ref = refs[4]
        copy_field = pltpu.make_async_copy(left_hbm, face_ref, sems.at[0])
        copy_field.start()
    copies = []
    for part in range(2):
        for a in range(3):
            to = left.at[pl.ds(part * count, count), pl.ds(a * sites, sites)]
            k = part * 3 + a
            copies.append(pltpu.make_async_copy(left_hbm.at[k], to, sems.at[1 + k]))
    if not first:
        copies.append(pltpu.make_async_copy(acc_hbm, acc, sems.at[7]))
    for copy in copies:
        copy.start()
    if roll:
        copy_field.wait()
    displace(face_ref, u_ref, d_ref, roll)
    for copy in copies:
        copy.wait()

    product = lax.dot_general(
        left[...], d_ref[...], (((1,), (1,)), ((), ())), preferred_element_type=jnp.float32
    )
    sum_re = product[:count, :n] + product[count:, n:]
    sum_im = product[:count, n:] - product[count:, :n]
    if n == count:
        acc[0] = sum_re - sum_re.T
        acc[1] = sum_im + sum_im.T
    else:
        if first:
            acc[...] = jnp.zeros_like(acc)
        acc[0, :, j] += sum_re
        acc[1, :, j] += sum_im
        acc[0, j, :] -= sum_re.T
        acc[1, j, :] += sum_im.T
    if last:
        send, keep = outs
        odd = odd_ref[0]
        send[...] = acc[1 - odd].astype(jnp.bfloat16)
        keep[...] = acc[odd]
    else:
        outs[0][...] = acc[...]


def direction(odd, left, field, u, acc, start, n, last):
    count, sites = left.shape[1:]
    roll = field is None
    first = acc is None
    operands = [odd, left] + ([] if roll else [field]) + [u] + ([] if first else [acc])
    anywhere = pl.BlockSpec(memory_space=pl.ANY)
    vmem = pl.BlockSpec(memory_space=pltpu.VMEM)
    specs = [pl.BlockSpec(memory_space=pltpu.SMEM), anywhere] + ([] if roll else [vmem]) + [vmem]
    specs += [] if first else [anywhere]
    if last:
        shape = [
            jax.ShapeDtypeStruct((count, count), jnp.bfloat16),
            jax.ShapeDtypeStruct((count, count), jnp.float32),
        ]
    else:
        shape = [jax.ShapeDtypeStruct((2, count, count), jnp.float32)]
    return pl.pallas_call(
        functools.partial(kernel, roll, first, last, start),
        out_shape=shape,
        in_specs=specs,
        out_specs=[vmem] * len(shape),
        scratch_shapes=[
            pltpu.VMEM((2 * count, 3 * sites), jnp.bfloat16),
            pltpu.VMEM((2 * n, 3 * sites), jnp.bfloat16),
            pltpu.VMEM((2, count, count), jnp.float32),
            pltpu.SemaphoreType.DMA((8,)),
        ]
        + [pltpu.VMEM((6, n, sites), jnp.bfloat16)] * roll,
        compiler_params=pltpu.CompilerParams(vmem_limit_bytes=40 * 2**20),
        cost_estimate=pl.CostEstimate(
            flops=8 * count * n * 3 * sites,
            bytes_accessed=20 * count * sites,
            transcendentals=0,
        ),
    )(*operands)


def shards(vectors, links):
    slabs = lax.axis_size("gz")
    count, planes, sites = vectors.shape[1], vectors.shape[3], vectors.shape[4]
    assert planes == 1 and slabs % 2 == 0
    own = count // slabs
    scale = 1.0 / math.sqrt(12.0 * sites * planes * slabs)
    odd = (lax.axis_index("gz") % 2).astype(jnp.int32).reshape(1)
    field = jnp.transpose(vectors, (0, 2, 3, 1, 4)).reshape(6, count, sites)
    n = count // CHUNKS
    faces = [passed_along(field[:, c * n : (c + 1) * n], "gz", -1) for c in range(CHUNKS)]
    links_x = links[:, 0].reshape(18, sites)
    links_z = links[:, 1].reshape(18, sites)

    def exchanged(send, keep):
        chip = (keep + swapped(send, "gz").astype(jnp.float32)).astype(jnp.bfloat16)
        got = lax.all_to_all(chip.reshape(slabs, own, count), "gz", 0, 0)
        got = got.reshape(slabs // 2, 2, own, count)
        return jnp.sum(got.astype(jnp.float32), axis=0)

    sum_x = exchanged(*direction(odd, field, None, links_x, None, 0, count, True))
    acc = None
    for c, face in enumerate(faces):
        out = direction(odd, field, face, links_z, acc, c * n, n, c == CHUNKS - 1)
        acc = out[0]
    sum_z = exchanged(*out)
    both = jnp.concatenate([sum_x, sum_z], axis=0)
    return jnp.transpose(both, (1, 0, 2)) * scale


def solution(mesh):
    return jax.shard_map(
        shards,
        mesh=mesh,
        in_specs=(P("grp", None, None, "gz", None), P("grp", None, None, None, "gz", None)),
        out_specs=P("gz", "grp", None),
        check_vma=False,
    )
```

time: 83.9 us -> 76 us (0.906)
  waiting for transfers between devices: 39.9 us -> 16.1 us
  local copies, waits for them, and re-layouts: 5.92 us -> 12.2 us
  Pallas kernels: 22.4 us -> 26.3 us
  other arithmetic: 0.19 us -> 3.76 us
  starting transfers between devices: 15 us -> 16.9 us
    ppermute x1 -> x3, waiting for transfers between devices: 24.4 us -> 4.93 us  [passed_along(): return lax.ppermute(block, axis, route)]
    all_to_all x2, waiting for transfers between devices: 15.5 us -> 9.56 us  [exchanged(): got = lax.all_to_all(chip.reshape(slabs, own, count), 'gz', 0, 0)]
    slice x0 -> x1, local copies, waits for them, and re-layouts: none -> 4 us  [shards(): field[:, c * n:(c + 1) * n]]
    pallas_call x2 -> x4, Pallas kernels: 22.4 us -> 26.3 us  [direction(): pl.pallas_call(functools.partial(kernel, roll, first, last, start), out_s...]
    convert_element_type x0 -> x2, other arithmetic: none -> 2.69 us  [exchanged(): chip = (keep + swapped(send, 'gz').astype(jnp.float32)).astype(jnp.bfloat16)]
    ppermute x0 -> x2, waiting for transfers between devices: none -> 1.58 us  [swapped(): lax.ppermute(block, axis, [(i, i ^ 1) for i in range(lax.axis_size(axis))])]
    another operation x1, local copies, waits for them, and re-layouts: 0.03 us -> 1.54 us  [shards(): links_x = links[:, 0].reshape(18, sites)]
    another operation x1, local copies, waits for them, and re-layouts: 0.03 us -> 1.54 us  [shards(): links_z = links[:, 1].reshape(18, sites)]
  transfers between devices with their start and end apart: 3 -> 7, of which waited for: 2 -> 3; matrix products, arithmetic and copies ran while one was open for 2% -> 11% of each run, Pallas kernels for 27% -> 35%
where the time goes in v2:
time: 76 us; the launch traced here: 75.3 us
  Pallas kernels  26.3 us (35%)
  starting transfers between devices  16.9 us (22%)
  waiting for transfers between devices  16.1 us (21%)
  local copies, waits for them, and re-layouts  12.2 us (16%)
  other arithmetic  3.76 us (5%)
    pallas_call x4, Pallas kernels, direction(): pl.pallas_call(functools.partial(kernel, roll, first, last, start), out_s...  26.3 us
    all_to_all x2, starting transfers between devices, exchanged(): got = lax.all_to_all(chip.reshape(slabs, own, count), 'gz', 0, 0)  10.2 us
    all_to_all x2, waiting for transfers between devices, exchanged(): got = lax.all_to_all(chip.reshape(slabs, own, count), 'gz', 0, 0)  9.56 us
    ppermute x3, starting transfers between devices, passed_along(): return lax.ppermute(block, axis, route)  6.15 us
    ppermute x3, waiting for transfers between devices, passed_along(): return lax.ppermute(block, axis, route)  4.93 us
    slice x1, local copies, waits for them, and re-layouts, shards(): field[:, c * n:(c + 1) * n]  4 us
    convert_element_type x2, other arithmetic, exchanged(): chip = (keep + swapped(send, 'gz').astype(jnp.float32)).astype(jnp.bfloat16)  2.69 us
    unnamed x10, local copies, waits for them, and re-layouts  2.58 us
  transfers between devices with their start and end apart: 7, of which 3 were waited for; matrix products, arithmetic and copies ran while one was open for 11% of the time, Pallas kernels for 35%

profile of v2, /device:TPU:0, one launch (start us, length us, event | category | flops | bytes accessed | tf_op | source)
XLA Modules:
  0.0 75.3 jit_solution(9684584668736893063)
XLA Ops:
  0.0 0.0 copy-start
  0.0 4.0 %fusion.1 = (bf16[6,128,768]{2,1,0:T(8,128)(2,1)}, bf16[6,128,768]{2,1,0:T(8,128)(2,1)}, bf16[6,128,768]{2,1,0:T(8,128)(2,1)}) fusion(bf16[6,384,768]{2,1,0:T(8,128)(2,1)} %bitcast.12), kind=kLoop, calls=%fused_computation.8 | loop fusion | bytes 7077888 | tf_op jit(solution)/shard_map/slice | solution.py:178
  4.0 5.4 %collective-permute-start.3 = (bf16[6,128,768]{2,1,0:T(8,128)(2,1)}, bf16[6,128,768]{2,1,0:T(8,128)(2,1)}, u32[]{:S(2)}, u32[]{:S(2)}) collective-permute-start(bf16[6,128,768]{2,1,0:T(8,128)(2,1)} %get-tuple-element.15), channel_id=1, source_target_pairs={{1,0},{2,1},{3,2},{4,3},{5,4},{6,5},{7,6},{8,7},{9,8},{10,9},{11,1... | collective-permute-start | bytes 3538952 | tf_op jit(solution)/shard_map/ppermute | solution.py:20
  9.5 0.7 collective-permute-start.2
  10.1 0.0 collective-permute-start.1
  10.2 1.8 %slice_reduce_fusion.1 = (f32[2,3,3,768]{3,2,1,0:T(4,128)}, f32[2,3,3,768]{3,2,1,0:T(4,128)}) fusion(f32[2,2,3,3,1,768]{5,4,3,2,1,0:T(1,128)} %param.3), kind=kLoop, calls=%fused_computation.7 | loop fusion | bytes 221184 | tf_op jit(solution)/shard_map/slice | solution.py:179
  12.0 1.5 %reshape_squeeze.6.refs_1_ = f32[18,768]{1,0:T(8,128)} reshape(f32[2,3,3,768]{3,2,1,0:T(4,128)} %get-tuple-element.13) | data formatting | bytes 110592 | tf_op jit(solution)/shard_map/reshape;squeeze | solution.py:179
  13.5 0.0 copy-done
  13.5 0.0 copy-start.4
  13.5 0.9 %copy-done.4 = f32[18,768]{1,0:T(8,128)S(1)} copy-done((f32[18,768]{1,0:T(8,128)S(1)}, f32[18,768]{1,0:T(8,128)}, u32[]{:S(2)}) %copy-start.4) | copy-done | bytes 55320
  14.4 13.6 %shard_map.28 = (bf16[384,384]{1,0:T(8,128)(2,1)}, f32[384,384]{1,0:T(8,128)S(1)}) custom-call(s32[1]{0:T(128)} %bitcast.odd_ref, bf16[6,384,768]{2,1,0:T(8,128)(2,1)S(1)} %bitcast.13, f32[18,768]{1,0:T(8,128)S(1)} %copy-done.4), custom_call_target="tpu_custom_call" | custom-call | flops 2717908992 | bytes 5898240 | tf_op jit(solution)/shard_map/pallas_call | solution.py:148
  28.0 0.0 copy-start.3
  28.0 0.8 %copy-done.3 = f32[384,384]{1,0:T(8,128)} copy-done((f32[384,384]{1,0:T(8,128)}, f32[384,384]{1,0:T(8,128)S(1)}, u32[]{:S(2)}) %copy-start.3) | copy-done | bytes 589848
  28.8 0.5 collective-permute-start
  29.3 1.5 %reshape_squeeze.7.refs_2_ = f32[18,768]{1,0:T(8,128)} reshape(f32[2,3,3,768]{3,2,1,0:T(4,128)} %get-tuple-element.14) | data formatting | bytes 110592 | tf_op jit(solution)/shard_map/reshape;squeeze | solution.py:180
  30.8 0.0 collective-permute-done
  30.9 1.9 %add_convert_fusion.1 = bf16[384,384]{1,0:T(8,128)(2,1)} fusion(f32[384,384]{1,0:T(8,128)} %copy-done.3, bf16[384,384]{1,0:T(8,128)(2,1)} %collective-permute-done), kind=kLoop, calls=%fused_computation.3 | loop fusion | flops 442368 | bytes 1179648 | tf_op jit(solution)/shard_map/convert_element_type | solution.py:183
  32.8 4.2 %all-to-all-start = ((bf16[16,24,384]{2,1,0:T(8,128)(2,1)}), bf16[16,24,384]{2,1,0:T(8,128)(2,1)}, u32[]{:S(2)}, u32[]{:S(2)}) async-start(bf16[16,24,384]{2,1,0:T(8,128)(2,1)} %bitcast.18), calls=%async_computation | async-start | bytes 589824 | tf_op jit(solution)/shard_map/all_to_all | solution.py:184
  37.0 0.0 collective-permute-done.3.refs_1_
  37.0 0.0 copy-start.1
  37.0 0.9 %copy-done.1 = f32[18,768]{1,0:T(8,128)S(1)} copy-done((f32[18,768]{1,0:T(8,128)S(1)}, f32[18,768]{1,0:T(8,128)}, u32[]{:S(2)}) %copy-start.1) | copy-done | bytes 55320
  37.9 0.0 copy-start.2
  37.9 4.1 %shard_map.29.refs_3_ = f32[2,384,384]{2,1,0:T(8,128)S(1)} custom-call(s32[1]{0:T(128)} %bitcast.odd_ref, bf16[6,384,768]{2,1,0:T(8,128)(2,1)S(1)} %bitcast.14, bf16[6,128,768]{2,1,0:T(8,128)(2,1)} %collective-permute-done.3.refs_1_, f32[18,768]{1,0:T(8,128)S(1)} %copy-done.1), custom_call_target="tpu_custom_call" | custom-call | flops 905969664 | bytes 5898240 | tf_op jit(solution)/shard_map/pallas_call | solution.py:148
  41.9 0.0 collective-permute-done.2.refs_1_
  41.9 0.0 copy-done.2
  41.9 4.3 %shard_map.30.refs_3_ = f32[2,384,384]{2,1,0:T(8,128)S(1)} custom-call(s32[1]{0:T(128)} %bitcast.odd_ref, bf16[6,384,768]{2,1,0:T(8,128)(2,1)S(1)} %bitcast.15, bf16[6,128,768]{2,1,0:T(8,128)(2,1)} %collective-permute-done.2.refs_1_, f32[18,768]{1,0:T(8,128)S(1)} %copy-done.2, f32[2,384,384]{2,1,0:T(8,128)S(1)} %shard_map.29.refs_3_), custom_call_target="tpu_custom_call" | custom-call | flops 905969664 | bytes 5898240 | tf_op jit(solution)/shard_map/pallas_call | solution.py:148
  46.3 4.9 %collective-permute-done.1.refs_1_ = bf16[6,128,768]{2,1,0:T(8,128)(2,1)} collective-permute-done((bf16[6,128,768]{2,1,0:T(8,128)(2,1)}, bf16[6,128,768]{2,1,0:T(8,128)(2,1)}, u32[]{:S(2)}, u32[]{:S(2)}) %collective-permute-start.1) | collective-permute-done | bytes 1179680 | tf_op jit(solution)/shard_map/ppermute | solution.py:20
  51.2 4.3 %shard_map.31 = (bf16[384,384]{1,0:T(8,128)(2,1)S(1)}, f32[384,384]{1,0:T(8,128)S(1)}) custom-call(s32[1]{0:T(128)} %bitcast.odd_ref, bf16[6,384,768]{2,1,0:T(8,128)(2,1)S(1)} %bitcast.16, bf16[6,128,768]{2,1,0:T(8,128)(2,1)} %collective-permute-done.1.refs_1_, f32[18,768]{1,0:T(8,128)S(1)} %copy-done.2, f32[2,384,384]{2,1,0:T(8,128)S(1)} %shard_map.30.refs_3_), custom_call_target="tpu_custom_call" | custom-call | flops 905969664 | bytes 5898240 | tf_op jit(solution)/shard_map/pallas_call | solution.py:148
  55.5 0.1 collective-permute-start.4
  55.6 1.6 %collective-permute-done.4 = bf16[384,384]{1,0:T(8,128)(2,1)S(1)} collective-permute-done((bf16[384,384]{1,0:T(8,128)(2,1)S(1)}, bf16[384,384]{1,0:T(8,128)(2,1)S(1)}, u32[]{:S(2)}, u32[]{:S(2)}) %collective-permute-start.4) | collective-permute-done | bytes 294944 | tf_op jit(solution)/shard_map/ppermute | solution.py:24
  57.2 0.8 %add_convert_fusion = bf16[384,384]{1,0:T(8,128)(2,1)} fusion(f32[384,384]{1,0:T(8,128)S(1)} %get-tuple-element.11, bf16[384,384]{1,0:T(8,128)(2,1)S(1)} %collective-permute-done.4), kind=kLoop, calls=%fused_computation.2 | loop fusion | flops 442368 | bytes 1179648 | tf_op jit(solution)/shard_map/convert_element_type | solution.py:183
  58.0 0.0 all-to-all-done
  58.0 6.0 %all-to-all-start.1 = ((bf16[16,24,384]{2,1,0:T(8,128)(2,1)}), bf16[16,24,384]{2,1,0:T(8,128)(2,1)S(1)}, u32[]{:S(2)}, u32[]{:S(2)}) async-start(bf16[16,24,384]{2,1,0:T(8,128)(2,1)} %bitcast.6), calls=%async_computation.1 | async-start | bytes 589824 | tf_op jit(solution)/shard_map/all_to_all | solution.py:184
  64.0 1.0 %convert_reduce_fusion.1 = f32[2,24,384]{2,1,0:T(8,128)S(1)} fusion(bf16[8,2,24,384]{3,2,1,0:T(8,128)(2,1)} %bitcast.9), kind=kLoop, calls=%fused_computation.1 | loop fusion | flops 276480 | bytes 368640 | tf_op jit(solution)/shard_map/reduce_sum | solution.py:186
  65.0 9.6 %all-to-all-done.1 = bf16[16,24,384]{2,1,0:T(8,128)(2,1)S(1)} async-done(((bf16[16,24,384]{2,1,0:T(8,128)(2,1)}), bf16[16,24,384]{2,1,0:T(8,128)(2,1)S(1)}, u32[]{:S(2)}, u32[]{:S(2)}) %all-to-all-start.1) | async-done | bytes 294944 | tf_op jit(solution)/shard_map/all_to_all | solution.py:184
  74.6 0.7 copy.3
  (2 shorter events, 0.1 us)
Async XLA Ops:
  0.0 13.5 %copy-start = (bf16[2,384,3,1,768]{4,1,3,2,0:T(8,128)(2,1)S(1)}, bf16[2,384,3,1,768]{4,1,3,2,0:T(8,128)(2,1)}, u32[]{:S(2)}) copy-start(bf16[2,384,3,1,768]{4,1,3,2,0:T(8,128)(2,1)} %param.2) | copy-start | bytes 10616836
  4.0 33.0 %collective-permute-start.3 = (bf16[6,128,768]{2,1,0:T(8,128)(2,1)}, bf16[6,128,768]{2,1,0:T(8,128)(2,1)}, u32[]{:S(2)}, u32[]{:S(2)}) collective-permute-start(bf16[6,128,768]{2,1,0:T(8,128)(2,1)} %get-tuple-element.15), channel_id=1, source_target_pairs={{1,0},{2,1},{3,2},{4,3},{5,4},{6,5},{7,6},{8,7},{9,8},{10,9},{11,1... | collective-permute-start | bytes 3538952 | tf_op jit(solution)/shard_map/ppermute | solution.py:20
  9.5 32.5 %collective-permute-start.2 = (bf16[6,128,768]{2,1,0:T(8,128)(2,1)}, bf16[6,128,768]{2,1,0:T(8,128)(2,1)}, u32[]{:S(2)}, u32[]{:S(2)}) collective-permute-start(bf16[6,128,768]{2,1,0:T(8,128)(2,1)} %get-tuple-element.16), channel_id=1, source_target_pairs={{1,0},{2,1},{3,2},{4,3},{5,4},{6,5},{7,6},{8,7},{9,8},{10,9},{11,1... | collective-permute-start | bytes 3538952 | tf_op jit(solution)/shard_map/ppermute | solution.py:20
  10.1 41.1 %collective-permute-start.1 = (bf16[6,128,768]{2,1,0:T(8,128)(2,1)}, bf16[6,128,768]{2,1,0:T(8,128)(2,1)}, u32[]{:S(2)}, u32[]{:S(2)}) collective-permute-start(bf16[6,128,768]{2,1,0:T(8,128)(2,1)} %get-tuple-element.17), channel_id=1, source_target_pairs={{1,0},{2,1},{3,2},{4,3},{5,4},{6,5},{7,6},{8,7},{9,8},{10,9},{11,1... | collective-permute-start | bytes 3538952 | tf_op jit(solution)/shard_map/ppermute | solution.py:20
  13.5 0.9 %copy-start.4 = (f32[18,768]{1,0:T(8,128)S(1)}, f32[18,768]{1,0:T(8,128)}, u32[]{:S(2)}) copy-start(f32[18,768]{1,0:T(8,128)} %reshape_squeeze.6.refs_1_) | copy-start | bytes 165892
  28.0 0.8 %copy-start.3 = (f32[384,384]{1,0:T(8,128)}, f32[384,384]{1,0:T(8,128)S(1)}, u32[]{:S(2)}) copy-start(f32[384,384]{1,0:T(8,128)S(1)} %get-tuple-element.9) | copy-start | bytes 1769476
  28.8 2.0 %collective-permute-start = (bf16[384,384]{1,0:T(8,128)(2,1)}, bf16[384,384]{1,0:T(8,128)(2,1)}, u32[]{:S(2)}, u32[]{:S(2)}) collective-permute-start(bf16[384,384]{1,0:T(8,128)(2,1)} %get-tuple-element.10), channel_id=1, source_target_pairs={{0,1},{1,0},{2,3},{3,2},{4,5},{5,4},{6,7},{7,6},{8,9},{9,8},{10,11... | collective-permute-start | bytes 884744 | tf_op jit(solution)/shard_map/ppermute | solution.py:24
  32.8 25.2 %all-to-all-start = ((bf16[16,24,384]{2,1,0:T(8,128)(2,1)}), bf16[16,24,384]{2,1,0:T(8,128)(2,1)}, u32[]{:S(2)}, u32[]{:S(2)}) async-start(bf16[16,24,384]{2,1,0:T(8,128)(2,1)} %bitcast.18), calls=%async_computation | async-start | bytes 589824 | tf_op jit(solution)/shard_map/all_to_all | solution.py:184
  37.0 0.9 %copy-start.1 = (f32[18,768]{1,0:T(8,128)S(1)}, f32[18,768]{1,0:T(8,128)}, u32[]{:S(2)}) copy-start(f32[18,768]{1,0:T(8,128)} %reshape_squeeze.7.refs_2_) | copy-start | bytes 165892
  37.9 4.1 %copy-start.2 = (f32[18,768]{1,0:T(8,128)S(1)}, f32[18,768]{1,0:T(8,128)}, u32[]{:S(2)}) copy-start(f32[18,768]{1,0:T(8,128)} %reshape_squeeze.7.refs_2_) | copy-start | bytes 165892
  55.5 1.6 %collective-permute-start.4 = (bf16[384,384]{1,0:T(8,128)(2,1)S(1)}, bf16[384,384]{1,0:T(8,128)(2,1)S(1)}, u32[]{:S(2)}, u32[]{:S(2)}) collective-permute-start(bf16[384,384]{1,0:T(8,128)(2,1)S(1)} %get-tuple-element.12), channel_id=1, source_target_pairs={{0,1},{1,0},{2,3},{3,2},{4,5},{5,4},{6,7},{7,6},{8,9},{9,8},{10,11... | collective-permute-start | bytes 884744 | tf_op jit(solution)/shard_map/ppermute | solution.py:24
  58.0 16.6 %all-to-all-start.1 = ((bf16[16,24,384]{2,1,0:T(8,128)(2,1)}), bf16[16,24,384]{2,1,0:T(8,128)(2,1)S(1)}, u32[]{:S(2)}, u32[]{:S(2)}) async-start(bf16[16,24,384]{2,1,0:T(8,128)(2,1)} %bitcast.6), calls=%async_computation.1 | async-start | bytes 589824 | tf_op jit(solution)/shard_map/all_to_all | solution.py:184

commit v3 on v0

v3 whole, which is shorter than its diff:
```python
import functools
import math

import jax
import jax.numpy as jnp
from jax import lax
from jax.experimental import pallas as pl
from jax.experimental.pallas import tpu as pltpu
from jax.sharding import PartitionSpec as P

X = 64
LANES = 128
ROWS = 16
VMEM = pl.BlockSpec(memory_space=pltpu.VMEM)
SMEM = pl.BlockSpec(memory_space=pltpu.SMEM)


def passed_along(block, axis, distance):
    devices = range(lax.axis_size(axis))
    route = [((i - distance) % len(devices), i) for i in devices]
    return lax.ppermute(block, axis, route)


def swapped(block, axis):
    return lax.ppermute(block, axis, [(i, i ^ 1) for i in range(lax.axis_size(axis))])


def displace(field_ref, links_ref, mu, a, d_ref, roll):
    sites = field_ref.shape[2]
    n = field_ref.shape[1]
    half = ROWS // 2
    for t in range(sites // LANES):
        lanes = slice(t * LANES, (t + 1) * LANES)

        def link(part, b):
            row = ((part * 2 + mu) * 3 + a) * 3 + b
            return jnp.broadcast_to(links_ref[row : row + 1, lanes], (half, LANES))

        ur = [link(0, b) for b in range(3)]
        ui = [link(1, b) for b in range(3)]
        if roll:
            lane = lax.broadcasted_iota(jnp.int32, (half, LANES), 1)
            last = (lane & (X - 1)) == X - 1

        def around(value):
            return jnp.where(last, pltpu.roll(value, X - 1, 1), pltpu.roll(value, LANES - 1, 1))

        def body(m, carry):
            first = m * ROWS if isinstance(m, int) else pl.multiple_of(m * ROWS, ROWS)
            v = [field_ref[k, pl.ds(first, ROWS), lanes].astype(jnp.float32) for k in range(6)]
            outs_r, outs_i = [], []
            for h in range(2):
                rows = slice(h * half, (h + 1) * half)
                re = [v[b][rows] for b in range(3)]
                im = [v[3 + b][rows] for b in range(3)]
                if roll:
                    re, im = [around(r) for r in re], [around(i) for i in im]
                dr = ur[0] * re[0] - ui[0] * im[0]
                di = ur[0] * im[0] + ui[0] * re[0]
                for b in (1, 2):
                    dr = dr + (ur[b] * re[b] - ui[b] * im[b])
                    di = di + (ur[b] * im[b] + ui[b] * re[b])
                outs_r.append(dr)
                outs_i.append(di)
            d_ref[pl.ds(first, ROWS), lanes] = jnp.concatenate(outs_r, axis=0).astype(jnp.bfloat16)
            d_ref[pl.ds(n + first, ROWS), lanes] = jnp.concatenate(outs_i, axis=0).astype(jnp.bfloat16)
            return carry

        if n <= LANES:
            for m in range(n // ROWS):
                body(m, 0)
        else:
            lax.fori_loop(0, n // ROWS, body, 0, unroll=4)


def by_halves(slabs, own):
    return own % 8 == 0 and slabs & (slabs - 1) == 0


def halving_order(k, chips):
    bits = chips.bit_length() - 1
    return sum(((k >> b) & 1) << (bits - 1 - b) for b in range(bits))


def kernel(mu, first, last, start, slabs, where_ref, *refs):
    refs = list(refs)
    left_ref = refs.pop(0)
    field_ref = left_ref if mu == 0 else refs.pop(0)
    links_ref = refs.pop(0)
    acc_in = None if first else refs.pop(0)
    outs = [refs.pop(0) for _ in range(2 if last else 1)]
    d_refs = [refs.pop(0) for _ in range(3)]
    acc = refs.pop(0) if last else outs[0]
    count = left_ref.shape[1]
    n = field_ref.shape[1]
    j = slice(start, start + n)

    product = [None, None]
    for a in range(3):
        displace(field_ref, links_ref, mu, a, d_refs[a], mu == 0)
        for part in range(2):
            term = lax.dot_general(
                left_ref[part * 3 + a], d_refs[a][...], (((1,), (1,)), ((), ())),
                preferred_element_type=jnp.float32,
            )
            product[part] = term if a == 0 else product[part] + term
    sum_re = product[0][:, :n] + product[1][:, n:]
    sum_im = product[0][:, n:] - product[1][:, :n]
    if n == count:
        acc[0] = sum_re - sum_re.T
        acc[1] = sum_im + sum_im.T
    else:
        acc[...] = jnp.zeros_like(acc) if first else acc_in[...]
        acc[0, :, j] += sum_re
        acc[1, :, j] += sum_im
        acc[0, j, :] -= sum_re.T
        acc[1, j, :] += sum_im.T
    if not last:
        return
    send, keep = outs
    core, chip = where_ref[0], where_ref[1]
    own = count // slabs
    if not by_halves(slabs, own):
        send[...] = acc[1 - core].astype(jnp.bfloat16)
        keep[...] = acc[core]
        return
    for k in range(slabs // 2):
        if mu == 0:
            to = halving_order(k, slabs // 2) * 2
        else:
            to = lax.rem(chip + k, slabs // 2) * 2
        block = slice(k * 2 * own, (k + 1) * 2 * own)

        def rows(which):
            at = pl.ds(pl.multiple_of((to + which) * own, 8), own)
            return jnp.concatenate([acc[0, at, :], acc[1, at, :]], axis=0)

        send[block, :] = rows(1 - core).astype(jnp.bfloat16)
        keep[block, :] = rows(core)


def direction(where, left, field, links, acc, start, n, last, slabs):
    count, sites = left.shape[1:]
    mu = 0 if field is None else 1
    first = acc is None
    operands = [where, left] + [field] * mu + [links] + ([] if first else [acc])
    square = (2, count, count)
    if last:
        shape = [
            jax.ShapeDtypeStruct((count, count), jnp.bfloat16),
            jax.ShapeDtypeStruct((count, count), jnp.float32),
        ]
    else:
        shape = [jax.ShapeDtypeStruct(square, jnp.float32)]
    return pl.pallas_call(
        functools.partial(kernel, mu, first, last, start, slabs),
        out_shape=shape,
        in_specs=[SMEM] + [VMEM] * (len(operands) - 1),
        out_specs=[VMEM] * len(shape),
        scratch_shapes=[pltpu.VMEM((2 * n, sites), jnp.bfloat16)] * 3
        + [pltpu.VMEM(square, jnp.float32)] * last,
        compiler_params=pltpu.CompilerParams(vmem_limit_bytes=36 * 2**20),
        cost_estimate=pl.CostEstimate(
            flops=8 * count * n * 3 * sites,
            bytes_accessed=12 * count * sites,
            transcendentals=0,
        ),
    )(*operands)


def halve_kernel(bit, where_ref, kept_ref, got_ref, send_ref, keep_ref):
    size = keep_ref.shape[0]
    mine = (where_ref[1] >> bit) & 1

    def total(which):
        rows = pl.ds(pl.multiple_of(which * size, ROWS), size)
        return kept_ref[rows, :] + got_ref[rows, :].astype(jnp.float32)

    send_ref[...] = total(1 - mine).astype(jnp.bfloat16)
    keep_ref[...] = total(mine)


def halved(where, send, keep, slabs):
    for bit in range(slabs.bit_length() - 1):
        got = lax.ppermute(send, "gz", [(i, i ^ (1 << bit)) for i in range(slabs)])
        if bit == slabs.bit_length() - 2:
            return [keep, got]
        half = (send.shape[0] // 2, send.shape[1])
        send, keep = pl.pallas_call(
            functools.partial(halve_kernel, bit),
            out_shape=[
                jax.ShapeDtypeStruct(half, jnp.bfloat16),
                jax.ShapeDtypeStruct(half, jnp.float32),
            ],
            in_specs=[SMEM, VMEM, VMEM],
            out_specs=[VMEM] * 2,
        )(where, keep, got)


def add_kernel(kept_ref, got_ref, own_ref, *block_refs):
    size = own_ref.shape[0]
    own_ref[...] = kept_ref[:size, :] + got_ref[:size, :].astype(jnp.float32)
    for k, ref in enumerate(block_refs):
        rows = slice((k + 1) * size, (k + 2) * size)
        ref[...] = (kept_ref[rows, :] + got_ref[rows, :].astype(jnp.float32)).astype(jnp.bfloat16)


def chips_terms(send, keep, slabs):
    count = send.shape[0]
    block = (count // (slabs // 2), count)
    others = slabs // 2 - 1
    got = swapped(send, "gz")
    mine, *blocks = pl.pallas_call(
        add_kernel,
        out_shape=[jax.ShapeDtypeStruct(block, jnp.float32)]
        + [jax.ShapeDtypeStruct(block, jnp.bfloat16)] * others,
        in_specs=[VMEM] * 2,
        out_specs=[VMEM] * (others + 1),
    )(keep, got)
    return [mine] + [passed_along(b, "gz", 2 * (k + 1)) for k, b in enumerate(blocks)]


def final_kernel(scale, out_ref, x_refs, z_refs):
    own = out_ref.shape[0]
    for m, refs in enumerate((x_refs, z_refs)):
        total = refs[0][...]
        for ref in refs[1:]:
            total = total + ref[...].astype(jnp.float32)
        total = total * scale
        out_ref[:, 2 * m, :] = total[:own]
        out_ref[:, 2 * m + 1, :] = total[own:]


def assembled(terms_x, terms_z, own, scale):
    count = terms_x[0].shape[1]
    n = len(terms_x)
    operands = [*terms_x, *terms_z]

    def body(*refs):
        final_kernel(scale, refs[-1], refs[:n], refs[n:-1])

    return pl.pallas_call(
        body,
        out_shape=jax.ShapeDtypeStruct((own, 4, count), jnp.float32),
        in_specs=[VMEM] * len(operands),
        out_specs=VMEM,
    )(*operands)


def shards(vectors, links):
    slabs = lax.axis_size("gz")
    count, planes, sites = vectors.shape[1], vectors.shape[3], vectors.shape[4]
    assert planes == 1 and slabs % 2 == 0
    own = count // slabs
    scale = 1.0 / math.sqrt(12.0 * sites * planes * slabs)
    index = lax.axis_index("gz").astype(jnp.int32)
    where = jnp.stack([index & 1, index >> 1])
    field = jnp.transpose(vectors, (0, 2, 3, 1, 4)).reshape(6, count, sites)
    links = links.reshape(36, sites)
    starts = [0, count // 6, count // 2, count - count // 6, count]
    faces, rest = [], field
    for low, high in zip(starts, starts[1:]):
        piece = rest[:, low:high]
        faces.append(passed_along(piece, "gz", -1))
        piece, rest = lax.optimization_barrier((piece, rest))

    out_x = direction(where, field, None, links, None, 0, count, True, slabs)
    if by_halves(slabs, own):
        terms_x = halved(where, *out_x, slabs)
        faces[-2], *terms_x = lax.optimization_barrier((faces[-2], *terms_x))
    acc = None
    for c, face in enumerate(faces):
        n = starts[c + 1] - starts[c]
        out_z = direction(where, field, face, links, acc, starts[c], n, c == len(faces) - 1, slabs)
        acc = out_z[0]
    if by_halves(slabs, own):
        return assembled(terms_x, chips_terms(*out_z, slabs), own, scale)

    def exchanged(send, keep):
        chip = (keep + swapped(send, "gz").astype(jnp.float32)).astype(jnp.bfloat16)
        got = lax.all_to_all(chip.reshape(slabs, own, count), "gz", 0, 0)
        got = got.reshape(slabs // 2, 2, own, count)
        return jnp.sum(got.astype(jnp.float32), axis=0)

    both = jnp.concatenate([exchanged(*out_x), exchanged(*out_z)], axis=0)
    return jnp.transpose(both, (1, 0, 2)) * scale


def solution(mesh):
    return jax.shard_map(
        shards,
        mesh=mesh,
        in_specs=(P("grp", None, None, "gz", None), P("grp", None, None, None, "gz", None)),
        out_specs=P("gz", "grp", None),
        check_vma=False,
    )
```

time: 225 us -> 101 us (0.45)
  waiting for transfers between devices: 94.8 us -> 18.5 us
  local copies, waits for them, and re-layouts: 60.3 us -> 15.4 us
  matrix products: 40.7 us -> 0 us
  Pallas kernels: 0 us -> 38.8 us
  starting transfers between devices: 5.45 us -> 25.9 us
  between operations: 14.3 us -> 0.16 us
  other arithmetic: 8.02 us -> 1.93 us
    unnamed x2 -> x0, waiting for transfers between devices: 94.8 us -> none
    dot_general x16 -> x0, matrix products: 40.7 us -> none  [the longest x8 24 us: contract(): return jnp.einsum('ab...,vb...->va...', first, second)]
    pallas_call x0 -> x10, Pallas kernels: none -> 38.8 us  [the longest x5 29.8 us: direction(): pl.pallas_call(functools.partial(kernel, mu, first, last, start, slabs),...]
    another operation x4 -> x0, local copies, waits for them, and re-layouts: 21.4 us -> none
    ppermute x0 -> x5, waiting for transfers between devices: none -> 15.6 us  [the longest x4 14 us: halved(): got = lax.ppermute(send, 'gz', [(i, i ^ 1 << bit) for i in range(slabs)])]
    unnamed x54 -> x34, local copies, waits for them, and re-layouts: 20.3 us -> 6.09 us
    ppermute x1 -> x11, starting transfers between devices: 5.44 us -> 19.2 us  [passed_along(): return lax.ppermute(block, axis, route)]
    ppermute x0 -> x5, starting transfers between devices: none -> 6.72 us  [the longest x4 6.72 us: halved(): got = lax.ppermute(send, 'gz', [(i, i ^ 1 << bit) for i in range(slabs)])]
  transfers between devices with their start and end apart: 2 -> 16, of which waited for: 1 -> 6; matrix products, arithmetic and copies ran while one was open for 22% -> 4% of each run, Pallas kernels for 0% -> 32%
where the time goes in v3:
time: 101 us
  Pallas kernels  38.8 us (38%)
  starting transfers between devices  25.9 us (26%)
  waiting for transfers between devices  18.5 us (18%)
  local copies, waits for them, and re-layouts  15.4 us (15%)
  other arithmetic  1.93 us (2%)
    pallas_call x5, Pallas kernels, direction(): pl.pallas_call(functools.partial(kernel, mu, first, last, start, slabs),...  29.8 us
    ppermute x11, starting transfers between devices, passed_along(): return lax.ppermute(block, axis, route)  19.2 us
    ppermute x4, waiting for transfers between devices, halved(): got = lax.ppermute(send, 'gz', [(i, i ^ 1 << bit) for i in range(slabs)])  14 us
    slice x4, local copies, waits for them, and re-layouts, shards(): piece = rest[:, low:high]  7.7 us
    ppermute x4, starting transfers between devices, halved(): got = lax.ppermute(send, 'gz', [(i, i ^ 1 << bit) for i in range(slabs)])  6.72 us
    unnamed x34, local copies, waits for them, and re-layouts  6.09 us
    pallas_call x3, Pallas kernels, halved(): pl.pallas_call(functools.partial(halve_kernel, bit), out_shape=[jax.Shape...  5.38 us
    ppermute x11, waiting for transfers between devices, passed_along(): return lax.ppermute(block, axis, route)  2.94 us
  transfers between devices with their start and end apart: 16, of which 6 were waited for; matrix products, arithmetic and copies ran while one was open for 4% of the time, Pallas kernels for 32%

profile of v3, /device:TPU:0, one launch (start us, length us, event | category | flops | bytes accessed | tf_op | source)
XLA Modules:
  0.0 100.8 jit_solution(15382152210914007456)
XLA Ops:
  0.0 1.9 %slice.16 = bf16[6,64,768]{2,1,0:T(8,128)(2,1)} slice(bf16[6,384,768]{2,1,0:T(8,128)(2,1)} %bitcast.5), slice={[0:6], [0:64], [0:768]} | slice | bytes 1179648 | tf_op jit(solution)/shard_map/slice | solution.py:263
  2.0 2.5 %slice.13 = bf16[6,128,768]{2,1,0:T(8,128)(2,1)} slice(bf16[6,384,768]{2,1,0:T(8,128)(2,1)} %bitcast.6), slice={[0:6], [64:192], [0:768]} | slice | bytes 2359296 | tf_op jit(solution)/shard_map/slice | solution.py:263
  4.5 2.4 %slice.14 = bf16[6,128,768]{2,1,0:T(8,128)(2,1)} slice(bf16[6,384,768]{2,1,0:T(8,128)(2,1)} %bitcast.7), slice={[0:6], [192:320], [0:768]} | slice | bytes 2359296 | tf_op jit(solution)/shard_map/slice | solution.py:263
  6.8 5.4 %collective-permute-start = (bf16[6,128,768]{2,1,0:T(8,128)(2,1)}, bf16[6,128,768]{2,1,0:T(8,128)(2,1)}, u32[]{:S(2)}, u32[]{:S(2)}) collective-permute-start(bf16[6,128,768]{2,1,0:T(8,128)(2,1)} %slice.14), channel_id=1, source_target_pairs={{1,0},{2,1},{3,2},{4,3},{5,4},{6,5},{7,6},{8,7},{9,8},{10,9},{11,1... | collective-permute-start | bytes 3538952 | tf_op jit(solution)/shard_map/ppermute | solution.py:21
  12.3 0.7 collective-permute-start.6
  13.0 0.0 collective-permute-start.7
  13.0 1.9 %reduce = f32[2,2,3,3,768]{4,3,2,1,0:T(4,128)} reduce(f32[2,2,3,3,1,768]{5,4,3,2,1,0:T(1,128)} %param.3, f32[]{:T(128)} %constant.8), dimensions={4}, to_apply=%param.3.reduce_sub_computation | reduce | bytes 221188 | tf_op args[1]
  14.8 1.6 %reshape.7.refs_1_.refs_2_ = f32[36,768]{1,0:T(8,128)} reshape(f32[2,2,3,3,768]{4,3,2,1,0:T(4,128)} %reduce) | data formatting | bytes 221184 | tf_op jit(solution)/shard_map/reshape | solution.py:259
  16.5 0.1 pad_add_fusion.where_ref
  16.6 0.0 copy-done
  16.6 0.9 copy-done.1
  17.5 17.7 %shard_map.28 = (bf16[384,384]{1,0:T(8,128)(2,1)S(1)}, f32[384,384]{1,0:T(8,128)S(1)}) custom-call(s32[2]{0:T(128)S(1)} %pad_add_fusion.where_ref, bf16[6,384,768]{2,1,0:T(8,128)(2,1)S(1)} %bitcast.8, f32[36,768]{1,0:T(8,128)S(1)} %copy-done.1), custom_call_target="tpu_custom_call" | custom-call | flops 2717908992 | bytes 3538944 | tf_op jit(solution)/shard_map/pallas_call | solution.py:155
  35.2 0.0 copy-done.5
  35.2 0.0 copy-start.4
  35.2 0.8 copy-done.4
  36.0 0.5 collective-permute-start.1
  36.5 0.9 slice.15
  37.3 1.0 collective-permute-start.5
  38.3 0.0 collective-permute-done.1.got_ref
  38.3 0.8 copy-done.8
  39.1 2.0 %shard_map.29 = (bf16[192,384]{1,0:T(8,128)(2,1)}, f32[192,384]{1,0:T(8,128)}) custom-call(s32[2]{0:T(128)} %copy-done.5, f32[384,384]{1,0:T(8,128)} %copy-done.4, bf16[384,384]{1,0:T(8,128)(2,1)} %copy-done.8), custom_call_target="tpu_custom_call" | custom-call | tf_op jit(solution)/shard_map/pallas_call | solution.py:189
  41.1 0.7 collective-permute-start.2
  41.8 10.9 %collective-permute-done.2.got_ref = bf16[192,384]{1,0:T(8,128)(2,1)} collective-permute-done((bf16[192,384]{1,0:T(8,128)(2,1)}, bf16[192,384]{1,0:T(8,128)(2,1)}, u32[]{:S(2)}, u32[]{:S(2)}) %collective-permute-start.2) | collective-permute-done | bytes 147488 | tf_op jit(solution)/shard_map/ppermute | solution.py:185
  52.7 1.7 %shard_map.30 = (bf16[96,384]{1,0:T(8,128)(2,1)}, f32[96,384]{1,0:T(8,128)}) custom-call(s32[2]{0:T(128)} %copy-done.5, f32[192,384]{1,0:T(8,128)} %get-tuple-element.33.kept_ref, bf16[192,384]{1,0:T(8,128)(2,1)} %collective-permute-done.2.got_ref), custom_call_target="tpu_custom_call" | custom-call | tf_op jit(solution)/shard_map/pallas_call | solution.py:189
  54.5 1.6 %collective-permute-start.3 = (bf16[96,384]{1,0:T(8,128)(2,1)}, bf16[96,384]{1,0:T(8,128)(2,1)}, u32[]{:S(2)}, u32[]{:S(2)}) collective-permute-start(bf16[96,384]{1,0:T(8,128)(2,1)} %get-tuple-element.36), channel_id=1, source_target_pairs={{0,4},{1,5},{2,6},{3,7},{4,0},{5,1},{6,2},{7,3},{8,12},{9,13},{10,... | collective-permute-start | bytes 221192 | tf_op jit(solution)/shard_map/ppermute | solution.py:185
  56.0 3.1 %collective-permute-done.3.got_ref = bf16[96,384]{1,0:T(8,128)(2,1)} collective-permute-done((bf16[96,384]{1,0:T(8,128)(2,1)}, bf16[96,384]{1,0:T(8,128)(2,1)}, u32[]{:S(2)}, u32[]{:S(2)}) %collective-permute-start.3) | collective-permute-done | bytes 73760 | tf_op jit(solution)/shard_map/ppermute | solution.py:185
  59.1 1.6 %shard_map.31 = (bf16[48,384]{1,0:T(8,128)(2,1)}, f32[48,384]{1,0:T(8,128)}) custom-call(s32[2]{0:T(128)} %copy-done.5, f32[96,384]{1,0:T(8,128)} %get-tuple-element.35.kept_ref, bf16[96,384]{1,0:T(8,128)(2,1)} %collective-permute-done.3.got_ref), custom_call_target="tpu_custom_call" | custom-call | tf_op jit(solution)/shard_map/pallas_call | solution.py:189
  60.8 4.0 %collective-permute-start.4 = (bf16[48,384]{1,0:T(8,128)(2,1)}, bf16[48,384]{1,0:T(8,128)(2,1)S(1)}, u32[]{:S(2)}, u32[]{:S(2)}) collective-permute-start(bf16[48,384]{1,0:T(8,128)(2,1)} %get-tuple-element.38), channel_id=1, source_target_pairs={{0,8},{1,9},{2,10},{3,11},{4,12},{5,13},{6,14},{7,15},{8,0},{9,1},... | collective-permute-start | bytes 110600 | tf_op jit(solution)/shard_map/ppermute | solution.py:185
  64.7 0.0 collective-permute-done.7.refs_1_
  64.7 0.0 copy-done.6
  64.7 0.9 copy-done.2
  65.6 2.5 %shard_map.32.refs_3_ = f32[2,384,384]{2,1,0:T(8,128)S(1)} custom-call(s32[2]{0:T(128)S(1)} %copy-done.6, bf16[6,384,768]{2,1,0:T(8,128)(2,1)S(1)} %bitcast.10, bf16[6,64,768]{2,1,0:T(8,128)(2,1)} %collective-permute-done.7.refs_1_, f32[36,768]{1,0:T(8,128)S(1)} %copy-done.2), custom_call_target="tpu_custom_call" | custom-call | flops 452984832 | bytes 3538944 | tf_op jit(solution)/shard_map/pallas_call | solution.py:155
  68.2 0.0 collective-permute-done.4.refs_1_
  68.2 0.0 copy-start.9
  68.2 0.0 collective-permute-done.refs_1_
  68.2 0.6 copy-done.9
  68.8 0.0 collective-permute-done.6.refs_1_
  68.8 3.5 %shard_map.33.refs_3_ = f32[2,384,384]{2,1,0:T(8,128)S(1)} custom-call(s32[2]{0:T(128)S(1)} %copy-done.6, bf16[6,384,768]{2,1,0:T(8,128)(2,1)S(1)} %bitcast.11, bf16[6,128,768]{2,1,0:T(8,128)(2,1)} %collective-permute-done.6.refs_1_, f32[36,768]{1,0:T(8,128)S(1)} %copy-done.2, f32[2,384,384]{2,1,0:T(8,128)S(1)} %shard_map.32.refs_3_), custom_call_target="tpu_custom_call" | custom-call | flops 905969664 | bytes 3538944 | tf_op jit(solution)/shard_map/pallas_call | solution.py:155
  72.3 3.5 %shard_map.34.refs_3_ = f32[2,384,384]{2,1,0:T(8,128)S(1)} custom-call(s32[2]{0:T(128)S(1)} %copy-done.6, bf16[6,384,768]{2,1,0:T(8,128)(2,1)S(1)} %bitcast.12, bf16[6,128,768]{2,1,0:T(8,128)(2,1)} %collective-permute-done.refs_1_, f32[36,768]{1,0:T(8,128)S(1)} %copy-done.2, f32[2,384,384]{2,1,0:T(8,128)S(1)} %shard_map.33.refs_3_), custom_call_target="tpu_custom_call" | custom-call | flops 905969664 | bytes 3538944 | tf_op jit(solution)/shard_map/pallas_call | solution.py:155
  75.7 0.0 collective-permute-done.5.refs_1_
  75.7 2.7 %shard_map.35 = (bf16[384,384]{1,0:T(8,128)(2,1)S(1)}, f32[384,384]{1,0:T(8,128)S(1)}) custom-call(s32[2]{0:T(128)S(1)} %copy-done.6, bf16[6,384,768]{2,1,0:T(8,128)(2,1)S(1)} %bitcast.13, bf16[6,64,768]{2,1,0:T(8,128)(2,1)} %collective-permute-done.5.refs_1_, f32[36,768]{1,0:T(8,128)S(1)} %copy-done.2, f32[2,384,384]{2,1,0:T(8,128)S(1)} %shard_map.34.refs_3_), custom_call_target="tpu_custom_call" | custom-call | flops 452984832 | bytes 3538944 | tf_op jit(solution)/shard_map/pallas_call | solution.py:155
  78.4 0.0 copy-start.3
  78.4 0.8 copy-done.3
  79.2 0.0 collective-permute-start.8
  79.2 1.6 %collective-permute-done.8.got_ref = bf16[384,384]{1,0:T(8,128)(2,1)S(1)} collective-permute-done((bf16[384,384]{1,0:T(8,128)(2,1)S(1)}, bf16[384,384]{1,0:T(8,128)(2,1)S(1)}, u32[]{:S(2)}, u32[]{:S(2)}) %collective-permute-start.8) | collective-permute-done | bytes 294944 | tf_op jit(solution)/shard_map/ppermute | solution.py:25
  80.8 0.7 copy-done.7
  81.5 1.9 %shard_map.36 = (f32[48,384]{1,0:T(8,128)}, bf16[48,384]{1,0:T(8,128)(2,1)}, bf16[48,384]{1,0:T(8,128)(2,1)}, bf16[48,384]{1,0:T(8,128)(2,1)}, bf16[48,384]{1,0:...) custom-call(f32[384,384]{1,0:T(8,128)} %copy-done.3, ...), custom_call_target="tpu_custom_call" | custom-call | tf_op jit(solution)/shard_map/pallas_call | solution.py:213
  83.4 2.5 %collective-permute-start.9 = (bf16[48,384]{1,0:T(8,128)(2,1)}, bf16[48,384]{1,0:T(8,128)(2,1)S(1)}, u32[]{:S(2)}, u32[]{:S(2)}) collective-permute-start(bf16[48,384]{1,0:T(8,128)(2,1)} %get-tuple-element.46), channel_id=1, source_target_pairs={{14,0},{15,1},{0,2},{1,3},{2,4},{3,5},{4,6},{5,7},{6,8},{7,9},{8,1... | collective-permute-start | bytes 110600 | tf_op jit(solution)/shard_map/ppermute | solution.py:21
  85.9 1.9 %collective-permute-start.10 = (bf16[48,384]{1,0:T(8,128)(2,1)}, bf16[48,384]{1,0:T(8,128)(2,1)S(1)}, u32[]{:S(2)}, u32[]{:S(2)}) collective-permute-start(bf16[48,384]{1,0:T(8,128)(2,1)} %get-tuple-element.47), channel_id=1, source_target_pairs={{12,0},{13,1},{14,2},{15,3},{0,4},{1,5},{2,6},{3,7},{4,8},{5,9},{6... | collective-permute-start | bytes 110600 | tf_op jit(solution)/shard_map/ppermute | solution.py:21
  87.8 0.6 collective-permute-start.11
  88.4 2.2 %collective-permute-start.12 = (bf16[48,384]{1,0:T(8,128)(2,1)}, bf16[48,384]{1,0:T(8,128)(2,1)S(1)}, u32[]{:S(2)}, u32[]{:S(2)}) collective-permute-start(bf16[48,384]{1,0:T(8,128)(2,1)} %get-tuple-element.49), channel_id=1, source_target_pairs={{8,0},{9,1},{10,2},{11,3},{12,4},{13,5},{14,6},{15,7},{0,8},{1,9},... | collective-permute-start | bytes 110600 | tf_op jit(solution)/shard_map/ppermute | solution.py:21
  90.6 2.6 %collective-permute-start.13 = (bf16[48,384]{1,0:T(8,128)(2,1)}, bf16[48,384]{1,0:T(8,128)(2,1)S(1)}, u32[]{:S(2)}, u32[]{:S(2)}) collective-permute-start(bf16[48,384]{1,0:T(8,128)(2,1)} %get-tuple-element.50), channel_id=1, source_target_pairs={{6,0},{7,1},{8,2},{9,3},{10,4},{11,5},{12,6},{13,7},{14,8},{15,9},... | collective-permute-start | bytes 110600 | tf_op jit(solution)/shard_map/ppermute | solution.py:21
  93.2 0.0 collective-permute-done.9.refs_3_
  93.2 1.0 %collective-permute-start.14 = (bf16[48,384]{1,0:T(8,128)(2,1)}, bf16[48,384]{1,0:T(8,128)(2,1)S(1)}, u32[]{:S(2)}, u32[]{:S(2)}) collective-permute-start(bf16[48,384]{1,0:T(8,128)(2,1)} %get-tuple-element.51), channel_id=1, source_target_pairs={{4,0},{5,1},{6,2},{7,3},{8,4},{9,5},{10,6},{11,7},{12,8},{13,9},{1... | collective-permute-start | bytes 110600 | tf_op jit(solution)/shard_map/ppermute | solution.py:21
  94.2 0.0 collective-permute-done.10.refs_4_
  94.2 1.2 %collective-permute-start.15 = (bf16[48,384]{1,0:T(8,128)(2,1)}, bf16[48,384]{1,0:T(8,128)(2,1)S(1)}, u32[]{:S(2)}, u32[]{:S(2)}) collective-permute-start(bf16[48,384]{1,0:T(8,128)(2,1)} %get-tuple-element.52), channel_id=1, source_target_pairs={{2,0},{3,1},{4,2},{5,3},{6,4},{7,5},{8,6},{9,7},{10,8},{11,9},{12,... | collective-permute-start | bytes 110600 | tf_op jit(solution)/shard_map/ppermute | solution.py:21
  95.5 0.0 collective-permute-done.11.refs_5_
  95.5 0.0 collective-permute-done.12.refs_6_
  95.5 0.3 collective-permute-done.13.refs_7_
  95.8 1.5 %collective-permute-done.14.refs_8_ = bf16[48,384]{1,0:T(8,128)(2,1)S(1)} collective-permute-done((bf16[48,384]{1,0:T(8,128)(2,1)}, bf16[48,384]{1,0:T(8,128)(2,1)S(1)}, u32[]{:S(2)}, u32[]{:S(2)}) %collective-permute-start.14) | collective-permute-done | bytes 36896 | tf_op jit(solution)/shard_map/ppermute | solution.py:21
  97.4 1.0 %collective-permute-done.15.refs_9_ = bf16[48,384]{1,0:T(8,128)(2,1)S(1)} collective-permute-done((bf16[48,384]{1,0:T(8,128)(2,1)}, bf16[48,384]{1,0:T(8,128)(2,1)S(1)}, u32[]{:S(2)}, u32[]{:S(2)}) %collective-permute-start.15) | collective-permute-done | bytes 36896 | tf_op jit(solution)/shard_map/ppermute | solution.py:21
  98.4 0.0 copy-done.10
  98.5 0.6 copy-done.16
  99.0 1.8 %shard_map.37 = f32[24,4,384]{2,1,0:T(4,128)} custom-call(f32[48,384]{1,0:T(8,128)} %get-tuple-element.39.refs_0_, bf16[48,384]{1,0:T(8,128)(2,1)} %copy-done.9, f32[48,384]{1,0:T(8,128)} %get-tuple-element.45.refs_2_, bf16[48,384]{1,0:T(8,128)(2,1)} %copy-done.10, bf16[48,384]{1,0:T(8,128)(2,1)} %copy-done.11, bf16[48,384]{1,0:T(8,128)(2,1)} %copy-done.12, ...), custom_call_target="tpu_custom_call" | custom-call | tf_op jit(solution)/shard_map/pallas_call | solution.py:242
  (19 shorter events, 0.0 us)
Async XLA Ops:
  1.9 14.6 %copy-start = (bf16[2,384,3,1,768]{4,1,3,2,0:T(8,128)(2,1)S(1)}, bf16[2,384,3,1,768]{4,1,3,2,0:T(8,128)(2,1)}, u32[]{:S(2)}) copy-start(bf16[2,384,3,1,768]{4,1,3,2,0:T(8,128)(2,1)} %param.2) | copy-start | bytes 10616836
  6.8 61.4 %collective-permute-start = (bf16[6,128,768]{2,1,0:T(8,128)(2,1)}, bf16[6,128,768]{2,1,0:T(8,128)(2,1)}, u32[]{:S(2)}, u32[]{:S(2)}) collective-permute-start(bf16[6,128,768]{2,1,0:T(8,128)(2,1)} %slice.14), channel_id=1, source_target_pairs={{1,0},{2,1},{3,2},{4,3},{5,4},{6,5},{7,6},{8,7},{9,8},{10,9},{11,1... | collective-permute-start | bytes 3538952 | tf_op jit(solution)/shard_map/ppermute | solution.py:21
  12.3 56.5 %collective-permute-start.6 = (bf16[6,128,768]{2,1,0:T(8,128)(2,1)}, bf16[6,128,768]{2,1,0:T(8,128)(2,1)}, u32[]{:S(2)}, u32[]{:S(2)}) collective-permute-start(bf16[6,128,768]{2,1,0:T(8,128)(2,1)} %slice.13), channel_id=1, source_target_pairs={{1,0},{2,1},{3,2},{4,3},{5,4},{6,5},{7,6},{8,7},{9,8},{10,9},{11,1... | collective-permute-start | bytes 3538952 | tf_op jit(solution)/shard_map/ppermute | solution.py:21
  13.0 51.8 %collective-permute-start.7 = (bf16[6,64,768]{2,1,0:T(8,128)(2,1)}, bf16[6,64,768]{2,1,0:T(8,128)(2,1)}, u32[]{:S(2)}, u32[]{:S(2)}) collective-permute-start(bf16[6,64,768]{2,1,0:T(8,128)(2,1)} %slice.16), channel_id=1, source_target_pairs={{1,0},{2,1},{3,2},{4,3},{5,4},{6,5},{7,6},{8,7},{9,8},{10,9},{11,1... | collective-permute-start | bytes 1769480 | tf_op jit(solution)/shard_map/ppermute | solution.py:21
  16.6 0.9 copy-start.1
  17.5 17.7 %copy-start.5 = (s32[2]{0:T(128)}, s32[2]{0:T(128)S(1)}, u32[]{:S(2)}) copy-start(s32[2]{0:T(128)S(1)} %pad_add_fusion.where_ref) | copy-start | bytes 28
  35.2 0.8 copy-start.4
  36.0 28.7 %copy-start.6 = (s32[2]{0:T(128)S(1)}, s32[2]{0:T(128)}, u32[]{:S(2)}) copy-start(s32[2]{0:T(128)} %copy-done.5) | copy-start | bytes 28
  36.0 2.3 %collective-permute-start.1 = (bf16[384,384]{1,0:T(8,128)(2,1)S(1)}, bf16[384,384]{1,0:T(8,128)(2,1)S(1)}, u32[]{:S(2)}, u32[]{:S(2)}) collective-permute-start(bf16[384,384]{1,0:T(8,128)(2,1)S(1)} %get-tuple-element.32), channel_id=1, source_target_pairs={{0,1},{1,0},{2,3},{3,2},{4,5},{5,4},{6,7},{7,6},{8,9},{9,8},{10,11... | collective-permute-start | bytes 884744 | tf_op jit(solution)/shard_map/ppermute | solution.py:185
  37.3 38.4 %collective-permute-start.5 = (bf16[6,64,768]{2,1,0:T(8,128)(2,1)}, bf16[6,64,768]{2,1,0:T(8,128)(2,1)}, u32[]{:S(2)}, u32[]{:S(2)}) collective-permute-start(bf16[6,64,768]{2,1,0:T(8,128)(2,1)} %slice.15), channel_id=1, source_target_pairs={{1,0},{2,1},{3,2},{4,3},{5,4},{6,5},{7,6},{8,7},{9,8},{10,9},{11,1... | collective-permute-start | bytes 1769480 | tf_op jit(solution)/shard_map/ppermute | solution.py:21
  38.3 0.8 copy-start.8
  41.1 11.6 %collective-permute-start.2 = (bf16[192,384]{1,0:T(8,128)(2,1)}, bf16[192,384]{1,0:T(8,128)(2,1)}, u32[]{:S(2)}, u32[]{:S(2)}) collective-permute-start(bf16[192,384]{1,0:T(8,128)(2,1)} %get-tuple-element.34), channel_id=1, source_target_pairs={{0,2},{1,3},{2,0},{3,1},{4,6},{5,7},{6,4},{7,5},{8,10},{9,11},{10,... | collective-permute-start | bytes 442376 | tf_op jit(solution)/shard_map/ppermute | solution.py:185
  54.5 4.7 %collective-permute-start.3 = (bf16[96,384]{1,0:T(8,128)(2,1)}, bf16[96,384]{1,0:T(8,128)(2,1)}, u32[]{:S(2)}, u32[]{:S(2)}) collective-permute-start(bf16[96,384]{1,0:T(8,128)(2,1)} %get-tuple-element.36), channel_id=1, source_target_pairs={{0,4},{1,5},{2,6},{3,7},{4,0},{5,1},{6,2},{7,3},{8,12},{9,13},{10,... | collective-permute-start | bytes 221192 | tf_op jit(solution)/shard_map/ppermute | solution.py:185
  60.8 7.4 %collective-permute-start.4 = (bf16[48,384]{1,0:T(8,128)(2,1)}, bf16[48,384]{1,0:T(8,128)(2,1)S(1)}, u32[]{:S(2)}, u32[]{:S(2)}) collective-permute-start(bf16[48,384]{1,0:T(8,128)(2,1)} %get-tuple-element.38), channel_id=1, source_target_pairs={{0,8},{1,9},{2,10},{3,11},{4,12},{5,13},{6,14},{7,15},{8,0},{9,1},... | collective-permute-start | bytes 110600 | tf_op jit(solution)/shard_map/ppermute | solution.py:185
  64.7 0.9 copy-start.2
  68.2 0.6 copy-start.9
  78.4 0.8 copy-start.3
  79.2 1.6 %collective-permute-start.8 = (bf16[384,384]{1,0:T(8,128)(2,1)S(1)}, bf16[384,384]{1,0:T(8,128)(2,1)S(1)}, u32[]{:S(2)}, u32[]{:S(2)}) collective-permute-start(bf16[384,384]{1,0:T(8,128)(2,1)S(1)} %get-tuple-element.44), channel_id=1, source_target_pairs={{0,1},{1,0},{2,3},{3,2},{4,5},{5,4},{6,7},{7,6},{8,9},{9,8},{10,11... | collective-permute-start | bytes 884744 | tf_op jit(solution)/shard_map/ppermute | solution.py:25
  80.8 0.7 copy-start.7
  83.4 9.8 %collective-permute-start.9 = (bf16[48,384]{1,0:T(8,128)(2,1)}, bf16[48,384]{1,0:T(8,128)(2,1)S(1)}, u32[]{:S(2)}, u32[]{:S(2)}) collective-permute-start(bf16[48,384]{1,0:T(8,128)(2,1)} %get-tuple-element.46), channel_id=1, source_target_pairs={{14,0},{15,1},{0,2},{1,3},{2,4},{3,5},{4,6},{5,7},{6,8},{7,9},{8,1... | collective-permute-start | bytes 110600 | tf_op jit(solution)/shard_map/ppermute | solution.py:21
  85.9 8.4 %collective-permute-start.10 = (bf16[48,384]{1,0:T(8,128)(2,1)}, bf16[48,384]{1,0:T(8,128)(2,1)S(1)}, u32[]{:S(2)}, u32[]{:S(2)}) collective-permute-start(bf16[48,384]{1,0:T(8,128)(2,1)} %get-tuple-element.47), channel_id=1, source_target_pairs={{12,0},{13,1},{14,2},{15,3},{0,4},{1,5},{2,6},{3,7},{4,8},{5,9},{6... | collective-permute-start | bytes 110600 | tf_op jit(solution)/shard_map/ppermute | solution.py:21
  87.8 7.7 %collective-permute-start.11 = (bf16[48,384]{1,0:T(8,128)(2,1)}, bf16[48,384]{1,0:T(8,128)(2,1)S(1)}, u32[]{:S(2)}, u32[]{:S(2)}) collective-permute-start(bf16[48,384]{1,0:T(8,128)(2,1)} %get-tuple-element.48), channel_id=1, source_target_pairs={{10,0},{11,1},{12,2},{13,3},{14,4},{15,5},{0,6},{1,7},{2,8},{3,9},... | collective-permute-start | bytes 110600 | tf_op jit(solution)/shard_map/ppermute | solution.py:21
  88.4 7.1 %collective-permute-start.12 = (bf16[48,384]{1,0:T(8,128)(2,1)}, bf16[48,384]{1,0:T(8,128)(2,1)S(1)}, u32[]{:S(2)}, u32[]{:S(2)}) collective-permute-start(bf16[48,384]{1,0:T(8,128)(2,1)} %get-tuple-element.49), channel_id=1, source_target_pairs={{8,0},{9,1},{10,2},{11,3},{12,4},{13,5},{14,6},{15,7},{0,8},{1,9},... | collective-permute-start | bytes 110600 | tf_op jit(solution)/shard_map/ppermute | solution.py:21
  90.6 5.3 %collective-permute-start.13 = (bf16[48,384]{1,0:T(8,128)(2,1)}, bf16[48,384]{1,0:T(8,128)(2,1)S(1)}, u32[]{:S(2)}, u32[]{:S(2)}) collective-permute-start(bf16[48,384]{1,0:T(8,128)(2,1)} %get-tuple-element.50), channel_id=1, source_target_pairs={{6,0},{7,1},{8,2},{9,3},{10,4},{11,5},{12,6},{13,7},{14,8},{15,9},... | collective-permute-start | bytes 110600 | tf_op jit(solution)/shard_map/ppermute | solution.py:21
  93.2 5.2 %copy-start.10 = (bf16[48,384]{1,0:T(8,128)(2,1)}, bf16[48,384]{1,0:T(8,128)(2,1)S(1)}, u32[]{:S(2)}) copy-start(bf16[48,384]{1,0:T(8,128)(2,1)S(1)} %collective-permute-done.9.refs_3_) | copy-start | bytes 110596
  93.2 4.2 %collective-permute-start.14 = (bf16[48,384]{1,0:T(8,128)(2,1)}, bf16[48,384]{1,0:T(8,128)(2,1)S(1)}, u32[]{:S(2)}, u32[]{:S(2)}) collective-permute-start(bf16[48,384]{1,0:T(8,128)(2,1)} %get-tuple-element.51), channel_id=1, source_target_pairs={{4,0},{5,1},{6,2},{7,3},{8,4},{9,5},{10,6},{11,7},{12,8},{13,9},{1... | collective-permute-start | bytes 110600 | tf_op jit(solution)/shard_map/ppermute | solution.py:21
  94.2 4.2 %copy-start.11 = (bf16[48,384]{1,0:T(8,128)(2,1)}, bf16[48,384]{1,0:T(8,128)(2,1)S(1)}, u32[]{:S(2)}) copy-start(bf16[48,384]{1,0:T(8,128)(2,1)S(1)} %collective-permute-done.10.refs_4_) | copy-start | bytes 110596
  94.2 4.2 %collective-permute-start.15 = (bf16[48,384]{1,0:T(8,128)(2,1)}, bf16[48,384]{1,0:T(8,128)(2,1)S(1)}, u32[]{:S(2)}, u32[]{:S(2)}) collective-permute-start(bf16[48,384]{1,0:T(8,128)(2,1)} %get-tuple-element.52), channel_id=1, source_target_pairs={{2,0},{3,1},{4,2},{5,3},{6,4},{7,5},{8,6},{9,7},{10,8},{11,9},{12,... | collective-permute-start | bytes 110600 | tf_op jit(solution)/shard_map/ppermute | solution.py:21
  95.5 2.9 %copy-start.12 = (bf16[48,384]{1,0:T(8,128)(2,1)}, bf16[48,384]{1,0:T(8,128)(2,1)S(1)}, u32[]{:S(2)}) copy-start(bf16[48,384]{1,0:T(8,128)(2,1)S(1)} %collective-permute-done.11.refs_5_) | copy-start | bytes 110596
  95.5 2.9 %copy-start.13 = (bf16[48,384]{1,0:T(8,128)(2,1)}, bf16[48,384]{1,0:T(8,128)(2,1)S(1)}, u32[]{:S(2)}) copy-start(bf16[48,384]{1,0:T(8,128)(2,1)S(1)} %collective-permute-done.12.refs_6_) | copy-start | bytes 110596
  95.8 2.6 %copy-start.14 = (bf16[48,384]{1,0:T(8,128)(2,1)}, bf16[48,384]{1,0:T(8,128)(2,1)S(1)}, u32[]{:S(2)}) copy-start(bf16[48,384]{1,0:T(8,128)(2,1)S(1)} %collective-permute-done.13.refs_7_) | copy-start | bytes 110596
  97.4 1.1 %copy-start.15 = (bf16[48,384]{1,0:T(8,128)(2,1)}, bf16[48,384]{1,0:T(8,128)(2,1)S(1)}, u32[]{:S(2)}) copy-start(bf16[48,384]{1,0:T(8,128)(2,1)S(1)} %collective-permute-done.14.refs_8_) | copy-start | bytes 110596
  98.4 0.6 copy-start.16

commit v4 on v1

v4 whole, which is shorter than its diff:
```python
import functools
import math

import jax
import jax.numpy as jnp
from jax import lax
from jax.experimental import pallas as pl
from jax.experimental.pallas import tpu as pltpu
from jax.sharding import PartitionSpec as P

X = 64
LANES = 128
ROWS = 16
VMEM = pl.BlockSpec(memory_space=pltpu.VMEM)
SMEM = pl.BlockSpec(memory_space=pltpu.SMEM)
ANY = pl.BlockSpec(memory_space=pl.ANY)


def passed_along(block, axis, distance):
    devices = range(lax.axis_size(axis))
    route = [((i - distance) % len(devices), i) for i in devices]
    return lax.ppermute(block, axis, route)


def swapped(block, axis):
    return lax.ppermute(block, axis, [(i, i ^ 1) for i in range(lax.axis_size(axis))])


def times_links(field_ref, links_ref, mu, adjoint, roll, store):
    count, sites = field_ref.shape[1:]
    for t in range(sites // LANES):
        lanes = slice(t * LANES, (t + 1) * LANES)

        def link(part, a, b):
            row = ((part * 2 + mu) * 3 + a) * 3 + b
            value = jnp.broadcast_to(links_ref[row : row + 1, lanes], (ROWS, LANES))
            return -value if adjoint and part == 1 else value

        def links_of(part, a):
            return [link(part, b, a) if adjoint else link(part, a, b) for b in range(3)]

        u = [[links_of(p, a) for a in range(3)] for p in range(2)]
        if roll:
            lane = lax.broadcasted_iota(jnp.int32, (ROWS, LANES), 1)
            last = (lane & (X - 1)) == X - 1

        def body(m, carry):
            rows = pl.ds(pl.multiple_of(m * ROWS, ROWS), ROWS)
            v = []
            for k in range(6):
                value = field_ref[k, rows, lanes].astype(jnp.float32)
                if roll:
                    ahead = pltpu.roll(value, LANES - 1, 1)
                    around = pltpu.roll(value, X - 1, 1)
                    value = jnp.where(last, around, ahead)
                v.append(value)
            re, im = v[:3], v[3:]
            for a in range(3):
                ur, ui = u[0][a], u[1][a]
                dr = ur[0] * re[0] - ui[0] * im[0]
                di = ur[0] * im[0] + ui[0] * re[0]
                for b in (1, 2):
                    dr = dr + (ur[b] * re[b] - ui[b] * im[b])
                    di = di + (ur[b] * im[b] + ui[b] * re[b])
                store(0, a, m, lanes, dr.astype(jnp.bfloat16))
                store(1, a, m, lanes, di.astype(jnp.bfloat16))
            return carry

        lax.fori_loop(0, count // ROWS, body, 0, unroll=2)


def rows_by_own(slabs, own):
    return slabs % 2 == 0 and own % 8 == 0


def finish(left_of, right_of, slabs, core, acc, send, keep, ready=lambda b: None):
    count = send.shape[0]
    own = count // slabs
    product = [None, None]
    for b in range(3):
        ready(b)
        for part in range(2):
            term = lax.dot_general(
                left_of(part, b), right_of(b), (((1,), (1,)), ((), ())),
                preferred_element_type=jnp.float32,
            )
            product[part] = term if b == 0 else product[part] + term
    sum_re = product[0][:, :count] + product[1][:, count:]
    sum_im = product[0][:, count:] - product[1][:, :count]
    acc[0] = sum_re - sum_re.T
    acc[1] = sum_im + sum_im.T
    if not rows_by_own(slabs, own):
        send[...] = acc[1 - core].astype(jnp.bfloat16)
        keep[...] = acc[core]
        return
    for k in range(slabs // 2):
        block = slice(k * 2 * own, (k + 1) * 2 * own)

        def rows(which):
            at = pl.ds(pl.multiple_of((2 * k + which) * own, 8), own)
            return jnp.concatenate([acc[0, at, :], acc[1, at, :]], axis=0)

        send[block, :] = rows(1 - core).astype(jnp.bfloat16)
        keep[block, :] = rows(core)


def x_kernel(slabs, core_ref, field_ref, links_ref, send, keep, right, acc):
    count = field_ref.shape[1]

    def store(part, a, m, lanes, value):
        right[a, pl.ds(pl.multiple_of(part * count + m * ROWS, ROWS), ROWS), lanes] = value

    times_links(field_ref, links_ref, 0, False, True, store)
    finish(
        lambda part, b: field_ref[part * 3 + b], lambda b: right[b],
        slabs, core_ref[0], acc, send, keep,
    )


def w_kernel(field_ref, links_ref, w_ref):
    def store(part, a, m, lanes, value):
        w_ref[part * 3 + a, pl.ds(pl.multiple_of(m * ROWS, ROWS), ROWS), lanes] = value

    times_links(field_ref, links_ref, 1, True, False, store)


def z_kernel(slabs, core_ref, w_ref, face_hbm, send, keep, right, acc, sems):
    count = w_ref.shape[1]
    copies = []
    for b in range(3):
        for part in range(2):
            to = right.at[b, pl.ds(part * count, count)]
            k = part * 3 + b
            copies.append(pltpu.make_async_copy(face_hbm.at[k], to, sems.at[k]))
    for copy in copies:
        copy.start()

    def ready(b):
        copies[2 * b].wait()
        copies[2 * b + 1].wait()

    finish(
        lambda part, b: w_ref[part * 3 + b], lambda b: right[b],
        slabs, core_ref[0], acc, send, keep, ready,
    )


def call(body, outs, specs, scratch, mib, flops, moved):
    return pl.pallas_call(
        body,
        out_shape=outs,
        in_specs=specs,
        out_specs=[VMEM] * len(outs),
        scratch_shapes=scratch,
        compiler_params=pltpu.CompilerParams(vmem_limit_bytes=mib * 2**20),
        cost_estimate=pl.CostEstimate(flops=flops, bytes_accessed=moved, transcendentals=0),
    )


def shards(vectors, links):
    slabs = lax.axis_size("gz")
    count, planes, sites = vectors.shape[1], vectors.shape[3], vectors.shape[4]
    assert planes == 1 and slabs % 2 == 0
    own = count // slabs
    scale = 1.0 / math.sqrt(12.0 * sites * planes * slabs)
    core = (lax.axis_index("gz").astype(jnp.int32) & 1).reshape(1)
    field = jnp.transpose(vectors, (0, 2, 3, 1, 4)).reshape(6, count, sites)
    links = links.reshape(36, sites)
    face = passed_along(field, "gz", -1)

    flops = 24 * count * count * sites
    moved = 12 * count * sites
    halves = [
        jax.ShapeDtypeStruct((count, count), jnp.bfloat16),
        jax.ShapeDtypeStruct((count, count), jnp.float32),
    ]
    scratch = [
        pltpu.VMEM((3, 2 * count, sites), jnp.bfloat16),
        pltpu.VMEM((2, count, count), jnp.float32),
    ]
    send_x, keep_x = call(
        functools.partial(x_kernel, slabs), halves, [SMEM, VMEM, VMEM], scratch, 28, flops, moved
    )(core, field, links)
    (w,) = call(
        w_kernel, [jax.ShapeDtypeStruct(field.shape, jnp.bfloat16)], [VMEM, VMEM], [], 16,
        count * sites * 66, 2 * moved,
    )(field, links)

    def exchanged(send, keep):
        chip = (keep + swapped(send, "gz").astype(jnp.float32)).astype(jnp.bfloat16)
        if rows_by_own(slabs, own):
            groups = [list(range(c, slabs, 2)) for c in range(2)]
            chip = chip.reshape(slabs // 2, 2 * own, count)
            got = lax.all_to_all(chip, "gz", 0, 0, axis_index_groups=groups)
            return jnp.sum(got.astype(jnp.float32), axis=0).reshape(2, own, count)
        got = lax.all_to_all(chip.reshape(slabs, own, count), "gz", 0, 0)
        got = got.reshape(slabs // 2, 2, own, count)
        return jnp.sum(got.astype(jnp.float32), axis=0)

    sum_x = exchanged(send_x, keep_x)
    face, sum_x, w = lax.optimization_barrier((face, sum_x, w))
    send_z, keep_z = call(
        functools.partial(z_kernel, slabs), halves, [SMEM, VMEM, ANY],
        scratch + [pltpu.SemaphoreType.DMA((6,))], 28, flops, moved,
    )(core, w, face)
    both = jnp.concatenate([sum_x, exchanged(send_z, keep_z)], axis=0)
    return jnp.transpose(both, (1, 0, 2)) * scale


def solution(mesh):
    return jax.shard_map(
        shards,
        mesh=mesh,
        in_specs=(P("grp", None, None, "gz", None), P("grp", None, None, None, "gz", None)),
        out_specs=P("gz", "grp", None),
        check_vma=False,
    )
```

time: 83.9 us -> 78.3 us (0.933)
  waiting for transfers between devices: 39.9 us -> 19 us
  blocking collectives: 0 us -> 16.2 us
  starting transfers between devices: 15 us -> 9.65 us
  local copies, waits for them, and re-layouts: 5.92 us -> 9 us
  other arithmetic: 0.19 us -> 3.12 us
  Pallas kernels: 22.4 us -> 20.9 us
    ppermute x1, waiting for transfers between devices: 24.4 us -> 0.01 us  [passed_along(): return lax.ppermute(block, axis, route)]
    all_to_all x0 -> x1, blocking collectives: none -> 16.2 us  [exchanged(): got = lax.all_to_all(chip, 'gz', 0, 0, axis_index_groups=groups)]
    all_to_all x2 -> x1, starting transfers between devices: 9.57 us -> 4.06 us  [exchanged(): got = lax.all_to_all(chip, 'gz', 0, 0, axis_index_groups=groups)]
    unnamed x4 -> x12, local copies, waits for them, and re-layouts: 4 us -> 7.59 us
    ppermute x0 -> x2, waiting for transfers between devices: none -> 3.14 us  [swapped(): lax.ppermute(block, axis, [(i, i ^ 1) for i in range(lax.axis_size(axis))])]
    pallas_call x2 -> x3, Pallas kernels: 22.4 us -> 20.9 us  [the longest x1 12.2 us: shards(): call(functools.partial(x_kernel, slabs), halves, [SMEM, VMEM, VMEM], scra...]
    unnamed x0 -> x1, other arithmetic: none -> 1.2 us
    slice x1 -> x0, local copies, waits for them, and re-layouts: 1.16 us -> none  [shards(): links_x = links[:, 0].reshape(18, sites)]
  transfers between devices with their start and end apart: 3 -> 4, of which waited for: 2 -> 3; matrix products, arithmetic and copies ran while one was open for 2% -> 5% of each run, Pallas kernels for 27% -> 20%
where the time goes in v4:
time: 78.3 us; the launch traced here: 77.9 us
  Pallas kernels  20.9 us (27%)
  waiting for transfers between devices  19 us (24%)
  blocking collectives  16.2 us (21%)
  starting transfers between devices  9.65 us (12%)
  local copies, waits for them, and re-layouts  9 us (11%)
  other arithmetic  3.12 us (4%)
    all_to_all x1, blocking collectives, exchanged(): got = lax.all_to_all(chip, 'gz', 0, 0, axis_index_groups=groups)  16.2 us
    all_to_all x1, waiting for transfers between devices, exchanged(): got = lax.all_to_all(chip, 'gz', 0, 0, axis_index_groups=groups)  15.8 us
    pallas_call x1, Pallas kernels, shards(): call(functools.partial(x_kernel, slabs), halves, [SMEM, VMEM, VMEM], scra...  12.2 us
    unnamed x12, local copies, waits for them, and re-layouts  7.59 us
    ppermute x1, starting transfers between devices, passed_along(): return lax.ppermute(block, axis, route)  5.44 us
    pallas_call x1, Pallas kernels, shards(): call(functools.partial(z_kernel, slabs), halves, [SMEM, VMEM, ANY], scrat...  5.05 us
    all_to_all x1, starting transfers between devices, exchanged(): got = lax.all_to_all(chip, 'gz', 0, 0, axis_index_groups=groups)  4.06 us
    pallas_call x1, Pallas kernels, shards(): call(w_kernel, [jax.ShapeDtypeStruct(field.shape, jnp.bfloat16)], [VMEM,...  3.64 us
  transfers between devices with their start and end apart: 4, of which 3 were waited for; matrix products, arithmetic and copies ran while one was open for 5% of the time, Pallas kernels for 20%

profile of v4, /device:TPU:0, one launch (start us, length us, event | category | flops | bytes accessed | tf_op | source)
XLA Modules:
  0.0 77.9 jit_solution(827945546413598469)
XLA Ops:
  0.0 5.4 %collective-permute-start = (bf16[6,384,768]{2,1,0:T(8,128)(2,1)}, bf16[6,384,768]{2,1,0:T(8,128)(2,1)}, u32[]{:S(2)}, u32[]{:S(2)}) collective-permute-start(bf16[6,384,768]{2,1,0:T(8,128)(2,1)} %bitcast.10), channel_id=1, source_target_pairs={{1,0},{2,1},{3,2},{4,3},{5,4},{6,5},{7,6},{8,7},{9,8},{10,9},{11,1... | collective-permute-start | bytes 10616840 | tf_op jit(solution)/shard_map/ppermute | solution.py:22
  5.4 1.2 %reduce = f32[2,2,3,3,768]{4,3,2,1,0:T(4,128)S(1)} reduce(f32[2,2,3,3,1,768]{5,4,3,2,1,0:T(1,128)} %param.3, f32[]{:T(128)} %constant.12), dimensions={4}, to_apply=%param.3.reduce_sub_computation | reduce | bytes 221188 | tf_op args[1]
  6.6 0.7 reshape.23.links_ref
  7.3 0.0 copy-start
  7.3 2.0 %copy-done = bf16[2,384,3,1,768]{4,1,3,2,0:T(8,128)(2,1)S(1)} copy-done((bf16[2,384,3,1,768]{4,1,3,2,0:T(8,128)(2,1)S(1)}, bf16[2,384,3,1,768]{4,1,3,2,0:T(8,128)(2,1)}, u32[]{:S(2)}) %copy-start) | copy-done | bytes 3538968
  9.3 0.0 copy-start.4
  9.4 0.9 %copy-done.4 = f32[36,768]{1,0:T(8,128)S(1)} copy-done((f32[36,768]{1,0:T(8,128)S(1)}, f32[36,768]{1,0:T(8,128)}, u32[]{:S(2)}) %copy-start.4) | copy-done | bytes 110616
  10.3 0.0 copy-start.1
  10.3 12.2 %shard_map.28 = (bf16[384,384]{1,0:T(8,128)(2,1)S(1)}, f32[384,384]{1,0:T(8,128)S(1)}) custom-call(s32[1]{0:T(128)} %bitcast.2.core_ref, bf16[6,384,768]{2,1,0:T(8,128)(2,1)S(1)} %bitcast.11, f32[36,768]{1,0:T(8,128)S(1)} %copy-done.4), custom_call_target="tpu_custom_call" | custom-call | flops 2717908992 | bytes 3538944 | tf_op jit(solution)/shard_map/pallas_call | solution.py:181
  22.4 0.1 collective-permute-start.1
  22.5 1.6 %collective-permute-done.1 = bf16[384,384]{1,0:T(8,128)(2,1)S(1)} collective-permute-done((bf16[384,384]{1,0:T(8,128)(2,1)S(1)}, bf16[384,384]{1,0:T(8,128)(2,1)S(1)}, u32[]{:S(2)}, u32[]{:S(2)}) %collective-permute-start.1) | collective-permute-done | bytes 294944 | tf_op jit(solution)/shard_map/ppermute | solution.py:26
  24.1 0.8 %add_convert_fusion.1 = bf16[384,384]{1,0:T(8,128)(2,1)} fusion(f32[384,384]{1,0:T(8,128)S(1)} %get-tuple-element.12, bf16[384,384]{1,0:T(8,128)(2,1)S(1)} %collective-permute-done.1), kind=kLoop, calls=%fused_computation.3 | loop fusion | flops 442368 | bytes 1179648 | tf_op jit(solution)/shard_map/convert_element_type | solution.py:190
  24.9 4.1 %all-to-all-start = ((bf16[8,48,384]{2,1,0:T(8,128)(2,1)}), bf16[8,48,384]{2,1,0:T(8,128)(2,1)}, u32[]{:S(2)}, u32[]{:S(2)}) async-start(bf16[8,48,384]{2,1,0:T(8,128)(2,1)} %bitcast.13), calls=%async_computation | async-start | bytes 589824 | tf_op jit(solution)/shard_map/all_to_all | solution.py:194
  28.9 0.0 copy-done.1
  28.9 0.0 copy-start.5
  28.9 0.9 %copy-done.5 = f32[36,768]{1,0:T(8,128)S(1)} copy-done((f32[36,768]{1,0:T(8,128)S(1)}, f32[36,768]{1,0:T(8,128)}, u32[]{:S(2)}) %copy-start.5) | copy-done | bytes 110616
  29.8 3.6 %shard_map.29.w_ref = bf16[6,384,768]{2,1,0:T(8,128)(2,1)S(1)} custom-call(bf16[6,384,768]{2,1,0:T(8,128)(2,1)S(1)} %bitcast.12, f32[36,768]{1,0:T(8,128)S(1)} %copy-done.5), custom_call_target="tpu_custom_call" | custom-call | flops 19464192 | bytes 7077888 | tf_op jit(solution)/shard_map/pallas_call | solution.py:184
  33.5 0.0 copy-start.2
  33.5 1.8 %copy-done.2 = bf16[6,384,768]{2,1,0:T(8,128)(2,1)} copy-done((bf16[6,384,768]{2,1,0:T(8,128)(2,1)}, bf16[6,384,768]{2,1,0:T(8,128)(2,1)S(1)}, u32[]{:S(2)}) %copy-start.2) | copy-done | bytes 3538968
  35.3 15.8 %all-to-all-done = bf16[8,48,384]{2,1,0:T(8,128)(2,1)} async-done(((bf16[8,48,384]{2,1,0:T(8,128)(2,1)}), bf16[8,48,384]{2,1,0:T(8,128)(2,1)}, u32[]{:S(2)}, u32[]{:S(2)}) %all-to-all-start) | async-done | bytes 294944 | tf_op jit(solution)/shard_map/all_to_all | solution.py:194
  51.1 1.0 %convert_reduce_fusion.1 = f32[48,384]{1,0:T(8,128)S(1)} fusion(bf16[8,48,384]{2,1,0:T(8,128)(2,1)} %all-to-all-done), kind=kLoop, calls=%fused_computation.2 | loop fusion | flops 276480 | bytes 368640 | tf_op jit(solution)/shard_map/reduce_sum | solution.py:195
  52.1 0.0 collective-permute-done.face_hbm
  52.1 0.0 copy-start.3
  52.1 2.0 %copy-done.3 = bf16[6,384,768]{2,1,0:T(8,128)(2,1)S(1)} copy-done((bf16[6,384,768]{2,1,0:T(8,128)(2,1)S(1)}, bf16[6,384,768]{2,1,0:T(8,128)(2,1)}, u32[]{:S(2)}) %copy-start.3) | copy-done | bytes 3538968
  54.1 5.0 %shard_map.30 = (bf16[384,384]{1,0:T(8,128)(2,1)S(1)}, f32[384,384]{1,0:T(8,128)S(1)}) custom-call(s32[1]{0:T(128)} %bitcast.2.core_ref, bf16[6,384,768]{2,1,0:T(8,128)(2,1)S(1)} %copy-done.3, bf16[6,384,768]{2,1,0:T(8,128)(2,1)} %collective-permute-done.face_hbm), custom_call_target="tpu_custom_call" | custom-call | flops 2717908992 | bytes 3538944 | tf_op jit(solution)/shard_map/pallas_call | solution.py:202
  59.2 0.1 collective-permute-start.2
  59.3 1.6 %collective-permute-done.2 = bf16[384,384]{1,0:T(8,128)(2,1)S(1)} collective-permute-done((bf16[384,384]{1,0:T(8,128)(2,1)S(1)}, bf16[384,384]{1,0:T(8,128)(2,1)S(1)}, u32[]{:S(2)}, u32[]{:S(2)}) %collective-permute-start.2) | collective-permute-done | bytes 294944 | tf_op jit(solution)/shard_map/ppermute | solution.py:26
  60.8 0.1 add_convert_fusion
  60.9 16.2 %all_to_all.10 = bf16[8,48,384]{2,1,0:T(8,128)(2,1)S(1)} all-to-all(bf16[8,48,384]{2,1,0:T(8,128)(2,1)S(1)} %bitcast.14), channel_id=1, replica_groups={{0,2,4,6,8,10,12,14},{1,3,5,7,9,11,13,15},{16,18,20,22,24,26,28,30},{17..., dimensions={0} | all-to-all | bytes 589824 | tf_op jit(solution)/shard_map/all_to_all | solution.py:194
  77.2 0.7 copy.3
  (2 shorter events, 0.1 us)
Async XLA Ops:
  0.0 52.1 %collective-permute-start = (bf16[6,384,768]{2,1,0:T(8,128)(2,1)}, bf16[6,384,768]{2,1,0:T(8,128)(2,1)}, u32[]{:S(2)}, u32[]{:S(2)}) collective-permute-start(bf16[6,384,768]{2,1,0:T(8,128)(2,1)} %bitcast.10), channel_id=1, source_target_pairs={{1,0},{2,1},{3,2},{4,3},{5,4},{6,5},{7,6},{8,7},{9,8},{10,9},{11,1... | collective-permute-start | bytes 10616840 | tf_op jit(solution)/shard_map/ppermute | solution.py:22
  7.3 2.0 %copy-start = (bf16[2,384,3,1,768]{4,1,3,2,0:T(8,128)(2,1)S(1)}, bf16[2,384,3,1,768]{4,1,3,2,0:T(8,128)(2,1)}, u32[]{:S(2)}) copy-start(bf16[2,384,3,1,768]{4,1,3,2,0:T(8,128)(2,1)} %param.2) | copy-start | bytes 10616836
  9.3 0.9 %copy-start.4 = (f32[36,768]{1,0:T(8,128)S(1)}, f32[36,768]{1,0:T(8,128)}, u32[]{:S(2)}) copy-start(f32[36,768]{1,0:T(8,128)} %reshape.23.links_ref) | copy-start | bytes 331780
  10.3 18.7 %copy-start.1 = (bf16[2,384,3,1,768]{4,1,3,2,0:T(8,128)(2,1)S(1)}, bf16[2,384,3,1,768]{4,1,3,2,0:T(8,128)(2,1)}, u32[]{:S(2)}) copy-start(bf16[2,384,3,1,768]{4,1,3,2,0:T(8,128)(2,1)} %param.2) | copy-start | bytes 10616836
  22.4 1.6 %collective-permute-start.1 = (bf16[384,384]{1,0:T(8,128)(2,1)S(1)}, bf16[384,384]{1,0:T(8,128)(2,1)S(1)}, u32[]{:S(2)}, u32[]{:S(2)}) collective-permute-start(bf16[384,384]{1,0:T(8,128)(2,1)S(1)} %get-tuple-element.13), channel_id=1, source_target_pairs={{0,1},{1,0},{2,3},{3,2},{4,5},{5,4},{6,7},{7,6},{8,9},{9,8},{10,11... | collective-permute-start | bytes 884744 | tf_op jit(solution)/shard_map/ppermute | solution.py:26
  24.9 26.3 %all-to-all-start = ((bf16[8,48,384]{2,1,0:T(8,128)(2,1)}), bf16[8,48,384]{2,1,0:T(8,128)(2,1)}, u32[]{:S(2)}, u32[]{:S(2)}) async-start(bf16[8,48,384]{2,1,0:T(8,128)(2,1)} %bitcast.13), calls=%async_computation | async-start | bytes 589824 | tf_op jit(solution)/shard_map/all_to_all | solution.py:194
  28.9 0.9 %copy-start.5 = (f32[36,768]{1,0:T(8,128)S(1)}, f32[36,768]{1,0:T(8,128)}, u32[]{:S(2)}) copy-start(f32[36,768]{1,0:T(8,128)} %reshape.23.links_ref) | copy-start | bytes 331780
  33.5 1.8 %copy-start.2 = (bf16[6,384,768]{2,1,0:T(8,128)(2,1)}, bf16[6,384,768]{2,1,0:T(8,128)(2,1)S(1)}, u32[]{:S(2)}) copy-start(bf16[6,384,768]{2,1,0:T(8,128)(2,1)S(1)} %shard_map.29.w_ref) | copy-start | bytes 10616836
  52.1 2.0 %copy-start.3 = (bf16[6,384,768]{2,1,0:T(8,128)(2,1)S(1)}, bf16[6,384,768]{2,1,0:T(8,128)(2,1)}, u32[]{:S(2)}) copy-start(bf16[6,384,768]{2,1,0:T(8,128)(2,1)} %copy-done.2) | copy-start | bytes 10616836
  59.2 1.6 %collective-permute-start.2 = (bf16[384,384]{1,0:T(8,128)(2,1)S(1)}, bf16[384,384]{1,0:T(8,128)(2,1)S(1)}, u32[]{:S(2)}, u32[]{:S(2)}) collective-permute-start(bf16[384,384]{1,0:T(8,128)(2,1)S(1)} %get-tuple-element.18), channel_id=1, source_target_pairs={{0,1},{1,0},{2,3},{3,2},{4,5},{5,4},{6,7},{7,6},{8,9},{9,8},{10,11... | collective-permute-start | bytes 884744 | tf_op jit(solution)/shard_map/ppermute | solution.py:26

commit v5 on v4

--- a/solution.py
+++ b/solution.py
@@ -179,10 +179,10 @@
         pltpu.VMEM((2, count, count), jnp.float32),
     ]
     send_x, keep_x = call(
-        functools.partial(x_kernel, slabs), halves, [SMEM, VMEM, VMEM], scratch, 28, flops, moved
+        functools.partial(x_kernel, slabs), halves, [SMEM, VMEM, VMEM], scratch, 22, flops, moved
     )(core, field, links)
     (w,) = call(
-        w_kernel, [jax.ShapeDtypeStruct(field.shape, jnp.bfloat16)], [VMEM, VMEM], [], 16,
+        w_kernel, [jax.ShapeDtypeStruct(field.shape, jnp.bfloat16)], [VMEM, VMEM], [], 12,
         count * sites * 66, 2 * moved,
     )(field, links)
 
@@ -198,10 +198,9 @@
         return jnp.sum(got.astype(jnp.float32), axis=0)
 
     sum_x = exchanged(send_x, keep_x)
-    face, sum_x, w = lax.optimization_barrier((face, sum_x, w))
     send_z, keep_z = call(
         functools.partial(z_kernel, slabs), halves, [SMEM, VMEM, ANY],
-        scratch + [pltpu.SemaphoreType.DMA((6,))], 28, flops, moved,
+        scratch + [pltpu.SemaphoreType.DMA((6,))], 18, flops, moved,
     )(core, w, face)
     both = jnp.concatenate([sum_x, exchanged(send_z, keep_z)], axis=0)
     return jnp.transpose(both, (1, 0, 2)) * scale

time: 78.3 us -> 80.7 us (1.031)
  waiting for transfers between devices: 19 us -> 38.3 us
  blocking collectives: 16.2 us -> 0 us
  local copies, waits for them, and re-layouts: 9 us -> 2.75 us
  starting transfers between devices: 9.65 us -> 15.5 us
    ppermute x1, waiting for transfers between devices: 0.01 us -> 20.1 us  [passed_along(): return lax.ppermute(block, axis, route)]
    all_to_all x1 -> x0, blocking collectives: 16.2 us -> none  [exchanged(): got = lax.all_to_all(chip, 'gz', 0, 0, axis_index_groups=groups)]
    all_to_all x1 -> x2, starting transfers between devices: 4.06 us -> 9.89 us  [exchanged(): got = lax.all_to_all(chip, 'gz', 0, 0, axis_index_groups=groups)]
    unnamed x12 -> x2, local copies, waits for them, and re-layouts: 7.59 us -> 2 us
    ppermute x2, waiting for transfers between devices: 3.14 us -> 0.01 us  [swapped(): lax.ppermute(block, axis, [(i, i ^ 1) for i in range(lax.axis_size(axis))])]
    all_to_all x1 -> x2, waiting for transfers between devices: 15.8 us -> 18.1 us  [exchanged(): got = lax.all_to_all(chip, 'gz', 0, 0, axis_index_groups=groups)]
    reduce_sum x2, other arithmetic: 1.05 us -> 0.08 us  [exchanged(): return jnp.sum(got.astype(jnp.float32), axis=0).reshape(2, own, count)]
  transfers between devices with their start and end apart: 4 -> 5, of which waited for: 3 -> 3; matrix products, arithmetic and copies ran while one was open for 5% -> 4% of each run, Pallas kernels for 20% -> 26%
where the time goes in v5:
time: 80.7 us; the launch traced here: 80.3 us
  waiting for transfers between devices  38.3 us (47%)
  Pallas kernels  20.9 us (26%)
  starting transfers between devices  15.5 us (19%)
  other arithmetic  2.83 us (4%)
  local copies, waits for them, and re-layouts  2.75 us (3%)
    ppermute x1, waiting for transfers between devices, passed_along(): return lax.ppermute(block, axis, route)  20.1 us
    all_to_all x2, waiting for transfers between devices, exchanged(): got = lax.all_to_all(chip, 'gz', 0, 0, axis_index_groups=groups)  18.1 us
    pallas_call x1, Pallas kernels, shards(): call(functools.partial(x_kernel, slabs), halves, [SMEM, VMEM, VMEM], scra...  12.2 us
    all_to_all x2, starting transfers between devices, exchanged(): got = lax.all_to_all(chip, 'gz', 0, 0, axis_index_groups=groups)  9.89 us
    ppermute x1, starting transfers between devices, passed_along(): return lax.ppermute(block, axis, route)  5.44 us
    pallas_call x1, Pallas kernels, shards(): call(functools.partial(z_kernel, slabs), halves, [SMEM, VMEM, ANY], scrat...  5.05 us
    pallas_call x1, Pallas kernels, shards(): call(w_kernel, [jax.ShapeDtypeStruct(field.shape, jnp.bfloat16)], [VMEM,...  3.65 us
    unnamed x2, local copies, waits for them, and re-layouts  2 us
  transfers between devices with their start and end apart: 5, of which 3 were waited for; matrix products, arithmetic and copies ran while one was open for 4% of the time, Pallas kernels for 26%

profile of v5, /device:TPU:0, one launch (start us, length us, event | category | flops | bytes accessed | tf_op | source)
XLA Modules:
  0.0 80.3 jit_solution(16805017943106214916)
XLA Ops:
  0.0 5.4 %collective-permute-start.1 = (bf16[6,384,768]{2,1,0:T(8,128)(2,1)}, bf16[6,384,768]{2,1,0:T(8,128)(2,1)}, u32[]{:S(2)}, u32[]{:S(2)}) collective-permute-start(bf16[6,384,768]{2,1,0:T(8,128)(2,1)} %bitcast.10), channel_id=1, source_target_pairs={{1,0},{2,1},{3,2},{4,3},{5,4},{6,5},{7,6},{8,7},{9,8},{10,9},{11,1... | collective-permute-start | bytes 10616840 | tf_op jit(solution)/shard_map/ppermute | solution.py:22
  5.4 1.2 %reduce = f32[2,2,3,3,768]{4,3,2,1,0:T(4,128)S(1)} reduce(f32[2,2,3,3,1,768]{5,4,3,2,1,0:T(1,128)} %param.3, f32[]{:T(128)} %constant.12), dimensions={4}, to_apply=%param.3.reduce_sub_computation | reduce | bytes 221188 | tf_op args[1]
  6.6 0.1 reshape.23.links_ref
  6.7 0.0 copy-start
  6.7 2.0 %copy-done = bf16[2,384,3,1,768]{4,1,3,2,0:T(8,128)(2,1)S(1)} copy-done((bf16[2,384,3,1,768]{4,1,3,2,0:T(8,128)(2,1)S(1)}, bf16[2,384,3,1,768]{4,1,3,2,0:T(8,128)(2,1)}, u32[]{:S(2)}) %copy-start) | copy-done | bytes 3538968
  8.7 12.2 %shard_map.28 = (bf16[384,384]{1,0:T(8,128)(2,1)S(1)}, f32[384,384]{1,0:T(8,128)S(1)}) custom-call(s32[1]{0:T(128)} %bitcast.core_ref, bf16[6,384,768]{2,1,0:T(8,128)(2,1)S(1)} %bitcast.11, f32[36,768]{1,0:T(8,128)S(1)} %reshape.23.links_ref), custom_call_target="tpu_custom_call" | custom-call | flops 2717908992 | bytes 3538944 | tf_op jit(solution)/shard_map/pallas_call | solution.py:181
  20.9 0.1 collective-permute-start
  21.0 3.6 %shard_map.29.w_ref = bf16[6,384,768]{2,1,0:T(8,128)(2,1)S(1)} custom-call(bf16[6,384,768]{2,1,0:T(8,128)(2,1)S(1)} %bitcast.12, f32[36,768]{1,0:T(8,128)S(1)} %reshape.23.links_ref), custom_call_target="tpu_custom_call" | custom-call | flops 19464192 | bytes 7077888 | tf_op jit(solution)/shard_map/pallas_call | solution.py:184
  24.6 20.1 %collective-permute-done.1.face_hbm = bf16[6,384,768]{2,1,0:T(8,128)(2,1)} collective-permute-done((bf16[6,384,768]{2,1,0:T(8,128)(2,1)}, bf16[6,384,768]{2,1,0:T(8,128)(2,1)}, u32[]{:S(2)}, u32[]{:S(2)}) %collective-permute-start.1) | collective-permute-done | bytes 3538976 | tf_op jit(solution)/shard_map/ppermute | solution.py:22
  44.8 5.1 %shard_map.30 = (bf16[384,384]{1,0:T(8,128)(2,1)S(1)}, f32[384,384]{1,0:T(8,128)S(1)}) custom-call(s32[1]{0:T(128)} %bitcast.core_ref, bf16[6,384,768]{2,1,0:T(8,128)(2,1)S(1)} %shard_map.29.w_ref, bf16[6,384,768]{2,1,0:T(8,128)(2,1)} %collective-permute-done.1.face_hbm), custom_call_target="tpu_custom_call" | custom-call | flops 2717908992 | bytes 3538944 | tf_op jit(solution)/shard_map/pallas_call | solution.py:201
  49.8 0.1 collective-permute-start.2
  49.9 0.0 collective-permute-done
  49.9 0.8 add_convert_fusion.1
  50.7 6.2 %all-to-all-start = ((bf16[8,48,384]{2,1,0:T(8,128)(2,1)}), bf16[8,48,384]{2,1,0:T(8,128)(2,1)S(1)}, u32[]{:S(2)}, u32[]{:S(2)}) async-start(bf16[8,48,384]{2,1,0:T(8,128)(2,1)} %bitcast.3), calls=%async_computation | async-start | bytes 589824 | tf_op jit(solution)/shard_map/all_to_all | solution.py:194
  56.9 0.0 collective-permute-done.2
  56.9 0.8 add_convert_fusion
  57.7 9.0 %all-to-all-done = bf16[8,48,384]{2,1,0:T(8,128)(2,1)S(1)} async-done(((bf16[8,48,384]{2,1,0:T(8,128)(2,1)}), bf16[8,48,384]{2,1,0:T(8,128)(2,1)S(1)}, u32[]{:S(2)}, u32[]{:S(2)}) %all-to-all-start) | async-done | bytes 294944 | tf_op jit(solution)/shard_map/all_to_all | solution.py:194
  66.7 3.6 %all-to-all-start.1 = ((bf16[8,48,384]{2,1,0:T(8,128)(2,1)}), bf16[8,48,384]{2,1,0:T(8,128)(2,1)S(1)}, u32[]{:S(2)}, u32[]{:S(2)}) async-start(bf16[8,48,384]{2,1,0:T(8,128)(2,1)} %bitcast.6), calls=%async_computation.1 | async-start | bytes 589824 | tf_op jit(solution)/shard_map/all_to_all | solution.py:194
  70.4 9.1 %all-to-all-done.1 = bf16[8,48,384]{2,1,0:T(8,128)(2,1)S(1)} async-done(((bf16[8,48,384]{2,1,0:T(8,128)(2,1)}), bf16[8,48,384]{2,1,0:T(8,128)(2,1)S(1)}, u32[]{:S(2)}, u32[]{:S(2)}) %all-to-all-start.1) | async-done | bytes 294944 | tf_op jit(solution)/shard_map/all_to_all | solution.py:194
  79.6 0.7 copy.3
  (3 shorter events, 0.1 us)
Async XLA Ops:
  0.0 44.8 %collective-permute-start.1 = (bf16[6,384,768]{2,1,0:T(8,128)(2,1)}, bf16[6,384,768]{2,1,0:T(8,128)(2,1)}, u32[]{:S(2)}, u32[]{:S(2)}) collective-permute-start(bf16[6,384,768]{2,1,0:T(8,128)(2,1)} %bitcast.10), channel_id=1, source_target_pairs={{1,0},{2,1},{3,2},{4,3},{5,4},{6,5},{7,6},{8,7},{9,8},{10,9},{11,1... | collective-permute-start | bytes 10616840 | tf_op jit(solution)/shard_map/ppermute | solution.py:22
  6.7 2.0 %copy-start = (bf16[2,384,3,1,768]{4,1,3,2,0:T(8,128)(2,1)S(1)}, bf16[2,384,3,1,768]{4,1,3,2,0:T(8,128)(2,1)}, u32[]{:S(2)}) copy-start(bf16[2,384,3,1,768]{4,1,3,2,0:T(8,128)(2,1)} %param.2) | copy-start | bytes 10616836
  20.9 29.0 %collective-permute-start = (bf16[384,384]{1,0:T(8,128)(2,1)S(1)}, bf16[384,384]{1,0:T(8,128)(2,1)S(1)}, u32[]{:S(2)}, u32[]{:S(2)}) collective-permute-start(bf16[384,384]{1,0:T(8,128)(2,1)S(1)} %get-tuple-element.10), channel_id=1, source_target_pairs={{0,1},{1,0},{2,3},{3,2},{4,5},{5,4},{6,7},{7,6},{8,9},{9,8},{10,11... | collective-permute-start | bytes 884744 | tf_op jit(solution)/shard_map/ppermute | solution.py:26
  49.8 7.1 %collective-permute-start.2 = (bf16[384,384]{1,0:T(8,128)(2,1)S(1)}, bf16[384,384]{1,0:T(8,128)(2,1)S(1)}, u32[]{:S(2)}, u32[]{:S(2)}) collective-permute-start(bf16[384,384]{1,0:T(8,128)(2,1)S(1)} %get-tuple-element.12), channel_id=1, source_target_pairs={{0,1},{1,0},{2,3},{3,2},{4,5},{5,4},{6,7},{7,6},{8,9},{9,8},{10,11... | collective-permute-start | bytes 884744 | tf_op jit(solution)/shard_map/ppermute | solution.py:26
  50.7 16.0 %all-to-all-start = ((bf16[8,48,384]{2,1,0:T(8,128)(2,1)}), bf16[8,48,384]{2,1,0:T(8,128)(2,1)S(1)}, u32[]{:S(2)}, u32[]{:S(2)}) async-start(bf16[8,48,384]{2,1,0:T(8,128)(2,1)} %bitcast.3), calls=%async_computation | async-start | bytes 589824 | tf_op jit(solution)/shard_map/all_to_all | solution.py:194
  66.7 12.8 %all-to-all-start.1 = ((bf16[8,48,384]{2,1,0:T(8,128)(2,1)}), bf16[8,48,384]{2,1,0:T(8,128)(2,1)S(1)}, u32[]{:S(2)}, u32[]{:S(2)}) async-start(bf16[8,48,384]{2,1,0:T(8,128)(2,1)} %bitcast.6), calls=%async_computation.1 | async-start | bytes 589824 | tf_op jit(solution)/shard_map/all_to_all | solution.py:194

commit v6 on v5

--- a/solution.py
+++ b/solution.py
@@ -117,7 +117,9 @@
     )
 
 
-def w_kernel(field_ref, links_ref, w_ref):
+def w_kernel(field_ref, links_ref, keep_ref, got_ref, w_ref, chip_ref):
+    chip_ref[...] = (keep_ref[...] + got_ref[...].astype(jnp.float32)).astype(jnp.bfloat16)
+
     def store(part, a, m, lanes, value):
         w_ref[part * 3 + a, pl.ds(pl.multiple_of(m * ROWS, ROWS), ROWS), lanes] = value
 
@@ -181,28 +183,29 @@
     send_x, keep_x = call(
         functools.partial(x_kernel, slabs), halves, [SMEM, VMEM, VMEM], scratch, 22, flops, moved
     )(core, field, links)
-    (w,) = call(
-        w_kernel, [jax.ShapeDtypeStruct(field.shape, jnp.bfloat16)], [VMEM, VMEM], [], 12,
+    w, chip_x = call(
+        w_kernel, [jax.ShapeDtypeStruct(field.shape, jnp.bfloat16), halves[0]], [VMEM] * 4, [], 12,
         count * sites * 66, 2 * moved,
-    )(field, links)
-
-    def exchanged(send, keep):
-        chip = (keep + swapped(send, "gz").astype(jnp.float32)).astype(jnp.bfloat16)
+    )(field, links, keep_x, swapped(send_x, "gz"))
+
+    def exchanged(chip):
         if rows_by_own(slabs, own):
             groups = [list(range(c, slabs, 2)) for c in range(2)]
             chip = chip.reshape(slabs // 2, 2 * own, count)
-            got = lax.all_to_all(chip, "gz", 0, 0, axis_index_groups=groups)
-            return jnp.sum(got.astype(jnp.float32), axis=0).reshape(2, own, count)
+            got = lax.psum_scatter(chip, "gz", scatter_dimension=0, axis_index_groups=groups)
+            return got.astype(jnp.float32).reshape(2, own, count)
         got = lax.all_to_all(chip.reshape(slabs, own, count), "gz", 0, 0)
         got = got.reshape(slabs // 2, 2, own, count)
         return jnp.sum(got.astype(jnp.float32), axis=0)
 
-    sum_x = exchanged(send_x, keep_x)
+    sum_x = exchanged(chip_x)
+    core, sum_x = lax.optimization_barrier((core, sum_x))
     send_z, keep_z = call(
         functools.partial(z_kernel, slabs), halves, [SMEM, VMEM, ANY],
         scratch + [pltpu.SemaphoreType.DMA((6,))], 18, flops, moved,
     )(core, w, face)
-    both = jnp.concatenate([sum_x, exchanged(send_z, keep_z)], axis=0)
+    chip_z = (keep_z + swapped(send_z, "gz").astype(jnp.float32)).astype(jnp.bfloat16)
+    both = jnp.concatenate([sum_x, exchanged(chip_z)], axis=0)
     return jnp.transpose(both, (1, 0, 2)) * scale
 
 

time: 80.7 us -> 171 us (2.12)
  waiting for transfers between devices: 38.3 us -> 120 us
  between operations: 0.09 us -> 13.5 us
  starting transfers between devices: 15.5 us -> 5.63 us
  local copies, waits for them, and re-layouts: 2.75 us -> 6.54 us
    reduce_scatter x0 -> x2, waiting for transfers between devices: none -> 117 us  [exchanged(): lax.psum_scatter(chip, 'gz', scatter_dimension=0, axis_index_groups=groups)]
    ppermute x1, waiting for transfers between devices: 20.1 us -> 0.01 us  [passed_along(): return lax.ppermute(block, axis, route)]
    all_to_all x2 -> x0, waiting for transfers between devices: 18.1 us -> none  [exchanged(): got = lax.all_to_all(chip, 'gz', 0, 0, axis_index_groups=groups)]
    all_to_all x2 -> x0, starting transfers between devices: 9.89 us -> none  [exchanged(): got = lax.all_to_all(chip, 'gz', 0, 0, axis_index_groups=groups)]
    unnamed x2 -> x6, local copies, waits for them, and re-layouts: 2 us -> 5.79 us
    ppermute x2, waiting for transfers between devices: 0.01 us -> 3.14 us  [swapped(): lax.ppermute(block, axis, [(i, i ^ 1) for i in range(lax.axis_size(axis))])]
  transfers between devices with their start and end apart: 5 -> 5, of which waited for: 3 -> 4; matrix products, arithmetic and copies ran while one was open for 4% -> 1% of each run, Pallas kernels for 26% -> 10%
where the time goes in v6:
time: 171 us
  waiting for transfers between devices  120 us (70%)
  Pallas kernels  21.6 us (13%)
  between operations  13.5 us (8%)
  local copies, waits for them, and re-layouts  6.54 us (4%)
  starting transfers between devices  5.63 us (3%)
  other arithmetic  3.53 us (2%)
    reduce_scatter x2, waiting for transfers between devices, exchanged(): lax.psum_scatter(chip, 'gz', scatter_dimension=0, axis_index_groups=groups)  117 us
    pallas_call x1, Pallas kernels, shards(): call(functools.partial(x_kernel, slabs), halves, [SMEM, VMEM, VMEM], scra...  12.2 us
    unnamed x6, local copies, waits for them, and re-layouts  5.79 us
    ppermute x1, starting transfers between devices, passed_along(): return lax.ppermute(block, axis, route)  5.44 us
    pallas_call x1, Pallas kernels, shards(): call(functools.partial(z_kernel, slabs), halves, [SMEM, VMEM, ANY], scrat...  5.05 us
    pallas_call x1, Pallas kernels, shards(): call(w_kernel, [jax.ShapeDtypeStruct(field.shape, jnp.bfloat16), halves[0...  4.4 us
  transfers between devices with their start and end apart: 5, of which 4 were waited for; matrix products, arithmetic and copies ran while one was open for 1% of the time, Pallas kernels for 10%

profile of v6, /device:TPU:0, one launch (start us, length us, event | category | flops | bytes accessed | tf_op | source)
XLA Modules:
  0.0 171.0 jit_solution(7297900505297714348)
XLA Ops:
  6.5 0.0 reduce-scatter.3.cloned.1.call-start
  6.5 5.4 %collective-permute-start.1 = (bf16[6,384,768]{2,1,0:T(8,128)(2,1)}, bf16[6,384,768]{2,1,0:T(8,128)(2,1)}, u32[]{:S(2)}, u32[]{:S(2)}) collective-permute-start(bf16[6,384,768]{2,1,0:T(8,128)(2,1)} %bitcast.12), channel_id=1, source_target_pairs={{1,0},{2,1},{3,2},{4,3},{5,4},{6,5},{7,6},{8,7},{9,8},{10,9},{11,1... | collective-permute-start | bytes 10616840 | tf_op jit(solution)/shard_map/ppermute | solution.py:22
  12.0 1.2 reduce
  13.2 0.1 reshape.25.links_ref
  13.2 0.0 copy-start
  13.3 2.0 %copy-done = bf16[2,384,3,1,768]{4,1,3,2,0:T(8,128)(2,1)S(1)} copy-done((bf16[2,384,3,1,768]{4,1,3,2,0:T(8,128)(2,1)S(1)}, bf16[2,384,3,1,768]{4,1,3,2,0:T(8,128)(2,1)}, u32[]{:S(2)}) %copy-start) | copy-done | bytes 3538968
  15.3 12.2 %shard_map.28 = (bf16[384,384]{1,0:T(8,128)(2,1)S(1)}, f32[384,384]{1,0:T(8,128)S(1)}) custom-call(s32[1]{0:T(128)} %bitcast.core_ref, bf16[6,384,768]{2,1,0:T(8,128)(2,1)S(1)} %bitcast.13, f32[36,768]{1,0:T(8,128)S(1)} %reshape.25.links_ref), custom_call_target="tpu_custom_call" | custom-call | flops 2717908992 | bytes 3538944 | tf_op jit(solution)/shard_map/pallas_call | solution.py:183
  27.4 0.1 collective-permute-start
  27.5 1.6 collective-permute-done.got_ref
  29.1 4.4 %shard_map.29 = (bf16[6,384,768]{2,1,0:T(8,128)(2,1)S(1)}, bf16[384,384]{1,0:T(8,128)(2,1)}) custom-call(bf16[6,384,768]{2,1,0:T(8,128)(2,1)S(1)} %bitcast.14, f32[36,768]{1,0:T(8,128)S(1)} %reshape.25.links_ref, f32[384,384]{1,0:T(8,128)S(1)} %get-tuple-element.13.keep_ref, bf16[384,384]{1,0:T(8,128)(2,1)S(1)} %collective-permute-done.got_ref), custom_call_target="tpu_custom_call" | custom-call | flops 19464192 | bytes 7077888 | tf_op jit(solution)/shard_map/pallas_call | solution.py:186
  33.5 0.0 copy-start.1
  33.5 1.8 %copy-done.1 = bf16[6,384,768]{2,1,0:T(8,128)(2,1)} copy-done((bf16[6,384,768]{2,1,0:T(8,128)(2,1)}, bf16[6,384,768]{2,1,0:T(8,128)(2,1)S(1)}, u32[]{:S(2)}) %copy-start.1) | copy-done | bytes 3538968
  35.3 0.0 reduce-scatter.3.cloned.1.call-update
  35.3 0.0 reduce-scatter.5.cloned.1.call-start
  35.3 59.1 %reduce-scatter.3.cloned.1.call-done = bf16[1,48,384]{2,1,0:T(8,128)(2,1)} async-done(((bf16[8,48,384]{2,1,0:T(8,128)(2,1)}), bf16[1,48,384]{2,1,0:T(8,128)(2,1)}) %reduce-scatter.3.cloned.1.call-update) | async-done | bytes 36880 | tf_op jit(solution)/shard_map/reduce_scatter | solution.py:195
  94.4 0.8 convert.2
  95.2 0.0 collective-permute-done.1.face_hbm
  95.2 0.0 copy-start.2
  95.2 2.0 %copy-done.2 = bf16[6,384,768]{2,1,0:T(8,128)(2,1)S(1)} copy-done((bf16[6,384,768]{2,1,0:T(8,128)(2,1)S(1)}, bf16[6,384,768]{2,1,0:T(8,128)(2,1)}, u32[]{:S(2)}) %copy-start.2) | copy-done | bytes 3538968
  97.2 5.1 %shard_map.30 = (bf16[384,384]{1,0:T(8,128)(2,1)S(1)}, f32[384,384]{1,0:T(8,128)S(1)}) custom-call(s32[1]{0:T(128)} %bitcast.core_ref, bf16[6,384,768]{2,1,0:T(8,128)(2,1)S(1)} %copy-done.2, bf16[6,384,768]{2,1,0:T(8,128)(2,1)} %collective-permute-done.1.face_hbm), custom_call_target="tpu_custom_call" | custom-call | flops 2717908992 | bytes 3538944 | tf_op jit(solution)/shard_map/pallas_call | solution.py:203
  102.3 0.1 collective-permute-start.2
  102.3 1.6 collective-permute-done.2
  103.9 0.8 add_convert_fusion
  104.7 0.0 reduce-scatter.5.cloned.1.call-update
  104.7 57.9 %reduce-scatter.5.cloned.1.call-done = bf16[1,48,384]{2,1,0:T(8,128)(2,1)} async-done(((bf16[8,48,384]{2,1,0:T(8,128)(2,1)}), bf16[1,48,384]{2,1,0:T(8,128)(2,1)}) %reduce-scatter.5.cloned.1.call-update) | async-done | bytes 36880 | tf_op jit(solution)/shard_map/reduce_scatter | solution.py:195
  162.7 0.8 convert.3
  163.4 0.7 copy.3
  (1 shorter events, 0.0 us)
Async XLA Ops:
  6.5 87.9 %reduce-scatter.3.cloned.1.call-start = ((), (), s32[]{:S(2)}) async-start(), calls=%async_computation.2 | async-start | bytes 331776 | tf_op jit(solution)/shard_map/reduce_scatter | solution.py:195
  6.5 88.7 %collective-permute-start.1 = (bf16[6,384,768]{2,1,0:T(8,128)(2,1)}, bf16[6,384,768]{2,1,0:T(8,128)(2,1)}, u32[]{:S(2)}, u32[]{:S(2)}) collective-permute-start(bf16[6,384,768]{2,1,0:T(8,128)(2,1)} %bitcast.12), channel_id=1, source_target_pairs={{1,0},{2,1},{3,2},{4,3},{5,4},{6,5},{7,6},{8,7},{9,8},{10,9},{11,1... | collective-permute-start | bytes 10616840 | tf_op jit(solution)/shard_map/ppermute | solution.py:22
  13.2 2.0 %copy-start = (bf16[2,384,3,1,768]{4,1,3,2,0:T(8,128)(2,1)S(1)}, bf16[2,384,3,1,768]{4,1,3,2,0:T(8,128)(2,1)}, u32[]{:S(2)}) copy-start(bf16[2,384,3,1,768]{4,1,3,2,0:T(8,128)(2,1)} %param.2) | copy-start | bytes 10616836
  27.4 1.6 collective-permute-start
  33.5 1.8 %copy-start.1 = (bf16[6,384,768]{2,1,0:T(8,128)(2,1)}, bf16[6,384,768]{2,1,0:T(8,128)(2,1)S(1)}, u32[]{:S(2)}) copy-start(bf16[6,384,768]{2,1,0:T(8,128)(2,1)S(1)} %get-tuple-element.18.w_ref) | copy-start | bytes 10616836
  35.3 127.4 %reduce-scatter.5.cloned.1.call-start = ((), (), s32[]{:S(2)}) async-start(), calls=%async_computation.3 | async-start | bytes 331776 | tf_op jit(solution)/shard_map/reduce_scatter | solution.py:195
  95.2 2.0 %copy-start.2 = (bf16[6,384,768]{2,1,0:T(8,128)(2,1)S(1)}, bf16[6,384,768]{2,1,0:T(8,128)(2,1)}, u32[]{:S(2)}) copy-start(bf16[6,384,768]{2,1,0:T(8,128)(2,1)} %copy-done.1) | copy-start | bytes 10616836
  102.3 1.6 collective-permute-start.2
Sparse Core Ops, SparseCore 0:
  35.4 58.9 reduce-scatter.2
  104.8 57.7 reduce-scatter.4

commit v7 on v6

--- a/solution.py
+++ b/solution.py
@@ -73,20 +73,13 @@
     return slabs % 2 == 0 and own % 8 == 0
 
 
-def finish(left_of, right_of, slabs, core, acc, send, keep, ready=lambda b: None):
+def inner(left, right):
+    return lax.dot_general(left, right, (((1,), (1,)), ((), ())), preferred_element_type=jnp.float32)
+
+
+def finish(sum_re, sum_im, slabs, core, acc, send, keep):
     count = send.shape[0]
     own = count // slabs
-    product = [None, None]
-    for b in range(3):
-        ready(b)
-        for part in range(2):
-            term = lax.dot_general(
-                left_of(part, b), right_of(b), (((1,), (1,)), ((), ())),
-                preferred_element_type=jnp.float32,
-            )
-            product[part] = term if b == 0 else product[part] + term
-    sum_re = product[0][:, :count] + product[1][:, count:]
-    sum_im = product[0][:, count:] - product[1][:, :count]
     acc[0] = sum_re - sum_re.T
     acc[1] = sum_im + sum_im.T
     if not rows_by_own(slabs, own):
@@ -111,40 +104,49 @@
         right[a, pl.ds(pl.multiple_of(part * count + m * ROWS, ROWS), ROWS), lanes] = value
 
     times_links(field_ref, links_ref, 0, False, True, store)
-    finish(
-        lambda part, b: field_ref[part * 3 + b], lambda b: right[b],
-        slabs, core_ref[0], acc, send, keep,
-    )
-
-
-def w_kernel(field_ref, links_ref, keep_ref, got_ref, w_ref, chip_ref):
-    chip_ref[...] = (keep_ref[...] + got_ref[...].astype(jnp.float32)).astype(jnp.bfloat16)
-
-    def store(part, a, m, lanes, value):
-        w_ref[part * 3 + a, pl.ds(pl.multiple_of(m * ROWS, ROWS), ROWS), lanes] = value
-
-    times_links(field_ref, links_ref, 1, True, False, store)
-
-
-def z_kernel(slabs, core_ref, w_ref, face_hbm, send, keep, right, acc, sems):
-    count = w_ref.shape[1]
-    copies = []
+    product = [None, None]
     for b in range(3):
         for part in range(2):
-            to = right.at[b, pl.ds(part * count, count)]
-            k = part * 3 + b
-            copies.append(pltpu.make_async_copy(face_hbm.at[k], to, sems.at[k]))
-    for copy in copies:
-        copy.start()
-
-    def ready(b):
-        copies[2 * b].wait()
-        copies[2 * b + 1].wait()
-
-    finish(
-        lambda part, b: w_ref[part * 3 + b], lambda b: right[b],
-        slabs, core_ref[0], acc, send, keep, ready,
-    )
+            term = inner(field_ref[part * 3 + b], right[b])
+            product[part] = term if b == 0 else product[part] + term
+    sum_re = product[0][:, :count] + product[1][:, count:]
+    sum_im = product[0][:, count:] - product[1][:, :count]
+    finish(sum_re, sum_im, slabs, core_ref[0], acc, send, keep)
+
+
+def w_kernel(field_ref, links_ref, keep_ref, got_ref, w_ref, chip_ref):
+    count, sites = field_ref.shape[1:]
+    chip_ref[...] = (keep_ref[...] + got_ref[...].astype(jnp.float32)).astype(jnp.bfloat16)
+
+    def store(part, a, m, lanes, value):
+        rows = pl.ds(pl.multiple_of(part * count + m * ROWS, ROWS), ROWS)
+        w_ref[rows, slice(a * sites + lanes.start, a * sites + lanes.stop)] = value
+
+    times_links(field_ref, links_ref, 1, True, False, store)
+
+
+def z_kernel(slabs, core_ref, w_ref, face_hbm, send, keep, right, product, acc, sems):
+    count, sites = face_hbm.shape[1:]
+    tile = 2 * LANES
+    tiles = []
+    for low in range(0, 2 * count, tile):
+        copies = []
+        for part in range(2):
+            start, stop = max(low, part * count), min(low + tile, (part + 1) * count)
+            for b in range(3 if start < stop else 0):
+                to = right.at[pl.ds(start, stop - start), pl.ds(b * sites, sites)]
+                of = face_hbm.at[part * 3 + b, pl.ds(start - part * count, stop - start)]
+                copies.append(pltpu.make_async_copy(of, to, sems.at[(low // tile) * 6 + part * 3 + b]))
+        for copy in copies:
+            copy.start()
+        tiles.append((slice(low, min(low + tile, 2 * count)), copies))
+    for rows, copies in tiles:
+        for copy in copies:
+            copy.wait()
+        product[:, rows] = inner(w_ref[...], right[rows, :])
+    sum_re = product[:count, :count] + product[count:, count:]
+    sum_im = product[:count, count:] - product[count:, :count]
+    finish(sum_re, sum_im, slabs, core_ref[0], acc, send, keep)
 
 
 def call(body, outs, specs, scratch, mib, flops, moved):
@@ -176,36 +178,45 @@
         jax.ShapeDtypeStruct((count, count), jnp.bfloat16),
         jax.ShapeDtypeStruct((count, count), jnp.float32),
     ]
-    scratch = [
-        pltpu.VMEM((3, 2 * count, sites), jnp.bfloat16),
-        pltpu.VMEM((2, count, count), jnp.float32),
-    ]
+    whole = (2 * count, 3 * sites)
+    square = pltpu.VMEM((2, count, count), jnp.float32)
     send_x, keep_x = call(
-        functools.partial(x_kernel, slabs), halves, [SMEM, VMEM, VMEM], scratch, 22, flops, moved
+        functools.partial(x_kernel, slabs), halves, [SMEM, VMEM, VMEM],
+        [pltpu.VMEM((3, 2 * count, sites), jnp.bfloat16), square], 22, flops, moved,
     )(core, field, links)
     w, chip_x = call(
-        w_kernel, [jax.ShapeDtypeStruct(field.shape, jnp.bfloat16), halves[0]], [VMEM] * 4, [], 12,
+        w_kernel, [jax.ShapeDtypeStruct(whole, jnp.bfloat16), halves[0]], [VMEM] * 4, [], 12,
         count * sites * 66, 2 * moved,
     )(field, links, keep_x, swapped(send_x, "gz"))
 
+    if rows_by_own(slabs, own):
+        groups = [list(range(c, slabs, 2)) for c in range(2)]
+        blocks = (slabs // 2, 1, 2 * own, count)
+    else:
+        groups = None
+        blocks = (slabs // 2, 2, own, count)
+
     def exchanged(chip):
-        if rows_by_own(slabs, own):
-            groups = [list(range(c, slabs, 2)) for c in range(2)]
-            chip = chip.reshape(slabs // 2, 2 * own, count)
-            got = lax.psum_scatter(chip, "gz", scatter_dimension=0, axis_index_groups=groups)
-            return got.astype(jnp.float32).reshape(2, own, count)
-        got = lax.all_to_all(chip.reshape(slabs, own, count), "gz", 0, 0)
-        got = got.reshape(slabs // 2, 2, own, count)
-        return jnp.sum(got.astype(jnp.float32), axis=0)
-
-    sum_x = exchanged(chip_x)
-    core, sum_x = lax.optimization_barrier((core, sum_x))
+        chip = chip.reshape((-1,) + blocks[2:])
+        return lax.all_to_all(chip, "gz", 0, 0, axis_index_groups=groups)
+
+    def total(got):
+        return jnp.sum(got.reshape(blocks).astype(jnp.float32), axis=0).reshape(2, own, count)
+
+    got_x = exchanged(chip_x)
     send_z, keep_z = call(
         functools.partial(z_kernel, slabs), halves, [SMEM, VMEM, ANY],
-        scratch + [pltpu.SemaphoreType.DMA((6,))], 18, flops, moved,
+        [
+            pltpu.VMEM(whole, jnp.bfloat16),
+            pltpu.VMEM((2 * count, 2 * count), jnp.float32),
+            square,
+            pltpu.SemaphoreType.DMA((6 * -(-count // LANES),)),
+        ],
+        20, flops, moved,
     )(core, w, face)
+    send_z, got_x = lax.optimization_barrier((send_z, got_x))
     chip_z = (keep_z + swapped(send_z, "gz").astype(jnp.float32)).astype(jnp.bfloat16)
-    both = jnp.concatenate([sum_x, exchanged(chip_z)], axis=0)
+    both = jnp.concatenate([total(got_x), total(exchanged(chip_z))], axis=0)
     return jnp.transpose(both, (1, 0, 2)) * scale
 
 

time: 171 us -> 75.5 us (0.44)
  waiting for transfers between devices: 120 us -> 28.1 us
  between operations: 13.5 us -> 0.09 us
  starting transfers between devices: 5.63 us -> 14.9 us
    reduce_scatter x2 -> x0, waiting for transfers between devices: 117 us -> none  [exchanged(): lax.psum_scatter(chip, 'gz', scatter_dimension=0, axis_index_groups=groups)]
    ppermute x1, waiting for transfers between devices: 0.01 us -> 14.9 us  [passed_along(): return lax.ppermute(block, axis, route)]
    all_to_all x0 -> x2, waiting for transfers between devices: none -> 10.1 us  [exchanged(): return lax.all_to_all(chip, 'gz', 0, 0, axis_index_groups=groups)]
    all_to_all x0 -> x2, starting transfers between devices: none -> 9.33 us  [exchanged(): return lax.all_to_all(chip, 'gz', 0, 0, axis_index_groups=groups)]
  transfers between devices with their start and end apart: 5 -> 5, of which waited for: 4 -> 4; matrix products, arithmetic and copies ran while one was open for 1% -> 2% of each run, Pallas kernels for 10% -> 31%
where the time goes in v7:
time: 75.5 us; the launch traced here: 75.1 us
  waiting for transfers between devices  28.1 us (37%)
  Pallas kernels  23.3 us (31%)
  starting transfers between devices  14.9 us (20%)
  local copies, waits for them, and re-layouts  6.56 us (9%)
  other arithmetic  2.08 us (3%)
    ppermute x1, waiting for transfers between devices, passed_along(): return lax.ppermute(block, axis, route)  14.9 us
    pallas_call x1, Pallas kernels, shards(): call(functools.partial(x_kernel, slabs), halves, [SMEM, VMEM, VMEM], [plt...  12.2 us
    all_to_all x2, waiting for transfers between devices, exchanged(): return lax.all_to_all(chip, 'gz', 0, 0, axis_index_groups=groups)  10.1 us
    all_to_all x2, starting transfers between devices, exchanged(): return lax.all_to_all(chip, 'gz', 0, 0, axis_index_groups=groups)  9.33 us
    pallas_call x1, Pallas kernels, shards(): call(functools.partial(z_kernel, slabs), halves, [SMEM, VMEM, ANY], [pltp...  6.71 us
    unnamed x6, local copies, waits for them, and re-layouts  5.8 us
    ppermute x1, starting transfers between devices, passed_along(): return lax.ppermute(block, axis, route)  5.44 us
    pallas_call x1, Pallas kernels, shards(): call(w_kernel, [jax.ShapeDtypeStruct(whole, jnp.bfloat16), halves[0]], [V...  4.45 us
  transfers between devices with their start and end apart: 5, of which 4 were waited for; matrix products, arithmetic and copies ran while one was open for 2% of the time, Pallas kernels for 31%

profile of v7, /device:TPU:0, one launch (start us, length us, event | category | flops | bytes accessed | tf_op | source)
XLA Modules:
  0.0 75.1 jit_solution(1403831484954225822)
XLA Ops:
  0.0 5.4 %collective-permute-start.1 = (bf16[6,384,768]{2,1,0:T(8,128)(2,1)}, bf16[6,384,768]{2,1,0:T(8,128)(2,1)}, u32[]{:S(2)}, u32[]{:S(2)}) collective-permute-start(bf16[6,384,768]{2,1,0:T(8,128)(2,1)} %bitcast.10), channel_id=1, source_target_pairs={{1,0},{2,1},{3,2},{4,3},{5,4},{6,5},{7,6},{8,7},{9,8},{10,9},{11,1... | collective-permute-start | bytes 10616840 | tf_op jit(solution)/shard_map/ppermute | solution.py:22
  5.4 1.2 %reduce.4 = f32[2,2,3,3,768]{4,3,2,1,0:T(4,128)S(1)} reduce(f32[2,2,3,3,1,768]{5,4,3,2,1,0:T(1,128)} %param.3, f32[]{:T(128)} %constant.12), dimensions={4}, to_apply=%param.3.reduce_sub_computation | reduce | bytes 221188 | tf_op args[1]
  6.6 0.1 reshape.31.links_ref
  6.7 0.0 copy-start
  6.7 2.0 %copy-done = bf16[2,384,3,1,768]{4,1,3,2,0:T(8,128)(2,1)S(1)} copy-done((bf16[2,384,3,1,768]{4,1,3,2,0:T(8,128)(2,1)S(1)}, bf16[2,384,3,1,768]{4,1,3,2,0:T(8,128)(2,1)}, u32[]{:S(2)}) %copy-start) | copy-done | bytes 3538968
  8.7 12.2 %shard_map.28 = (bf16[384,384]{1,0:T(8,128)(2,1)S(1)}, f32[384,384]{1,0:T(8,128)S(1)}) custom-call(s32[1]{0:T(128)} %bitcast.core_ref, bf16[6,384,768]{2,1,0:T(8,128)(2,1)S(1)} %bitcast.11, f32[36,768]{1,0:T(8,128)S(1)} %reshape.31.links_ref), custom_call_target="tpu_custom_call" | custom-call | flops 2717908992 | bytes 3538944 | tf_op jit(solution)/shard_map/pallas_call | solution.py:183
  20.9 0.1 collective-permute-start
  21.0 1.6 %collective-permute-done.got_ref = bf16[384,384]{1,0:T(8,128)(2,1)S(1)} collective-permute-done((bf16[384,384]{1,0:T(8,128)(2,1)S(1)}, bf16[384,384]{1,0:T(8,128)(2,1)S(1)}, u32[]{:S(2)}, u32[]{:S(2)}) %collective-permute-start) | collective-permute-done | bytes 294944 | tf_op jit(solution)/shard_map/ppermute | solution.py:26
  22.5 4.4 %shard_map.29 = (bf16[768,2304]{1,0:T(8,128)(2,1)S(1)}, bf16[384,384]{1,0:T(8,128)(2,1)}) custom-call(bf16[6,384,768]{2,1,0:T(8,128)(2,1)S(1)} %bitcast.12, f32[36,768]{1,0:T(8,128)S(1)} %reshape.31.links_ref, f32[384,384]{1,0:T(8,128)S(1)} %get-tuple-element.13.keep_ref, bf16[384,384]{1,0:T(8,128)(2,1)S(1)} %collective-permute-done.got_ref), custom_call_target="tpu_custom_call" | custom-call | flops 19464192 | bytes 7077888 | tf_op jit(solution)/shard_map/pallas_call | solution.py:187
  27.0 0.0 copy-start.1
  27.0 1.8 %copy-done.1 = bf16[768,2304]{1,0:T(8,128)(2,1)} copy-done((bf16[768,2304]{1,0:T(8,128)(2,1)}, bf16[768,2304]{1,0:T(8,128)(2,1)S(1)}, u32[]{:S(2)}) %copy-start.1) | copy-done | bytes 3538968
  28.8 3.4 %all-to-all-start = ((bf16[8,48,384]{2,1,0:T(8,128)(2,1)}), bf16[8,48,384]{2,1,0:T(8,128)(2,1)S(1)}, u32[]{:S(2)}, u32[]{:S(2)}) async-start(bf16[8,48,384]{2,1,0:T(8,128)(2,1)} %bitcast.4), calls=%async_computation | async-start | bytes 589824 | tf_op jit(solution)/shard_map/all_to_all | solution.py:201
  32.2 14.9 %collective-permute-done.1.face_hbm = bf16[6,384,768]{2,1,0:T(8,128)(2,1)} collective-permute-done((bf16[6,384,768]{2,1,0:T(8,128)(2,1)}, bf16[6,384,768]{2,1,0:T(8,128)(2,1)}, u32[]{:S(2)}, u32[]{:S(2)}) %collective-permute-start.1) | collective-permute-done | bytes 3538976 | tf_op jit(solution)/shard_map/ppermute | solution.py:22
  47.1 0.0 copy-start.2
  47.1 2.0 %copy-done.2 = bf16[768,2304]{1,0:T(8,128)(2,1)S(1)} copy-done((bf16[768,2304]{1,0:T(8,128)(2,1)S(1)}, bf16[768,2304]{1,0:T(8,128)(2,1)}, u32[]{:S(2)}) %copy-start.2) | copy-done | bytes 3538968
  49.1 6.7 %shard_map.30 = (bf16[384,384]{1,0:T(8,128)(2,1)S(1)}, f32[384,384]{1,0:T(8,128)S(1)}) custom-call(s32[1]{0:T(128)} %bitcast.core_ref, bf16[768,2304]{1,0:T(8,128)(2,1)S(1)} %copy-done.2, bf16[6,384,768]{2,1,0:T(8,128)(2,1)} %collective-permute-done.1.face_hbm), custom_call_target="tpu_custom_call" | custom-call | flops 2717908992 | bytes 3538944 | tf_op jit(solution)/shard_map/pallas_call | solution.py:207
  55.9 0.0 all-to-all-done
  55.9 0.1 collective-permute-start.2
  55.9 1.6 %collective-permute-done.2 = bf16[384,384]{1,0:T(8,128)(2,1)S(1)} collective-permute-done((bf16[384,384]{1,0:T(8,128)(2,1)S(1)}, bf16[384,384]{1,0:T(8,128)(2,1)S(1)}, u32[]{:S(2)}, u32[]{:S(2)}) %collective-permute-start.2) | collective-permute-done | bytes 294944 | tf_op jit(solution)/shard_map/ppermute | solution.py:26
  57.5 0.8 %add_convert_fusion = bf16[384,384]{1,0:T(8,128)(2,1)} fusion(f32[384,384]{1,0:T(8,128)S(1)} %get-tuple-element.19, bf16[384,384]{1,0:T(8,128)(2,1)S(1)} %collective-permute-done.2), kind=kLoop, calls=%fused_computation.1 | loop fusion | flops 442368 | bytes 1179648 | tf_op jit(solution)/shard_map/convert_element_type | solution.py:218
  58.3 5.9 %all-to-all-start.1 = ((bf16[8,48,384]{2,1,0:T(8,128)(2,1)}), bf16[8,48,384]{2,1,0:T(8,128)(2,1)S(1)}, u32[]{:S(2)}, u32[]{:S(2)}) async-start(bf16[8,48,384]{2,1,0:T(8,128)(2,1)} %bitcast.6), calls=%async_computation.1 | async-start | bytes 589824 | tf_op jit(solution)/shard_map/all_to_all | solution.py:201
  64.3 10.1 %all-to-all-done.1 = bf16[8,48,384]{2,1,0:T(8,128)(2,1)S(1)} async-done(((bf16[8,48,384]{2,1,0:T(8,128)(2,1)}), bf16[8,48,384]{2,1,0:T(8,128)(2,1)S(1)}, u32[]{:S(2)}, u32[]{:S(2)}) %all-to-all-start.1) | async-done | bytes 294944 | tf_op jit(solution)/shard_map/all_to_all | solution.py:201
  74.4 0.7 copy.3
  (3 shorter events, 0.1 us)
Async XLA Ops:
  0.0 47.1 %collective-permute-start.1 = (bf16[6,384,768]{2,1,0:T(8,128)(2,1)}, bf16[6,384,768]{2,1,0:T(8,128)(2,1)}, u32[]{:S(2)}, u32[]{:S(2)}) collective-permute-start(bf16[6,384,768]{2,1,0:T(8,128)(2,1)} %bitcast.10), channel_id=1, source_target_pairs={{1,0},{2,1},{3,2},{4,3},{5,4},{6,5},{7,6},{8,7},{9,8},{10,9},{11,1... | collective-permute-start | bytes 10616840 | tf_op jit(solution)/shard_map/ppermute | solution.py:22
  6.7 2.0 %copy-start = (bf16[2,384,3,1,768]{4,1,3,2,0:T(8,128)(2,1)S(1)}, bf16[2,384,3,1,768]{4,1,3,2,0:T(8,128)(2,1)}, u32[]{:S(2)}) copy-start(bf16[2,384,3,1,768]{4,1,3,2,0:T(8,128)(2,1)} %param.2) | copy-start | bytes 10616836
  20.9 1.6 %collective-permute-start = (bf16[384,384]{1,0:T(8,128)(2,1)S(1)}, bf16[384,384]{1,0:T(8,128)(2,1)S(1)}, u32[]{:S(2)}, u32[]{:S(2)}) collective-permute-start(bf16[384,384]{1,0:T(8,128)(2,1)S(1)} %get-tuple-element.14), channel_id=1, source_target_pairs={{0,1},{1,0},{2,3},{3,2},{4,5},{5,4},{6,7},{7,6},{8,9},{9,8},{10,11... | collective-permute-start | bytes 884744 | tf_op jit(solution)/shard_map/ppermute | solution.py:26
  27.0 1.8 %copy-start.1 = (bf16[768,2304]{1,0:T(8,128)(2,1)}, bf16[768,2304]{1,0:T(8,128)(2,1)S(1)}, u32[]{:S(2)}) copy-start(bf16[768,2304]{1,0:T(8,128)(2,1)S(1)} %get-tuple-element.15.w_ref) | copy-start | bytes 10616836
  28.8 27.1 %all-to-all-start = ((bf16[8,48,384]{2,1,0:T(8,128)(2,1)}), bf16[8,48,384]{2,1,0:T(8,128)(2,1)S(1)}, u32[]{:S(2)}, u32[]{:S(2)}) async-start(bf16[8,48,384]{2,1,0:T(8,128)(2,1)} %bitcast.4), calls=%async_computation | async-start | bytes 589824 | tf_op jit(solution)/shard_map/all_to_all | solution.py:201
  47.1 2.0 %copy-start.2 = (bf16[768,2304]{1,0:T(8,128)(2,1)S(1)}, bf16[768,2304]{1,0:T(8,128)(2,1)}, u32[]{:S(2)}) copy-start(bf16[768,2304]{1,0:T(8,128)(2,1)} %copy-done.1) | copy-start | bytes 10616836
  55.9 1.6 %collective-permute-start.2 = (bf16[384,384]{1,0:T(8,128)(2,1)S(1)}, bf16[384,384]{1,0:T(8,128)(2,1)S(1)}, u32[]{:S(2)}, u32[]{:S(2)}) collective-permute-start(bf16[384,384]{1,0:T(8,128)(2,1)S(1)} %get-tuple-element.20), channel_id=1, source_target_pairs={{0,1},{1,0},{2,3},{3,2},{4,5},{5,4},{6,7},{7,6},{8,9},{9,8},{10,11... | collective-permute-start | bytes 884744 | tf_op jit(solution)/shard_map/ppermute | solution.py:26
  58.3 16.0 %all-to-all-start.1 = ((bf16[8,48,384]{2,1,0:T(8,128)(2,1)}), bf16[8,48,384]{2,1,0:T(8,128)(2,1)S(1)}, u32[]{:S(2)}, u32[]{:S(2)}) async-start(bf16[8,48,384]{2,1,0:T(8,128)(2,1)} %bitcast.6), calls=%async_computation.1 | async-start | bytes 589824 | tf_op jit(solution)/shard_map/all_to_all | solution.py:201

commit v8 on v7

--- a/solution.py
+++ b/solution.py
@@ -70,14 +70,14 @@
 
 
 def rows_by_own(slabs, own):
-    return slabs % 2 == 0 and own % 8 == 0
+    return slabs % 4 == 0 and own % 8 == 0
 
 
 def inner(left, right):
     return lax.dot_general(left, right, (((1,), (1,)), ((), ())), preferred_element_type=jnp.float32)
 
 
-def finish(sum_re, sum_im, slabs, core, acc, send, keep):
+def finish(sum_re, sum_im, slabs, core, order, acc, send, keep):
     count = send.shape[0]
     own = count // slabs
     acc[0] = sum_re - sum_re.T
@@ -90,14 +90,14 @@
         block = slice(k * 2 * own, (k + 1) * 2 * own)
 
         def rows(which):
-            at = pl.ds(pl.multiple_of((2 * k + which) * own, 8), own)
+            at = pl.ds(pl.multiple_of((2 * order[k] + which) * own, 8), own)
             return jnp.concatenate([acc[0, at, :], acc[1, at, :]], axis=0)
 
         send[block, :] = rows(1 - core).astype(jnp.bfloat16)
         keep[block, :] = rows(core)
 
 
-def x_kernel(slabs, core_ref, field_ref, links_ref, send, keep, right, acc):
+def x_kernel(slabs, where_ref, field_ref, links_ref, send, keep, right, acc):
     count = field_ref.shape[1]
 
     def store(part, a, m, lanes, value):
@@ -111,42 +111,48 @@
             product[part] = term if b == 0 else product[part] + term
     sum_re = product[0][:, :count] + product[1][:, count:]
     sum_im = product[0][:, count:] - product[1][:, :count]
-    finish(sum_re, sum_im, slabs, core_ref[0], acc, send, keep)
+    finish(sum_re, sum_im, slabs, where_ref[0], range(slabs // 2), acc, send, keep)
 
 
 def w_kernel(field_ref, links_ref, keep_ref, got_ref, w_ref, chip_ref):
-    count, sites = field_ref.shape[1:]
     chip_ref[...] = (keep_ref[...] + got_ref[...].astype(jnp.float32)).astype(jnp.bfloat16)
 
     def store(part, a, m, lanes, value):
-        rows = pl.ds(pl.multiple_of(part * count + m * ROWS, ROWS), ROWS)
-        w_ref[rows, slice(a * sites + lanes.start, a * sites + lanes.stop)] = value
+        w_ref[part * 3 + a, pl.ds(pl.multiple_of(m * ROWS, ROWS), ROWS), lanes] = value
 
     times_links(field_ref, links_ref, 1, True, False, store)
 
 
-def z_kernel(slabs, core_ref, w_ref, face_hbm, send, keep, right, product, acc, sems):
-    count, sites = face_hbm.shape[1:]
-    tile = 2 * LANES
-    tiles = []
-    for low in range(0, 2 * count, tile):
-        copies = []
+def z_order(chip, chips):
+    along = chips // 2
+    ahead = [lax.rem((chip >> 1) + r, along) * 2 for r in range(along)]
+    low = chip & 1
+    return [to + 1 - low for to in ahead] + [to + low for to in ahead]
+
+
+def z_kernel(slabs, where_ref, w_hbm, face_hbm, send, keep, left, right, acc, sems):
+    count = w_hbm.shape[1]
+    copies = []
+    for b in range(3):
+        group = []
         for part in range(2):
-            start, stop = max(low, part * count), min(low + tile, (part + 1) * count)
-            for b in range(3 if start < stop else 0):
-                to = right.at[pl.ds(start, stop - start), pl.ds(b * sites, sites)]
-                of = face_hbm.at[part * 3 + b, pl.ds(start - part * count, stop - start)]
-                copies.append(pltpu.make_async_copy(of, to, sems.at[(low // tile) * 6 + part * 3 + b]))
-        for copy in copies:
+            k = part * 3 + b
+            rows = pl.ds(part * count, count)
+            group.append(pltpu.make_async_copy(face_hbm.at[k], right.at[b, rows], sems.at[k]))
+            group.append(pltpu.make_async_copy(w_hbm.at[k], left.at[k], sems.at[6 + k]))
+        for copy in group:
             copy.start()
-        tiles.append((slice(low, min(low + tile, 2 * count)), copies))
-    for rows, copies in tiles:
-        for copy in copies:
+        copies.append(group)
+    product = [None, None]
+    for b in range(3):
+        for copy in copies[b]:
             copy.wait()
-        product[:, rows] = inner(w_ref[...], right[rows, :])
-    sum_re = product[:count, :count] + product[count:, count:]
-    sum_im = product[:count, count:] - product[count:, :count]
-    finish(sum_re, sum_im, slabs, core_ref[0], acc, send, keep)
+        for part in range(2):
+            term = inner(left[part * 3 + b], right[b])
+            product[part] = term if b == 0 else product[part] + term
+    sum_re = product[0][:, :count] + product[1][:, count:]
+    sum_im = product[0][:, count:] - product[1][:, :count]
+    finish(sum_re, sum_im, slabs, where_ref[0], z_order(where_ref[1], slabs // 2), acc, send, keep)
 
 
 def call(body, outs, specs, scratch, mib, flops, moved):
@@ -167,7 +173,8 @@
     assert planes == 1 and slabs % 2 == 0
     own = count // slabs
     scale = 1.0 / math.sqrt(12.0 * sites * planes * slabs)
-    core = (lax.axis_index("gz").astype(jnp.int32) & 1).reshape(1)
+    index = lax.axis_index("gz").astype(jnp.int32)
+    where = jnp.stack([index & 1, index >> 1])
     field = jnp.transpose(vectors, (0, 2, 3, 1, 4)).reshape(6, count, sites)
     links = links.reshape(36, sites)
     face = passed_along(field, "gz", -1)
@@ -178,14 +185,14 @@
         jax.ShapeDtypeStruct((count, count), jnp.bfloat16),
         jax.ShapeDtypeStruct((count, count), jnp.float32),
     ]
-    whole = (2 * count, 3 * sites)
+    stacked = pltpu.VMEM((3, 2 * count, sites), jnp.bfloat16)
     square = pltpu.VMEM((2, count, count), jnp.float32)
     send_x, keep_x = call(
         functools.partial(x_kernel, slabs), halves, [SMEM, VMEM, VMEM],
-        [pltpu.VMEM((3, 2 * count, sites), jnp.bfloat16), square], 22, flops, moved,
-    )(core, field, links)
+        [stacked, square], 22, flops, moved,
+    )(where, field, links)
     w, chip_x = call(
-        w_kernel, [jax.ShapeDtypeStruct(whole, jnp.bfloat16), halves[0]], [VMEM] * 4, [], 12,
+        w_kernel, [jax.ShapeDtypeStruct(field.shape, jnp.bfloat16), halves[0]], [VMEM] * 4, [], 12,
         count * sites * 66, 2 * moved,
     )(field, links, keep_x, swapped(send_x, "gz"))
 
@@ -205,18 +212,27 @@
 
     got_x = exchanged(chip_x)
     send_z, keep_z = call(
-        functools.partial(z_kernel, slabs), halves, [SMEM, VMEM, ANY],
+        functools.partial(z_kernel, slabs), halves, [SMEM, ANY, ANY],
         [
-            pltpu.VMEM(whole, jnp.bfloat16),
-            pltpu.VMEM((2 * count, 2 * count), jnp.float32),
-            square,
-            pltpu.SemaphoreType.DMA((6 * -(-count // LANES),)),
+            pltpu.VMEM(field.shape, jnp.bfloat16), stacked, square, pltpu.SemaphoreType.DMA((12,)),
         ],
-        20, flops, moved,
-    )(core, w, face)
+        58, flops, moved,
+    )(where, w, face)
     send_z, got_x = lax.optimization_barrier((send_z, got_x))
-    chip_z = (keep_z + swapped(send_z, "gz").astype(jnp.float32)).astype(jnp.bfloat16)
-    both = jnp.concatenate([total(got_x), total(exchanged(chip_z))], axis=0)
+    chip_z = keep_z + swapped(send_z, "gz").astype(jnp.float32)
+    if rows_by_own(slabs, own):
+        half = count // 2
+        other = chip_z[:half].astype(jnp.bfloat16)
+        near = lax.ppermute(other, "gz", [(i, i ^ 2) for i in range(slabs)])
+        line = chip_z[half:] + near.astype(jnp.float32)
+        total_z = line[: 2 * own]
+        for r in range(1, slabs // 4):
+            block = line[r * 2 * own : (r + 1) * 2 * own].astype(jnp.bfloat16)
+            total_z = total_z + passed_along(block, "gz", 4 * r).astype(jnp.float32)
+        total_z = total_z.reshape(2, own, count)
+    else:
+        total_z = total(exchanged(chip_z.astype(jnp.bfloat16)))
+    both = jnp.concatenate([total(got_x), total_z], axis=0)
     return jnp.transpose(both, (1, 0, 2)) * scale
 
 

time: 75.5 us -> 73.4 us (0.972)
  local copies, waits for them, and re-layouts: 6.56 us -> 4.58 us
  starting transfers between devices: 14.9 us -> 13.4 us
  Pallas kernels: 23.3 us -> 24.4 us
    all_to_all x2 -> x1, waiting for transfers between devices: 10.1 us -> 0.01 us  [exchanged(): return lax.all_to_all(chip, 'gz', 0, 0, axis_index_groups=groups)]
    all_to_all x2 -> x1, starting transfers between devices: 9.33 us -> 3.42 us  [exchanged(): return lax.all_to_all(chip, 'gz', 0, 0, axis_index_groups=groups)]
    ppermute x0 -> x1, waiting for transfers between devices: none -> 5.88 us  [shards(): near = lax.ppermute(other, 'gz', [(i, i ^ 2) for i in range(slabs)])]
    ppermute x1 -> x4, starting transfers between devices: 5.44 us -> 9.74 us  [passed_along(): return lax.ppermute(block, axis, route)]
    ppermute x1 -> x4, waiting for transfers between devices: 14.9 us -> 18.8 us  [passed_along(): return lax.ppermute(block, axis, route)]
    unnamed x6, local copies, waits for them, and re-layouts: 5.8 us -> 3.79 us
    add x0 -> x2, other arithmetic: none -> 1.16 us  [the longest x1 1.13 us: shards(): chip_z = keep_z + swapped(send_z, 'gz').astype(jnp.float32)]
    pallas_call x3, Pallas kernels: 23.3 us -> 24.4 us  [the longest x1 12.7 us: shards(): call(functools.partial(x_kernel, slabs), halves, [SMEM, VMEM, VMEM], [sta...]
  transfers between devices with their start and end apart: 5 -> 8, of which waited for: 4 -> 6; matrix products, arithmetic and copies ran while one was open for 2% -> 2% of each run, Pallas kernels for 31% -> 33%
where the time goes in v8:
time: 73.4 us; the launch traced here: 73 us
  waiting for transfers between devices  28 us (38%)
  Pallas kernels  24.4 us (33%)
  starting transfers between devices  13.4 us (18%)
  local copies, waits for them, and re-layouts  4.58 us (6%)
  other arithmetic  2.53 us (3%)
    ppermute x4, waiting for transfers between devices, passed_along(): return lax.ppermute(block, axis, route)  18.8 us
    pallas_call x1, Pallas kernels, shards(): call(functools.partial(x_kernel, slabs), halves, [SMEM, VMEM, VMEM], [sta...  12.7 us
    ppermute x4, starting transfers between devices, passed_along(): return lax.ppermute(block, axis, route)  9.74 us
    pallas_call x1, Pallas kernels, shards(): call(functools.partial(z_kernel, slabs), halves, [SMEM, ANY, ANY], [pltpu...  7.36 us
    ppermute x1, waiting for transfers between devices, shards(): near = lax.ppermute(other, 'gz', [(i, i ^ 2) for i in range(slabs)])  5.88 us
    pallas_call x1, Pallas kernels, shards(): call(w_kernel, [jax.ShapeDtypeStruct(field.shape, jnp.bfloat16), halves[0...  4.37 us
    unnamed x6, local copies, waits for them, and re-layouts  3.79 us
    all_to_all x1, starting transfers between devices, exchanged(): return lax.all_to_all(chip, 'gz', 0, 0, axis_index_groups=groups)  3.42 us
  transfers between devices with their start and end apart: 8, of which 6 were waited for; matrix products, arithmetic and copies ran while one was open for 2% of the time, Pallas kernels for 33%

profile of v8, /device:TPU:0, one launch (start us, length us, event | category | flops | bytes accessed | tf_op | source)
XLA Modules:
  0.0 73.0 jit_solution(84123863453348744)
XLA Ops:
  0.0 5.4 %collective-permute-start.1 = (bf16[6,384,768]{2,1,0:T(8,128)(2,1)}, bf16[6,384,768]{2,1,0:T(8,128)(2,1)}, u32[]{:S(2)}, u32[]{:S(2)}) collective-permute-start(bf16[6,384,768]{2,1,0:T(8,128)(2,1)} %bitcast.10), channel_id=1, source_target_pairs={{1,0},{2,1},{3,2},{4,3},{5,4},{6,5},{7,6},{8,7},{9,8},{10,9},{11,1... | collective-permute-start | bytes 10616840 | tf_op jit(solution)/shard_map/ppermute | solution.py:22
  5.4 1.2 %reduce.2 = f32[2,2,3,3,768]{4,3,2,1,0:T(4,128)S(1)} reduce(f32[2,2,3,3,1,768]{5,4,3,2,1,0:T(1,128)} %param.3, f32[]{:T(128)} %constant.12), dimensions={4}, to_apply=%param.3.reduce_sub_computation | reduce | bytes 221188 | tf_op args[1]
  6.6 0.1 reshape.20.links_ref
  6.7 0.1 pad_add_fusion.where_ref
  6.8 0.0 copy-start
  6.8 2.0 %copy-done = bf16[2,384,3,1,768]{4,1,3,2,0:T(8,128)(2,1)S(1)} copy-done((bf16[2,384,3,1,768]{4,1,3,2,0:T(8,128)(2,1)S(1)}, bf16[2,384,3,1,768]{4,1,3,2,0:T(8,128)(2,1)}, u32[]{:S(2)}) %copy-start) | copy-done | bytes 3538968
  8.8 0.0 copy-start.2
  8.8 12.7 %shard_map.28 = (bf16[384,384]{1,0:T(8,128)(2,1)S(1)}, f32[384,384]{1,0:T(8,128)S(1)}) custom-call(s32[2]{0:T(128)S(1)} %pad_add_fusion.where_ref, bf16[6,384,768]{2,1,0:T(8,128)(2,1)S(1)} %bitcast.11, f32[36,768]{1,0:T(8,128)S(1)} %reshape.20.links_ref), custom_call_target="tpu_custom_call" | custom-call | flops 2717908992 | bytes 3538944 | tf_op jit(solution)/shard_map/pallas_call | solution.py:190
  21.5 0.0 copy-done.2
  21.5 0.1 collective-permute-start
  21.6 1.6 %collective-permute-done.got_ref = bf16[384,384]{1,0:T(8,128)(2,1)S(1)} collective-permute-done((bf16[384,384]{1,0:T(8,128)(2,1)S(1)}, bf16[384,384]{1,0:T(8,128)(2,1)S(1)}, u32[]{:S(2)}, u32[]{:S(2)}) %collective-permute-start) | collective-permute-done | bytes 294944 | tf_op jit(solution)/shard_map/ppermute | solution.py:26
  23.2 4.4 %shard_map.29 = (bf16[6,384,768]{2,1,0:T(8,128)(2,1)S(1)}, bf16[384,384]{1,0:T(8,128)(2,1)}) custom-call(bf16[6,384,768]{2,1,0:T(8,128)(2,1)S(1)} %bitcast.12, f32[36,768]{1,0:T(8,128)S(1)} %reshape.20.links_ref, f32[384,384]{1,0:T(8,128)S(1)} %get-tuple-element.13.keep_ref, bf16[384,384]{1,0:T(8,128)(2,1)S(1)} %collective-permute-done.got_ref), custom_call_target="tpu_custom_call" | custom-call | flops 19464192 | bytes 7077888 | tf_op jit(solution)/shard_map/pallas_call | solution.py:194
  27.5 0.0 copy-start.1
  27.5 1.8 %copy-done.1 = bf16[6,384,768]{2,1,0:T(8,128)(2,1)} copy-done((bf16[6,384,768]{2,1,0:T(8,128)(2,1)}, bf16[6,384,768]{2,1,0:T(8,128)(2,1)S(1)}, u32[]{:S(2)}) %copy-start.1) | copy-done | bytes 3538968
  29.3 3.4 %all-to-all-start = ((bf16[8,48,384]{2,1,0:T(8,128)(2,1)}), bf16[8,48,384]{2,1,0:T(8,128)(2,1)S(1)}, u32[]{:S(2)}, u32[]{:S(2)}) async-start(bf16[8,48,384]{2,1,0:T(8,128)(2,1)} %bitcast.5), calls=%async_computation | async-start | bytes 589824 | tf_op jit(solution)/shard_map/all_to_all | solution.py:208
  32.8 14.4 %collective-permute-done.1.face_hbm = bf16[6,384,768]{2,1,0:T(8,128)(2,1)} collective-permute-done((bf16[6,384,768]{2,1,0:T(8,128)(2,1)}, bf16[6,384,768]{2,1,0:T(8,128)(2,1)}, u32[]{:S(2)}, u32[]{:S(2)}) %collective-permute-start.1) | collective-permute-done | bytes 3538976 | tf_op jit(solution)/shard_map/ppermute | solution.py:22
  47.1 7.4 %shard_map.30 = (bf16[384,384]{1,0:T(8,128)(2,1)}, f32[384,384]{1,0:T(8,128)}) custom-call(s32[2]{0:T(128)} %copy-done.2, bf16[6,384,768]{2,1,0:T(8,128)(2,1)} %copy-done.1, bf16[6,384,768]{2,1,0:T(8,128)(2,1)} %collective-permute-done.1.face_hbm), custom_call_target="tpu_custom_call" | custom-call | flops 2717908992 | bytes 3538944 | tf_op jit(solution)/shard_map/pallas_call | solution.py:214
  54.5 0.0 all-to-all-done
  54.5 0.1 collective-permute-start.2
  54.6 1.8 %collective-permute-done.2 = bf16[384,384]{1,0:T(8,128)(2,1)S(1)} collective-permute-done((bf16[384,384]{1,0:T(8,128)(2,1)}, bf16[384,384]{1,0:T(8,128)(2,1)S(1)}, u32[]{:S(2)}, u32[]{:S(2)}) %collective-permute-start.2) | collective-permute-done | bytes 294944 | tf_op jit(solution)/shard_map/ppermute | solution.py:26
  56.4 1.1 %convert_add_fusion = f32[384,384]{1,0:T(8,128)S(1)} fusion(f32[384,384]{1,0:T(8,128)} %get-tuple-element.19, bf16[384,384]{1,0:T(8,128)(2,1)S(1)} %collective-permute-done.2), kind=kLoop, calls=%fused_computation | loop fusion | flops 294912 | bytes 1474560 | tf_op jit(solution)/shard_map/add | solution.py:222
  57.5 0.1 collective-permute-start.3
  57.6 5.9 %collective-permute-done.3 = bf16[192,384]{1,0:T(8,128)(2,1)S(1)} collective-permute-done((bf16[192,384]{1,0:T(8,128)(2,1)S(1)}, bf16[192,384]{1,0:T(8,128)(2,1)S(1)}, u32[]{:S(2)}, u32[]{:S(2)}) %collective-permute-start.3) | collective-permute-done | bytes 147488 | tf_op jit(solution)/shard_map/ppermute | solution.py:226
  63.5 0.8 %collective-permute-start.4 = (bf16[48,384]{1,0:T(8,128)(2,1)S(1)}, bf16[48,384]{1,0:T(8,128)(2,1)S(1)}, u32[]{:S(2)}, u32[]{:S(2)}) collective-permute-start(bf16[48,384]{1,0:T(8,128)(2,1)S(1)} %get-tuple-element.23), channel_id=1, source_target_pairs={{12,0},{13,1},{14,2},{15,3},{0,4},{1,5},{2,6},{3,7},{4,8},{5,9},{6... | collective-permute-start | bytes 110600 | tf_op jit(solution)/shard_map/ppermute | solution.py:22
  64.4 3.0 %collective-permute-start.6 = (bf16[48,384]{1,0:T(8,128)(2,1)S(1)}, bf16[48,384]{1,0:T(8,128)(2,1)S(1)}, u32[]{:S(2)}, u32[]{:S(2)}) collective-permute-start(bf16[48,384]{1,0:T(8,128)(2,1)S(1)} %get-tuple-element.24), channel_id=1, source_target_pairs={{4,0},{5,1},{6,2},{7,3},{8,4},{9,5},{10,6},{11,7},{12,8},{13,9},{1... | collective-permute-start | bytes 110600 | tf_op jit(solution)/shard_map/ppermute | solution.py:22
  67.4 0.4 collective-permute-start.5
  67.9 1.5 %collective-permute-done.4 = bf16[48,384]{1,0:T(8,128)(2,1)S(1)} collective-permute-done((bf16[48,384]{1,0:T(8,128)(2,1)S(1)}, bf16[48,384]{1,0:T(8,128)(2,1)S(1)}, u32[]{:S(2)}, u32[]{:S(2)}) %collective-permute-start.4) | collective-permute-done | bytes 36896 | tf_op jit(solution)/shard_map/ppermute | solution.py:22
  69.4 0.0 collective-permute-done.6
  69.4 2.9 %collective-permute-done.5 = bf16[48,384]{1,0:T(8,128)(2,1)S(1)} collective-permute-done((bf16[48,384]{1,0:T(8,128)(2,1)S(1)}, bf16[48,384]{1,0:T(8,128)(2,1)S(1)}, u32[]{:S(2)}, u32[]{:S(2)}) %collective-permute-start.5) | collective-permute-done | bytes 36896 | tf_op jit(solution)/shard_map/ppermute | solution.py:22
  72.3 0.7 copy.4
  (6 shorter events, 0.2 us)
Async XLA Ops:
  0.0 47.1 %collective-permute-start.1 = (bf16[6,384,768]{2,1,0:T(8,128)(2,1)}, bf16[6,384,768]{2,1,0:T(8,128)(2,1)}, u32[]{:S(2)}, u32[]{:S(2)}) collective-permute-start(bf16[6,384,768]{2,1,0:T(8,128)(2,1)} %bitcast.10), channel_id=1, source_target_pairs={{1,0},{2,1},{3,2},{4,3},{5,4},{6,5},{7,6},{8,7},{9,8},{10,9},{11,1... | collective-permute-start | bytes 10616840 | tf_op jit(solution)/shard_map/ppermute | solution.py:22
  6.8 2.0 %copy-start = (bf16[2,384,3,1,768]{4,1,3,2,0:T(8,128)(2,1)S(1)}, bf16[2,384,3,1,768]{4,1,3,2,0:T(8,128)(2,1)}, u32[]{:S(2)}) copy-start(bf16[2,384,3,1,768]{4,1,3,2,0:T(8,128)(2,1)} %param.2) | copy-start | bytes 10616836
  8.8 12.7 %copy-start.2 = (s32[2]{0:T(128)}, s32[2]{0:T(128)S(1)}, u32[]{:S(2)}) copy-start(s32[2]{0:T(128)S(1)} %pad_add_fusion.where_ref) | copy-start | bytes 28
  21.5 1.6 %collective-permute-start = (bf16[384,384]{1,0:T(8,128)(2,1)S(1)}, bf16[384,384]{1,0:T(8,128)(2,1)S(1)}, u32[]{:S(2)}, u32[]{:S(2)}) collective-permute-start(bf16[384,384]{1,0:T(8,128)(2,1)S(1)} %get-tuple-element.14), channel_id=1, source_target_pairs={{0,1},{1,0},{2,3},{3,2},{4,5},{5,4},{6,7},{7,6},{8,9},{9,8},{10,11... | collective-permute-start | bytes 884744 | tf_op jit(solution)/shard_map/ppermute | solution.py:26
  27.5 1.8 %copy-start.1 = (bf16[6,384,768]{2,1,0:T(8,128)(2,1)}, bf16[6,384,768]{2,1,0:T(8,128)(2,1)S(1)}, u32[]{:S(2)}) copy-start(bf16[6,384,768]{2,1,0:T(8,128)(2,1)S(1)} %get-tuple-element.15.w_hbm) | copy-start | bytes 10616836
  29.3 25.2 %all-to-all-start = ((bf16[8,48,384]{2,1,0:T(8,128)(2,1)}), bf16[8,48,384]{2,1,0:T(8,128)(2,1)S(1)}, u32[]{:S(2)}, u32[]{:S(2)}) async-start(bf16[8,48,384]{2,1,0:T(8,128)(2,1)} %bitcast.5), calls=%async_computation | async-start | bytes 589824 | tf_op jit(solution)/shard_map/all_to_all | solution.py:208
  54.5 1.9 %collective-permute-start.2 = (bf16[384,384]{1,0:T(8,128)(2,1)}, bf16[384,384]{1,0:T(8,128)(2,1)S(1)}, u32[]{:S(2)}, u32[]{:S(2)}) collective-permute-start(bf16[384,384]{1,0:T(8,128)(2,1)} %get-tuple-element.20), channel_id=1, source_target_pairs={{0,1},{1,0},{2,3},{3,2},{4,5},{5,4},{6,7},{7,6},{8,9},{9,8},{10,11... | collective-permute-start | bytes 884744 | tf_op jit(solution)/shard_map/ppermute | solution.py:26
  57.5 6.0 %collective-permute-start.3 = (bf16[192,384]{1,0:T(8,128)(2,1)S(1)}, bf16[192,384]{1,0:T(8,128)(2,1)S(1)}, u32[]{:S(2)}, u32[]{:S(2)}) collective-permute-start(bf16[192,384]{1,0:T(8,128)(2,1)S(1)} %slice.41), channel_id=1, source_target_pairs={{0,2},{1,3},{2,0},{3,1},{4,6},{5,7},{6,4},{7,5},{8,10},{9,11},{10,... | collective-permute-start | bytes 442376 | tf_op jit(solution)/shard_map/ppermute | solution.py:226
  63.5 5.8 %collective-permute-start.4 = (bf16[48,384]{1,0:T(8,128)(2,1)S(1)}, bf16[48,384]{1,0:T(8,128)(2,1)S(1)}, u32[]{:S(2)}, u32[]{:S(2)}) collective-permute-start(bf16[48,384]{1,0:T(8,128)(2,1)S(1)} %get-tuple-element.23), channel_id=1, source_target_pairs={{12,0},{13,1},{14,2},{15,3},{0,4},{1,5},{2,6},{3,7},{4,8},{5,9},{6... | collective-permute-start | bytes 110600 | tf_op jit(solution)/shard_map/ppermute | solution.py:22
  64.4 5.0 %collective-permute-start.6 = (bf16[48,384]{1,0:T(8,128)(2,1)S(1)}, bf16[48,384]{1,0:T(8,128)(2,1)S(1)}, u32[]{:S(2)}, u32[]{:S(2)}) collective-permute-start(bf16[48,384]{1,0:T(8,128)(2,1)S(1)} %get-tuple-element.24), channel_id=1, source_target_pairs={{4,0},{5,1},{6,2},{7,3},{8,4},{9,5},{10,6},{11,7},{12,8},{13,9},{1... | collective-permute-start | bytes 110600 | tf_op jit(solution)/shard_map/ppermute | solution.py:22
  67.4 4.9 %collective-permute-start.5 = (bf16[48,384]{1,0:T(8,128)(2,1)S(1)}, bf16[48,384]{1,0:T(8,128)(2,1)S(1)}, u32[]{:S(2)}, u32[]{:S(2)}) collective-permute-start(bf16[48,384]{1,0:T(8,128)(2,1)S(1)} %get-tuple-element.25), channel_id=1, source_target_pairs={{8,0},{9,1},{10,2},{11,3},{12,4},{13,5},{14,6},{15,7},{0,8},{1,9},... | collective-permute-start | bytes 110600 | tf_op jit(solution)/shard_map/ppermute | solution.py:22

commit v9 on v8

--- a/solution.py
+++ b/solution.py
@@ -114,9 +114,7 @@
     finish(sum_re, sum_im, slabs, where_ref[0], range(slabs // 2), acc, send, keep)
 
 
-def w_kernel(field_ref, links_ref, keep_ref, got_ref, w_ref, chip_ref):
-    chip_ref[...] = (keep_ref[...] + got_ref[...].astype(jnp.float32)).astype(jnp.bfloat16)
-
+def w_kernel(field_ref, links_ref, after_ref, w_ref):
     def store(part, a, m, lanes, value):
         w_ref[part * 3 + a, pl.ds(pl.multiple_of(m * ROWS, ROWS), ROWS), lanes] = value
 
@@ -130,8 +128,8 @@
     return [to + 1 - low for to in ahead] + [to + low for to in ahead]
 
 
-def z_kernel(slabs, where_ref, w_hbm, face_hbm, send, keep, left, right, acc, sems):
-    count = w_hbm.shape[1]
+def z_kernel(slabs, where_ref, w_ref, face_hbm, send, keep, right, acc, sems):
+    count = w_ref.shape[1]
     copies = []
     for b in range(3):
         group = []
@@ -139,7 +137,6 @@
             k = part * 3 + b
             rows = pl.ds(part * count, count)
             group.append(pltpu.make_async_copy(face_hbm.at[k], right.at[b, rows], sems.at[k]))
-            group.append(pltpu.make_async_copy(w_hbm.at[k], left.at[k], sems.at[6 + k]))
         for copy in group:
             copy.start()
         copies.append(group)
@@ -148,7 +145,7 @@
         for copy in copies[b]:
             copy.wait()
         for part in range(2):
-            term = inner(left[part * 3 + b], right[b])
+            term = inner(w_ref[part * 3 + b], right[b])
             product[part] = term if b == 0 else product[part] + term
     sum_re = product[0][:, :count] + product[1][:, count:]
     sum_im = product[0][:, count:] - product[1][:, :count]
@@ -189,12 +186,13 @@
     square = pltpu.VMEM((2, count, count), jnp.float32)
     send_x, keep_x = call(
         functools.partial(x_kernel, slabs), halves, [SMEM, VMEM, VMEM],
-        [stacked, square], 22, flops, moved,
+        [stacked, square], 16, flops, moved,
     )(where, field, links)
-    w, chip_x = call(
-        w_kernel, [jax.ShapeDtypeStruct(field.shape, jnp.bfloat16), halves[0]], [VMEM] * 4, [], 12,
+    chip_x = (keep_x + swapped(send_x, "gz").astype(jnp.float32)).astype(jnp.bfloat16)
+    (w,) = call(
+        w_kernel, [jax.ShapeDtypeStruct(field.shape, jnp.bfloat16)], [VMEM, VMEM, ANY], [], 10,
         count * sites * 66, 2 * moved,
-    )(field, links, keep_x, swapped(send_x, "gz"))
+    )(field, links, chip_x)
 
     if rows_by_own(slabs, own):
         groups = [list(range(c, slabs, 2)) for c in range(2)]
@@ -212,11 +210,8 @@
 
     got_x = exchanged(chip_x)
     send_z, keep_z = call(
-        functools.partial(z_kernel, slabs), halves, [SMEM, ANY, ANY],
-        [
-            pltpu.VMEM(field.shape, jnp.bfloat16), stacked, square, pltpu.SemaphoreType.DMA((12,)),
-        ],
-        58, flops, moved,
+        functools.partial(z_kernel, slabs), halves, [SMEM, VMEM, ANY],
+        [stacked, square, pltpu.SemaphoreType.DMA((6,))], 14, flops, moved,
     )(where, w, face)
     send_z, got_x = lax.optimization_barrier((send_z, got_x))
     chip_z = keep_z + swapped(send_z, "gz").astype(jnp.float32)

time: 73.4 us -> 70.4 us (0.959)
  waiting for transfers between devices: 28 us -> 24.5 us
  Pallas kernels: 24.4 us -> 21.9 us
  local copies, waits for them, and re-layouts: 4.58 us -> 6.23 us
    ppermute x4, waiting for transfers between devices: 18.8 us -> 15.5 us  [passed_along(): return lax.ppermute(block, axis, route)]
    pallas_call x2, Pallas kernels: 11.7 us -> 9.23 us  [the longest x1 5.59 us: shards(): call(functools.partial(z_kernel, slabs), halves, [SMEM, VMEM, ANY], [stac...]
    add x1, other arithmetic: 1.13 us -> 0.07 us  [shards(): chip_z = keep_z + swapped(send_z, 'gz').astype(jnp.float32)]
    unnamed x6 -> x10, local copies, waits for them, and re-layouts: 3.79 us -> 4.79 us
    reduce_sum x1, other arithmetic: 0.04 us -> 1.01 us  [total(): jnp.sum(got.reshape(blocks).astype(jnp.float32), axis=0)]
    convert_element_type x0 -> x1, other arithmetic: none -> 0.78 us  [shards(): (keep_x + swapped(send_x, 'gz').astype(jnp.float32)).astype(jnp.bfloat16)]
  transfers between devices with their start and end apart: 8 -> 8, of which waited for: 6 -> 6; matrix products, arithmetic and copies ran while one was open for 2% -> 5% of each run, Pallas kernels for 33% -> 31%
where the time goes in v9:
time: 70.4 us; the launch traced here: 70 us
  waiting for transfers between devices  24.5 us (35%)
  Pallas kernels  21.9 us (31%)
  starting transfers between devices  14 us (20%)
  local copies, waits for them, and re-layouts  6.23 us (9%)
  other arithmetic  3.2 us (5%)
    ppermute x4, waiting for transfers between devices, passed_along(): return lax.ppermute(block, axis, route)  15.5 us
    pallas_call x1, Pallas kernels, shards(): call(functools.partial(x_kernel, slabs), halves, [SMEM, VMEM, VMEM], [sta...  12.7 us
    ppermute x4, starting transfers between devices, passed_along(): return lax.ppermute(block, axis, route)  9.74 us
    ppermute x1, waiting for transfers between devices, shards(): near = lax.ppermute(other, 'gz', [(i, i ^ 2) for i in range(slabs)])  5.88 us
    pallas_call x1, Pallas kernels, shards(): call(functools.partial(z_kernel, slabs), halves, [SMEM, VMEM, ANY], [stac...  5.59 us
    unnamed x10, local copies, waits for them, and re-layouts  4.79 us
    all_to_all x1, starting transfers between devices, exchanged(): return lax.all_to_all(chip, 'gz', 0, 0, axis_index_groups=groups)  4.06 us
    pallas_call x1, Pallas kernels, shards(): call(w_kernel, [jax.ShapeDtypeStruct(field.shape, jnp.bfloat16)], [VMEM,...  3.64 us
  transfers between devices with their start and end apart: 8, of which 6 were waited for; matrix products, arithmetic and copies ran while one was open for 5% of the time, Pallas kernels for 31%

profile of v9, /device:TPU:0, one launch (start us, length us, event | category | flops | bytes accessed | tf_op | source)
XLA Modules:
  0.0 70.0 jit_solution(7299151315577124858)
XLA Ops:
  0.0 5.4 %collective-permute-start.1 = (bf16[6,384,768]{2,1,0:T(8,128)(2,1)}, bf16[6,384,768]{2,1,0:T(8,128)(2,1)}, u32[]{:S(2)}, u32[]{:S(2)}) collective-permute-start(bf16[6,384,768]{2,1,0:T(8,128)(2,1)} %bitcast.10), channel_id=1, source_target_pairs={{1,0},{2,1},{3,2},{4,3},{5,4},{6,5},{7,6},{8,7},{9,8},{10,9},{11,1... | collective-permute-start | bytes 10616840 | tf_op jit(solution)/shard_map/ppermute | solution.py:22
  5.4 1.2 %reduce.2 = f32[2,2,3,3,768]{4,3,2,1,0:T(4,128)S(1)} reduce(f32[2,2,3,3,1,768]{5,4,3,2,1,0:T(1,128)} %param.3, f32[]{:T(128)} %constant.12), dimensions={4}, to_apply=%param.3.reduce_sub_computation | reduce | bytes 221188 | tf_op args[1]
  6.6 0.7 %reshape.20.links_ref = f32[36,768]{1,0:T(8,128)} reshape(f32[2,2,3,3,768]{4,3,2,1,0:T(4,128)S(1)} %reduce.2) | data formatting | bytes 221184 | tf_op jit(solution)/shard_map/reshape | solution.py:176
  7.3 0.1 pad_add_fusion.where_ref
  7.4 0.0 copy-start
  7.4 2.0 %copy-done = bf16[2,384,3,1,768]{4,1,3,2,0:T(8,128)(2,1)S(1)} copy-done((bf16[2,384,3,1,768]{4,1,3,2,0:T(8,128)(2,1)S(1)}, bf16[2,384,3,1,768]{4,1,3,2,0:T(8,128)(2,1)}, u32[]{:S(2)}) %copy-start) | copy-done | bytes 3538968
  9.4 0.0 copy-start.3
  9.4 0.9 %copy-done.3 = f32[36,768]{1,0:T(8,128)S(1)} copy-done((f32[36,768]{1,0:T(8,128)S(1)}, f32[36,768]{1,0:T(8,128)}, u32[]{:S(2)}) %copy-start.3) | copy-done | bytes 110616
  10.3 0.0 copy-start.1
  10.3 12.7 %shard_map.28 = (bf16[384,384]{1,0:T(8,128)(2,1)S(1)}, f32[384,384]{1,0:T(8,128)S(1)}) custom-call(s32[2]{0:T(128)S(1)} %pad_add_fusion.where_ref, bf16[6,384,768]{2,1,0:T(8,128)(2,1)S(1)} %bitcast.11, f32[36,768]{1,0:T(8,128)S(1)} %copy-done.3), custom_call_target="tpu_custom_call" | custom-call | flops 2717908992 | bytes 3538944 | tf_op jit(solution)/shard_map/pallas_call | solution.py:187
  23.0 0.1 collective-permute-start
  23.1 1.6 %collective-permute-done = bf16[384,384]{1,0:T(8,128)(2,1)S(1)} collective-permute-done((bf16[384,384]{1,0:T(8,128)(2,1)S(1)}, bf16[384,384]{1,0:T(8,128)(2,1)S(1)}, u32[]{:S(2)}, u32[]{:S(2)}) %collective-permute-start) | collective-permute-done | bytes 294944 | tf_op jit(solution)/shard_map/ppermute | solution.py:26
  24.7 0.8 %add_convert_fusion.after_ref = bf16[384,384]{1,0:T(8,128)(2,1)} fusion(f32[384,384]{1,0:T(8,128)S(1)} %get-tuple-element.11, bf16[384,384]{1,0:T(8,128)(2,1)S(1)} %collective-permute-done), kind=kLoop, calls=%fused_computation.2 | loop fusion | flops 442368 | bytes 1179648 | tf_op jit(solution)/shard_map/convert_element_type | solution.py:191
  25.5 4.1 %all-to-all-start = ((bf16[8,48,384]{2,1,0:T(8,128)(2,1)}), bf16[8,48,384]{2,1,0:T(8,128)(2,1)}, u32[]{:S(2)}, u32[]{:S(2)}) async-start(bf16[8,48,384]{2,1,0:T(8,128)(2,1)} %bitcast.13), calls=%async_computation | async-start | bytes 589824 | tf_op jit(solution)/shard_map/all_to_all | solution.py:206
  29.5 0.0 copy-done.1
  29.5 0.0 copy-start.2
  29.6 1.0 %copy-done.2 = bf16[384,384]{1,0:T(8,128)(2,1)S(1)} copy-done((bf16[384,384]{1,0:T(8,128)(2,1)S(1)}, bf16[384,384]{1,0:T(8,128)(2,1)}, u32[]{:S(2)}) %copy-start.2) | copy-done | bytes 294936
  30.5 0.0 copy-start.4
  30.5 0.9 %copy-done.4 = f32[36,768]{1,0:T(8,128)S(1)} copy-done((f32[36,768]{1,0:T(8,128)S(1)}, f32[36,768]{1,0:T(8,128)}, u32[]{:S(2)}) %copy-start.4) | copy-done | bytes 110616
  31.4 3.6 %shard_map.29.w_ref = bf16[6,384,768]{2,1,0:T(8,128)(2,1)S(1)} custom-call(bf16[6,384,768]{2,1,0:T(8,128)(2,1)S(1)} %bitcast.12, f32[36,768]{1,0:T(8,128)S(1)} %copy-done.4, bf16[384,384]{1,0:T(8,128)(2,1)S(1)} %copy-done.2), custom_call_target="tpu_custom_call" | custom-call | flops 19464192 | bytes 7077888 | tf_op jit(solution)/shard_map/pallas_call | solution.py:192
  35.1 12.1 %collective-permute-done.1.face_hbm = bf16[6,384,768]{2,1,0:T(8,128)(2,1)} collective-permute-done((bf16[6,384,768]{2,1,0:T(8,128)(2,1)}, bf16[6,384,768]{2,1,0:T(8,128)(2,1)}, u32[]{:S(2)}, u32[]{:S(2)}) %collective-permute-start.1) | collective-permute-done | bytes 3538976 | tf_op jit(solution)/shard_map/ppermute | solution.py:22
  47.1 5.6 %shard_map.30 = (bf16[384,384]{1,0:T(8,128)(2,1)S(1)}, f32[384,384]{1,0:T(8,128)S(1)}) custom-call(s32[2]{0:T(128)S(1)} %pad_add_fusion.where_ref, bf16[6,384,768]{2,1,0:T(8,128)(2,1)S(1)} %shard_map.29.w_ref, bf16[6,384,768]{2,1,0:T(8,128)(2,1)} %collective-permute-done.1.face_hbm), custom_call_target="tpu_custom_call" | custom-call | flops 2717908992 | bytes 3538944 | tf_op jit(solution)/shard_map/pallas_call | solution.py:212
  52.7 0.0 all-to-all-done
  52.7 0.1 collective-permute-start.2
  52.8 1.6 %collective-permute-done.2 = bf16[384,384]{1,0:T(8,128)(2,1)S(1)} collective-permute-done((bf16[384,384]{1,0:T(8,128)(2,1)S(1)}, bf16[384,384]{1,0:T(8,128)(2,1)S(1)}, u32[]{:S(2)}, u32[]{:S(2)}) %collective-permute-start.2) | collective-permute-done | bytes 294944 | tf_op jit(solution)/shard_map/ppermute | solution.py:26
  54.4 0.1 convert_add_fusion
  54.5 0.1 collective-permute-start.3
  54.6 5.9 %collective-permute-done.3 = bf16[192,384]{1,0:T(8,128)(2,1)S(1)} collective-permute-done((bf16[192,384]{1,0:T(8,128)(2,1)S(1)}, bf16[192,384]{1,0:T(8,128)(2,1)S(1)}, u32[]{:S(2)}, u32[]{:S(2)}) %collective-permute-start.3) | collective-permute-done | bytes 147488 | tf_op jit(solution)/shard_map/ppermute | solution.py:221
  60.5 0.8 %collective-permute-start.4 = (bf16[48,384]{1,0:T(8,128)(2,1)S(1)}, bf16[48,384]{1,0:T(8,128)(2,1)S(1)}, u32[]{:S(2)}, u32[]{:S(2)}) collective-permute-start(bf16[48,384]{1,0:T(8,128)(2,1)S(1)} %get-tuple-element.19), channel_id=1, source_target_pairs={{12,0},{13,1},{14,2},{15,3},{0,4},{1,5},{2,6},{3,7},{4,8},{5,9},{6... | collective-permute-start | bytes 110600 | tf_op jit(solution)/shard_map/ppermute | solution.py:22
  61.3 3.0 %collective-permute-start.6 = (bf16[48,384]{1,0:T(8,128)(2,1)S(1)}, bf16[48,384]{1,0:T(8,128)(2,1)S(1)}, u32[]{:S(2)}, u32[]{:S(2)}) collective-permute-start(bf16[48,384]{1,0:T(8,128)(2,1)S(1)} %get-tuple-element.20), channel_id=1, source_target_pairs={{4,0},{5,1},{6,2},{7,3},{8,4},{9,5},{10,6},{11,7},{12,8},{13,9},{1... | collective-permute-start | bytes 110600 | tf_op jit(solution)/shard_map/ppermute | solution.py:22
  64.4 0.4 collective-permute-start.5
  64.8 1.0 %convert_reduce_fusion = f32[48,384]{1,0:T(8,128)S(1)} fusion(bf16[8,48,384]{2,1,0:T(8,128)(2,1)} %all-to-all-done), kind=kLoop, calls=%fused_computation.1 | loop fusion | flops 276480 | bytes 368640 | tf_op jit(solution)/shard_map/reduce_sum | solution.py:209
  65.8 0.5 collective-permute-done.4
  66.3 0.0 collective-permute-done.6
  66.3 2.9 %collective-permute-done.5 = bf16[48,384]{1,0:T(8,128)(2,1)S(1)} collective-permute-done((bf16[48,384]{1,0:T(8,128)(2,1)S(1)}, bf16[48,384]{1,0:T(8,128)(2,1)S(1)}, u32[]{:S(2)}, u32[]{:S(2)}) %collective-permute-start.5) | collective-permute-done | bytes 36896 | tf_op jit(solution)/shard_map/ppermute | solution.py:22
  69.3 0.7 %copy.4 = f32[24,4,384]{2,1,0:T(4,128)} copy(f32[24,4,384]{2,0,1:T(8,128)S(1)} %fusion) | data formatting | bytes 294912 | tf_op jit(solution)/shard_map/mul | solution.py:231
  (5 shorter events, 0.1 us)
Async XLA Ops:
  0.0 47.1 %collective-permute-start.1 = (bf16[6,384,768]{2,1,0:T(8,128)(2,1)}, bf16[6,384,768]{2,1,0:T(8,128)(2,1)}, u32[]{:S(2)}, u32[]{:S(2)}) collective-permute-start(bf16[6,384,768]{2,1,0:T(8,128)(2,1)} %bitcast.10), channel_id=1, source_target_pairs={{1,0},{2,1},{3,2},{4,3},{5,4},{6,5},{7,6},{8,7},{9,8},{10,9},{11,1... | collective-permute-start | bytes 10616840 | tf_op jit(solution)/shard_map/ppermute | solution.py:22
  7.4 2.0 %copy-start = (bf16[2,384,3,1,768]{4,1,3,2,0:T(8,128)(2,1)S(1)}, bf16[2,384,3,1,768]{4,1,3,2,0:T(8,128)(2,1)}, u32[]{:S(2)}) copy-start(bf16[2,384,3,1,768]{4,1,3,2,0:T(8,128)(2,1)} %param.2) | copy-start | bytes 10616836
  9.4 0.9 %copy-start.3 = (f32[36,768]{1,0:T(8,128)S(1)}, f32[36,768]{1,0:T(8,128)}, u32[]{:S(2)}) copy-start(f32[36,768]{1,0:T(8,128)} %reshape.20.links_ref) | copy-start | bytes 331780
  10.3 19.2 %copy-start.1 = (bf16[2,384,3,1,768]{4,1,3,2,0:T(8,128)(2,1)S(1)}, bf16[2,384,3,1,768]{4,1,3,2,0:T(8,128)(2,1)}, u32[]{:S(2)}) copy-start(bf16[2,384,3,1,768]{4,1,3,2,0:T(8,128)(2,1)} %param.2) | copy-start | bytes 10616836
  23.0 1.6 %collective-permute-start = (bf16[384,384]{1,0:T(8,128)(2,1)S(1)}, bf16[384,384]{1,0:T(8,128)(2,1)S(1)}, u32[]{:S(2)}, u32[]{:S(2)}) collective-permute-start(bf16[384,384]{1,0:T(8,128)(2,1)S(1)} %get-tuple-element.12), channel_id=1, source_target_pairs={{0,1},{1,0},{2,3},{3,2},{4,5},{5,4},{6,7},{7,6},{8,9},{9,8},{10,11... | collective-permute-start | bytes 884744 | tf_op jit(solution)/shard_map/ppermute | solution.py:26
  25.5 27.3 %all-to-all-start = ((bf16[8,48,384]{2,1,0:T(8,128)(2,1)}), bf16[8,48,384]{2,1,0:T(8,128)(2,1)}, u32[]{:S(2)}, u32[]{:S(2)}) async-start(bf16[8,48,384]{2,1,0:T(8,128)(2,1)} %bitcast.13), calls=%async_computation | async-start | bytes 589824 | tf_op jit(solution)/shard_map/all_to_all | solution.py:206
  29.5 1.0 %copy-start.2 = (bf16[384,384]{1,0:T(8,128)(2,1)S(1)}, bf16[384,384]{1,0:T(8,128)(2,1)}, u32[]{:S(2)}) copy-start(bf16[384,384]{1,0:T(8,128)(2,1)} %add_convert_fusion.after_ref) | copy-start | bytes 884740
  30.5 0.9 %copy-start.4 = (f32[36,768]{1,0:T(8,128)S(1)}, f32[36,768]{1,0:T(8,128)}, u32[]{:S(2)}) copy-start(f32[36,768]{1,0:T(8,128)} %reshape.20.links_ref) | copy-start | bytes 331780
  52.7 1.6 %collective-permute-start.2 = (bf16[384,384]{1,0:T(8,128)(2,1)S(1)}, bf16[384,384]{1,0:T(8,128)(2,1)S(1)}, u32[]{:S(2)}, u32[]{:S(2)}) collective-permute-start(bf16[384,384]{1,0:T(8,128)(2,1)S(1)} %get-tuple-element.16), channel_id=1, source_target_pairs={{0,1},{1,0},{2,3},{3,2},{4,5},{5,4},{6,7},{7,6},{8,9},{9,8},{10,11... | collective-permute-start | bytes 884744 | tf_op jit(solution)/shard_map/ppermute | solution.py:26
  54.5 6.0 %collective-permute-start.3 = (bf16[192,384]{1,0:T(8,128)(2,1)S(1)}, bf16[192,384]{1,0:T(8,128)(2,1)S(1)}, u32[]{:S(2)}, u32[]{:S(2)}) collective-permute-start(bf16[192,384]{1,0:T(8,128)(2,1)S(1)} %slice.41), channel_id=1, source_target_pairs={{0,2},{1,3},{2,0},{3,1},{4,6},{5,7},{6,4},{7,5},{8,10},{9,11},{10,... | collective-permute-start | bytes 442376 | tf_op jit(solution)/shard_map/ppermute | solution.py:221
  60.5 5.8 %collective-permute-start.4 = (bf16[48,384]{1,0:T(8,128)(2,1)S(1)}, bf16[48,384]{1,0:T(8,128)(2,1)S(1)}, u32[]{:S(2)}, u32[]{:S(2)}) collective-permute-start(bf16[48,384]{1,0:T(8,128)(2,1)S(1)} %get-tuple-element.19), channel_id=1, source_target_pairs={{12,0},{13,1},{14,2},{15,3},{0,4},{1,5},{2,6},{3,7},{4,8},{5,9},{6... | collective-permute-start | bytes 110600 | tf_op jit(solution)/shard_map/ppermute | solution.py:22
  61.3 5.0 %collective-permute-start.6 = (bf16[48,384]{1,0:T(8,128)(2,1)S(1)}, bf16[48,384]{1,0:T(8,128)(2,1)S(1)}, u32[]{:S(2)}, u32[]{:S(2)}) collective-permute-start(bf16[48,384]{1,0:T(8,128)(2,1)S(1)} %get-tuple-element.20), channel_id=1, source_target_pairs={{4,0},{5,1},{6,2},{7,3},{8,4},{9,5},{10,6},{11,7},{12,8},{13,9},{1... | collective-permute-start | bytes 110600 | tf_op jit(solution)/shard_map/ppermute | solution.py:22
  64.4 4.9 %collective-permute-start.5 = (bf16[48,384]{1,0:T(8,128)(2,1)S(1)}, bf16[48,384]{1,0:T(8,128)(2,1)S(1)}, u32[]{:S(2)}, u32[]{:S(2)}) collective-permute-start(bf16[48,384]{1,0:T(8,128)(2,1)S(1)} %get-tuple-element.21), channel_id=1, source_target_pairs={{8,0},{9,1},{10,2},{11,3},{12,4},{13,5},{14,6},{15,7},{0,8},{1,9},... | collective-permute-start | bytes 110600 | tf_op jit(solution)/shard_map/ppermute | solution.py:22

commit v10 on v9

--- a/solution.py
+++ b/solution.py
@@ -77,6 +77,13 @@
     return lax.dot_general(left, right, (((1,), (1,)), ((), ())), preferred_element_type=jnp.float32)
 
 
+def block_order(chip, chips):
+    along = chips // 2
+    ahead = [lax.rem((chip >> 1) + r, along) * 2 for r in range(along)]
+    low = chip & 1
+    return [to + 1 - low for to in ahead] + [to + low for to in ahead]
+
+
 def finish(sum_re, sum_im, slabs, core, order, acc, send, keep):
     count = send.shape[0]
     own = count // slabs
@@ -111,21 +118,14 @@
             product[part] = term if b == 0 else product[part] + term
     sum_re = product[0][:, :count] + product[1][:, count:]
     sum_im = product[0][:, count:] - product[1][:, :count]
-    finish(sum_re, sum_im, slabs, where_ref[0], range(slabs // 2), acc, send, keep)
-
-
-def w_kernel(field_ref, links_ref, after_ref, w_ref):
+    finish(sum_re, sum_im, slabs, where_ref[0], block_order(where_ref[1], slabs // 2), acc, send, keep)
+
+
+def w_kernel(field_ref, links_ref, w_ref):
     def store(part, a, m, lanes, value):
         w_ref[part * 3 + a, pl.ds(pl.multiple_of(m * ROWS, ROWS), ROWS), lanes] = value
 
     times_links(field_ref, links_ref, 1, True, False, store)
-
-
-def z_order(chip, chips):
-    along = chips // 2
-    ahead = [lax.rem((chip >> 1) + r, along) * 2 for r in range(along)]
-    low = chip & 1
-    return [to + 1 - low for to in ahead] + [to + low for to in ahead]
 
 
 def z_kernel(slabs, where_ref, w_ref, face_hbm, send, keep, right, acc, sems):
@@ -149,7 +149,7 @@
             product[part] = term if b == 0 else product[part] + term
     sum_re = product[0][:, :count] + product[1][:, count:]
     sum_im = product[0][:, count:] - product[1][:, :count]
-    finish(sum_re, sum_im, slabs, where_ref[0], z_order(where_ref[1], slabs // 2), acc, send, keep)
+    finish(sum_re, sum_im, slabs, where_ref[0], block_order(where_ref[1], slabs // 2), acc, send, keep)
 
 
 def call(body, outs, specs, scratch, mib, flops, moved):
@@ -188,46 +188,42 @@
         functools.partial(x_kernel, slabs), halves, [SMEM, VMEM, VMEM],
         [stacked, square], 16, flops, moved,
     )(where, field, links)
-    chip_x = (keep_x + swapped(send_x, "gz").astype(jnp.float32)).astype(jnp.bfloat16)
     (w,) = call(
-        w_kernel, [jax.ShapeDtypeStruct(field.shape, jnp.bfloat16)], [VMEM, VMEM, ANY], [], 10,
+        w_kernel, [jax.ShapeDtypeStruct(field.shape, jnp.bfloat16)], [VMEM, VMEM], [], 10,
         count * sites * 66, 2 * moved,
-    )(field, links, chip_x)
-
-    if rows_by_own(slabs, own):
-        groups = [list(range(c, slabs, 2)) for c in range(2)]
-        blocks = (slabs // 2, 1, 2 * own, count)
-    else:
-        groups = None
-        blocks = (slabs // 2, 2, own, count)
+    )(field, links)
+    chip_x = keep_x + swapped(send_x, "gz").astype(jnp.float32)
+    other_x = chip_x[: count // 2].astype(jnp.bfloat16)
+    face, other_x = lax.optimization_barrier((face, other_x))
+
+    def from_neighbour(other):
+        return lax.ppermute(other, "gz", [(i, i ^ 2) for i in range(slabs)]).astype(jnp.float32)
+
+    def total(line):
+        result = line[: 2 * own]
+        for r in range(1, slabs // 4):
+            block = line[r * 2 * own : (r + 1) * 2 * own].astype(jnp.bfloat16)
+            result = result + passed_along(block, "gz", 4 * r).astype(jnp.float32)
+        return result.reshape(2, own, count)
 
     def exchanged(chip):
-        chip = chip.reshape((-1,) + blocks[2:])
-        return lax.all_to_all(chip, "gz", 0, 0, axis_index_groups=groups)
-
-    def total(got):
-        return jnp.sum(got.reshape(blocks).astype(jnp.float32), axis=0).reshape(2, own, count)
-
-    got_x = exchanged(chip_x)
+        chip = chip.astype(jnp.bfloat16).reshape(slabs, own, count)
+        got = lax.all_to_all(chip, "gz", 0, 0).reshape(slabs // 2, 2, own, count)
+        return jnp.sum(got.astype(jnp.float32), axis=0)
+
+    near_x = from_neighbour(other_x) if rows_by_own(slabs, own) else None
     send_z, keep_z = call(
         functools.partial(z_kernel, slabs), halves, [SMEM, VMEM, ANY],
         [stacked, square, pltpu.SemaphoreType.DMA((6,))], 14, flops, moved,
     )(where, w, face)
-    send_z, got_x = lax.optimization_barrier((send_z, got_x))
     chip_z = keep_z + swapped(send_z, "gz").astype(jnp.float32)
     if rows_by_own(slabs, own):
         half = count // 2
-        other = chip_z[:half].astype(jnp.bfloat16)
-        near = lax.ppermute(other, "gz", [(i, i ^ 2) for i in range(slabs)])
-        line = chip_z[half:] + near.astype(jnp.float32)
-        total_z = line[: 2 * own]
-        for r in range(1, slabs // 4):
-            block = line[r * 2 * own : (r + 1) * 2 * own].astype(jnp.bfloat16)
-            total_z = total_z + passed_along(block, "gz", 4 * r).astype(jnp.float32)
-        total_z = total_z.reshape(2, own, count)
+        near_z = from_neighbour(chip_z[:half].astype(jnp.bfloat16))
+        totals = [total(chip_x[half:] + near_x), total(chip_z[half:] + near_z)]
     else:
-        total_z = total(exchanged(chip_z.astype(jnp.bfloat16)))
-    both = jnp.concatenate([total(got_x), total_z], axis=0)
+        totals = [exchanged(chip_x), exchanged(chip_z)]
+    both = jnp.concatenate(totals, axis=0)
     return jnp.transpose(both, (1, 0, 2)) * scale
 
 

time: 70.4 us -> 70.2 us (level)
  local copies, waits for them, and re-layouts: 6.23 us -> 2.2 us
  starting transfers between devices: 14 us -> 17.2 us
  waiting for transfers between devices: 24.5 us -> 26.2 us
  other arithmetic: 3.2 us -> 2.27 us
    ppermute x4 -> x7, waiting for transfers between devices: 15.5 us -> 24.5 us  [passed_along(): return lax.ppermute(block, axis, route)]
    ppermute x1 -> x2, waiting for transfers between devices: 5.88 us -> 0.23 us  [from_neighbour(): lax.ppermute(other, 'gz', [(i, i ^ 2) for i in range(slabs)])]
    ppermute x4 -> x7, starting transfers between devices: 9.74 us -> 15 us  [passed_along(): return lax.ppermute(block, axis, route)]
    all_to_all x1 -> x0, starting transfers between devices: 4.06 us -> none  [exchanged(): return lax.all_to_all(chip, 'gz', 0, 0, axis_index_groups=groups)]
    unnamed x10 -> x4, local copies, waits for them, and re-layouts: 4.79 us -> 2 us
    ppermute x1 -> x2, starting transfers between devices: 0.07 us -> 2.08 us  [from_neighbour(): lax.ppermute(other, 'gz', [(i, i ^ 2) for i in range(slabs)])]
    ppermute x2, waiting for transfers between devices: 3.14 us -> 1.51 us  [swapped(): lax.ppermute(block, axis, [(i, i ^ 1) for i in range(lax.axis_size(axis))])]
    reduce_sum x1 -> x0, other arithmetic: 1.01 us -> none  [total(): jnp.sum(got.reshape(blocks).astype(jnp.float32), axis=0)]
  transfers between devices with their start and end apart: 8 -> 11, of which waited for: 6 -> 5; matrix products, arithmetic and copies ran while one was open for 5% -> 2% of each run, Pallas kernels for 31% -> 31%
where the time goes in v10:
time: 70.2 us; the launch traced here: 70 us
  waiting for transfers between devices  26.2 us (37%)
  Pallas kernels  21.9 us (31%)
  starting transfers between devices  17.2 us (25%)
  other arithmetic  2.27 us (3%)
  local copies, waits for them, and re-layouts  2.2 us (3%)
    ppermute x7, waiting for transfers between devices, passed_along(): return lax.ppermute(block, axis, route)  24.5 us
    ppermute x7, starting transfers between devices, passed_along(): return lax.ppermute(block, axis, route)  15 us
    pallas_call x1, Pallas kernels, shards(): call(functools.partial(x_kernel, slabs), halves, [SMEM, VMEM, VMEM], [sta...  12.7 us
    pallas_call x1, Pallas kernels, shards(): call(functools.partial(z_kernel, slabs), halves, [SMEM, VMEM, ANY], [stac...  5.59 us
    pallas_call x1, Pallas kernels, shards(): call(w_kernel, [jax.ShapeDtypeStruct(field.shape, jnp.bfloat16)], [VMEM,...  3.65 us
    ppermute x2, starting transfers between devices, from_neighbour(): lax.ppermute(other, 'gz', [(i, i ^ 2) for i in range(slabs)])  2.08 us
    unnamed x4, local copies, waits for them, and re-layouts  2 us
    ppermute x2, waiting for transfers between devices, swapped(): lax.ppermute(block, axis, [(i, i ^ 1) for i in range(lax.axis_size(axis))])  1.51 us
  transfers between devices with their start and end apart: 11, of which 5 were waited for; matrix products, arithmetic and copies ran while one was open for 2% of the time, Pallas kernels for 31%

profile of v10, /device:TPU:0, one launch (start us, length us, event | category | flops | bytes accessed | tf_op | source)
XLA Modules:
  0.0 70.0 jit_solution(8732785541792873393)
XLA Ops:
  0.0 5.4 %collective-permute-start.1 = (bf16[6,384,768]{2,1,0:T(8,128)(2,1)}, bf16[6,384,768]{2,1,0:T(8,128)(2,1)}, u32[]{:S(2)}, u32[]{:S(2)}) collective-permute-start(bf16[6,384,768]{2,1,0:T(8,128)(2,1)} %bitcast.9), channel_id=1, source_target_pairs={{1,0},{2,1},{3,2},{4,3},{5,4},{6,5},{7,6},{8,7},{9,8},{10,9},{11,1... | collective-permute-start | bytes 10616840 | tf_op jit(solution)/shard_map/ppermute | solution.py:22
  5.4 1.2 %reduce = f32[2,2,3,3,768]{4,3,2,1,0:T(4,128)S(1)} reduce(f32[2,2,3,3,1,768]{5,4,3,2,1,0:T(1,128)} %param.3, f32[]{:T(128)} %constant.10), dimensions={4}, to_apply=%param.3.reduce_sub_computation | reduce | bytes 221188 | tf_op args[1]
  6.6 0.1 reshape.13.links_ref
  6.7 0.1 pad_add_fusion.where_ref
  6.8 0.0 copy-start
  6.8 2.0 %copy-done = bf16[2,384,3,1,768]{4,1,3,2,0:T(8,128)(2,1)S(1)} copy-done((bf16[2,384,3,1,768]{4,1,3,2,0:T(8,128)(2,1)S(1)}, bf16[2,384,3,1,768]{4,1,3,2,0:T(8,128)(2,1)}, u32[]{:S(2)}) %copy-start) | copy-done | bytes 3538968
  8.8 0.0 copy-start.1
  8.8 12.7 %shard_map.28 = (bf16[384,384]{1,0:T(8,128)(2,1)S(1)}, f32[384,384]{1,0:T(8,128)S(1)}) custom-call(s32[2]{0:T(128)S(1)} %pad_add_fusion.where_ref, bf16[6,384,768]{2,1,0:T(8,128)(2,1)S(1)} %bitcast.10, f32[36,768]{1,0:T(8,128)S(1)} %reshape.13.links_ref), custom_call_target="tpu_custom_call" | custom-call | flops 2717908992 | bytes 3538944 | tf_op jit(solution)/shard_map/pallas_call | solution.py:187
  21.5 0.1 collective-permute-start
  21.6 0.0 copy-done.1
  21.6 3.6 %shard_map.29.w_ref = bf16[6,384,768]{2,1,0:T(8,128)(2,1)S(1)} custom-call(bf16[6,384,768]{2,1,0:T(8,128)(2,1)S(1)} %bitcast.11, f32[36,768]{1,0:T(8,128)S(1)} %reshape.13.links_ref), custom_call_target="tpu_custom_call" | custom-call | flops 19464192 | bytes 7077888 | tf_op jit(solution)/shard_map/pallas_call | solution.py:191
  25.2 0.0 collective-permute-done
  25.3 0.1 convert_add_fusion.1
  25.4 19.4 %collective-permute-done.1.face_hbm = bf16[6,384,768]{2,1,0:T(8,128)(2,1)} collective-permute-done((bf16[6,384,768]{2,1,0:T(8,128)(2,1)}, bf16[6,384,768]{2,1,0:T(8,128)(2,1)}, u32[]{:S(2)}, u32[]{:S(2)}) %collective-permute-start.1) | collective-permute-done | bytes 3538976 | tf_op jit(solution)/shard_map/ppermute | solution.py:22
  44.8 0.0 collective-permute-start.2
  44.8 5.6 %shard_map.30 = (bf16[384,384]{1,0:T(8,128)(2,1)S(1)}, f32[384,384]{1,0:T(8,128)S(1)}) custom-call(s32[2]{0:T(128)S(1)} %pad_add_fusion.where_ref, bf16[6,384,768]{2,1,0:T(8,128)(2,1)S(1)} %shard_map.29.w_ref, bf16[6,384,768]{2,1,0:T(8,128)(2,1)} %collective-permute-done.1.face_hbm), custom_call_target="tpu_custom_call" | custom-call | flops 2717908992 | bytes 3538944 | tf_op jit(solution)/shard_map/pallas_call | solution.py:215
  50.4 0.1 collective-permute-start.6
  50.4 0.0 collective-permute-done.2
  50.5 1.5 %collective-permute-done.6 = bf16[384,384]{1,0:T(8,128)(2,1)S(1)} collective-permute-done((bf16[384,384]{1,0:T(8,128)(2,1)S(1)}, bf16[384,384]{1,0:T(8,128)(2,1)S(1)}, u32[]{:S(2)}, u32[]{:S(2)}) %collective-permute-start.6) | collective-permute-done | bytes 294944 | tf_op jit(solution)/shard_map/ppermute | solution.py:26
  52.0 0.1 convert_add_fusion
  52.1 2.1 %collective-permute-start.7 = (bf16[192,384]{1,0:T(8,128)(2,1)S(1)}, bf16[192,384]{1,0:T(8,128)(2,1)S(1)}, u32[]{:S(2)}, u32[]{:S(2)}) collective-permute-start(bf16[192,384]{1,0:T(8,128)(2,1)S(1)} %slice.82), channel_id=1, source_target_pairs={{0,2},{1,3},{2,0},{3,1},{4,6},{5,7},{6,4},{7,5},{8,10},{9,11},{10,... | collective-permute-start | bytes 442376 | tf_op jit(solution)/shard_map/ppermute | solution.py:200
  54.2 0.1 collective-permute-start.3
  54.3 3.8 %collective-permute-start.4 = (bf16[48,384]{1,0:T(8,128)(2,1)S(1)}, bf16[48,384]{1,0:T(8,128)(2,1)S(1)}, u32[]{:S(2)}, u32[]{:S(2)}) collective-permute-start(bf16[48,384]{1,0:T(8,128)(2,1)S(1)} %get-tuple-element.23), channel_id=1, source_target_pairs={{8,0},{9,1},{10,2},{11,3},{12,4},{13,5},{14,6},{15,7},{0,8},{1,9},... | collective-permute-start | bytes 110600 | tf_op jit(solution)/shard_map/ppermute | solution.py:22
  58.1 0.0 collective-permute-start.5
  58.1 0.2 collective-permute-done.7
  58.4 5.0 %collective-permute-start.10 = (bf16[48,384]{1,0:T(8,128)(2,1)S(1)}, bf16[48,384]{1,0:T(8,128)(2,1)S(1)}, u32[]{:S(2)}, u32[]{:S(2)}) collective-permute-start(bf16[48,384]{1,0:T(8,128)(2,1)S(1)} %get-tuple-element.25), channel_id=1, source_target_pairs={{4,0},{5,1},{6,2},{7,3},{8,4},{9,5},{10,6},{11,7},{12,8},{13,9},{1... | collective-permute-start | bytes 110600 | tf_op jit(solution)/shard_map/ppermute | solution.py:22
  63.4 0.0 collective-permute-start.8
  63.4 0.0 collective-permute-done.3
  63.4 0.6 collective-permute-start.9
  64.0 0.0 collective-permute-done.4
  64.0 0.0 collective-permute-done.5
  64.1 0.9 %collective-permute-done.10 = bf16[48,384]{1,0:T(8,128)(2,1)S(1)} collective-permute-done((bf16[48,384]{1,0:T(8,128)(2,1)S(1)}, bf16[48,384]{1,0:T(8,128)(2,1)S(1)}, u32[]{:S(2)}, u32[]{:S(2)}) %collective-permute-start.10) | collective-permute-done | bytes 36896 | tf_op jit(solution)/shard_map/ppermute | solution.py:22
  65.0 4.1 %collective-permute-done.8 = bf16[48,384]{1,0:T(8,128)(2,1)S(1)} collective-permute-done((bf16[48,384]{1,0:T(8,128)(2,1)S(1)}, bf16[48,384]{1,0:T(8,128)(2,1)S(1)}, u32[]{:S(2)}, u32[]{:S(2)}) %collective-permute-start.8) | collective-permute-done | bytes 36896 | tf_op jit(solution)/shard_map/ppermute | solution.py:22
  69.2 0.0 collective-permute-done.9
  69.2 0.7 %fusion = f32[24,4,384]{2,1,0:T(4,128)} fusion(f32[2,24,384]{2,0,1:T(2,128)S(1)} %copy.4, f32[2,24,384]{2,0,1:T(2,128)S(1)} %copy.3), kind=kLoop, calls=%fused_computation.7 | loop fusion | flops 73728 | bytes 294912 | tf_op jit(solution)/shard_map/mul | solution.py:227
  (10 shorter events, 0.3 us)
Async XLA Ops:
  0.0 44.8 %collective-permute-start.1 = (bf16[6,384,768]{2,1,0:T(8,128)(2,1)}, bf16[6,384,768]{2,1,0:T(8,128)(2,1)}, u32[]{:S(2)}, u32[]{:S(2)}) collective-permute-start(bf16[6,384,768]{2,1,0:T(8,128)(2,1)} %bitcast.9), channel_id=1, source_target_pairs={{1,0},{2,1},{3,2},{4,3},{5,4},{6,5},{7,6},{8,7},{9,8},{10,9},{11,1... | collective-permute-start | bytes 10616840 | tf_op jit(solution)/shard_map/ppermute | solution.py:22
  6.8 2.0 %copy-start = (bf16[2,384,3,1,768]{4,1,3,2,0:T(8,128)(2,1)S(1)}, bf16[2,384,3,1,768]{4,1,3,2,0:T(8,128)(2,1)}, u32[]{:S(2)}) copy-start(bf16[2,384,3,1,768]{4,1,3,2,0:T(8,128)(2,1)} %param.2) | copy-start | bytes 10616836
  8.8 12.8 %copy-start.1 = (bf16[2,384,3,1,768]{4,1,3,2,0:T(8,128)(2,1)S(1)}, bf16[2,384,3,1,768]{4,1,3,2,0:T(8,128)(2,1)}, u32[]{:S(2)}) copy-start(bf16[2,384,3,1,768]{4,1,3,2,0:T(8,128)(2,1)} %param.2) | copy-start | bytes 10616836
  21.5 3.7 %collective-permute-start = (bf16[384,384]{1,0:T(8,128)(2,1)S(1)}, bf16[384,384]{1,0:T(8,128)(2,1)S(1)}, u32[]{:S(2)}, u32[]{:S(2)}) collective-permute-start(bf16[384,384]{1,0:T(8,128)(2,1)S(1)} %get-tuple-element.12), channel_id=1, source_target_pairs={{0,1},{1,0},{2,3},{3,2},{4,5},{5,4},{6,7},{7,6},{8,9},{9,8},{10,11... | collective-permute-start | bytes 884744 | tf_op jit(solution)/shard_map/ppermute | solution.py:26
  44.8 5.7 %collective-permute-start.2 = (bf16[192,384]{1,0:T(8,128)(2,1)S(1)}, bf16[192,384]{1,0:T(8,128)(2,1)S(1)}, u32[]{:S(2)}, u32[]{:S(2)}) collective-permute-start(bf16[192,384]{1,0:T(8,128)(2,1)S(1)} %slice.83), channel_id=1, source_target_pairs={{0,2},{1,3},{2,0},{3,1},{4,6},{5,7},{6,4},{7,5},{8,10},{9,11},{10,... | collective-permute-start | bytes 442376 | tf_op jit(solution)/shard_map/ppermute | solution.py:200
  50.4 1.6 %collective-permute-start.6 = (bf16[384,384]{1,0:T(8,128)(2,1)S(1)}, bf16[384,384]{1,0:T(8,128)(2,1)S(1)}, u32[]{:S(2)}, u32[]{:S(2)}) collective-permute-start(bf16[384,384]{1,0:T(8,128)(2,1)S(1)} %get-tuple-element.16), channel_id=1, source_target_pairs={{0,1},{1,0},{2,3},{3,2},{4,5},{5,4},{6,7},{7,6},{8,9},{9,8},{10,11... | collective-permute-start | bytes 884744 | tf_op jit(solution)/shard_map/ppermute | solution.py:26
  52.1 6.2 %collective-permute-start.7 = (bf16[192,384]{1,0:T(8,128)(2,1)S(1)}, bf16[192,384]{1,0:T(8,128)(2,1)S(1)}, u32[]{:S(2)}, u32[]{:S(2)}) collective-permute-start(bf16[192,384]{1,0:T(8,128)(2,1)S(1)} %slice.82), channel_id=1, source_target_pairs={{0,2},{1,3},{2,0},{3,1},{4,6},{5,7},{6,4},{7,5},{8,10},{9,11},{10,... | collective-permute-start | bytes 442376 | tf_op jit(solution)/shard_map/ppermute | solution.py:200
  54.2 9.2 %collective-permute-start.3 = (bf16[48,384]{1,0:T(8,128)(2,1)S(1)}, bf16[48,384]{1,0:T(8,128)(2,1)S(1)}, u32[]{:S(2)}, u32[]{:S(2)}) collective-permute-start(bf16[48,384]{1,0:T(8,128)(2,1)S(1)} %get-tuple-element.21), channel_id=1, source_target_pairs={{12,0},{13,1},{14,2},{15,3},{0,4},{1,5},{2,6},{3,7},{4,8},{5,9},{6... | collective-permute-start | bytes 110600 | tf_op jit(solution)/shard_map/ppermute | solution.py:22
  54.3 9.8 %collective-permute-start.4 = (bf16[48,384]{1,0:T(8,128)(2,1)S(1)}, bf16[48,384]{1,0:T(8,128)(2,1)S(1)}, u32[]{:S(2)}, u32[]{:S(2)}) collective-permute-start(bf16[48,384]{1,0:T(8,128)(2,1)S(1)} %get-tuple-element.23), channel_id=1, source_target_pairs={{8,0},{9,1},{10,2},{11,3},{12,4},{13,5},{14,6},{15,7},{0,8},{1,9},... | collective-permute-start | bytes 110600 | tf_op jit(solution)/shard_map/ppermute | solution.py:22
  58.1 6.0 %collective-permute-start.5 = (bf16[48,384]{1,0:T(8,128)(2,1)S(1)}, bf16[48,384]{1,0:T(8,128)(2,1)S(1)}, u32[]{:S(2)}, u32[]{:S(2)}) collective-permute-start(bf16[48,384]{1,0:T(8,128)(2,1)S(1)} %get-tuple-element.22), channel_id=1, source_target_pairs={{4,0},{5,1},{6,2},{7,3},{8,4},{9,5},{10,6},{11,7},{12,8},{13,9},{1... | collective-permute-start | bytes 110600 | tf_op jit(solution)/shard_map/ppermute | solution.py:22
  58.4 6.7 %collective-permute-start.10 = (bf16[48,384]{1,0:T(8,128)(2,1)S(1)}, bf16[48,384]{1,0:T(8,128)(2,1)S(1)}, u32[]{:S(2)}, u32[]{:S(2)}) collective-permute-start(bf16[48,384]{1,0:T(8,128)(2,1)S(1)} %get-tuple-element.25), channel_id=1, source_target_pairs={{4,0},{5,1},{6,2},{7,3},{8,4},{9,5},{10,6},{11,7},{12,8},{13,9},{1... | collective-permute-start | bytes 110600 | tf_op jit(solution)/shard_map/ppermute | solution.py:22
  63.4 5.8 %collective-permute-start.8 = (bf16[48,384]{1,0:T(8,128)(2,1)S(1)}, bf16[48,384]{1,0:T(8,128)(2,1)S(1)}, u32[]{:S(2)}, u32[]{:S(2)}) collective-permute-start(bf16[48,384]{1,0:T(8,128)(2,1)S(1)} %get-tuple-element.24), channel_id=1, source_target_pairs={{12,0},{13,1},{14,2},{15,3},{0,4},{1,5},{2,6},{3,7},{4,8},{5,9},{6... | collective-permute-start | bytes 110600 | tf_op jit(solution)/shard_map/ppermute | solution.py:22
  63.4 5.8 %collective-permute-start.9 = (bf16[48,384]{1,0:T(8,128)(2,1)S(1)}, bf16[48,384]{1,0:T(8,128)(2,1)S(1)}, u32[]{:S(2)}, u32[]{:S(2)}) collective-permute-start(bf16[48,384]{1,0:T(8,128)(2,1)S(1)} %get-tuple-element.26), channel_id=1, source_target_pairs={{8,0},{9,1},{10,2},{11,3},{12,4},{13,5},{14,6},{15,7},{0,8},{1,9},... | collective-permute-start | bytes 110600 | tf_op jit(solution)/shard_map/ppermute | solution.py:22

commit v11 on v9

--- a/solution.py
+++ b/solution.py
@@ -26,20 +26,16 @@
     return lax.ppermute(block, axis, [(i, i ^ 1) for i in range(lax.axis_size(axis))])
 
 
-def times_links(field_ref, links_ref, mu, adjoint, roll, store):
+def times_links(field_ref, coef_ref, roll, store):
     count, sites = field_ref.shape[1:]
     for t in range(sites // LANES):
         lanes = slice(t * LANES, (t + 1) * LANES)
 
-        def link(part, a, b):
-            row = ((part * 2 + mu) * 3 + a) * 3 + b
-            value = jnp.broadcast_to(links_ref[row : row + 1, lanes], (ROWS, LANES))
-            return -value if adjoint and part == 1 else value
-
-        def links_of(part, a):
-            return [link(part, b, a) if adjoint else link(part, a, b) for b in range(3)]
-
-        u = [[links_of(p, a) for a in range(3)] for p in range(2)]
+        def coef(part, a, b):
+            row = (part * 3 + a) * 3 + b
+            return jnp.broadcast_to(coef_ref[row : row + 1, lanes], (ROWS, LANES))
+
+        u = [[[coef(p, a, b) for b in range(3)] for a in range(3)] for p in range(2)]
         if roll:
             lane = lax.broadcasted_iota(jnp.int32, (ROWS, LANES), 1)
             last = (lane & (X - 1)) == X - 1
@@ -103,7 +99,7 @@
     def store(part, a, m, lanes, value):
         right[a, pl.ds(pl.multiple_of(part * count + m * ROWS, ROWS), ROWS), lanes] = value
 
-    times_links(field_ref, links_ref, 0, False, True, store)
+    times_links(field_ref, links_ref, True, store)
     product = [None, None]
     for b in range(3):
         for part in range(2):
@@ -114,11 +110,29 @@
     finish(sum_re, sum_im, slabs, where_ref[0], range(slabs // 2), acc, send, keep)
 
 
-def w_kernel(field_ref, links_ref, after_ref, w_ref):
+def cut_kernel(where_ref, field_hbm, half_hbm, sems):
+    half = half_hbm.shape[2]
+    lanes = pl.ds(pl.multiple_of(where_ref[0] * half, LANES), half)
+    copies = [
+        pltpu.make_async_copy(field_hbm.at[k, :, lanes], half_hbm.at[k], sems.at[k])
+        for k in range(field_hbm.shape[0])
+    ]
+    for copy in copies:
+        copy.start()
+    for copy in copies:
+        copy.wait()
+
+
+def b_kernel(field_ref, coef_ref, after_ref, b_ref):
+    count, sites = field_ref.shape[1:]
+    half = sites // 2
+
     def store(part, a, m, lanes, value):
-        w_ref[part * 3 + a, pl.ds(pl.multiple_of(m * ROWS, ROWS), ROWS), lanes] = value
-
-    times_links(field_ref, links_ref, 1, True, False, store)
+        rows = pl.ds(pl.multiple_of(part * count + m * ROWS, ROWS), ROWS)
+        start = a * half + lanes.start % half
+        b_ref[lanes.start // half, rows, start : start + LANES] = value
+
+    times_links(field_ref, coef_ref, False, store)
 
 
 def z_order(chip, chips):
@@ -128,36 +142,44 @@
     return [to + 1 - low for to in ahead] + [to + low for to in ahead]
 
 
-def z_kernel(slabs, where_ref, w_ref, face_hbm, send, keep, right, acc, sems):
-    count = w_ref.shape[1]
+def z_kernel(near, slabs, where_ref, b_ref, got_hbm, *refs):
+    if near:
+        out, right, sems = refs
+    else:
+        before, send, keep, right, acc, sems = refs
+    count, half = got_hbm.shape[1], right.shape[1] // 3
+    core = where_ref[0]
+    which = core if near else 1 - core
+    lanes = pl.ds(pl.multiple_of(which * half, LANES), half) if near else pl.ds(0, half)
     copies = []
-    for b in range(3):
-        group = []
-        for part in range(2):
+    for part in range(2):
+        for b in range(3):
             k = part * 3 + b
-            rows = pl.ds(part * count, count)
-            group.append(pltpu.make_async_copy(face_hbm.at[k], right.at[b, rows], sems.at[k]))
-        for copy in group:
-            copy.start()
-        copies.append(group)
-    product = [None, None]
-    for b in range(3):
-        for copy in copies[b]:
-            copy.wait()
-        for part in range(2):
-            term = inner(w_ref[part * 3 + b], right[b])
-            product[part] = term if b == 0 else product[part] + term
-    sum_re = product[0][:, :count] + product[1][:, count:]
-    sum_im = product[0][:, count:] - product[1][:, :count]
-    finish(sum_re, sum_im, slabs, where_ref[0], z_order(where_ref[1], slabs // 2), acc, send, keep)
-
-
-def call(body, outs, specs, scratch, mib, flops, moved):
+            to = right.at[pl.ds(part * count, count), pl.ds(b * half, half)]
+            copies.append(pltpu.make_async_copy(got_hbm.at[k, :, lanes], to, sems.at[k]))
+    for copy in copies:
+        copy.start()
+    for copy in copies:
+        copy.wait()
+    sign = (1 - 2 * which).astype(jnp.float32)
+    from_re = inner(b_ref[which, :count, :], right[...])
+    from_im = inner(b_ref[which, count:, :], right[...])
+    sum_re = (from_re[:, :count] + from_im[:, count:]) * sign
+    sum_im = (from_re[:, count:] - from_im[:, :count]) * sign
+    if near:
+        out[0] = sum_re
+        out[1] = sum_im
+    else:
+        order = z_order(where_ref[1], slabs // 2)
+        finish(before[0] + sum_re, before[1] + sum_im, slabs, core, order, acc, send, keep)
+
+
+def call(body, outs, specs, scratch, mib, flops, moved, where=VMEM):
     return pl.pallas_call(
         body,
         out_shape=outs,
         in_specs=specs,
-        out_specs=[VMEM] * len(outs),
+        out_specs=[where] * len(outs),
         scratch_shapes=scratch,
         compiler_params=pltpu.CompilerParams(vmem_limit_bytes=mib * 2**20),
         cost_estimate=pl.CostEstimate(flops=flops, bytes_accessed=moved, transcendentals=0),
@@ -173,8 +195,19 @@
     index = lax.axis_index("gz").astype(jnp.int32)
     where = jnp.stack([index & 1, index >> 1])
     field = jnp.transpose(vectors, (0, 2, 3, 1, 4)).reshape(6, count, sites)
-    links = links.reshape(36, sites)
-    face = passed_along(field, "gz", -1)
+    half = sites // 2
+    (cut,) = call(
+        cut_kernel, [jax.ShapeDtypeStruct((6, count, half), vectors.dtype)], [SMEM, ANY],
+        [pltpu.SemaphoreType.DMA((6,))], 60, 0, 12 * count * half, ANY,
+    )(where, field)
+    far = lax.ppermute(cut, "gz", [(i, (i + i % 2 * 2 - 1) % slabs) for i in range(slabs)])
+    near = swapped(field, "gz")
+    links = links.reshape(2, 2, 3, 3, sites)
+    links_x, links_z = links[:, 0].reshape(18, sites), links[:, 1]
+    conjugate = jnp.array([1.0, -1.0], jnp.float32).reshape(2, 1, 1, 1)
+    adjoint = jnp.transpose(links_z[..., :half], (0, 2, 1, 3)) * conjugate
+    coefs = jnp.concatenate([adjoint, passed_along(links_z[..., half:], "gz", 1)], axis=-1)
+    coefs = coefs.reshape(18, sites)
 
     flops = 24 * count * count * sites
     moved = 12 * count * sites
@@ -187,12 +220,18 @@
     send_x, keep_x = call(
         functools.partial(x_kernel, slabs), halves, [SMEM, VMEM, VMEM],
         [stacked, square], 16, flops, moved,
-    )(where, field, links)
+    )(where, field, links_x)
     chip_x = (keep_x + swapped(send_x, "gz").astype(jnp.float32)).astype(jnp.bfloat16)
-    (w,) = call(
-        w_kernel, [jax.ShapeDtypeStruct(field.shape, jnp.bfloat16)], [VMEM, VMEM, ANY], [], 10,
-        count * sites * 66, 2 * moved,
-    )(field, links, chip_x)
+    (prepared,) = call(
+        b_kernel, [jax.ShapeDtypeStruct((2, 2 * count, 3 * half), jnp.bfloat16)], [VMEM, VMEM, ANY],
+        [], 10, count * sites * 66, 2 * moved,
+    )(field, coefs, chip_x)
+    right = [pltpu.VMEM((2 * count, 3 * half), jnp.bfloat16)]
+    sems = [pltpu.SemaphoreType.DMA((6,))]
+    (first,) = call(
+        functools.partial(z_kernel, True, slabs), [jax.ShapeDtypeStruct((2, count, count), jnp.float32)],
+        [SMEM, VMEM, ANY], right + sems, 14, flops // 2, moved // 2,
+    )(where, prepared, near)
 
     if rows_by_own(slabs, own):
         groups = [list(range(c, slabs, 2)) for c in range(2)]
@@ -210,16 +249,16 @@
 
     got_x = exchanged(chip_x)
     send_z, keep_z = call(
-        functools.partial(z_kernel, slabs), halves, [SMEM, VMEM, ANY],
-        [stacked, square, pltpu.SemaphoreType.DMA((6,))], 14, flops, moved,
-    )(where, w, face)
+        functools.partial(z_kernel, False, slabs), halves, [SMEM, VMEM, ANY, VMEM],
+        right + [square] + sems, 14, flops // 2, moved // 2,
+    )(where, prepared, far, first)
     send_z, got_x = lax.optimization_barrier((send_z, got_x))
     chip_z = keep_z + swapped(send_z, "gz").astype(jnp.float32)
     if rows_by_own(slabs, own):
-        half = count // 2
-        other = chip_z[:half].astype(jnp.bfloat16)
+        rows = count // 2
+        other = chip_z[:rows].astype(jnp.bfloat16)
         near = lax.ppermute(other, "gz", [(i, i ^ 2) for i in range(slabs)])
-        line = chip_z[half:] + near.astype(jnp.float32)
+        line = chip_z[rows:] + near.astype(jnp.float32)
         total_z = line[: 2 * own]
         for r in range(1, slabs // 4):
             block = line[r * 2 * own : (r + 1) * 2 * own].astype(jnp.bfloat16)

time: 70.4 us -> 135 us (1.92)
  Pallas kernels: 21.9 us -> 79.6 us
  starting transfers between devices: 14 us -> 33.9 us
  waiting for transfers between devices: 24.5 us -> 6.96 us
  local copies, waits for them, and re-layouts: 6.23 us -> 9.92 us
    pallas_call x2 -> x4, Pallas kernels: 9.23 us -> 66.9 us  [the longest x1 55.6 us: shards(): call(cut_kernel, [jax.ShapeDtypeStruct((6, count, half), vectors.dtype)],...]
    ppermute x2 -> x3, starting transfers between devices: 0.14 us -> 15.1 us  [swapped(): lax.ppermute(block, axis, [(i, i ^ 1) for i in range(lax.axis_size(axis))])]
    ppermute x4, waiting for transfers between devices: 15.5 us -> 1.59 us  [passed_along(): return lax.ppermute(block, axis, route)]
    ppermute x0 -> x1, starting transfers between devices: none -> 5.73 us  [shards(): lax.ppermute(cut, 'gz', [(i, (i + i % 2 * 2 - 1) % slabs) for i in range(...]
    ppermute x4, starting transfers between devices: 9.74 us -> 6.05 us  [passed_along(): return lax.ppermute(block, axis, route)]
    ppermute x1, starting transfers between devices: 0.07 us -> 2.91 us  [shards(): near = lax.ppermute(other, 'gz', [(i, i ^ 2) for i in range(slabs)])]
    slice x1 -> x4, local copies, waits for them, and re-layouts: 0.02 us -> 2.02 us  [the longest x2 1.38 us: shards(): links_x, links_z = (links[:, 0].reshape(18, sites), links[:, 1])]
    unnamed x10 -> x17, local copies, waits for them, and re-layouts: 4.79 us -> 2.81 us
  transfers between devices with their start and end apart: 8 -> 10, of which waited for: 6 -> 4; matrix products, arithmetic and copies ran while one was open for 5% -> 8% of each run, Pallas kernels for 31% -> 59%
where the time goes in v11:
time: 135 us
  Pallas kernels  79.6 us (59%)
  starting transfers between devices  33.9 us (25%)
  local copies, waits for them, and re-layouts  9.92 us (7%)
  waiting for transfers between devices  6.96 us (5%)
  other arithmetic  4.1 us (3%)
    pallas_call x1, Pallas kernels, shards(): call(cut_kernel, [jax.ShapeDtypeStruct((6, count, half), vectors.dtype)],...  55.6 us
    ppermute x3, starting transfers between devices, swapped(): lax.ppermute(block, axis, [(i, i ^ 1) for i in range(lax.axis_size(axis))])  15.1 us
    pallas_call x1, Pallas kernels, shards(): call(functools.partial(x_kernel, slabs), halves, [SMEM, VMEM, VMEM], [sta...  12.7 us
    ppermute x4, starting transfers between devices, passed_along(): return lax.ppermute(block, axis, route)  6.05 us
    ppermute x1, starting transfers between devices, shards(): lax.ppermute(cut, 'gz', [(i, (i + i % 2 * 2 - 1) % slabs) for i in range(...  5.73 us
    ppermute x1, waiting for transfers between devices, shards(): near = lax.ppermute(other, 'gz', [(i, i ^ 2) for i in range(slabs)])  4.15 us
    all_to_all x1, starting transfers between devices, exchanged(): return lax.all_to_all(chip, 'gz', 0, 0, axis_index_groups=groups)  4.07 us
    pallas_call x1, Pallas kernels, shards(): call(functools.partial(z_kernel, False, slabs), halves, [SMEM, VMEM, ANY,...  4 us
  transfers between devices with their start and end apart: 10, of which 4 were waited for; matrix products, arithmetic and copies ran while one was open for 8% of the time, Pallas kernels for 59%

profile of v11, /device:TPU:0, one launch (start us, length us, event | category | flops | bytes accessed | tf_op | source)
XLA Modules:
  0.0 134.6 jit_solution(13437756936457696150)
XLA Ops:
  0.0 0.0 copy-start
  0.0 0.5 collective-permute-start.3
  0.5 0.0 copy-start.6
  0.5 0.6 pad_add_fusion.where_ref
  1.0 0.0 copy-start.4
  1.0 55.6 %shard_map.39 = bf16[6,384,384]{2,1,0:T(8,128)(2,1)} custom-call(s32[2]{0:T(128)} %pad_add_fusion.where_ref, bf16[6,384,768]{2,1,0:T(8,128)(2,1)} %bitcast.22), custom_call_target="tpu_custom_call" | custom-call | bytes 1769472 | tf_op jit(solution)/shard_map/pallas_call | solution.py:199
  56.6 5.7 %collective-permute-start.2 = (bf16[6,384,384]{2,1,0:T(8,128)(2,1)}, bf16[6,384,384]{2,1,0:T(8,128)(2,1)}, u32[]{:S(2)}, u32[]{:S(2)}) collective-permute-start(bf16[6,384,384]{2,1,0:T(8,128)(2,1)} %shard_map.39), channel_id=1, source_target_pairs={{0,15},{1,2},{2,1},{3,4},{4,3},{5,6},{6,5},{7,8},{8,7},{9,10},{10,... | collective-permute-start | bytes 5308424 | tf_op jit(solution)/shard_map/ppermute | solution.py:203
  62.3 0.0 copy-done.6
  62.3 0.1 copy.19
  62.4 1.4 %slice_reduce_fusion = (f32[2,3,3,768]{3,2,1,0:T(4,128)}, f32[2,1,3,3,768]{4,1,3,2,0:T(1,128)}) fusion(f32[2,2,3,3,768]{4,1,3,2,0:T(2,128)S(1)} %bitcast.26), kind=kLoop, calls=%fused_computation.11 | loop fusion | bytes 221184 | tf_op jit(solution)/shard_map/slice | solution.py:206
  63.7 1.5 %reshape_squeeze.3.links_ref = f32[18,768]{1,0:T(8,128)} reshape(f32[2,3,3,768]{3,2,1,0:T(4,128)} %get-tuple-element.22) | data formatting | bytes 110592 | tf_op jit(solution)/shard_map/reshape;squeeze | solution.py:206
  65.3 0.0 copy-done
  65.3 0.0 copy-done.4
  65.3 0.0 copy-start.3
  65.3 0.9 copy-done.3
  66.1 0.0 copy-start.5
  66.2 0.0 copy-start.7
  66.2 12.7 %shard_map.37 = (bf16[384,384]{1,0:T(8,128)(2,1)S(1)}, f32[384,384]{1,0:T(8,128)S(1)}) custom-call(s32[2]{0:T(128)S(1)} %copy-done.4, bf16[6,384,768]{2,1,0:T(8,128)(2,1)S(1)} %bitcast.23, f32[18,768]{1,0:T(8,128)S(1)} %copy-done.3), custom_call_target="tpu_custom_call" | custom-call | flops 2717908992 | bytes 3538944 | tf_op jit(solution)/shard_map/pallas_call | solution.py:220
  78.9 0.1 collective-permute-start.1
  78.9 0.0 copy-done.5
  79.0 0.6 slice.46
  79.6 0.5 collective-permute-start
  80.1 0.7 copy.20
  80.8 0.0 collective-permute-done.1
  80.8 0.8 add_convert_fusion.after_ref
  81.5 4.1 %all-to-all-start = ((bf16[8,48,384]{2,1,0:T(8,128)(2,1)}), bf16[8,48,384]{2,1,0:T(8,128)(2,1)}, u32[]{:S(2)}, u32[]{:S(2)}) async-start(bf16[8,48,384]{2,1,0:T(8,128)(2,1)} %bitcast.25), calls=%async_computation | async-start | bytes 589824 | tf_op jit(solution)/shard_map/all_to_all | solution.py:245
  85.6 0.0 copy-done.7
  85.6 0.8 fusion.3
  86.5 0.0 collective-permute-done
  86.5 0.8 pad_maximum_fusion
  87.2 0.7 copy.12
  87.9 1.5 %reshape.26.coef_ref = f32[18,768]{1,0:T(8,128)} reshape(f32[2,3,3,768]{3,2,1,0:T(4,128)} %copy.12) | data formatting | bytes 110592 | tf_op jit(solution)/shard_map/reshape | solution.py:210
  89.4 0.0 copy-start.1
  89.4 1.0 copy-done.1
  90.4 0.0 copy-start.2
  90.4 0.9 copy-done.2
  91.3 3.6 %shard_map.38.b_ref = bf16[2,768,1152]{2,1,0:T(8,128)(2,1)S(1)} custom-call(bf16[6,384,768]{2,1,0:T(8,128)(2,1)S(1)} %bitcast.24, f32[18,768]{1,0:T(8,128)S(1)} %copy-done.2, bf16[384,384]{1,0:T(8,128)(2,1)S(1)} %copy-done.1), custom_call_target="tpu_custom_call" | custom-call | flops 19464192 | bytes 7077888 | tf_op jit(solution)/shard_map/pallas_call | solution.py:225
  94.9 0.0 collective-permute-done.3.got_hbm
  94.9 3.7 %shard_map.40.refs_0_ = f32[2,384,384]{2,1,0:T(8,128)S(1)} custom-call(s32[2]{0:T(128)S(1)} %copy-done.4, bf16[2,768,1152]{2,1,0:T(8,128)(2,1)S(1)} %shard_map.38.b_ref, bf16[6,384,768]{2,1,0:T(8,128)(2,1)} %collective-permute-done.3.got_hbm), custom_call_target="tpu_custom_call" | custom-call | flops 1358954496 | bytes 1769472 | tf_op jit(solution)/shard_map/pallas_call | solution.py:231
  98.7 0.0 collective-permute-done.2.got_hbm
  98.7 4.0 %shard_map.41 = (bf16[384,384]{1,0:T(8,128)(2,1)S(1)}, f32[384,384]{1,0:T(8,128)S(1)}) custom-call(s32[2]{0:T(128)S(1)} %copy-done.4, bf16[2,768,1152]{2,1,0:T(8,128)(2,1)S(1)} %shard_map.38.b_ref, bf16[6,384,384]{2,1,0:T(8,128)(2,1)} %collective-permute-done.2.got_hbm, f32[2,384,384]{2,1,0:T(8,128)S(1)} %shard_map.40.refs_0_), custom_call_target="tpu_custom_call" | custom-call | flops 1358954496 | bytes 1769472 | tf_op jit(solution)/shard_map/pallas_call | solution.py:251
  102.7 0.0 all-to-all-done
  102.7 14.6 %collective-permute-start.4 = (bf16[384,384]{1,0:T(8,128)(2,1)S(1)}, bf16[384,384]{1,0:T(8,128)(2,1)S(1)}, u32[]{:S(2)}, u32[]{:S(2)}) collective-permute-start(bf16[384,384]{1,0:T(8,128)(2,1)S(1)} %get-tuple-element.16), channel_id=1, source_target_pairs={{0,1},{1,0},{2,3},{3,2},{4,5},{5,4},{6,7},{7,6},{8,9},{9,8},{10,11... | collective-permute-start | bytes 884744 | tf_op jit(solution)/shard_map/ppermute | solution.py:26
  117.3 1.2 collective-permute-done.4
  118.5 0.1 convert_add_fusion
  118.6 2.9 %collective-permute-start.5 = (bf16[192,384]{1,0:T(8,128)(2,1)S(1)}, bf16[192,384]{1,0:T(8,128)(2,1)S(1)}, u32[]{:S(2)}, u32[]{:S(2)}) collective-permute-start(bf16[192,384]{1,0:T(8,128)(2,1)S(1)} %slice.65), channel_id=1, source_target_pairs={{0,2},{1,3},{2,0},{3,1},{4,6},{5,7},{6,4},{7,5},{8,10},{9,11},{10,... | collective-permute-start | bytes 442376 | tf_op jit(solution)/shard_map/ppermute | solution.py:260
  121.5 4.1 %collective-permute-done.5 = bf16[192,384]{1,0:T(8,128)(2,1)S(1)} collective-permute-done((bf16[192,384]{1,0:T(8,128)(2,1)S(1)}, bf16[192,384]{1,0:T(8,128)(2,1)S(1)}, u32[]{:S(2)}, u32[]{:S(2)}) %collective-permute-start.5) | collective-permute-done | bytes 147488 | tf_op jit(solution)/shard_map/ppermute | solution.py:260
  125.7 1.6 %collective-permute-start.6 = (bf16[48,384]{1,0:T(8,128)(2,1)S(1)}, bf16[48,384]{1,0:T(8,128)(2,1)S(1)}, u32[]{:S(2)}, u32[]{:S(2)}) collective-permute-start(bf16[48,384]{1,0:T(8,128)(2,1)S(1)} %get-tuple-element.19), channel_id=1, source_target_pairs={{12,0},{13,1},{14,2},{15,3},{0,4},{1,5},{2,6},{3,7},{4,8},{5,9},{6... | collective-permute-start | bytes 110600 | tf_op jit(solution)/shard_map/ppermute | solution.py:22
  127.3 2.6 %collective-permute-start.7 = (bf16[48,384]{1,0:T(8,128)(2,1)S(1)}, bf16[48,384]{1,0:T(8,128)(2,1)S(1)}, u32[]{:S(2)}, u32[]{:S(2)}) collective-permute-start(bf16[48,384]{1,0:T(8,128)(2,1)S(1)} %get-tuple-element.21), channel_id=1, source_target_pairs={{8,0},{9,1},{10,2},{11,3},{12,4},{13,5},{14,6},{15,7},{0,8},{1,9},... | collective-permute-start | bytes 110600 | tf_op jit(solution)/shard_map/ppermute | solution.py:22
  129.9 1.3 %collective-permute-start.8 = (bf16[48,384]{1,0:T(8,128)(2,1)S(1)}, bf16[48,384]{1,0:T(8,128)(2,1)S(1)}, u32[]{:S(2)}, u32[]{:S(2)}) collective-permute-start(bf16[48,384]{1,0:T(8,128)(2,1)S(1)} %get-tuple-element.20), channel_id=1, source_target_pairs={{4,0},{5,1},{6,2},{7,3},{8,4},{9,5},{10,6},{11,7},{12,8},{13,9},{1... | collective-permute-start | bytes 110600 | tf_op jit(solution)/shard_map/ppermute | solution.py:22
  131.3 1.0 convert_reduce_fusion
  132.3 0.0 collective-permute-done.6
  132.3 0.4 collective-permute-done.7
  132.7 1.2 collective-permute-done.8
  133.9 0.7 copy.13
  (6 shorter events, 0.1 us)
Async XLA Ops:
  0.0 65.3 %copy-start = (bf16[2,384,3,1,768]{4,1,3,2,0:T(8,128)(2,1)S(1)}, bf16[2,384,3,1,768]{4,1,3,2,0:T(8,128)(2,1)}, u32[]{:S(2)}) copy-start(bf16[2,384,3,1,768]{4,1,3,2,0:T(8,128)(2,1)} %param.3) | copy-start | bytes 10616836
  0.0 94.9 %collective-permute-start.3 = (bf16[6,384,768]{2,1,0:T(8,128)(2,1)}, bf16[6,384,768]{2,1,0:T(8,128)(2,1)}, u32[]{:S(2)}, u32[]{:S(2)}) collective-permute-start(bf16[6,384,768]{2,1,0:T(8,128)(2,1)} %bitcast.21), channel_id=1, source_target_pairs={{0,1},{1,0},{2,3},{3,2},{4,5},{5,4},{6,7},{7,6},{8,9},{9,8},{10,11... | collective-permute-start | bytes 10616840 | tf_op jit(solution)/shard_map/ppermute | solution.py:26
  0.5 61.9 %copy-start.6 = (f32[2,2,3,3,1,768]{5,4,3,2,1,0:T(1,128)S(1)}, f32[2,2,3,3,1,768]{5,4,3,2,1,0:T(1,128)}, u32[]{:S(2)}) copy-start(f32[2,2,3,3,1,768]{5,4,3,2,1,0:T(1,128)} %param.4) | copy-start | bytes 331780
  1.0 64.3 %copy-start.4 = (s32[2]{0:T(128)S(1)}, s32[2]{0:T(128)}, u32[]{:S(2)}) copy-start(s32[2]{0:T(128)} %pad_add_fusion.where_ref) | copy-start | bytes 28
  56.6 42.1 %collective-permute-start.2 = (bf16[6,384,384]{2,1,0:T(8,128)(2,1)}, bf16[6,384,384]{2,1,0:T(8,128)(2,1)}, u32[]{:S(2)}, u32[]{:S(2)}) collective-permute-start(bf16[6,384,384]{2,1,0:T(8,128)(2,1)} %shard_map.39), channel_id=1, source_target_pairs={{0,15},{1,2},{2,1},{3,4},{4,3},{5,6},{6,5},{7,8},{8,7},{9,10},{10,... | collective-permute-start | bytes 5308424 | tf_op jit(solution)/shard_map/ppermute | solution.py:203
  65.3 0.9 copy-start.3
  66.1 12.8 %copy-start.5 = (f32[2,1,3,3,768]{4,1,3,2,0:T(1,128)S(1)}, f32[2,1,3,3,768]{4,1,3,2,0:T(1,128)}, u32[]{:S(2)}) copy-start(f32[2,1,3,3,768]{4,1,3,2,0:T(1,128)} %get-tuple-element.23) | copy-start | bytes 165892
  66.2 19.5 %copy-start.7 = (f32[2]{0:T(128)S(1)}, f32[2]{0:T(128)}, u32[]{:S(2)}) copy-start(f32[2]{0:T(128)} %constant.12.clone) | copy-start | bytes 28
  78.9 1.9 %collective-permute-start.1 = (bf16[384,384]{1,0:T(8,128)(2,1)S(1)}, bf16[384,384]{1,0:T(8,128)(2,1)S(1)}, u32[]{:S(2)}, u32[]{:S(2)}) collective-permute-start(bf16[384,384]{1,0:T(8,128)(2,1)S(1)} %get-tuple-element.12), channel_id=1, source_target_pairs={{0,1},{1,0},{2,3},{3,2},{4,5},{5,4},{6,7},{7,6},{8,9},{9,8},{10,11... | collective-permute-start | bytes 884744 | tf_op jit(solution)/shard_map/ppermute | solution.py:26
  79.6 6.8 %collective-permute-start = (f32[2,3,3,384]{3,0,2,1:T(2,128)}, f32[2,3,3,384]{3,0,2,1:T(2,128)}, u32[]{:S(2)}, u32[]{:S(2)}) collective-permute-start(f32[2,3,3,384]{3,0,2,1:T(2,128)} %slice.46), channel_id=1, source_target_pairs={{15,0},{0,1},{1,2},{2,3},{3,4},{4,5},{5,6},{6,7},{7,8},{8,9},{9,10... | collective-permute-start | bytes 82952 | tf_op jit(solution)/shard_map/ppermute | solution.py:22
  81.5 21.1 %all-to-all-start = ((bf16[8,48,384]{2,1,0:T(8,128)(2,1)}), bf16[8,48,384]{2,1,0:T(8,128)(2,1)}, u32[]{:S(2)}, u32[]{:S(2)}) async-start(bf16[8,48,384]{2,1,0:T(8,128)(2,1)} %bitcast.25), calls=%async_computation | async-start | bytes 589824 | tf_op jit(solution)/shard_map/all_to_all | solution.py:245
  89.4 1.0 copy-start.1
  90.4 0.9 copy-start.2
  102.7 15.8 %collective-permute-start.4 = (bf16[384,384]{1,0:T(8,128)(2,1)S(1)}, bf16[384,384]{1,0:T(8,128)(2,1)S(1)}, u32[]{:S(2)}, u32[]{:S(2)}) collective-permute-start(bf16[384,384]{1,0:T(8,128)(2,1)S(1)} %get-tuple-element.16), channel_id=1, source_target_pairs={{0,1},{1,0},{2,3},{3,2},{4,5},{5,4},{6,7},{7,6},{8,9},{9,8},{10,11... | collective-permute-start | bytes 884744 | tf_op jit(solution)/shard_map/ppermute | solution.py:26
  118.6 7.1 %collective-permute-start.5 = (bf16[192,384]{1,0:T(8,128)(2,1)S(1)}, bf16[192,384]{1,0:T(8,128)(2,1)S(1)}, u32[]{:S(2)}, u32[]{:S(2)}) collective-permute-start(bf16[192,384]{1,0:T(8,128)(2,1)S(1)} %slice.65), channel_id=1, source_target_pairs={{0,2},{1,3},{2,0},{3,1},{4,6},{5,7},{6,4},{7,5},{8,10},{9,11},{10,... | collective-permute-start | bytes 442376 | tf_op jit(solution)/shard_map/ppermute | solution.py:260
  125.7 6.6 %collective-permute-start.6 = (bf16[48,384]{1,0:T(8,128)(2,1)S(1)}, bf16[48,384]{1,0:T(8,128)(2,1)S(1)}, u32[]{:S(2)}, u32[]{:S(2)}) collective-permute-start(bf16[48,384]{1,0:T(8,128)(2,1)S(1)} %get-tuple-element.19), channel_id=1, source_target_pairs={{12,0},{13,1},{14,2},{15,3},{0,4},{1,5},{2,6},{3,7},{4,8},{5,9},{6... | collective-permute-start | bytes 110600 | tf_op jit(solution)/shard_map/ppermute | solution.py:22
  127.3 5.4 %collective-permute-start.7 = (bf16[48,384]{1,0:T(8,128)(2,1)S(1)}, bf16[48,384]{1,0:T(8,128)(2,1)S(1)}, u32[]{:S(2)}, u32[]{:S(2)}) collective-permute-start(bf16[48,384]{1,0:T(8,128)(2,1)S(1)} %get-tuple-element.21), channel_id=1, source_target_pairs={{8,0},{9,1},{10,2},{11,3},{12,4},{13,5},{14,6},{15,7},{0,8},{1,9},... | collective-permute-start | bytes 110600 | tf_op jit(solution)/shard_map/ppermute | solution.py:22
  129.9 4.0 %collective-permute-start.8 = (bf16[48,384]{1,0:T(8,128)(2,1)S(1)}, bf16[48,384]{1,0:T(8,128)(2,1)S(1)}, u32[]{:S(2)}, u32[]{:S(2)}) collective-permute-start(bf16[48,384]{1,0:T(8,128)(2,1)S(1)} %get-tuple-element.20), channel_id=1, source_target_pairs={{4,0},{5,1},{6,2},{7,3},{8,4},{9,5},{10,6},{11,7},{12,8},{13,9},{1... | collective-permute-start | bytes 110600 | tf_op jit(solution)/shard_map/ppermute | solution.py:22

commit v12 on v11

--- a/solution.py
+++ b/solution.py
@@ -110,17 +110,24 @@
     finish(sum_re, sum_im, slabs, where_ref[0], range(slabs // 2), acc, send, keep)
 
 
-def cut_kernel(where_ref, field_hbm, half_hbm, sems):
-    half = half_hbm.shape[2]
-    lanes = pl.ds(pl.multiple_of(where_ref[0] * half, LANES), half)
-    copies = [
-        pltpu.make_async_copy(field_hbm.at[k, :, lanes], half_hbm.at[k], sems.at[k])
-        for k in range(field_hbm.shape[0])
-    ]
-    for copy in copies:
-        copy.start()
-    for copy in copies:
-        copy.wait()
+def cut_kernel(where_ref, field_ref, half_ref):
+    half_ref[...] = field_ref[...]
+
+
+def cut(where, field):
+    parts, count, sites = field.shape
+    block = (1, count, sites // 2)
+    return pl.pallas_call(
+        cut_kernel,
+        out_shape=jax.ShapeDtypeStruct((parts, count, sites // 2), field.dtype),
+        grid_spec=pltpu.PrefetchScalarGridSpec(
+            num_scalar_prefetch=1,
+            grid=(parts,),
+            in_specs=[pl.BlockSpec(block, lambda k, where_ref: (k, 0, where_ref[0]))],
+            out_specs=pl.BlockSpec(block, lambda k, where_ref: (k, 0, 0)),
+        ),
+        compiler_params=pltpu.CompilerParams(vmem_limit_bytes=60 * 2**20),
+    )(where, field)
 
 
 def b_kernel(field_ref, coef_ref, after_ref, b_ref):
@@ -174,12 +181,12 @@
         finish(before[0] + sum_re, before[1] + sum_im, slabs, core, order, acc, send, keep)
 
 
-def call(body, outs, specs, scratch, mib, flops, moved, where=VMEM):
+def call(body, outs, specs, scratch, mib, flops, moved):
     return pl.pallas_call(
         body,
         out_shape=outs,
         in_specs=specs,
-        out_specs=[where] * len(outs),
+        out_specs=[VMEM] * len(outs),
         scratch_shapes=scratch,
         compiler_params=pltpu.CompilerParams(vmem_limit_bytes=mib * 2**20),
         cost_estimate=pl.CostEstimate(flops=flops, bytes_accessed=moved, transcendentals=0),
@@ -196,14 +203,12 @@
     where = jnp.stack([index & 1, index >> 1])
     field = jnp.transpose(vectors, (0, 2, 3, 1, 4)).reshape(6, count, sites)
     half = sites // 2
-    (cut,) = call(
-        cut_kernel, [jax.ShapeDtypeStruct((6, count, half), vectors.dtype)], [SMEM, ANY],
-        [pltpu.SemaphoreType.DMA((6,))], 60, 0, 12 * count * half, ANY,
-    )(where, field)
-    far = lax.ppermute(cut, "gz", [(i, (i + i % 2 * 2 - 1) % slabs) for i in range(slabs)])
-    near = swapped(field, "gz")
+    piece = cut(where, field)
+    far = lax.ppermute(piece, "gz", [(i, (i + i % 2 * 2 - 1) % slabs) for i in range(slabs)])
     links = links.reshape(2, 2, 3, 3, sites)
     links_x, links_z = links[:, 0].reshape(18, sites), links[:, 1]
+    whole, links_x = lax.optimization_barrier((field, links_x))
+    near = swapped(whole, "gz")
     conjugate = jnp.array([1.0, -1.0], jnp.float32).reshape(2, 1, 1, 1)
     adjoint = jnp.transpose(links_z[..., :half], (0, 2, 1, 3)) * conjugate
     coefs = jnp.concatenate([adjoint, passed_along(links_z[..., half:], "gz", 1)], axis=-1)

time: 135 us -> 89.2 us (0.66)
  Pallas kernels: 79.6 us -> 29.5 us
  waiting for transfers between devices: 6.96 us -> 10.5 us
    pallas_call x1, Pallas kernels: 55.6 us -> 5.45 us  [cut(): pl.pallas_call(cut_kernel, out_shape=jax.ShapeDtypeStruct((parts, count,...]
    all_to_all x1, waiting for transfers between devices: 0.01 us -> 2.94 us  [exchanged(): return lax.all_to_all(chip, 'gz', 0, 0, axis_index_groups=groups)]
    unnamed x17 -> x15, local copies, waits for them, and re-layouts: 2.81 us -> 2.97 us
  transfers between devices with their start and end apart: 10 -> 10, of which waited for: 4 -> 6; matrix products, arithmetic and copies ran while one was open for 8% -> 8% of each run, Pallas kernels for 59% -> 33%
where the time goes in v12:
time: 89.2 us; the launch traced here: 88.5 us
  starting transfers between devices  34.1 us (38%)
  Pallas kernels  29.5 us (33%)
  waiting for transfers between devices  10.5 us (12%)
  local copies, waits for them, and re-layouts  10.1 us (11%)
  other arithmetic  4.14 us (5%)
    ppermute x3, starting transfers between devices, swapped(): lax.ppermute(block, axis, [(i, i ^ 1) for i in range(lax.axis_size(axis))])  15.4 us
    pallas_call x1, Pallas kernels, shards(): call(functools.partial(x_kernel, slabs), halves, [SMEM, VMEM, VMEM], [sta...  12.7 us
    ppermute x4, starting transfers between devices, passed_along(): return lax.ppermute(block, axis, route)  6.04 us
    ppermute x1, starting transfers between devices, shards(): lax.ppermute(piece, 'gz', [(i, (i + i % 2 * 2 - 1) % slabs) for i in rang...  5.67 us
    pallas_call x1, Pallas kernels, cut(): pl.pallas_call(cut_kernel, out_shape=jax.ShapeDtypeStruct((parts, count,...  5.45 us
    ppermute x1, waiting for transfers between devices, shards(): near = lax.ppermute(other, 'gz', [(i, i ^ 2) for i in range(slabs)])  4.15 us
    all_to_all x1, starting transfers between devices, exchanged(): return lax.all_to_all(chip, 'gz', 0, 0, axis_index_groups=groups)  4.06 us
    pallas_call x1, Pallas kernels, shards(): call(functools.partial(z_kernel, False, slabs), halves, [SMEM, VMEM, ANY,...  4 us
  transfers between devices with their start and end apart: 10, of which 6 were waited for; matrix products, arithmetic and copies ran while one was open for 8% of the time, Pallas kernels for 33%

profile of v12, /device:TPU:0, one launch (start us, length us, event | category | flops | bytes accessed | tf_op | source)
XLA Modules:
  0.0 88.5 jit_solution(10590934845690702282)
XLA Ops:
  0.0 0.0 copy-start
  0.0 1.1 %copy.19 = f32[2,2,3,3,1,768]{5,1,3,2,0,4:T(2,128)S(1)} copy(f32[2,2,3,3,1,768]{5,4,3,2,1,0:T(1,128)} %param.4) | data formatting | bytes 221184 | tf_op args[1]
  1.1 1.4 %slice_reduce_fusion = (f32[2,3,3,768]{3,2,1,0:T(4,128)}, f32[2,1,3,3,768]{4,1,3,2,0:T(1,128)}) fusion(f32[2,2,3,3,768]{4,1,3,2,0:T(2,128)S(1)} %bitcast.26), kind=kLoop, calls=%fused_computation.11 | loop fusion | bytes 221184 | tf_op jit(solution)/shard_map/slice | solution.py:209
  2.5 1.5 %reshape_squeeze.3.links_ref = f32[18,768]{1,0:T(8,128)} reshape(f32[2,3,3,768]{3,2,1,0:T(4,128)} %get-tuple-element.26) | data formatting | bytes 110592 | tf_op jit(solution)/shard_map/reshape;squeeze | solution.py:209
  4.0 0.5 collective-permute-start.3
  4.5 0.0 copy-start.3
  4.5 0.6 pad_add_fusion.where_ref
  5.1 0.0 copy-start.4
  5.1 5.5 %shard_map.39 = bf16[6,384,384]{2,1,0:T(8,128)(2,1)} custom-call(s32[2]{0:T(128)} %pad_add_fusion.where_ref, bf16[6,384,768]{2,1,0:T(8,128)(2,1)} %bitcast.22), custom_call_target="tpu_custom_call" | custom-call | tf_op jit(solution)/shard_map/pallas_call | solution.py:120
  10.5 0.0 copy-start.5
  10.5 0.0 copy-start.6
  10.5 5.7 %collective-permute-start.2 = (bf16[6,384,384]{2,1,0:T(8,128)(2,1)}, bf16[6,384,384]{2,1,0:T(8,128)(2,1)}, u32[]{:S(2)}, u32[]{:S(2)}) collective-permute-start(bf16[6,384,384]{2,1,0:T(8,128)(2,1)} %shard_map.39), channel_id=1, source_target_pairs={{0,15},{1,2},{2,1},{3,4},{4,3},{5,6},{6,5},{7,8},{8,7},{9,10},{10,... | collective-permute-start | bytes 5308424 | tf_op jit(solution)/shard_map/ppermute | solution.py:207
  16.2 0.0 copy-done
  16.2 0.0 copy-done.3
  16.2 0.0 copy-done.4
  16.2 12.7 %shard_map.37 = (bf16[384,384]{1,0:T(8,128)(2,1)S(1)}, f32[384,384]{1,0:T(8,128)S(1)}) custom-call(s32[2]{0:T(128)S(1)} %copy-done.4, bf16[6,384,768]{2,1,0:T(8,128)(2,1)S(1)} %bitcast.23, f32[18,768]{1,0:T(8,128)S(1)} %copy-done.3), custom_call_target="tpu_custom_call" | custom-call | flops 2717908992 | bytes 3538944 | tf_op jit(solution)/shard_map/pallas_call | solution.py:225
  28.9 0.1 collective-permute-start.1
  29.0 0.0 copy-done.5
  29.1 0.6 slice.46
  29.7 0.5 collective-permute-start
  30.2 0.7 copy.20
  30.8 0.0 collective-permute-done.1
  30.8 0.8 add_convert_fusion.after_ref
  31.6 4.1 %all-to-all-start = ((bf16[8,48,384]{2,1,0:T(8,128)(2,1)}), bf16[8,48,384]{2,1,0:T(8,128)(2,1)}, u32[]{:S(2)}, u32[]{:S(2)}) async-start(bf16[8,48,384]{2,1,0:T(8,128)(2,1)} %bitcast.25), calls=%async_computation | async-start | bytes 589824 | tf_op jit(solution)/shard_map/all_to_all | solution.py:250
  35.7 0.0 copy-done.6
  35.7 0.8 fusion.3
  36.5 0.6 collective-permute-done
  37.1 0.8 pad_maximum_fusion
  37.9 0.7 copy.12
  38.6 1.5 %reshape.26.coef_ref = f32[18,768]{1,0:T(8,128)} reshape(f32[2,3,3,768]{3,2,1,0:T(4,128)} %copy.12) | data formatting | bytes 110592 | tf_op jit(solution)/shard_map/reshape | solution.py:215
  40.1 0.0 copy-start.1
  40.1 1.0 %copy-done.1 = bf16[384,384]{1,0:T(8,128)(2,1)S(1)} copy-done((bf16[384,384]{1,0:T(8,128)(2,1)S(1)}, bf16[384,384]{1,0:T(8,128)(2,1)}, u32[]{:S(2)}) %copy-start.1) | copy-done | bytes 294936
  41.1 0.0 copy-start.2
  41.1 0.9 copy-done.2
  42.0 3.6 %shard_map.38.b_ref = bf16[2,768,1152]{2,1,0:T(8,128)(2,1)S(1)} custom-call(bf16[6,384,768]{2,1,0:T(8,128)(2,1)S(1)} %bitcast.24, f32[18,768]{1,0:T(8,128)S(1)} %copy-done.2, bf16[384,384]{1,0:T(8,128)(2,1)S(1)} %copy-done.1), custom_call_target="tpu_custom_call" | custom-call | flops 19464192 | bytes 7077888 | tf_op jit(solution)/shard_map/pallas_call | solution.py:230
  45.6 0.0 collective-permute-done.3.got_hbm
  45.6 3.7 %shard_map.40.refs_0_ = f32[2,384,384]{2,1,0:T(8,128)S(1)} custom-call(s32[2]{0:T(128)S(1)} %copy-done.4, bf16[2,768,1152]{2,1,0:T(8,128)(2,1)S(1)} %shard_map.38.b_ref, bf16[6,384,768]{2,1,0:T(8,128)(2,1)} %collective-permute-done.3.got_hbm), custom_call_target="tpu_custom_call" | custom-call | flops 1358954496 | bytes 1769472 | tf_op jit(solution)/shard_map/pallas_call | solution.py:236
  49.3 0.0 collective-permute-done.2.got_hbm
  49.4 4.0 %shard_map.41 = (bf16[384,384]{1,0:T(8,128)(2,1)S(1)}, f32[384,384]{1,0:T(8,128)S(1)}) custom-call(s32[2]{0:T(128)S(1)} %copy-done.4, bf16[2,768,1152]{2,1,0:T(8,128)(2,1)S(1)} %shard_map.38.b_ref, bf16[6,384,384]{2,1,0:T(8,128)(2,1)} %collective-permute-done.2.got_hbm, f32[2,384,384]{2,1,0:T(8,128)S(1)} %shard_map.40.refs_0_), custom_call_target="tpu_custom_call" | custom-call | flops 1358954496 | bytes 1769472 | tf_op jit(solution)/shard_map/pallas_call | solution.py:256
  53.4 2.9 %all-to-all-done = bf16[8,48,384]{2,1,0:T(8,128)(2,1)} async-done(((bf16[8,48,384]{2,1,0:T(8,128)(2,1)}), bf16[8,48,384]{2,1,0:T(8,128)(2,1)}, u32[]{:S(2)}, u32[]{:S(2)}) %all-to-all-start) | async-done | bytes 294944 | tf_op jit(solution)/shard_map/all_to_all | solution.py:250
  56.3 14.9 %collective-permute-start.4 = (bf16[384,384]{1,0:T(8,128)(2,1)S(1)}, bf16[384,384]{1,0:T(8,128)(2,1)S(1)}, u32[]{:S(2)}, u32[]{:S(2)}) collective-permute-start(bf16[384,384]{1,0:T(8,128)(2,1)S(1)} %get-tuple-element.20), channel_id=1, source_target_pairs={{0,1},{1,0},{2,3},{3,2},{4,5},{5,4},{6,7},{7,6},{8,9},{9,8},{10,11... | collective-permute-start | bytes 884744 | tf_op jit(solution)/shard_map/ppermute | solution.py:26
  71.2 1.2 %collective-permute-done.4 = bf16[384,384]{1,0:T(8,128)(2,1)S(1)} collective-permute-done((bf16[384,384]{1,0:T(8,128)(2,1)S(1)}, bf16[384,384]{1,0:T(8,128)(2,1)S(1)}, u32[]{:S(2)}, u32[]{:S(2)}) %collective-permute-start.4) | collective-permute-done | bytes 294944 | tf_op jit(solution)/shard_map/ppermute | solution.py:26
  72.4 0.1 convert_add_fusion
  72.5 2.9 %collective-permute-start.5 = (bf16[192,384]{1,0:T(8,128)(2,1)S(1)}, bf16[192,384]{1,0:T(8,128)(2,1)S(1)}, u32[]{:S(2)}, u32[]{:S(2)}) collective-permute-start(bf16[192,384]{1,0:T(8,128)(2,1)S(1)} %slice.65), channel_id=1, source_target_pairs={{0,2},{1,3},{2,0},{3,1},{4,6},{5,7},{6,4},{7,5},{8,10},{9,11},{10,... | collective-permute-start | bytes 442376 | tf_op jit(solution)/shard_map/ppermute | solution.py:265
  75.4 4.1 %collective-permute-done.5 = bf16[192,384]{1,0:T(8,128)(2,1)S(1)} collective-permute-done((bf16[192,384]{1,0:T(8,128)(2,1)S(1)}, bf16[192,384]{1,0:T(8,128)(2,1)S(1)}, u32[]{:S(2)}, u32[]{:S(2)}) %collective-permute-start.5) | collective-permute-done | bytes 147488 | tf_op jit(solution)/shard_map/ppermute | solution.py:265
  79.6 1.6 %collective-permute-start.6 = (bf16[48,384]{1,0:T(8,128)(2,1)S(1)}, bf16[48,384]{1,0:T(8,128)(2,1)S(1)}, u32[]{:S(2)}, u32[]{:S(2)}) collective-permute-start(bf16[48,384]{1,0:T(8,128)(2,1)S(1)} %get-tuple-element.23), channel_id=1, source_target_pairs={{12,0},{13,1},{14,2},{15,3},{0,4},{1,5},{2,6},{3,7},{4,8},{5,9},{6... | collective-permute-start | bytes 110600 | tf_op jit(solution)/shard_map/ppermute | solution.py:22
  81.2 2.6 %collective-permute-start.7 = (bf16[48,384]{1,0:T(8,128)(2,1)S(1)}, bf16[48,384]{1,0:T(8,128)(2,1)S(1)}, u32[]{:S(2)}, u32[]{:S(2)}) collective-permute-start(bf16[48,384]{1,0:T(8,128)(2,1)S(1)} %get-tuple-element.25), channel_id=1, source_target_pairs={{8,0},{9,1},{10,2},{11,3},{12,4},{13,5},{14,6},{15,7},{0,8},{1,9},... | collective-permute-start | bytes 110600 | tf_op jit(solution)/shard_map/ppermute | solution.py:22
  83.8 1.3 %collective-permute-start.8 = (bf16[48,384]{1,0:T(8,128)(2,1)S(1)}, bf16[48,384]{1,0:T(8,128)(2,1)S(1)}, u32[]{:S(2)}, u32[]{:S(2)}) collective-permute-start(bf16[48,384]{1,0:T(8,128)(2,1)S(1)} %get-tuple-element.24), channel_id=1, source_target_pairs={{4,0},{5,1},{6,2},{7,3},{8,4},{9,5},{10,6},{11,7},{12,8},{13,9},{1... | collective-permute-start | bytes 110600 | tf_op jit(solution)/shard_map/ppermute | solution.py:22
  85.2 1.0 %convert_reduce_fusion = f32[48,384]{1,0:T(8,128)S(1)} fusion(bf16[8,48,384]{2,1,0:T(8,128)(2,1)} %all-to-all-done), kind=kLoop, calls=%fused_computation.1 | loop fusion | flops 276480 | bytes 368640 | tf_op jit(solution)/shard_map/reduce_sum | solution.py:253
  86.2 0.0 collective-permute-done.6
  86.2 0.4 collective-permute-done.7
  86.6 1.2 %collective-permute-done.8 = bf16[48,384]{1,0:T(8,128)(2,1)S(1)} collective-permute-done((bf16[48,384]{1,0:T(8,128)(2,1)S(1)}, bf16[48,384]{1,0:T(8,128)(2,1)S(1)}, u32[]{:S(2)}, u32[]{:S(2)}) %collective-permute-start.8) | collective-permute-done | bytes 36896 | tf_op jit(solution)/shard_map/ppermute | solution.py:22
  87.8 0.7 copy.13
  (6 shorter events, 0.1 us)
Async XLA Ops:
  0.0 16.2 %copy-start = (bf16[2,384,3,1,768]{4,1,3,2,0:T(8,128)(2,1)S(1)}, bf16[2,384,3,1,768]{4,1,3,2,0:T(8,128)(2,1)}, u32[]{:S(2)}) copy-start(bf16[2,384,3,1,768]{4,1,3,2,0:T(8,128)(2,1)} %param.3) | copy-start | bytes 10616836
  4.0 41.6 %collective-permute-start.3 = (bf16[6,384,768]{2,1,0:T(8,128)(2,1)}, bf16[6,384,768]{2,1,0:T(8,128)(2,1)}, u32[]{:S(2)}, u32[]{:S(2)}) collective-permute-start(bf16[6,384,768]{2,1,0:T(8,128)(2,1)} %bitcast.21), channel_id=1, source_target_pairs={{0,1},{1,0},{2,3},{3,2},{4,5},{5,4},{6,7},{7,6},{8,9},{9,8},{10,11... | collective-permute-start | bytes 10616840 | tf_op jit(solution)/shard_map/ppermute | solution.py:26
  4.5 11.8 %copy-start.3 = (f32[18,768]{1,0:T(8,128)S(1)}, f32[18,768]{1,0:T(8,128)}, u32[]{:S(2)}) copy-start(f32[18,768]{1,0:T(8,128)} %reshape_squeeze.3.links_ref) | copy-start | bytes 165892
  5.1 11.1 %copy-start.4 = (s32[2]{0:T(128)S(1)}, s32[2]{0:T(128)}, u32[]{:S(2)}) copy-start(s32[2]{0:T(128)} %pad_add_fusion.where_ref) | copy-start | bytes 28
  10.5 18.5 %copy-start.5 = (f32[2,1,3,3,768]{4,1,3,2,0:T(1,128)S(1)}, f32[2,1,3,3,768]{4,1,3,2,0:T(1,128)}, u32[]{:S(2)}) copy-start(f32[2,1,3,3,768]{4,1,3,2,0:T(1,128)} %get-tuple-element.27) | copy-start | bytes 165892
  10.5 25.1 %copy-start.6 = (f32[2]{0:T(128)S(1)}, f32[2]{0:T(128)}, u32[]{:S(2)}) copy-start(f32[2]{0:T(128)} %constant.12.clone) | copy-start | bytes 28
  10.5 38.8 %collective-permute-start.2 = (bf16[6,384,384]{2,1,0:T(8,128)(2,1)}, bf16[6,384,384]{2,1,0:T(8,128)(2,1)}, u32[]{:S(2)}, u32[]{:S(2)}) collective-permute-start(bf16[6,384,384]{2,1,0:T(8,128)(2,1)} %shard_map.39), channel_id=1, source_target_pairs={{0,15},{1,2},{2,1},{3,4},{4,3},{5,6},{6,5},{7,8},{8,7},{9,10},{10,... | collective-permute-start | bytes 5308424 | tf_op jit(solution)/shard_map/ppermute | solution.py:207
  28.9 1.9 %collective-permute-start.1 = (bf16[384,384]{1,0:T(8,128)(2,1)S(1)}, bf16[384,384]{1,0:T(8,128)(2,1)S(1)}, u32[]{:S(2)}, u32[]{:S(2)}) collective-permute-start(bf16[384,384]{1,0:T(8,128)(2,1)S(1)} %get-tuple-element.15), channel_id=1, source_target_pairs={{0,1},{1,0},{2,3},{3,2},{4,5},{5,4},{6,7},{7,6},{8,9},{9,8},{10,11... | collective-permute-start | bytes 884744 | tf_op jit(solution)/shard_map/ppermute | solution.py:26
  29.7 7.5 %collective-permute-start = (f32[2,3,3,384]{3,0,2,1:T(2,128)}, f32[2,3,3,384]{3,0,2,1:T(2,128)}, u32[]{:S(2)}, u32[]{:S(2)}) collective-permute-start(f32[2,3,3,384]{3,0,2,1:T(2,128)} %slice.46), channel_id=1, source_target_pairs={{15,0},{0,1},{1,2},{2,3},{3,4},{4,5},{5,6},{6,7},{7,8},{8,9},{9,10... | collective-permute-start | bytes 82952 | tf_op jit(solution)/shard_map/ppermute | solution.py:22
  31.6 24.7 %all-to-all-start = ((bf16[8,48,384]{2,1,0:T(8,128)(2,1)}), bf16[8,48,384]{2,1,0:T(8,128)(2,1)}, u32[]{:S(2)}, u32[]{:S(2)}) async-start(bf16[8,48,384]{2,1,0:T(8,128)(2,1)} %bitcast.25), calls=%async_computation | async-start | bytes 589824 | tf_op jit(solution)/shard_map/all_to_all | solution.py:250
  40.1 1.0 %copy-start.1 = (bf16[384,384]{1,0:T(8,128)(2,1)S(1)}, bf16[384,384]{1,0:T(8,128)(2,1)}, u32[]{:S(2)}) copy-start(bf16[384,384]{1,0:T(8,128)(2,1)} %add_convert_fusion.after_ref) | copy-start | bytes 884740
  41.1 0.9 copy-start.2
  56.3 16.1 %collective-permute-start.4 = (bf16[384,384]{1,0:T(8,128)(2,1)S(1)}, bf16[384,384]{1,0:T(8,128)(2,1)S(1)}, u32[]{:S(2)}, u32[]{:S(2)}) collective-permute-start(bf16[384,384]{1,0:T(8,128)(2,1)S(1)} %get-tuple-element.20), channel_id=1, source_target_pairs={{0,1},{1,0},{2,3},{3,2},{4,5},{5,4},{6,7},{7,6},{8,9},{9,8},{10,11... | collective-permute-start | bytes 884744 | tf_op jit(solution)/shard_map/ppermute | solution.py:26
  72.5 7.1 %collective-permute-start.5 = (bf16[192,384]{1,0:T(8,128)(2,1)S(1)}, bf16[192,384]{1,0:T(8,128)(2,1)S(1)}, u32[]{:S(2)}, u32[]{:S(2)}) collective-permute-start(bf16[192,384]{1,0:T(8,128)(2,1)S(1)} %slice.65), channel_id=1, source_target_pairs={{0,2},{1,3},{2,0},{3,1},{4,6},{5,7},{6,4},{7,5},{8,10},{9,11},{10,... | collective-permute-start | bytes 442376 | tf_op jit(solution)/shard_map/ppermute | solution.py:265
  79.6 6.6 %collective-permute-start.6 = (bf16[48,384]{1,0:T(8,128)(2,1)S(1)}, bf16[48,384]{1,0:T(8,128)(2,1)S(1)}, u32[]{:S(2)}, u32[]{:S(2)}) collective-permute-start(bf16[48,384]{1,0:T(8,128)(2,1)S(1)} %get-tuple-element.23), channel_id=1, source_target_pairs={{12,0},{13,1},{14,2},{15,3},{0,4},{1,5},{2,6},{3,7},{4,8},{5,9},{6... | collective-permute-start | bytes 110600 | tf_op jit(solution)/shard_map/ppermute | solution.py:22
  81.2 5.4 %collective-permute-start.7 = (bf16[48,384]{1,0:T(8,128)(2,1)S(1)}, bf16[48,384]{1,0:T(8,128)(2,1)S(1)}, u32[]{:S(2)}, u32[]{:S(2)}) collective-permute-start(bf16[48,384]{1,0:T(8,128)(2,1)S(1)} %get-tuple-element.25), channel_id=1, source_target_pairs={{8,0},{9,1},{10,2},{11,3},{12,4},{13,5},{14,6},{15,7},{0,8},{1,9},... | collective-permute-start | bytes 110600 | tf_op jit(solution)/shard_map/ppermute | solution.py:22
  83.8 4.0 %collective-permute-start.8 = (bf16[48,384]{1,0:T(8,128)(2,1)S(1)}, bf16[48,384]{1,0:T(8,128)(2,1)S(1)}, u32[]{:S(2)}, u32[]{:S(2)}) collective-permute-start(bf16[48,384]{1,0:T(8,128)(2,1)S(1)} %get-tuple-element.24), channel_id=1, source_target_pairs={{4,0},{5,1},{6,2},{7,3},{8,4},{9,5},{10,6},{11,7},{12,8},{13,9},{1... | collective-permute-start | bytes 110600 | tf_op jit(solution)/shard_map/ppermute | solution.py:22

commit v13 on v10

--- a/solution.py
+++ b/solution.py
@@ -84,24 +84,18 @@
     return [to + 1 - low for to in ahead] + [to + low for to in ahead]
 
 
-def finish(sum_re, sum_im, slabs, core, order, acc, send, keep):
-    count = send.shape[0]
+def finish(sum_re, sum_im, slabs, chip, acc, store):
+    count = acc.shape[1]
     own = count // slabs
     acc[0] = sum_re - sum_re.T
     acc[1] = sum_im + sum_im.T
     if not rows_by_own(slabs, own):
-        send[...] = acc[1 - core].astype(jnp.bfloat16)
-        keep[...] = acc[core]
+        for k in range(2):
+            store(k, acc[k])
         return
-    for k in range(slabs // 2):
-        block = slice(k * 2 * own, (k + 1) * 2 * own)
-
-        def rows(which):
-            at = pl.ds(pl.multiple_of((2 * order[k] + which) * own, 8), own)
-            return jnp.concatenate([acc[0, at, :], acc[1, at, :]], axis=0)
-
-        send[block, :] = rows(1 - core).astype(jnp.bfloat16)
-        keep[block, :] = rows(core)
+    for k, to in enumerate(block_order(chip, slabs // 2)):
+        rows = [pl.ds(pl.multiple_of((2 * to + core) * own, 8), own) for core in range(2)]
+        store(k, jnp.concatenate([acc[part, at, :] for at in rows for part in range(2)], axis=0))
 
 
 def x_kernel(slabs, where_ref, field_ref, links_ref, send, keep, right, acc):
@@ -118,7 +112,13 @@
             product[part] = term if b == 0 else product[part] + term
     sum_re = product[0][:, :count] + product[1][:, count:]
     sum_im = product[0][:, count:] - product[1][:, :count]
-    finish(sum_re, sum_im, slabs, where_ref[0], block_order(where_ref[1], slabs // 2), acc, send, keep)
+
+    def store(k, rows):
+        size = rows.shape[0]
+        send[k * size : (k + 1) * size, :] = rows.astype(jnp.bfloat16)
+        keep[k * size : (k + 1) * size, :] = rows
+
+    finish(sum_re, sum_im, slabs, where_ref[1], acc, store)
 
 
 def w_kernel(field_ref, links_ref, w_ref):
@@ -128,7 +128,11 @@
     times_links(field_ref, links_ref, 1, True, False, store)
 
 
-def z_kernel(slabs, where_ref, w_ref, face_hbm, send, keep, right, acc, sems):
+def z_kernel(far, slabs, where_ref, w_ref, face_hbm, *refs):
+    if far:
+        before, other, mine, right, acc, sems = refs
+    else:
+        out, right, acc, sems = refs
     count = w_ref.shape[1]
     copies = []
     for b in range(3):
@@ -149,7 +153,20 @@
             product[part] = term if b == 0 else product[part] + term
     sum_re = product[0][:, :count] + product[1][:, count:]
     sum_im = product[0][:, count:] - product[1][:, :count]
-    finish(sum_re, sum_im, slabs, where_ref[0], block_order(where_ref[1], slabs // 2), acc, send, keep)
+
+    def store(k, rows):
+        size = rows.shape[0]
+        at = slice(k * size, (k + 1) * size)
+        if not far:
+            out[at, :] = rows.astype(jnp.bfloat16)
+            return
+        rows = rows + before[at, :].astype(jnp.float32)
+        if at.start < count:
+            other[at, :] = rows.astype(jnp.bfloat16)
+        else:
+            mine[at.start - count : at.stop - count, :] = rows
+
+    finish(sum_re, sum_im, slabs, where_ref[1], acc, store)
 
 
 def call(body, outs, specs, scratch, mib, flops, moved):
@@ -174,7 +191,8 @@
     where = jnp.stack([index & 1, index >> 1])
     field = jnp.transpose(vectors, (0, 2, 3, 1, 4)).reshape(6, count, sites)
     links = links.reshape(36, sites)
-    face = passed_along(field, "gz", -1)
+    far = lax.ppermute(field, "gz", [(i, (i - 1) % slabs) for i in range(0, slabs, 2)])
+    near = lax.ppermute(field, "gz", [(i, i - 1) for i in range(1, slabs, 2)])
 
     flops = 24 * count * count * sites
     moved = 12 * count * sites
@@ -182,48 +200,62 @@
         jax.ShapeDtypeStruct((count, count), jnp.bfloat16),
         jax.ShapeDtypeStruct((count, count), jnp.float32),
     ]
+    whole = [jax.ShapeDtypeStruct((2 * count, count), half.dtype) for half in halves]
     stacked = pltpu.VMEM((3, 2 * count, sites), jnp.bfloat16)
     square = pltpu.VMEM((2, count, count), jnp.float32)
     send_x, keep_x = call(
-        functools.partial(x_kernel, slabs), halves, [SMEM, VMEM, VMEM],
-        [stacked, square], 16, flops, moved,
+        functools.partial(x_kernel, slabs), whole, [SMEM, VMEM, VMEM],
+        [stacked, square], 18, flops, moved,
     )(where, field, links)
     (w,) = call(
         w_kernel, [jax.ShapeDtypeStruct(field.shape, jnp.bfloat16)], [VMEM, VMEM], [], 10,
         count * sites * 66, 2 * moved,
     )(field, links)
-    chip_x = keep_x + swapped(send_x, "gz").astype(jnp.float32)
-    other_x = chip_x[: count // 2].astype(jnp.bfloat16)
-    face, other_x = lax.optimization_barrier((face, other_x))
-
-    def from_neighbour(other):
-        return lax.ppermute(other, "gz", [(i, i ^ 2) for i in range(slabs)]).astype(jnp.float32)
-
-    def total(line):
-        result = line[: 2 * own]
+    scratch = [stacked, square, pltpu.SemaphoreType.DMA((6,))]
+    (early,) = call(
+        functools.partial(z_kernel, False, slabs), whole[:1], [SMEM, VMEM, ANY],
+        scratch, 16, flops, moved,
+    )(where, w, near)
+
+    def late(before):
+        return call(
+            functools.partial(z_kernel, True, slabs), halves, [SMEM, VMEM, ANY, VMEM],
+            scratch, 16, flops, moved,
+        )(where, w, far, before)
+
+    if not rows_by_own(slabs, own):
+
+        def exchanged(terms):
+            terms = terms.astype(jnp.bfloat16).reshape(2, slabs, own, count)
+            got = lax.all_to_all(jnp.transpose(terms, (1, 0, 2, 3)), "gz", 0, 0)
+            return jnp.sum(got.astype(jnp.float32), axis=0)
+
+        both = [exchanged(keep_x), exchanged(jnp.concatenate(late(early), axis=0))]
+        return jnp.transpose(jnp.concatenate(both, axis=0), (1, 0, 2)) * scale
+
+    def summed(other, mine, core):
+        members = range(core, slabs, 2)
+
+        def shifted(block, route):
+            return lax.ppermute(block, "gz", [(i, route(i) % slabs) for i in members]).astype(jnp.float32)
+
+        line = mine + shifted(other, lambda i: i ^ 2)
+        result = line[: 4 * own]
         for r in range(1, slabs // 4):
-            block = line[r * 2 * own : (r + 1) * 2 * own].astype(jnp.bfloat16)
-            result = result + passed_along(block, "gz", 4 * r).astype(jnp.float32)
-        return result.reshape(2, own, count)
-
-    def exchanged(chip):
-        chip = chip.astype(jnp.bfloat16).reshape(slabs, own, count)
-        got = lax.all_to_all(chip, "gz", 0, 0).reshape(slabs // 2, 2, own, count)
-        return jnp.sum(got.astype(jnp.float32), axis=0)
-
-    near_x = from_neighbour(other_x) if rows_by_own(slabs, own) else None
-    send_z, keep_z = call(
-        functools.partial(z_kernel, slabs), halves, [SMEM, VMEM, ANY],
-        [stacked, square, pltpu.SemaphoreType.DMA((6,))], 14, flops, moved,
-    )(where, w, face)
-    chip_z = keep_z + swapped(send_z, "gz").astype(jnp.float32)
-    if rows_by_own(slabs, own):
-        half = count // 2
-        near_z = from_neighbour(chip_z[:half].astype(jnp.bfloat16))
-        totals = [total(chip_x[half:] + near_x), total(chip_z[half:] + near_z)]
-    else:
-        totals = [exchanged(chip_x), exchanged(chip_z)]
-    both = jnp.concatenate(totals, axis=0)
+            block = line[r * 4 * own : (r + 1) * 4 * own].astype(jnp.bfloat16)
+            result = result + shifted(block, lambda i: i + 4 * r)
+        return result
+
+    got = lax.ppermute(send_x, "gz", [(i, i - 1) for i in range(1, slabs, 2)])
+    chip_x = keep_x + got.astype(jnp.float32)
+    sum_x = summed(chip_x[:count].astype(jnp.bfloat16), chip_x[count:], 0)
+    before = lax.ppermute(early, "gz", [(i, i + 1) for i in range(0, slabs, 2)])
+    sum_z = summed(*late(before), 1)
+    even = where[0] == 0
+    here, there = slice(0, 2 * own), slice(2 * own, 4 * own)
+    got = swapped(jnp.where(even, sum_x[there], sum_z[here]), "gz")
+    both = [jnp.where(even, sum_x[here], got), jnp.where(even, got, sum_z[there])]
+    both = jnp.concatenate(both, axis=0).reshape(4, own, count)
     return jnp.transpose(both, (1, 0, 2)) * scale
 
 

time: 70.2 us -> 80.6 us (1.15)
  waiting for transfers between devices: 26.2 us -> 5.53 us
  starting transfers between devices: 17.2 us -> 37.1 us
  Pallas kernels: 21.9 us -> 29 us
  local copies, waits for them, and re-layouts: 2.2 us -> 5.48 us
    ppermute x9 -> x12, waiting for transfers between devices: 24.7 us -> 4.62 us  [the longest x8 3.24 us: shifted(): lax.ppermute(block, 'gz', [(i, route(i) % slabs) for i in members])]
    ppermute x9 -> x12, starting transfers between devices: 17.1 us -> 32.8 us  [the longest x8 14.1 us: shifted(): lax.ppermute(block, 'gz', [(i, route(i) % slabs) for i in members])]
    pallas_call x2 -> x3, Pallas kernels: 18.3 us -> 25.3 us  [the longest x1 12.8 us: shards(): call(functools.partial(x_kernel, slabs), whole, [SMEM, VMEM, VMEM], [stac...]
    ppermute x2 -> x1, starting transfers between devices: 0.14 us -> 4.33 us  [swapped(): lax.ppermute(block, axis, [(i, i ^ 1) for i in range(lax.axis_size(axis))])]
    unnamed x4 -> x10, local copies, waits for them, and re-layouts: 2 us -> 3.92 us
    another operation x2, other arithmetic: 0.08 us -> 1.1 us
  transfers between devices with their start and end apart: 11 -> 13, of which waited for: 5 -> 3; matrix products, arithmetic and copies ran while one was open for 2% -> 4% of each run, Pallas kernels for 31% -> 36%
where the time goes in v13:
time: 80.6 us; the launch traced here: 80.1 us
  starting transfers between devices  37.1 us (46%)
  Pallas kernels  29 us (36%)
  waiting for transfers between devices  5.53 us (7%)
  local copies, waits for them, and re-layouts  5.48 us (7%)
  other arithmetic  2.64 us (3%)
    ppermute x8, starting transfers between devices, shifted(): lax.ppermute(block, 'gz', [(i, route(i) % slabs) for i in members])  14.1 us
    pallas_call x1, Pallas kernels, shards(): call(functools.partial(x_kernel, slabs), whole, [SMEM, VMEM, VMEM], [stac...  12.8 us
    ppermute x1, starting transfers between devices, shards(): lax.ppermute(field, 'gz', [(i, (i - 1) % slabs) for i in range(0, slabs,...  12.2 us
    pallas_call x1, Pallas kernels, shards(): call(functools.partial(z_kernel, False, slabs), whole[:1], [SMEM, VMEM, A...  6.41 us
    pallas_call x1, Pallas kernels, late(): call(functools.partial(z_kernel, True, slabs), halves, [SMEM, VMEM, ANY,...  6.16 us
    ppermute x1, starting transfers between devices, swapped(): lax.ppermute(block, axis, [(i, i ^ 1) for i in range(lax.axis_size(axis))])  4.33 us
    unnamed x10, local copies, waits for them, and re-layouts  3.92 us
    ppermute x1, starting transfers between devices, shards(): before = lax.ppermute(early, 'gz', [(i, i + 1) for i in range(0, slabs, 2)])  3.9 us
  transfers between devices with their start and end apart: 13, of which 3 were waited for; matrix products, arithmetic and copies ran while one was open for 4% of the time, Pallas kernels for 36%

profile of v13, /device:TPU:0, one launch (start us, length us, event | category | flops | bytes accessed | tf_op | source)
XLA Modules:
  0.0 80.1 jit_solution(18126270202376694489)
XLA Ops:
  0.0 1.3 %collective-permute-start.6 = (bf16[6,384,768]{2,1,0:T(8,128)(2,1)}, bf16[6,384,768]{2,1,0:T(8,128)(2,1)}, u32[]{:S(2)}, u32[]{:S(2)}) collective-permute-start(bf16[6,384,768]{2,1,0:T(8,128)(2,1)} %bitcast.9), channel_id=1, source_target_pairs={{1,0},{3,2},{5,4},{7,6},{9,8},{11,10},{13,12},{15,14},{17,16},{19,... | collective-permute-start | bytes 10616840 | tf_op jit(solution)/shard_map/ppermute | solution.py:195
  1.3 12.2 %collective-permute-start.5 = (bf16[6,384,768]{2,1,0:T(8,128)(2,1)}, bf16[6,384,768]{2,1,0:T(8,128)(2,1)}, u32[]{:S(2)}, u32[]{:S(2)}) collective-permute-start(bf16[6,384,768]{2,1,0:T(8,128)(2,1)} %bitcast.10), channel_id=1, source_target_pairs={{0,15},{2,1},{4,3},{6,5},{8,7},{10,9},{12,11},{14,13},{16,31},{18,... | collective-permute-start | bytes 10616840 | tf_op jit(solution)/shard_map/ppermute | solution.py:194
  13.5 1.2 %reduce = f32[2,2,3,3,768]{4,3,2,1,0:T(4,128)S(1)} reduce(f32[2,2,3,3,1,768]{5,4,3,2,1,0:T(1,128)} %param.3, f32[]{:T(128)} %constant.12), dimensions={4}, to_apply=%param.3.reduce_sub_computation | reduce | bytes 221188 | tf_op args[1]
  14.7 0.1 reshape.10.links_ref
  14.8 0.0 copy-start.1
  14.8 0.1 pad_add_fusion.where_ref
  14.8 0.0 copy-start
  14.8 2.0 %copy-done = bf16[2,384,3,1,768]{4,1,3,2,0:T(8,128)(2,1)S(1)} copy-done((bf16[2,384,3,1,768]{4,1,3,2,0:T(8,128)(2,1)S(1)}, bf16[2,384,3,1,768]{4,1,3,2,0:T(8,128)(2,1)}, u32[]{:S(2)}) %copy-start) | copy-done | bytes 3538968
  16.8 12.8 %shard_map.28 = (bf16[768,384]{1,0:T(8,128)(2,1)S(1)}, f32[768,384]{1,0:T(8,128)S(1)}) custom-call(s32[2]{0:T(128)S(1)} %pad_add_fusion.where_ref, bf16[6,384,768]{2,1,0:T(8,128)(2,1)S(1)} %bitcast.11, f32[36,768]{1,0:T(8,128)S(1)} %reshape.10.links_ref), custom_call_target="tpu_custom_call" | custom-call | flops 2717908992 | bytes 3538944 | tf_op jit(solution)/shard_map/pallas_call | solution.py:206
  29.6 0.0 copy-done.1
  29.6 1.3 %collective-permute-start = (bf16[768,384]{1,0:T(8,128)(2,1)S(1)}, bf16[768,384]{1,0:T(8,128)(2,1)S(1)}, u32[]{:S(2)}, u32[]{:S(2)}) collective-permute-start(bf16[768,384]{1,0:T(8,128)(2,1)S(1)} %get-tuple-element.10), channel_id=1, source_target_pairs={{1,0},{3,2},{5,4},{7,6},{9,8},{11,10},{13,12},{15,14},{17,16},{19,... | collective-permute-start | bytes 1769480 | tf_op jit(solution)/shard_map/ppermute | solution.py:249
  30.9 0.0 copy-start.2
  30.9 0.9 %copy-done.2 = f32[36,768]{1,0:T(8,128)S(1)} copy-done((f32[36,768]{1,0:T(8,128)S(1)}, f32[36,768]{1,0:T(8,128)}, u32[]{:S(2)}) %copy-start.2) | copy-done | bytes 110616
  31.8 3.6 %shard_map.29.w_ref = bf16[6,384,768]{2,1,0:T(8,128)(2,1)S(1)} custom-call(bf16[6,384,768]{2,1,0:T(8,128)(2,1)S(1)} %bitcast.12, f32[36,768]{1,0:T(8,128)S(1)} %copy-done.2), custom_call_target="tpu_custom_call" | custom-call | flops 19464192 | bytes 7077888 | tf_op jit(solution)/shard_map/pallas_call | solution.py:210
  35.5 0.0 collective-permute-done.6.face_hbm
  35.5 6.4 %shard_map.30 = bf16[768,384]{1,0:T(8,128)(2,1)} custom-call(s32[2]{0:T(128)S(1)} %pad_add_fusion.where_ref, bf16[6,384,768]{2,1,0:T(8,128)(2,1)S(1)} %shard_map.29.w_ref, bf16[6,384,768]{2,1,0:T(8,128)(2,1)} %collective-permute-done.6.face_hbm), custom_call_target="tpu_custom_call" | custom-call | flops 2717908992 | bytes 3538944 | tf_op jit(solution)/shard_map/pallas_call | solution.py:215
  41.9 3.9 %collective-permute-start.7 = (bf16[768,384]{1,0:T(8,128)(2,1)}, bf16[768,384]{1,0:T(8,128)(2,1)}, u32[]{:S(2)}, u32[]{:S(2)}) collective-permute-start(bf16[768,384]{1,0:T(8,128)(2,1)} %shard_map.30), channel_id=1, source_target_pairs={{0,1},{2,3},{4,5},{6,7},{8,9},{10,11},{12,13},{14,15},{16,17},{18,... | collective-permute-start | bytes 1769480 | tf_op jit(solution)/shard_map/ppermute | solution.py:252
  45.8 0.0 collective-permute-done
  45.8 0.1 convert_add_fusion
  45.9 0.0 copy-start.3
  45.9 1.0 %copy-done.3 = f32[768,384]{1,0:T(8,128)} copy-done((f32[768,384]{1,0:T(8,128)}, f32[768,384]{1,0:T(8,128)S(1)}, u32[]{:S(2)}) %copy-start.3) | copy-done | bytes 1179672
  47.0 0.8 slice.93
  47.7 1.9 %collective-permute-start.1 = (bf16[384,384]{1,0:T(8,128)(2,1)}, bf16[384,384]{1,0:T(8,128)(2,1)}, u32[]{:S(2)}, u32[]{:S(2)}) collective-permute-start(bf16[384,384]{1,0:T(8,128)(2,1)} %slice.93), channel_id=1, source_target_pairs={{0,2},{2,0},{4,6},{6,4},{8,10},{10,8},{12,14},{14,12},{16,18},{18,... | collective-permute-start | bytes 884744 | tf_op jit(solution)/shard_map/ppermute | solution.py:240
  49.6 0.0 copy-start.4
  49.6 1.4 %collective-permute-done.5.face_hbm = bf16[6,384,768]{2,1,0:T(8,128)(2,1)} collective-permute-done((bf16[6,384,768]{2,1,0:T(8,128)(2,1)}, bf16[6,384,768]{2,1,0:T(8,128)(2,1)}, u32[]{:S(2)}, u32[]{:S(2)}) %collective-permute-start.5) | collective-permute-done | bytes 3538976 | tf_op jit(solution)/shard_map/ppermute | solution.py:194
  51.0 0.0 collective-permute-done.7.refs_0_
  51.0 6.2 %shard_map.31 = (bf16[384,384]{1,0:T(8,128)(2,1)S(1)}, f32[384,384]{1,0:T(8,128)S(1)}) custom-call(s32[2]{0:T(128)S(1)} %pad_add_fusion.where_ref, bf16[6,384,768]{2,1,0:T(8,128)(2,1)S(1)} %shard_map.29.w_ref, bf16[6,384,768]{2,1,0:T(8,128)(2,1)} %collective-permute-done.5.face_hbm, bf16[768,384]{1,0:T(8,128)(2,1)} %collective-permute-done.7.refs_0_), custom_call_target="tpu_custom_call" | custom-call | flops 2717908992 | bytes 3538944 | tf_op jit(solution)/shard_map/pallas_call | solution.py:221
  57.2 0.7 collective-permute-start.8
  57.9 0.0 collective-permute-done.1
  57.9 0.0 copy-done.4
  57.9 1.0 %fusion.4 = (bf16[384,384]{1,0:T(8,128)(2,1)S(1)}, f32[384,384]{1,0:T(8,128)S(1)}) fusion(bf16[384,384]{1,0:T(8,128)(2,1)} %collective-permute-done.1, f32[768,384]{1,0:T(8,128)S(1)} %copy-done.4), kind=kLoop, calls=%fused_computation.16 | loop fusion | flops 442368 | bytes 1769472 | tf_op jit(solution)/shard_map/convert.5
  59.0 1.9 %collective-permute-start.2 = (bf16[96,384]{1,0:T(8,128)(2,1)S(1)}, bf16[96,384]{1,0:T(8,128)(2,1)S(1)}, u32[]{:S(2)}, u32[]{:S(2)}) collective-permute-start(bf16[96,384]{1,0:T(8,128)(2,1)S(1)} %get-tuple-element.17), channel_id=1, source_target_pairs={{0,4},{2,6},{4,8},{6,10},{8,12},{10,14},{12,0},{14,2},{16,20},{18,... | collective-permute-start | bytes 221192 | tf_op jit(solution)/shard_map/ppermute | solution.py:240
  60.9 5.7 %collective-permute-start.4 = (bf16[96,384]{1,0:T(8,128)(2,1)S(1)}, bf16[96,384]{1,0:T(8,128)(2,1)S(1)}, u32[]{:S(2)}, u32[]{:S(2)}) collective-permute-start(bf16[96,384]{1,0:T(8,128)(2,1)S(1)} %get-tuple-element.18), channel_id=1, source_target_pairs={{0,12},{2,14},{4,0},{6,2},{8,4},{10,6},{12,8},{14,10},{16,28},{18,... | collective-permute-start | bytes 221192 | tf_op jit(solution)/shard_map/ppermute | solution.py:240
  66.6 1.9 %collective-permute-start.3 = (bf16[96,384]{1,0:T(8,128)(2,1)S(1)}, bf16[96,384]{1,0:T(8,128)(2,1)S(1)}, u32[]{:S(2)}, u32[]{:S(2)}) collective-permute-start(bf16[96,384]{1,0:T(8,128)(2,1)S(1)} %get-tuple-element.19), channel_id=1, source_target_pairs={{0,8},{2,10},{4,12},{6,14},{8,0},{10,2},{12,4},{14,6},{16,24},{18,... | collective-permute-start | bytes 221192 | tf_op jit(solution)/shard_map/ppermute | solution.py:240
  68.6 0.0 collective-permute-done.8
  68.6 0.1 fusion.5
  68.7 0.7 collective-permute-start.9
  69.4 0.7 collective-permute-start.11
  70.0 0.0 collective-permute-done.2
  70.0 0.7 collective-permute-start.10
  70.7 0.0 collective-permute-done.4
  70.7 3.2 %collective-permute-done.3 = bf16[96,384]{1,0:T(8,128)(2,1)S(1)} collective-permute-done((bf16[96,384]{1,0:T(8,128)(2,1)S(1)}, bf16[96,384]{1,0:T(8,128)(2,1)S(1)}, u32[]{:S(2)}, u32[]{:S(2)}) %collective-permute-start.3) | collective-permute-done | bytes 73760 | tf_op jit(solution)/shard_map/ppermute | solution.py:240
  74.0 0.0 collective-permute-done.9
  74.0 0.0 collective-permute-done.11
  74.0 0.0 collective-permute-done.10
  74.1 4.3 %collective-permute-start.12 = (f32[48,384]{1,0:T(8,128)S(1)}, f32[48,384]{1,0:T(8,128)S(1)}, u32[]{:S(2)}, u32[]{:S(2)}) collective-permute-start(f32[48,384]{1,0:T(8,128)S(1)} %slice_select_fusion.1), channel_id=1, source_target_pairs={{0,1},{1,0},{2,3},{3,2},{4,5},{5,4},{6,7},{7,6},{8,9},{9,8},{10,11... | collective-permute-start | bytes 221192 | tf_op jit(solution)/shard_map/ppermute | solution.py:26
  78.4 0.9 %collective-permute-done.12 = f32[48,384]{1,0:T(8,128)S(1)} collective-permute-done((f32[48,384]{1,0:T(8,128)S(1)}, f32[48,384]{1,0:T(8,128)S(1)}, u32[]{:S(2)}, u32[]{:S(2)}) %collective-permute-start.12) | collective-permute-done | bytes 73760 | tf_op jit(solution)/shard_map/ppermute | solution.py:26
  79.4 0.7 copy.6
  (7 shorter events, 0.2 us)
Async XLA Ops:
  0.0 35.5 %collective-permute-start.6 = (bf16[6,384,768]{2,1,0:T(8,128)(2,1)}, bf16[6,384,768]{2,1,0:T(8,128)(2,1)}, u32[]{:S(2)}, u32[]{:S(2)}) collective-permute-start(bf16[6,384,768]{2,1,0:T(8,128)(2,1)} %bitcast.9), channel_id=1, source_target_pairs={{1,0},{3,2},{5,4},{7,6},{9,8},{11,10},{13,12},{15,14},{17,16},{19,... | collective-permute-start | bytes 10616840 | tf_op jit(solution)/shard_map/ppermute | solution.py:195
  1.3 49.7 %collective-permute-start.5 = (bf16[6,384,768]{2,1,0:T(8,128)(2,1)}, bf16[6,384,768]{2,1,0:T(8,128)(2,1)}, u32[]{:S(2)}, u32[]{:S(2)}) collective-permute-start(bf16[6,384,768]{2,1,0:T(8,128)(2,1)} %bitcast.10), channel_id=1, source_target_pairs={{0,15},{2,1},{4,3},{6,5},{8,7},{10,9},{12,11},{14,13},{16,31},{18,... | collective-permute-start | bytes 10616840 | tf_op jit(solution)/shard_map/ppermute | solution.py:194
  14.8 14.9 %copy-start.1 = (f32[36,768]{1,0:T(8,128)}, f32[36,768]{1,0:T(8,128)S(1)}, u32[]{:S(2)}) copy-start(f32[36,768]{1,0:T(8,128)S(1)} %reshape.10.links_ref) | copy-start | bytes 331780
  14.8 2.0 %copy-start = (bf16[2,384,3,1,768]{4,1,3,2,0:T(8,128)(2,1)S(1)}, bf16[2,384,3,1,768]{4,1,3,2,0:T(8,128)(2,1)}, u32[]{:S(2)}) copy-start(bf16[2,384,3,1,768]{4,1,3,2,0:T(8,128)(2,1)} %param.2) | copy-start | bytes 10616836
  29.6 16.2 %collective-permute-start = (bf16[768,384]{1,0:T(8,128)(2,1)S(1)}, bf16[768,384]{1,0:T(8,128)(2,1)S(1)}, u32[]{:S(2)}, u32[]{:S(2)}) collective-permute-start(bf16[768,384]{1,0:T(8,128)(2,1)S(1)} %get-tuple-element.10), channel_id=1, source_target_pairs={{1,0},{3,2},{5,4},{7,6},{9,8},{11,10},{13,12},{15,14},{17,16},{19,... | collective-permute-start | bytes 1769480 | tf_op jit(solution)/shard_map/ppermute | solution.py:249
  30.9 0.9 %copy-start.2 = (f32[36,768]{1,0:T(8,128)S(1)}, f32[36,768]{1,0:T(8,128)}, u32[]{:S(2)}) copy-start(f32[36,768]{1,0:T(8,128)} %copy-done.1) | copy-start | bytes 331780
  41.9 9.1 %collective-permute-start.7 = (bf16[768,384]{1,0:T(8,128)(2,1)}, bf16[768,384]{1,0:T(8,128)(2,1)}, u32[]{:S(2)}, u32[]{:S(2)}) collective-permute-start(bf16[768,384]{1,0:T(8,128)(2,1)} %shard_map.30), channel_id=1, source_target_pairs={{0,1},{2,3},{4,5},{6,7},{8,9},{10,11},{12,13},{14,15},{16,17},{18,... | collective-permute-start | bytes 1769480 | tf_op jit(solution)/shard_map/ppermute | solution.py:252
  45.9 1.0 %copy-start.3 = (f32[768,384]{1,0:T(8,128)}, f32[768,384]{1,0:T(8,128)S(1)}, u32[]{:S(2)}) copy-start(f32[768,384]{1,0:T(8,128)S(1)} %convert_add_fusion) | copy-start | bytes 3538948
  47.7 10.2 %collective-permute-start.1 = (bf16[384,384]{1,0:T(8,128)(2,1)}, bf16[384,384]{1,0:T(8,128)(2,1)}, u32[]{:S(2)}, u32[]{:S(2)}) collective-permute-start(bf16[384,384]{1,0:T(8,128)(2,1)} %slice.93), channel_id=1, source_target_pairs={{0,2},{2,0},{4,6},{6,4},{8,10},{10,8},{12,14},{14,12},{16,18},{18,... | collective-permute-start | bytes 884744 | tf_op jit(solution)/shard_map/ppermute | solution.py:240
  49.6 8.3 %copy-start.4 = (f32[768,384]{1,0:T(8,128)S(1)}, f32[768,384]{1,0:T(8,128)}, u32[]{:S(2)}) copy-start(f32[768,384]{1,0:T(8,128)} %copy-done.3) | copy-start | bytes 3538948
  57.2 11.4 %collective-permute-start.8 = (bf16[384,384]{1,0:T(8,128)(2,1)S(1)}, bf16[384,384]{1,0:T(8,128)(2,1)S(1)}, u32[]{:S(2)}, u32[]{:S(2)}) collective-permute-start(bf16[384,384]{1,0:T(8,128)(2,1)S(1)} %get-tuple-element.12), channel_id=1, source_target_pairs={{1,3},{3,1},{5,7},{7,5},{9,11},{11,9},{13,15},{15,13},{17,19},{19,... | collective-permute-start | bytes 884744 | tf_op jit(solution)/shard_map/ppermute | solution.py:240
  59.0 11.1 %collective-permute-start.2 = (bf16[96,384]{1,0:T(8,128)(2,1)S(1)}, bf16[96,384]{1,0:T(8,128)(2,1)S(1)}, u32[]{:S(2)}, u32[]{:S(2)}) collective-permute-start(bf16[96,384]{1,0:T(8,128)(2,1)S(1)} %get-tuple-element.17), channel_id=1, source_target_pairs={{0,4},{2,6},{4,8},{6,10},{8,12},{10,14},{12,0},{14,2},{16,20},{18,... | collective-permute-start | bytes 221192 | tf_op jit(solution)/shard_map/ppermute | solution.py:240
  60.9 9.8 %collective-permute-start.4 = (bf16[96,384]{1,0:T(8,128)(2,1)S(1)}, bf16[96,384]{1,0:T(8,128)(2,1)S(1)}, u32[]{:S(2)}, u32[]{:S(2)}) collective-permute-start(bf16[96,384]{1,0:T(8,128)(2,1)S(1)} %get-tuple-element.18), channel_id=1, source_target_pairs={{0,12},{2,14},{4,0},{6,2},{8,4},{10,6},{12,8},{14,10},{16,28},{18,... | collective-permute-start | bytes 221192 | tf_op jit(solution)/shard_map/ppermute | solution.py:240
  66.6 7.3 %collective-permute-start.3 = (bf16[96,384]{1,0:T(8,128)(2,1)S(1)}, bf16[96,384]{1,0:T(8,128)(2,1)S(1)}, u32[]{:S(2)}, u32[]{:S(2)}) collective-permute-start(bf16[96,384]{1,0:T(8,128)(2,1)S(1)} %get-tuple-element.19), channel_id=1, source_target_pairs={{0,8},{2,10},{4,12},{6,14},{8,0},{10,2},{12,4},{14,6},{16,24},{18,... | collective-permute-start | bytes 221192 | tf_op jit(solution)/shard_map/ppermute | solution.py:240
  68.7 5.3 %collective-permute-start.9 = (bf16[96,384]{1,0:T(8,128)(2,1)S(1)}, bf16[96,384]{1,0:T(8,128)(2,1)S(1)}, u32[]{:S(2)}, u32[]{:S(2)}) collective-permute-start(bf16[96,384]{1,0:T(8,128)(2,1)S(1)} %get-tuple-element.20), channel_id=1, source_target_pairs={{1,5},{3,7},{5,9},{7,11},{9,13},{11,15},{13,1},{15,3},{17,21},{19,... | collective-permute-start | bytes 221192 | tf_op jit(solution)/shard_map/ppermute | solution.py:240
  69.4 4.6 %collective-permute-start.11 = (bf16[96,384]{1,0:T(8,128)(2,1)S(1)}, bf16[96,384]{1,0:T(8,128)(2,1)S(1)}, u32[]{:S(2)}, u32[]{:S(2)}) collective-permute-start(bf16[96,384]{1,0:T(8,128)(2,1)S(1)} %get-tuple-element.21), channel_id=1, source_target_pairs={{1,13},{3,15},{5,1},{7,3},{9,5},{11,7},{13,9},{15,11},{17,29},{19,... | collective-permute-start | bytes 221192 | tf_op jit(solution)/shard_map/ppermute | solution.py:240
  70.0 4.0 %collective-permute-start.10 = (bf16[96,384]{1,0:T(8,128)(2,1)S(1)}, bf16[96,384]{1,0:T(8,128)(2,1)S(1)}, u32[]{:S(2)}, u32[]{:S(2)}) collective-permute-start(bf16[96,384]{1,0:T(8,128)(2,1)S(1)} %get-tuple-element.22), channel_id=1, source_target_pairs={{1,9},{3,11},{5,13},{7,15},{9,1},{11,3},{13,5},{15,7},{17,25},{19,... | collective-permute-start | bytes 221192 | tf_op jit(solution)/shard_map/ppermute | solution.py:240
  74.1 5.2 %collective-permute-start.12 = (f32[48,384]{1,0:T(8,128)S(1)}, f32[48,384]{1,0:T(8,128)S(1)}, u32[]{:S(2)}, u32[]{:S(2)}) collective-permute-start(f32[48,384]{1,0:T(8,128)S(1)} %slice_select_fusion.1), channel_id=1, source_target_pairs={{0,1},{1,0},{2,3},{3,2},{4,5},{5,4},{6,7},{7,6},{8,9},{9,8},{10,11... | collective-permute-start | bytes 221192 | tf_op jit(solution)/shard_map/ppermute | solution.py:26

commit v14 on v9

--- a/solution.py
+++ b/solution.py
@@ -77,24 +77,28 @@
     return lax.dot_general(left, right, (((1,), (1,)), ((), ())), preferred_element_type=jnp.float32)
 
 
-def finish(sum_re, sum_im, slabs, core, order, acc, send, keep):
-    count = send.shape[0]
+def finish(sum_re, sum_im, slabs, core, order, acc, sends, keeps):
+    count = acc.shape[1]
     own = count // slabs
     acc[0] = sum_re - sum_re.T
     acc[1] = sum_im + sum_im.T
     if not rows_by_own(slabs, own):
-        send[...] = acc[1 - core].astype(jnp.bfloat16)
-        keep[...] = acc[core]
+        size = count // 2
+        for piece in range(len(sends)):
+            at = slice(piece * size, (piece + 1) * size) if len(sends) == 2 else slice(0, count)
+            sends[piece][...] = acc[1 - core, at, :].astype(jnp.bfloat16)
+            keeps[piece][...] = acc[core, at, :]
         return
-    for k in range(slabs // 2):
-        block = slice(k * 2 * own, (k + 1) * 2 * own)
+    each = len(order) // len(sends)
+    for k, to in enumerate(order):
+        block = slice(k % each * 2 * own, (k % each + 1) * 2 * own)
 
         def rows(which):
-            at = pl.ds(pl.multiple_of((2 * order[k] + which) * own, 8), own)
+            at = pl.ds(pl.multiple_of((2 * to + which) * own, 8), own)
             return jnp.concatenate([acc[0, at, :], acc[1, at, :]], axis=0)
 
-        send[block, :] = rows(1 - core).astype(jnp.bfloat16)
-        keep[block, :] = rows(core)
+        sends[k // each][block, :] = rows(1 - core).astype(jnp.bfloat16)
+        keeps[k // each][block, :] = rows(core)
 
 
 def x_kernel(slabs, where_ref, field_ref, links_ref, send, keep, right, acc):
@@ -111,7 +115,7 @@
             product[part] = term if b == 0 else product[part] + term
     sum_re = product[0][:, :count] + product[1][:, count:]
     sum_im = product[0][:, count:] - product[1][:, :count]
-    finish(sum_re, sum_im, slabs, where_ref[0], range(slabs // 2), acc, send, keep)
+    finish(sum_re, sum_im, slabs, where_ref[0], range(slabs // 2), acc, [send], [keep])
 
 
 def w_kernel(field_ref, links_ref, after_ref, w_ref):
@@ -128,7 +132,8 @@
     return [to + 1 - low for to in ahead] + [to + low for to in ahead]
 
 
-def z_kernel(slabs, where_ref, w_ref, face_hbm, send, keep, right, acc, sems):
+def z_kernel(slabs, where_ref, w_ref, face_hbm, *refs):
+    sends, keeps, (right, acc, sems) = refs[:2], refs[2:4], refs[4:]
     count = w_ref.shape[1]
     copies = []
     for b in range(3):
@@ -149,7 +154,7 @@
             product[part] = term if b == 0 else product[part] + term
     sum_re = product[0][:, :count] + product[1][:, count:]
     sum_im = product[0][:, count:] - product[1][:, :count]
-    finish(sum_re, sum_im, slabs, where_ref[0], z_order(where_ref[1], slabs // 2), acc, send, keep)
+    finish(sum_re, sum_im, slabs, where_ref[0], z_order(where_ref[1], slabs // 2), acc, sends, keeps)
 
 
 def call(body, outs, specs, scratch, mib, flops, moved):
@@ -209,23 +214,26 @@
         return jnp.sum(got.reshape(blocks).astype(jnp.float32), axis=0).reshape(2, own, count)
 
     got_x = exchanged(chip_x)
-    send_z, keep_z = call(
-        functools.partial(z_kernel, slabs), halves, [SMEM, VMEM, ANY],
+    quarters = [jax.ShapeDtypeStruct((count // 2, count), h.dtype) for h in halves for _ in range(2)]
+    send_other, send_mine, keep_other, keep_mine = call(
+        functools.partial(z_kernel, slabs), quarters, [SMEM, VMEM, ANY],
         [stacked, square, pltpu.SemaphoreType.DMA((6,))], 14, flops, moved,
     )(where, w, face)
-    send_z, got_x = lax.optimization_barrier((send_z, got_x))
-    chip_z = keep_z + swapped(send_z, "gz").astype(jnp.float32)
+    send_other, got_x = lax.optimization_barrier((send_other, got_x))
+    other = keep_other + swapped(send_other, "gz").astype(jnp.float32)
+    mine = keep_mine + swapped(send_mine, "gz").astype(jnp.float32)
     if rows_by_own(slabs, own):
-        half = count // 2
-        other = chip_z[:half].astype(jnp.bfloat16)
-        near = lax.ppermute(other, "gz", [(i, i ^ 2) for i in range(slabs)])
-        line = chip_z[half:] + near.astype(jnp.float32)
-        total_z = line[: 2 * own]
-        for r in range(1, slabs // 4):
-            block = line[r * 2 * own : (r + 1) * 2 * own].astype(jnp.bfloat16)
+        along = slabs // 4
+        size = 2 * own
+        near = lax.ppermute(other.astype(jnp.bfloat16), "gz", [(i, i ^ 2) for i in range(slabs)])
+        line = mine + near.astype(jnp.float32)
+        total_z = line[:size]
+        for r in range(1, along):
+            block = line[r * size : (r + 1) * size].astype(jnp.bfloat16)
             total_z = total_z + passed_along(block, "gz", 4 * r).astype(jnp.float32)
         total_z = total_z.reshape(2, own, count)
     else:
+        chip_z = jnp.concatenate([other, mine], axis=0)
         total_z = total(exchanged(chip_z.astype(jnp.bfloat16)))
     both = jnp.concatenate([total(got_x), total_z], axis=0)
     return jnp.transpose(both, (1, 0, 2)) * scale

time: 70.4 us -> 70.1 us (level)
    ppermute x2 -> x3, waiting for transfers between devices: 3.14 us -> 2.52 us  [swapped(): lax.ppermute(block, axis, [(i, i ^ 1) for i in range(lax.axis_size(axis))])]
  transfers between devices with their start and end apart: 8 -> 9, of which waited for: 6 -> 7; matrix products, arithmetic and copies ran while one was open for 5% -> 5% of each run, Pallas kernels for 31% -> 31%
where the time goes in v14:
time: 70.1 us; the launch traced here: 69.8 us
  waiting for transfers between devices  23.8 us (34%)
  Pallas kernels  21.9 us (31%)
  starting transfers between devices  14.5 us (21%)
  local copies, waits for them, and re-layouts  6.21 us (9%)
  other arithmetic  3.19 us (5%)
    ppermute x4, waiting for transfers between devices, passed_along(): return lax.ppermute(block, axis, route)  15.5 us
    pallas_call x1, Pallas kernels, shards(): call(functools.partial(x_kernel, slabs), halves, [SMEM, VMEM, VMEM], [sta...  12.7 us
    ppermute x4, starting transfers between devices, passed_along(): return lax.ppermute(block, axis, route)  9.73 us
    ppermute x1, waiting for transfers between devices, shards(): lax.ppermute(other.astype(jnp.bfloat16), 'gz', [(i, i ^ 2) for i in range...  5.79 us
    pallas_call x1, Pallas kernels, shards(): call(functools.partial(z_kernel, slabs), quarters, [SMEM, VMEM, ANY], [st...  5.59 us
    unnamed x10, local copies, waits for them, and re-layouts  4.79 us
    all_to_all x1, starting transfers between devices, exchanged(): return lax.all_to_all(chip, 'gz', 0, 0, axis_index_groups=groups)  4.06 us
    pallas_call x1, Pallas kernels, shards(): call(w_kernel, [jax.ShapeDtypeStruct(field.shape, jnp.bfloat16)], [VMEM,...  3.64 us
  transfers between devices with their start and end apart: 9, of which 7 were waited for; matrix products, arithmetic and copies ran while one was open for 5% of the time, Pallas kernels for 31%

profile of v14, /device:TPU:0, one launch (start us, length us, event | category | flops | bytes accessed | tf_op | source)
XLA Modules:
  0.0 69.8 jit_solution(3946127684725369847)
XLA Ops:
  0.0 5.4 %collective-permute-start.1 = (bf16[6,384,768]{2,1,0:T(8,128)(2,1)}, bf16[6,384,768]{2,1,0:T(8,128)(2,1)}, u32[]{:S(2)}, u32[]{:S(2)}) collective-permute-start(bf16[6,384,768]{2,1,0:T(8,128)(2,1)} %bitcast.10), channel_id=1, source_target_pairs={{1,0},{2,1},{3,2},{4,3},{5,4},{6,5},{7,6},{8,7},{9,8},{10,9},{11,1... | collective-permute-start | bytes 10616840 | tf_op jit(solution)/shard_map/ppermute | solution.py:22
  5.4 1.2 %reduce.2 = f32[2,2,3,3,768]{4,3,2,1,0:T(4,128)S(1)} reduce(f32[2,2,3,3,1,768]{5,4,3,2,1,0:T(1,128)} %param.3, f32[]{:T(128)} %constant.12), dimensions={4}, to_apply=%param.3.reduce_sub_computation | reduce | bytes 221188 | tf_op args[1]
  6.6 0.7 %reshape.20.links_ref = f32[36,768]{1,0:T(8,128)} reshape(f32[2,2,3,3,768]{4,3,2,1,0:T(4,128)S(1)} %reduce.2) | data formatting | bytes 221184 | tf_op jit(solution)/shard_map/reshape | solution.py:181
  7.3 0.1 pad_add_fusion.where_ref
  7.4 0.0 copy-start
  7.4 2.0 %copy-done = bf16[2,384,3,1,768]{4,1,3,2,0:T(8,128)(2,1)S(1)} copy-done((bf16[2,384,3,1,768]{4,1,3,2,0:T(8,128)(2,1)S(1)}, bf16[2,384,3,1,768]{4,1,3,2,0:T(8,128)(2,1)}, u32[]{:S(2)}) %copy-start) | copy-done | bytes 3538968
  9.4 0.0 copy-start.3
  9.4 0.9 %copy-done.3 = f32[36,768]{1,0:T(8,128)S(1)} copy-done((f32[36,768]{1,0:T(8,128)S(1)}, f32[36,768]{1,0:T(8,128)}, u32[]{:S(2)}) %copy-start.3) | copy-done | bytes 110616
  10.3 0.0 copy-start.1
  10.3 12.7 %shard_map.28 = (bf16[384,384]{1,0:T(8,128)(2,1)S(1)}, f32[384,384]{1,0:T(8,128)S(1)}) custom-call(s32[2]{0:T(128)S(1)} %pad_add_fusion.where_ref, bf16[6,384,768]{2,1,0:T(8,128)(2,1)S(1)} %bitcast.11, f32[36,768]{1,0:T(8,128)S(1)} %copy-done.3), custom_call_target="tpu_custom_call" | custom-call | flops 2717908992 | bytes 3538944 | tf_op jit(solution)/shard_map/pallas_call | solution.py:192
  23.0 0.1 collective-permute-start
  23.1 1.6 %collective-permute-done = bf16[384,384]{1,0:T(8,128)(2,1)S(1)} collective-permute-done((bf16[384,384]{1,0:T(8,128)(2,1)S(1)}, bf16[384,384]{1,0:T(8,128)(2,1)S(1)}, u32[]{:S(2)}, u32[]{:S(2)}) %collective-permute-start) | collective-permute-done | bytes 294944 | tf_op jit(solution)/shard_map/ppermute | solution.py:26
  24.7 0.8 %add_convert_fusion.after_ref = bf16[384,384]{1,0:T(8,128)(2,1)} fusion(f32[384,384]{1,0:T(8,128)S(1)} %get-tuple-element.13, bf16[384,384]{1,0:T(8,128)(2,1)S(1)} %collective-permute-done), kind=kLoop, calls=%fused_computation.1 | loop fusion | flops 442368 | bytes 1179648 | tf_op jit(solution)/shard_map/convert_element_type | solution.py:196
  25.5 4.1 %all-to-all-start = ((bf16[8,48,384]{2,1,0:T(8,128)(2,1)}), bf16[8,48,384]{2,1,0:T(8,128)(2,1)}, u32[]{:S(2)}, u32[]{:S(2)}) async-start(bf16[8,48,384]{2,1,0:T(8,128)(2,1)} %bitcast.13), calls=%async_computation | async-start | bytes 589824 | tf_op jit(solution)/shard_map/all_to_all | solution.py:211
  29.5 0.0 copy-done.1
  29.5 0.0 copy-start.2
  29.6 1.0 %copy-done.2 = bf16[384,384]{1,0:T(8,128)(2,1)S(1)} copy-done((bf16[384,384]{1,0:T(8,128)(2,1)S(1)}, bf16[384,384]{1,0:T(8,128)(2,1)}, u32[]{:S(2)}) %copy-start.2) | copy-done | bytes 294936
  30.5 0.0 copy-start.4
  30.5 0.9 %copy-done.4 = f32[36,768]{1,0:T(8,128)S(1)} copy-done((f32[36,768]{1,0:T(8,128)S(1)}, f32[36,768]{1,0:T(8,128)}, u32[]{:S(2)}) %copy-start.4) | copy-done | bytes 110616
  31.4 3.6 %shard_map.29.w_ref = bf16[6,384,768]{2,1,0:T(8,128)(2,1)S(1)} custom-call(bf16[6,384,768]{2,1,0:T(8,128)(2,1)S(1)} %bitcast.12, f32[36,768]{1,0:T(8,128)S(1)} %copy-done.4, bf16[384,384]{1,0:T(8,128)(2,1)S(1)} %copy-done.2), custom_call_target="tpu_custom_call" | custom-call | flops 19464192 | bytes 7077888 | tf_op jit(solution)/shard_map/pallas_call | solution.py:197
  35.1 12.0 %collective-permute-done.1.face_hbm = bf16[6,384,768]{2,1,0:T(8,128)(2,1)} collective-permute-done((bf16[6,384,768]{2,1,0:T(8,128)(2,1)}, bf16[6,384,768]{2,1,0:T(8,128)(2,1)}, u32[]{:S(2)}, u32[]{:S(2)}) %collective-permute-start.1) | collective-permute-done | bytes 3538976 | tf_op jit(solution)/shard_map/ppermute | solution.py:22
  47.1 5.6 %shard_map.30 = (bf16[192,384]{1,0:T(8,128)(2,1)S(1)}, bf16[192,384]{1,0:T(8,128)(2,1)S(1)}, f32[192,384]{1,0:T(8,128)S(1)}, f32[192,384]{1,0:T(8,128)S(1)}) custom-call(s32[2]{0:T(128)S(1)} %pad_add_fusion.where_ref, bf16[6,384,768]{2,1,0:T(8,128)(2,1)S(1)} %shard_map.29.w_ref, bf16[6,384,768]{2,1,0:T(8,128)(2,1)} %collective-permute-done.1.face_hbm), custom_call_target="tpu_custom_call" | custom-call | flops 2717908992 | bytes 3538944 | tf_op jit(solution)/shard_map/pallas_call | solution.py:218
  52.7 0.0 all-to-all-done
  52.7 0.1 collective-permute-start.3
  52.8 0.5 collective-permute-start.2
  53.3 0.9 %collective-permute-done.3 = bf16[192,384]{1,0:T(8,128)(2,1)S(1)} collective-permute-done((bf16[192,384]{1,0:T(8,128)(2,1)S(1)}, bf16[192,384]{1,0:T(8,128)(2,1)S(1)}, u32[]{:S(2)}, u32[]{:S(2)}) %collective-permute-start.3) | collective-permute-done | bytes 147488 | tf_op jit(solution)/shard_map/ppermute | solution.py:26
  54.2 0.1 collective-permute-start.4
  54.3 0.1 collective-permute-done.2
  54.4 5.8 %collective-permute-done.4 = bf16[192,384]{1,0:T(8,128)(2,1)S(1)} collective-permute-done((bf16[192,384]{1,0:T(8,128)(2,1)S(1)}, bf16[192,384]{1,0:T(8,128)(2,1)S(1)}, u32[]{:S(2)}, u32[]{:S(2)}) %collective-permute-start.4) | collective-permute-done | bytes 147488 | tf_op jit(solution)/shard_map/ppermute | solution.py:228
  60.2 0.1 fusion.3
  60.3 0.8 %collective-permute-start.5 = (bf16[48,384]{1,0:T(8,128)(2,1)S(1)}, bf16[48,384]{1,0:T(8,128)(2,1)S(1)}, u32[]{:S(2)}, u32[]{:S(2)}) collective-permute-start(bf16[48,384]{1,0:T(8,128)(2,1)S(1)} %get-tuple-element.23), channel_id=1, source_target_pairs={{12,0},{13,1},{14,2},{15,3},{0,4},{1,5},{2,6},{3,7},{4,8},{5,9},{6... | collective-permute-start | bytes 110600 | tf_op jit(solution)/shard_map/ppermute | solution.py:22
  61.1 3.0 %collective-permute-start.7 = (bf16[48,384]{1,0:T(8,128)(2,1)S(1)}, bf16[48,384]{1,0:T(8,128)(2,1)S(1)}, u32[]{:S(2)}, u32[]{:S(2)}) collective-permute-start(bf16[48,384]{1,0:T(8,128)(2,1)S(1)} %get-tuple-element.24), channel_id=1, source_target_pairs={{4,0},{5,1},{6,2},{7,3},{8,4},{9,5},{10,6},{11,7},{12,8},{13,9},{1... | collective-permute-start | bytes 110600 | tf_op jit(solution)/shard_map/ppermute | solution.py:22
  64.1 0.4 collective-permute-start.6
  64.6 1.0 %convert_reduce_fusion = f32[48,384]{1,0:T(8,128)S(1)} fusion(bf16[8,48,384]{2,1,0:T(8,128)(2,1)} %all-to-all-done), kind=kLoop, calls=%fused_computation | loop fusion | flops 276480 | bytes 368640 | tf_op jit(solution)/shard_map/reduce_sum | solution.py:214
  65.6 0.5 collective-permute-done.5
  66.1 0.0 collective-permute-done.7
  66.1 2.9 %collective-permute-done.6 = bf16[48,384]{1,0:T(8,128)(2,1)S(1)} collective-permute-done((bf16[48,384]{1,0:T(8,128)(2,1)S(1)}, bf16[48,384]{1,0:T(8,128)(2,1)S(1)}, u32[]{:S(2)}, u32[]{:S(2)}) %collective-permute-start.6) | collective-permute-done | bytes 36896 | tf_op jit(solution)/shard_map/ppermute | solution.py:22
  69.1 0.7 %copy.4 = f32[24,4,384]{2,1,0:T(4,128)} copy(f32[24,4,384]{2,0,1:T(8,128)S(1)} %fusion) | data formatting | bytes 294912 | tf_op jit(solution)/shard_map/mul | solution.py:239
  (4 shorter events, 0.1 us)
Async XLA Ops:
  0.0 47.1 %collective-permute-start.1 = (bf16[6,384,768]{2,1,0:T(8,128)(2,1)}, bf16[6,384,768]{2,1,0:T(8,128)(2,1)}, u32[]{:S(2)}, u32[]{:S(2)}) collective-permute-start(bf16[6,384,768]{2,1,0:T(8,128)(2,1)} %bitcast.10), channel_id=1, source_target_pairs={{1,0},{2,1},{3,2},{4,3},{5,4},{6,5},{7,6},{8,7},{9,8},{10,9},{11,1... | collective-permute-start | bytes 10616840 | tf_op jit(solution)/shard_map/ppermute | solution.py:22
  7.4 2.0 %copy-start = (bf16[2,384,3,1,768]{4,1,3,2,0:T(8,128)(2,1)S(1)}, bf16[2,384,3,1,768]{4,1,3,2,0:T(8,128)(2,1)}, u32[]{:S(2)}) copy-start(bf16[2,384,3,1,768]{4,1,3,2,0:T(8,128)(2,1)} %param.2) | copy-start | bytes 10616836
  9.4 0.9 %copy-start.3 = (f32[36,768]{1,0:T(8,128)S(1)}, f32[36,768]{1,0:T(8,128)}, u32[]{:S(2)}) copy-start(f32[36,768]{1,0:T(8,128)} %reshape.20.links_ref) | copy-start | bytes 331780
  10.3 19.2 %copy-start.1 = (bf16[2,384,3,1,768]{4,1,3,2,0:T(8,128)(2,1)S(1)}, bf16[2,384,3,1,768]{4,1,3,2,0:T(8,128)(2,1)}, u32[]{:S(2)}) copy-start(bf16[2,384,3,1,768]{4,1,3,2,0:T(8,128)(2,1)} %param.2) | copy-start | bytes 10616836
  23.0 1.6 %collective-permute-start = (bf16[384,384]{1,0:T(8,128)(2,1)S(1)}, bf16[384,384]{1,0:T(8,128)(2,1)S(1)}, u32[]{:S(2)}, u32[]{:S(2)}) collective-permute-start(bf16[384,384]{1,0:T(8,128)(2,1)S(1)} %get-tuple-element.14), channel_id=1, source_target_pairs={{0,1},{1,0},{2,3},{3,2},{4,5},{5,4},{6,7},{7,6},{8,9},{9,8},{10,11... | collective-permute-start | bytes 884744 | tf_op jit(solution)/shard_map/ppermute | solution.py:26
  25.5 27.3 %all-to-all-start = ((bf16[8,48,384]{2,1,0:T(8,128)(2,1)}), bf16[8,48,384]{2,1,0:T(8,128)(2,1)}, u32[]{:S(2)}, u32[]{:S(2)}) async-start(bf16[8,48,384]{2,1,0:T(8,128)(2,1)} %bitcast.13), calls=%async_computation | async-start | bytes 589824 | tf_op jit(solution)/shard_map/all_to_all | solution.py:211
  29.5 1.0 %copy-start.2 = (bf16[384,384]{1,0:T(8,128)(2,1)S(1)}, bf16[384,384]{1,0:T(8,128)(2,1)}, u32[]{:S(2)}) copy-start(bf16[384,384]{1,0:T(8,128)(2,1)} %add_convert_fusion.after_ref) | copy-start | bytes 884740
  30.5 0.9 %copy-start.4 = (f32[36,768]{1,0:T(8,128)S(1)}, f32[36,768]{1,0:T(8,128)}, u32[]{:S(2)}) copy-start(f32[36,768]{1,0:T(8,128)} %reshape.20.links_ref) | copy-start | bytes 331780
  52.7 1.4 %collective-permute-start.3 = (bf16[192,384]{1,0:T(8,128)(2,1)S(1)}, bf16[192,384]{1,0:T(8,128)(2,1)S(1)}, u32[]{:S(2)}, u32[]{:S(2)}) collective-permute-start(bf16[192,384]{1,0:T(8,128)(2,1)S(1)} %get-tuple-element.20), channel_id=1, source_target_pairs={{0,1},{1,0},{2,3},{3,2},{4,5},{5,4},{6,7},{7,6},{8,9},{9,8},{10,11... | collective-permute-start | bytes 442376 | tf_op jit(solution)/shard_map/ppermute | solution.py:26
  52.8 1.6 %collective-permute-start.2 = (bf16[192,384]{1,0:T(8,128)(2,1)S(1)}, bf16[192,384]{1,0:T(8,128)(2,1)S(1)}, u32[]{:S(2)}, u32[]{:S(2)}) collective-permute-start(bf16[192,384]{1,0:T(8,128)(2,1)S(1)} %get-tuple-element.18), channel_id=1, source_target_pairs={{0,1},{1,0},{2,3},{3,2},{4,5},{5,4},{6,7},{7,6},{8,9},{9,8},{10,11... | collective-permute-start | bytes 442376 | tf_op jit(solution)/shard_map/ppermute | solution.py:26
  54.2 6.0 %collective-permute-start.4 = (bf16[192,384]{1,0:T(8,128)(2,1)S(1)}, bf16[192,384]{1,0:T(8,128)(2,1)S(1)}, u32[]{:S(2)}, u32[]{:S(2)}) collective-permute-start(bf16[192,384]{1,0:T(8,128)(2,1)S(1)} %add_convert_fusion.1), channel_id=1, source_target_pairs={{0,2},{1,3},{2,0},{3,1},{4,6},{5,7},{6,4},{7,5},{8,10},{9,11},{10,... | collective-permute-start | bytes 442376 | tf_op jit(solution)/shard_map/ppermute | solution.py:228
  60.3 5.8 %collective-permute-start.5 = (bf16[48,384]{1,0:T(8,128)(2,1)S(1)}, bf16[48,384]{1,0:T(8,128)(2,1)S(1)}, u32[]{:S(2)}, u32[]{:S(2)}) collective-permute-start(bf16[48,384]{1,0:T(8,128)(2,1)S(1)} %get-tuple-element.23), channel_id=1, source_target_pairs={{12,0},{13,1},{14,2},{15,3},{0,4},{1,5},{2,6},{3,7},{4,8},{5,9},{6... | collective-permute-start | bytes 110600 | tf_op jit(solution)/shard_map/ppermute | solution.py:22
  61.1 5.0 %collective-permute-start.7 = (bf16[48,384]{1,0:T(8,128)(2,1)S(1)}, bf16[48,384]{1,0:T(8,128)(2,1)S(1)}, u32[]{:S(2)}, u32[]{:S(2)}) collective-permute-start(bf16[48,384]{1,0:T(8,128)(2,1)S(1)} %get-tuple-element.24), channel_id=1, source_target_pairs={{4,0},{5,1},{6,2},{7,3},{8,4},{9,5},{10,6},{11,7},{12,8},{13,9},{1... | collective-permute-start | bytes 110600 | tf_op jit(solution)/shard_map/ppermute | solution.py:22
  64.1 4.9 %collective-permute-start.6 = (bf16[48,384]{1,0:T(8,128)(2,1)S(1)}, bf16[48,384]{1,0:T(8,128)(2,1)S(1)}, u32[]{:S(2)}, u32[]{:S(2)}) collective-permute-start(bf16[48,384]{1,0:T(8,128)(2,1)S(1)} %get-tuple-element.25), channel_id=1, source_target_pairs={{8,0},{9,1},{10,2},{11,3},{12,4},{13,5},{14,6},{15,7},{0,8},{1,9},... | collective-permute-start | bytes 110600 | tf_op jit(solution)/shard_map/ppermute | solution.py:22

commit v15 on v9

--- a/solution.py
+++ b/solution.py
@@ -70,7 +70,7 @@
 
 
 def rows_by_own(slabs, own):
-    return slabs % 4 == 0 and own % 8 == 0
+    return slabs % 4 == 0 and own % 8 == 0 and slabs & (slabs - 1) == 0
 
 
 def inner(left, right):
@@ -122,10 +122,10 @@
 
 
 def z_order(chip, chips):
-    along = chips // 2
-    ahead = [lax.rem((chip >> 1) + r, along) * 2 for r in range(along)]
-    low = chip & 1
-    return [to + 1 - low for to in ahead] + [to + low for to in ahead]
+    flips = [0]
+    for bit in reversed(range(chips.bit_length() - 1)):
+        flips = [flip | 1 << bit for flip in flips] + flips
+    return [chip ^ flip for flip in flips]
 
 
 def z_kernel(slabs, where_ref, w_ref, face_hbm, send, keep, right, acc, sems):
@@ -216,14 +216,12 @@
     send_z, got_x = lax.optimization_barrier((send_z, got_x))
     chip_z = keep_z + swapped(send_z, "gz").astype(jnp.float32)
     if rows_by_own(slabs, own):
-        half = count // 2
-        other = chip_z[:half].astype(jnp.bfloat16)
-        near = lax.ppermute(other, "gz", [(i, i ^ 2) for i in range(slabs)])
-        line = chip_z[half:] + near.astype(jnp.float32)
-        total_z = line[: 2 * own]
-        for r in range(1, slabs // 4):
-            block = line[r * 2 * own : (r + 1) * 2 * own].astype(jnp.bfloat16)
-            total_z = total_z + passed_along(block, "gz", 4 * r).astype(jnp.float32)
+        total_z = chip_z
+        for bit in range(1, slabs.bit_length() - 1):
+            half = total_z.shape[0] // 2
+            route = [(i, i ^ (1 << bit)) for i in range(slabs)]
+            got = lax.ppermute(total_z[:half].astype(jnp.bfloat16), "gz", route)
+            total_z = total_z[half:] + got.astype(jnp.float32)
         total_z = total_z.reshape(2, own, count)
     else:
         total_z = total(exchanged(chip_z.astype(jnp.bfloat16)))

time: 70.4 us -> 71 us (level)
  waiting for transfers between devices: 24.5 us -> 26.2 us
  starting transfers between devices: 14 us -> 12.9 us
    ppermute x1 -> x3, waiting for transfers between devices: 5.88 us -> 11.1 us  [shards(): got = lax.ppermute(total_z[:half].astype(jnp.bfloat16), 'gz', route)]
    ppermute x4 -> x1, starting transfers between devices: 9.74 us -> 5.44 us  [passed_along(): return lax.ppermute(block, axis, route)]
    ppermute x4 -> x1, waiting for transfers between devices: 15.5 us -> 12 us  [passed_along(): return lax.ppermute(block, axis, route)]
    ppermute x1 -> x3, starting transfers between devices: 0.07 us -> 3.21 us  [shards(): got = lax.ppermute(total_z[:half].astype(jnp.bfloat16), 'gz', route)]
  transfers between devices with their start and end apart: 8 -> 7, of which waited for: 6 -> 6; matrix products, arithmetic and copies ran while one was open for 5% -> 5% of each run, Pallas kernels for 31% -> 31%
where the time goes in v15:
time: 71 us; the launch traced here: 70.6 us
  waiting for transfers between devices  26.2 us (37%)
  Pallas kernels  21.9 us (31%)
  starting transfers between devices  12.9 us (18%)
  local copies, waits for them, and re-layouts  6.23 us (9%)
  other arithmetic  3.2 us (5%)
    pallas_call x1, Pallas kernels, shards(): call(functools.partial(x_kernel, slabs), halves, [SMEM, VMEM, VMEM], [sta...  12.7 us
    ppermute x1, waiting for transfers between devices, passed_along(): return lax.ppermute(block, axis, route)  12 us
    ppermute x3, waiting for transfers between devices, shards(): got = lax.ppermute(total_z[:half].astype(jnp.bfloat16), 'gz', route)  11.1 us
    pallas_call x1, Pallas kernels, shards(): call(functools.partial(z_kernel, slabs), halves, [SMEM, VMEM, ANY], [stac...  5.59 us
    ppermute x1, starting transfers between devices, passed_along(): return lax.ppermute(block, axis, route)  5.44 us
    unnamed x10, local copies, waits for them, and re-layouts  4.79 us
    all_to_all x1, starting transfers between devices, exchanged(): return lax.all_to_all(chip, 'gz', 0, 0, axis_index_groups=groups)  4.06 us
    pallas_call x1, Pallas kernels, shards(): call(w_kernel, [jax.ShapeDtypeStruct(field.shape, jnp.bfloat16)], [VMEM,...  3.64 us
  transfers between devices with their start and end apart: 7, of which 6 were waited for; matrix products, arithmetic and copies ran while one was open for 5% of the time, Pallas kernels for 31%

profile of v15, /device:TPU:0, one launch (start us, length us, event | category | flops | bytes accessed | tf_op | source)
XLA Modules:
  0.0 70.6 jit_solution(4506368552895412965)
XLA Ops:
  0.0 5.4 %collective-permute-start.1 = (bf16[6,384,768]{2,1,0:T(8,128)(2,1)}, bf16[6,384,768]{2,1,0:T(8,128)(2,1)}, u32[]{:S(2)}, u32[]{:S(2)}) collective-permute-start(bf16[6,384,768]{2,1,0:T(8,128)(2,1)} %bitcast.10), channel_id=1, source_target_pairs={{1,0},{2,1},{3,2},{4,3},{5,4},{6,5},{7,6},{8,7},{9,8},{10,9},{11,1... | collective-permute-start | bytes 10616840 | tf_op jit(solution)/shard_map/ppermute | solution.py:22
  5.4 1.2 %reduce.2 = f32[2,2,3,3,768]{4,3,2,1,0:T(4,128)S(1)} reduce(f32[2,2,3,3,1,768]{5,4,3,2,1,0:T(1,128)} %param.3, f32[]{:T(128)} %constant.12), dimensions={4}, to_apply=%param.3.reduce_sub_computation | reduce | bytes 221188 | tf_op args[1]
  6.6 0.7 reshape.20.links_ref
  7.3 0.1 pad_add_fusion.where_ref
  7.4 0.0 copy-start
  7.4 2.0 %copy-done = bf16[2,384,3,1,768]{4,1,3,2,0:T(8,128)(2,1)S(1)} copy-done((bf16[2,384,3,1,768]{4,1,3,2,0:T(8,128)(2,1)S(1)}, bf16[2,384,3,1,768]{4,1,3,2,0:T(8,128)(2,1)}, u32[]{:S(2)}) %copy-start) | copy-done | bytes 3538968
  9.4 0.0 copy-start.3
  9.4 0.9 %copy-done.3 = f32[36,768]{1,0:T(8,128)S(1)} copy-done((f32[36,768]{1,0:T(8,128)S(1)}, f32[36,768]{1,0:T(8,128)}, u32[]{:S(2)}) %copy-start.3) | copy-done | bytes 110616
  10.3 0.0 copy-start.1
  10.3 12.7 %shard_map.28 = (bf16[384,384]{1,0:T(8,128)(2,1)S(1)}, f32[384,384]{1,0:T(8,128)S(1)}) custom-call(s32[2]{0:T(128)S(1)} %pad_add_fusion.where_ref, bf16[6,384,768]{2,1,0:T(8,128)(2,1)S(1)} %bitcast.11, f32[36,768]{1,0:T(8,128)S(1)} %copy-done.3), custom_call_target="tpu_custom_call" | custom-call | flops 2717908992 | bytes 3538944 | tf_op jit(solution)/shard_map/pallas_call | solution.py:187
  23.0 0.1 collective-permute-start
  23.1 1.6 %collective-permute-done = bf16[384,384]{1,0:T(8,128)(2,1)S(1)} collective-permute-done((bf16[384,384]{1,0:T(8,128)(2,1)S(1)}, bf16[384,384]{1,0:T(8,128)(2,1)S(1)}, u32[]{:S(2)}, u32[]{:S(2)}) %collective-permute-start) | collective-permute-done | bytes 294944 | tf_op jit(solution)/shard_map/ppermute | solution.py:26
  24.7 0.8 %add_convert_fusion.after_ref = bf16[384,384]{1,0:T(8,128)(2,1)} fusion(f32[384,384]{1,0:T(8,128)S(1)} %get-tuple-element.11, bf16[384,384]{1,0:T(8,128)(2,1)S(1)} %collective-permute-done), kind=kLoop, calls=%fused_computation.2 | loop fusion | flops 442368 | bytes 1179648 | tf_op jit(solution)/shard_map/convert_element_type | solution.py:191
  25.5 4.1 %all-to-all-start = ((bf16[8,48,384]{2,1,0:T(8,128)(2,1)}), bf16[8,48,384]{2,1,0:T(8,128)(2,1)}, u32[]{:S(2)}, u32[]{:S(2)}) async-start(bf16[8,48,384]{2,1,0:T(8,128)(2,1)} %bitcast.13), calls=%async_computation | async-start | bytes 589824 | tf_op jit(solution)/shard_map/all_to_all | solution.py:206
  29.5 0.0 copy-done.1
  29.5 0.0 copy-start.2
  29.6 1.0 %copy-done.2 = bf16[384,384]{1,0:T(8,128)(2,1)S(1)} copy-done((bf16[384,384]{1,0:T(8,128)(2,1)S(1)}, bf16[384,384]{1,0:T(8,128)(2,1)}, u32[]{:S(2)}) %copy-start.2) | copy-done | bytes 294936
  30.5 0.0 copy-start.4
  30.5 0.9 %copy-done.4 = f32[36,768]{1,0:T(8,128)S(1)} copy-done((f32[36,768]{1,0:T(8,128)S(1)}, f32[36,768]{1,0:T(8,128)}, u32[]{:S(2)}) %copy-start.4) | copy-done | bytes 110616
  31.4 3.6 %shard_map.29.w_ref = bf16[6,384,768]{2,1,0:T(8,128)(2,1)S(1)} custom-call(bf16[6,384,768]{2,1,0:T(8,128)(2,1)S(1)} %bitcast.12, f32[36,768]{1,0:T(8,128)S(1)} %copy-done.4, bf16[384,384]{1,0:T(8,128)(2,1)S(1)} %copy-done.2), custom_call_target="tpu_custom_call" | custom-call | flops 19464192 | bytes 7077888 | tf_op jit(solution)/shard_map/pallas_call | solution.py:192
  35.1 12.0 %collective-permute-done.1.face_hbm = bf16[6,384,768]{2,1,0:T(8,128)(2,1)} collective-permute-done((bf16[6,384,768]{2,1,0:T(8,128)(2,1)}, bf16[6,384,768]{2,1,0:T(8,128)(2,1)}, u32[]{:S(2)}, u32[]{:S(2)}) %collective-permute-start.1) | collective-permute-done | bytes 3538976 | tf_op jit(solution)/shard_map/ppermute | solution.py:22
  47.1 5.6 %shard_map.30 = (bf16[384,384]{1,0:T(8,128)(2,1)S(1)}, f32[384,384]{1,0:T(8,128)S(1)}) custom-call(s32[2]{0:T(128)S(1)} %pad_add_fusion.where_ref, bf16[6,384,768]{2,1,0:T(8,128)(2,1)S(1)} %shard_map.29.w_ref, bf16[6,384,768]{2,1,0:T(8,128)(2,1)} %collective-permute-done.1.face_hbm), custom_call_target="tpu_custom_call" | custom-call | flops 2717908992 | bytes 3538944 | tf_op jit(solution)/shard_map/pallas_call | solution.py:212
  52.7 0.0 all-to-all-done
  52.7 0.1 collective-permute-start.2
  52.8 1.6 %collective-permute-done.2 = bf16[384,384]{1,0:T(8,128)(2,1)S(1)} collective-permute-done((bf16[384,384]{1,0:T(8,128)(2,1)S(1)}, bf16[384,384]{1,0:T(8,128)(2,1)S(1)}, u32[]{:S(2)}, u32[]{:S(2)}) %collective-permute-start.2) | collective-permute-done | bytes 294944 | tf_op jit(solution)/shard_map/ppermute | solution.py:26
  54.4 0.1 convert_add_fusion
  54.5 0.1 collective-permute-start.3
  54.6 5.9 %collective-permute-done.3 = bf16[192,384]{1,0:T(8,128)(2,1)S(1)} collective-permute-done((bf16[192,384]{1,0:T(8,128)(2,1)S(1)}, bf16[192,384]{1,0:T(8,128)(2,1)S(1)}, u32[]{:S(2)}, u32[]{:S(2)}) %collective-permute-start.3) | collective-permute-done | bytes 147488 | tf_op jit(solution)/shard_map/ppermute | solution.py:223
  60.5 0.9 %collective-permute-start.4 = (bf16[96,384]{1,0:T(8,128)(2,1)S(1)}, bf16[96,384]{1,0:T(8,128)(2,1)S(1)}, u32[]{:S(2)}, u32[]{:S(2)}) collective-permute-start(bf16[96,384]{1,0:T(8,128)(2,1)S(1)} %slice.40), channel_id=1, source_target_pairs={{0,4},{1,5},{2,6},{3,7},{4,0},{5,1},{6,2},{7,3},{8,12},{9,13},{10,... | collective-permute-start | bytes 221192 | tf_op jit(solution)/shard_map/ppermute | solution.py:223
  61.3 3.6 %collective-permute-done.4 = bf16[96,384]{1,0:T(8,128)(2,1)S(1)} collective-permute-done((bf16[96,384]{1,0:T(8,128)(2,1)S(1)}, bf16[96,384]{1,0:T(8,128)(2,1)S(1)}, u32[]{:S(2)}, u32[]{:S(2)}) %collective-permute-start.4) | collective-permute-done | bytes 73760 | tf_op jit(solution)/shard_map/ppermute | solution.py:223
  64.9 2.3 %collective-permute-start.5 = (bf16[48,384]{1,0:T(8,128)(2,1)S(1)}, bf16[48,384]{1,0:T(8,128)(2,1)S(1)}, u32[]{:S(2)}, u32[]{:S(2)}) collective-permute-start(bf16[48,384]{1,0:T(8,128)(2,1)S(1)} %slice.41), channel_id=1, source_target_pairs={{0,8},{1,9},{2,10},{3,11},{4,12},{5,13},{6,14},{7,15},{8,0},{9,1},... | collective-permute-start | bytes 110600 | tf_op jit(solution)/shard_map/ppermute | solution.py:223
  67.2 1.0 %convert_reduce_fusion = f32[48,384]{1,0:T(8,128)S(1)} fusion(bf16[8,48,384]{2,1,0:T(8,128)(2,1)} %all-to-all-done), kind=kLoop, calls=%fused_computation.1 | loop fusion | flops 276480 | bytes 368640 | tf_op jit(solution)/shard_map/reduce_sum | solution.py:209
  68.2 1.6 %collective-permute-done.5 = bf16[48,384]{1,0:T(8,128)(2,1)S(1)} collective-permute-done((bf16[48,384]{1,0:T(8,128)(2,1)S(1)}, bf16[48,384]{1,0:T(8,128)(2,1)S(1)}, u32[]{:S(2)}, u32[]{:S(2)}) %collective-permute-start.5) | collective-permute-done | bytes 36896 | tf_op jit(solution)/shard_map/ppermute | solution.py:223
  69.9 0.7 copy.4
  (7 shorter events, 0.1 us)
Async XLA Ops:
  0.0 47.1 %collective-permute-start.1 = (bf16[6,384,768]{2,1,0:T(8,128)(2,1)}, bf16[6,384,768]{2,1,0:T(8,128)(2,1)}, u32[]{:S(2)}, u32[]{:S(2)}) collective-permute-start(bf16[6,384,768]{2,1,0:T(8,128)(2,1)} %bitcast.10), channel_id=1, source_target_pairs={{1,0},{2,1},{3,2},{4,3},{5,4},{6,5},{7,6},{8,7},{9,8},{10,9},{11,1... | collective-permute-start | bytes 10616840 | tf_op jit(solution)/shard_map/ppermute | solution.py:22
  7.4 2.0 %copy-start = (bf16[2,384,3,1,768]{4,1,3,2,0:T(8,128)(2,1)S(1)}, bf16[2,384,3,1,768]{4,1,3,2,0:T(8,128)(2,1)}, u32[]{:S(2)}) copy-start(bf16[2,384,3,1,768]{4,1,3,2,0:T(8,128)(2,1)} %param.2) | copy-start | bytes 10616836
  9.4 0.9 %copy-start.3 = (f32[36,768]{1,0:T(8,128)S(1)}, f32[36,768]{1,0:T(8,128)}, u32[]{:S(2)}) copy-start(f32[36,768]{1,0:T(8,128)} %reshape.20.links_ref) | copy-start | bytes 331780
  10.3 19.2 %copy-start.1 = (bf16[2,384,3,1,768]{4,1,3,2,0:T(8,128)(2,1)S(1)}, bf16[2,384,3,1,768]{4,1,3,2,0:T(8,128)(2,1)}, u32[]{:S(2)}) copy-start(bf16[2,384,3,1,768]{4,1,3,2,0:T(8,128)(2,1)} %param.2) | copy-start | bytes 10616836
  23.0 1.6 %collective-permute-start = (bf16[384,384]{1,0:T(8,128)(2,1)S(1)}, bf16[384,384]{1,0:T(8,128)(2,1)S(1)}, u32[]{:S(2)}, u32[]{:S(2)}) collective-permute-start(bf16[384,384]{1,0:T(8,128)(2,1)S(1)} %get-tuple-element.12), channel_id=1, source_target_pairs={{0,1},{1,0},{2,3},{3,2},{4,5},{5,4},{6,7},{7,6},{8,9},{9,8},{10,11... | collective-permute-start | bytes 884744 | tf_op jit(solution)/shard_map/ppermute | solution.py:26
  25.5 27.3 %all-to-all-start = ((bf16[8,48,384]{2,1,0:T(8,128)(2,1)}), bf16[8,48,384]{2,1,0:T(8,128)(2,1)}, u32[]{:S(2)}, u32[]{:S(2)}) async-start(bf16[8,48,384]{2,1,0:T(8,128)(2,1)} %bitcast.13), calls=%async_computation | async-start | bytes 589824 | tf_op jit(solution)/shard_map/all_to_all | solution.py:206
  29.5 1.0 %copy-start.2 = (bf16[384,384]{1,0:T(8,128)(2,1)S(1)}, bf16[384,384]{1,0:T(8,128)(2,1)}, u32[]{:S(2)}) copy-start(bf16[384,384]{1,0:T(8,128)(2,1)} %add_convert_fusion.after_ref) | copy-start | bytes 884740
  30.5 0.9 %copy-start.4 = (f32[36,768]{1,0:T(8,128)S(1)}, f32[36,768]{1,0:T(8,128)}, u32[]{:S(2)}) copy-start(f32[36,768]{1,0:T(8,128)} %reshape.20.links_ref) | copy-start | bytes 331780
  52.7 1.6 %collective-permute-start.2 = (bf16[384,384]{1,0:T(8,128)(2,1)S(1)}, bf16[384,384]{1,0:T(8,128)(2,1)S(1)}, u32[]{:S(2)}, u32[]{:S(2)}) collective-permute-start(bf16[384,384]{1,0:T(8,128)(2,1)S(1)} %get-tuple-element.16), channel_id=1, source_target_pairs={{0,1},{1,0},{2,3},{3,2},{4,5},{5,4},{6,7},{7,6},{8,9},{9,8},{10,11... | collective-permute-start | bytes 884744 | tf_op jit(solution)/shard_map/ppermute | solution.py:26
  54.5 6.0 %collective-permute-start.3 = (bf16[192,384]{1,0:T(8,128)(2,1)S(1)}, bf16[192,384]{1,0:T(8,128)(2,1)S(1)}, u32[]{:S(2)}, u32[]{:S(2)}) collective-permute-start(bf16[192,384]{1,0:T(8,128)(2,1)S(1)} %slice.39), channel_id=1, source_target_pairs={{0,2},{1,3},{2,0},{3,1},{4,6},{5,7},{6,4},{7,5},{8,10},{9,11},{10,... | collective-permute-start | bytes 442376 | tf_op jit(solution)/shard_map/ppermute | solution.py:223
  60.5 4.4 %collective-permute-start.4 = (bf16[96,384]{1,0:T(8,128)(2,1)S(1)}, bf16[96,384]{1,0:T(8,128)(2,1)S(1)}, u32[]{:S(2)}, u32[]{:S(2)}) collective-permute-start(bf16[96,384]{1,0:T(8,128)(2,1)S(1)} %slice.40), channel_id=1, source_target_pairs={{0,4},{1,5},{2,6},{3,7},{4,0},{5,1},{6,2},{7,3},{8,12},{9,13},{10,... | collective-permute-start | bytes 221192 | tf_op jit(solution)/shard_map/ppermute | solution.py:223
  64.9 4.9 %collective-permute-start.5 = (bf16[48,384]{1,0:T(8,128)(2,1)S(1)}, bf16[48,384]{1,0:T(8,128)(2,1)S(1)}, u32[]{:S(2)}, u32[]{:S(2)}) collective-permute-start(bf16[48,384]{1,0:T(8,128)(2,1)S(1)} %slice.41), channel_id=1, source_target_pairs={{0,8},{1,9},{2,10},{3,11},{4,12},{5,13},{6,14},{7,15},{8,0},{9,1},... | collective-permute-start | bytes 110600 | tf_op jit(solution)/shard_map/ppermute | solution.py:223
